TPU v7x, 32 devices: a whole 2x2x4 slice. The times are simulated.
32 devices in a mesh: seq: 8 (over z, x), tp: 4 (over y, core).
Axes of the slice: x: 2, y: 2, z: 4, core: 2. Of those that a mesh axis runs over, the one named last changes fastest.
Arguments:
- tokens: bfloat16 [1024, 2048], P('seq'), may hold values from -6 to 6
- input_heads: bfloat16 [1024, 4096], P('seq', 'tp'), may hold values from -6 to 6
- z_gate: bfloat16 [1024, 4096], P('seq', 'tp'), may hold values from -6 to 6
- b_proj: bfloat16 [1024, 128], P('seq'), may hold values from -0.5 to 0.5
- c_proj: bfloat16 [1024, 128], P('seq'), may hold values from -0.5 to 0.5
- step_size: float32 [1024, 64], P('seq', 'tp'), may hold values from 0.5 to 2
- decay_log: float32 [1024, 64], P('seq', 'tp'), as said below
- skip_gain: float32 [64], P('tp'), may hold values from 0.5 to 2
- init_state: float32 [64, 64, 128], P('tp'), may hold values from -48 to 48
- norm_gain: float32 [4096], P('tp'), may hold values from 0.1 to 1.9
- out_weight: bfloat16 [4096, 2048], P('tp'), may hold values from -0.09375 to 0.09375
- moe_gain: float32 [2048], replicated, may hold values from 0.1 to 1.9
- routes: int32 [1024, 2], P('seq'), may hold values from 0 to 7, all different within a row; in each aligned block of 128 rows (0 to 127, 128 to 255, ...) at most 64 rows name the same one
- route_weights: float32 [1024, 2], P('seq'), may hold values from 0.2 to 1
- w_gate: bfloat16 [8, 2048, 2048], P('seq', None, 'tp'), may hold values from -0.125 to 0.125
- w_up: bfloat16 [8, 2048, 2048], P('seq', None, 'tp'), may hold values from -0.125 to 0.125
- w_down: bfloat16 [8, 2048, 2048], P('seq', 'tp'), may hold values from -0.125 to 0.125
Outputs:
- mixed_out: bfloat16 [1024, 2048], P('seq', 'tp')
Inputs may be any that keep to these rules, and one draw needn't show every extreme that they name: `decay_log`: every entry is negative. `routes`: the two experts of a row differ. In each aligned block of 128 rows (the rows of one device) no expert is named by more than 64 rows, a bound that some block reaches.
All inputs are finite; a program needn't handle non-finite values.
Results may differ from a plain program's by a relative error of at most 0.02.
Values may be sent and summed in bfloat16 or wider, within the bound.
No kernel may reach another device: no remote copies, remote signals or barrier semaphores. Data moves between devices by JAX's collectives and lax.ppermute only.
A program may use at most 128 MiB of HBM per device.

v0:
```python
import jax
import jax.numpy as jnp
from jax import lax
from jax.sharding import PartitionSpec as P


def entering(part, axis, combine, identity):
    place = lax.axis_index(axis)
    gathered = jax.tree.map(lambda a: lax.all_gather(a, axis), part)
    state = jax.tree.map(lambda a, e: jnp.zeros_like(a) + jnp.asarray(e, a.dtype), part, identity)

    def one(turn, state):
        return combine(
            state, jax.tree.map(lambda a: lax.dynamic_index_in_dim(a, turn, 0, False), gathered)
        )

    return lax.fori_loop(0, place, one, state)


def rms_rows(values, scale_gain):
    wide_vals = values.astype(jnp.float32)
    mean_sq = jnp.mean(wide_vals * wide_vals, axis=-1, keepdims=True)
    return (wide_vals * lax.rsqrt(mean_sq + 1e-05) * scale_gain).astype(jnp.bfloat16)


def merge_carry(first_part, second_part):
    decay_first, state_first = first_part
    decay_second, state_second = second_part
    return (decay_first * decay_second, decay_second[:, None, None] * state_first + state_second)


def body(
    tokens,
    input_heads,
    z_gate,
    b_proj,
    c_proj,
    step_size,
    decay_log,
    skip_gain,
    init_state,
    norm_gain,
    out_weight,
    moe_gain,
    routes,
    route_weights,
    w_gate,
    w_up,
    w_down,
):
    highest = lax.Precision.HIGHEST
    tok_rows = input_heads.shape[0]
    head_count = step_size.shape[1]
    head_size = init_state.shape[1]
    x_wide = input_heads.astype(jnp.float32).reshape(tok_rows, head_count, head_size)
    input_matrix_broad = b_proj.astype(jnp.float32)
    c_wide = c_proj.astype(jnp.float32)
    cum_decay = jnp.cumsum(decay_log, axis=0)
    end_decay = cum_decay[-1]
    positions = jnp.arange(tok_rows, dtype=jnp.int32)
    causal = positions[:, None] >= positions[None, :]
    scores = jnp.einsum("in,jn->ij", c_proj, b_proj, preferred_element_type=jnp.float32)
    cum_heads = cum_decay.T
    log_gap = cum_heads[:, :, None] - cum_heads[:, None, :]
    decay_mat = jnp.where(causal, jnp.exp(jnp.where(causal, log_gap, 0.0)), 0.0)
    mix_weights = decay_mat * scores[None] * step_size.T[:, None, :]
    intra_part = jnp.einsum("hij,jhp->ihp", mix_weights, x_wide, precision=highest)
    weighted = (jnp.exp(end_decay[None, :] - cum_decay) * step_size)[:, :, None] * x_wide
    local_state = jnp.einsum("jhp,jn->hpn", weighted, input_matrix_broad, precision=highest)
    block_decay = jnp.exp(end_decay)
    prior_decay, prior_state = entering(
        (block_decay, local_state),
        "seq",
        merge_carry,
        (jnp.ones_like(block_decay), jnp.zeros_like(local_state)),
    )
    arriving_rows = prior_decay[:, None, None] * init_state + prior_state
    inter_part = (
        jnp.einsum("in,hpn->ihp", c_wide, arriving_rows, precision=highest)
        * jnp.exp(cum_decay)[:, :, None]
    )
    ssd_out = intra_part + inter_part + skip_gain[None, :, None] * x_wide
    z_wide = z_gate.astype(jnp.float32).reshape(tok_rows, head_count, head_size)
    gated_vals = ssd_out * jax.nn.silu(z_wide)
    gated_vals = gated_vals * lax.rsqrt(
        jnp.mean(gated_vals * gated_vals, axis=2, keepdims=True) + 1e-05
    )
    normed = (gated_vals.reshape(tok_rows, head_count * head_size) * norm_gain).astype(jnp.bfloat16)
    partial_value = jnp.dot(normed, out_weight, preferred_element_type=jnp.float32)
    model_width = out_weight.shape[1]
    width_share = model_width // lax.axis_size("tp")
    col_start = lax.axis_index("tp") * width_share
    seq_count = lax.axis_size("seq")
    expert_count = w_gate.shape[0] * seq_count
    slot_count = 4 * tok_rows // seq_count
    top_count = routes.shape[1]
    flat_expert = routes.reshape(-1)
    onehot = (flat_expert[:, None] == jnp.arange(expert_count, dtype=jnp.int32)[None, :]).astype(
        jnp.int32
    )
    earlier_count = jnp.cumsum(onehot, axis=0) - onehot
    slot_rank = jnp.sum(earlier_count * onehot, axis=1)
    placed = flat_expert * slot_count + slot_rank
    owners = jnp.arange(top_count * tok_rows, dtype=jnp.int32) // top_count
    source = jnp.full((expert_count * slot_count,), tok_rows, jnp.int32).at[placed].set(owners)
    proj_sum = lax.psum(partial_value.astype(jnp.bfloat16), "tp").astype(jnp.float32)
    hidden_full = (tokens.astype(jnp.float32) + proj_sum).astype(jnp.bfloat16)
    moe_in = rms_rows(hidden_full, moe_gain)
    outgoing = jnp.take(moe_in, source, axis=0, mode="fill", fill_value=0).reshape(
        expert_count, slot_count, model_width
    )
    hidden = lax.dynamic_slice_in_dim(hidden_full, col_start, width_share, 1)
    moe_rows = lax.all_to_all(outgoing, "seq", split_axis=0, concat_axis=0, tiled=True)
    src_count, item_count, full_width = moe_rows.shape
    flat_rows = moe_rows.reshape(src_count * item_count, full_width)
    gate_val = jnp.dot(flat_rows, w_gate[0], preferred_element_type=jnp.float32)
    up_val = jnp.dot(flat_rows, w_up[0], preferred_element_type=jnp.float32)
    act_vals = (jax.nn.silu(gate_val) * up_val).astype(jnp.bfloat16)
    down_val = jnp.dot(act_vals, w_down[0], preferred_element_type=jnp.float32)
    summed = lax.psum_scatter(down_val.astype(jnp.bfloat16), "tp", scatter_dimension=1, tiled=True)
    results = summed.reshape(src_count, item_count, -1)
    returned = lax.all_to_all(results, "seq", split_axis=0, concat_axis=0, tiled=True)
    chosen_indices = jnp.take(
        returned.reshape(expert_count * slot_count, width_share), placed, axis=0
    ).reshape(tok_rows, top_count, width_share)
    mixed_out = hidden.astype(jnp.float32) + jnp.sum(
        route_weights[:, :, None] * chosen_indices.astype(jnp.float32), axis=1
    )
    return mixed_out.astype(jnp.bfloat16)


def solution(mesh):
    in_specs = (
        P("seq", None),
        P("seq", "tp"),
        P("seq", "tp"),
        P("seq", None),
        P("seq", None),
        P("seq", "tp"),
        P("seq", "tp"),
        P("tp"),
        P("tp", None, None),
        P("tp"),
        P("tp", None),
        P(),
        P("seq", None),
        P("seq", None),
        P("seq", None, "tp"),
        P("seq", None, "tp"),
        P("seq", "tp", None),
    )
    out_specs = P("seq", "tp")
    return jax.shard_map(body, mesh=mesh, in_specs=in_specs, out_specs=out_specs, check_vma=False)
```

profile of v0, /device:TPU:0, one launch (start us, length us, event | category | flops | bytes accessed | tf_op | source)
XLA Modules:
  0.0 262.4 jit_solution(10566711307105107493)
XLA Ops:
  6.6 0.9 copy.52
  7.5 0.2 reduce_window_sum.26
  7.7 0.8 copy.56
  8.6 1.1 copy.55
  9.8 1.9 fusion.26
  12.2 0.7 copy.53
  13.1 0.6 reduce-window.6
  13.7 0.2 slice_reduce_fusion
  14.0 0.1 mul.172
  14.3 1.4 scatter_custom_fusion
  15.7 0.6 broadcast_in_dim.65
  16.4 22.3 %all-gather.1 = f32[8,1,16]{2,1,0:T(1,128)S(1)} all-gather(f32[1,1,16]{2,1,0:T(1,128)S(1)} %get-tuple-element.60), channel_id=1, replica_groups=mesh['seq'=8,'tp'=4] {'seq'}, dimensions={0}, use_global_device_ids=true | all-gather | bytes 576 | tf_op jit(solution)/shard_map/all_gather | solution.py:9
  38.8 49.2 %all-gather.4.cloned.1.call-done = f32[128,64,128]{2,1,0:T(8,128)} async-done(((f32[16,64,128]{2,1,0:T(8,128)}), f32[128,64,128]{2,1,0:T(8,128)}) %all-gather.4.cloned.1.call-update) | async-done | bytes 4194320 | tf_op jit(solution)/shard_map/all_gather | solution.py:9
  88.1 1.5 fusion.14
  89.6 2.3 multiply_reduce_fusion.1
  92.0 0.2 fusion.27
  92.3 1.6 convolution_convert_fusion.1
  93.9 40.1 %all-reduce.2.cloned.1.call-done = bf16[128,2048]{1,0:T(8,128)(2,1)} async-done(((bf16[128,2048]{1,0:T(8,128)(2,1)}), bf16[128,2048]{1,0:T(8,128)(2,1)}) %all-reduce.2.cloned.1.call-update) | async-done | bytes 524304 | tf_op jit(solution)/shard_map/psum | solution.py:106
  134.1 1.3 fusion.15
  135.4 0.2 fusion.17
  135.6 3.3 %gather_fusion = bf16[512,2048]{1,0:T(8,128)(2,1)} fusion(bf16[128,2048]{1,0:T(8,128)(2,1)S(1)} %fusion.17, s32[1024]{0:T(1024)S(1)} %pad_clamp_fusion.1), kind=kCustom, calls=%fused_computation | custom fusion | bytes 4196352 | tf_op jit(solution)/shard_map/jit(_take)/gather | solution.py:109
  138.9 1.8 broadcast_select_fusion
  140.8 52.8 %all_to_all.10 = bf16[8,64,2048]{2,1,0:T(8,128)(2,1)S(1)} all-to-all(bf16[8,64,2048]{2,1,0:T(8,128)(2,1)S(1)} %broadcast_select_fusion), channel_id=1, replica_groups=mesh['seq'=8,'tp'=4] {'seq'}, dimensions={0} | all-to-all | bytes 4194304 | tf_op jit(solution)/shard_map/all_to_all | solution.py:113
  193.6 1.3 copy-done.2
  194.9 2.2 fusion.3
  197.1 6.3 %convolution_convert_fusion = bf16[512,2048]{1,0:T(8,128)(2,1)} fusion(bf16[1,512,2048]{2,1,0:T(8,128)(2,1)S(1)} %copy-done, bf16[512,2048]{1,0:T(8,128)(2,1)} %bitcast.78, bf16[1,2048,512]{2,1,0:T(8,128)(2,1)} %param.34, f32[512,512]{1,0:T(8,128)} %fusion.3), kind=kOutput, calls=%fused_computation.5 | convolution fusion | flops 2150105088 | bytes 9437184 | tf_op jit(solution)/shard_map/dot_general | solution.py:119
  203.4 29.6 %reduce-scatter.2.cloned.1.call-done = bf16[512,512]{1,0:T(8,128)(2,1)} async-done(((bf16[512,2048]{1,0:T(8,128)(2,1)}), bf16[512,512]{1,0:T(8,128)(2,1)}) %reduce-scatter.2.cloned.1.call-update) | async-done | bytes 524304 | tf_op jit(solution)/shard_map/reduce_scatter | solution.py:120
  233.0 5.5 %all-to-all-start.1 = ((bf16[8,64,512]{2,1,0:T(8,128)(2,1)}), bf16[8,64,512]{2,1,0:T(8,128)(2,1)S(1)}, u32[]{:S(2)}, u32[]{:S(2)}) async-start(bf16[8,64,512]{2,1,0:T(8,128)(2,1)} %bitcast.84), calls=%async_computation.2 | async-start | bytes 1048576 | tf_op jit(solution)/shard_map/all_to_all | solution.py:122
  239.0 14.0 %all-to-all-done.1 = bf16[8,64,512]{2,1,0:T(8,128)(2,1)S(1)} async-done(((bf16[8,64,512]{2,1,0:T(8,128)(2,1)}), bf16[8,64,512]{2,1,0:T(8,128)(2,1)S(1)}, u32[]{:S(2)}, u32[]{:S(2)}) %all-to-all-start.1) | async-done | bytes 524320 | tf_op jit(solution)/shard_map/all_to_all | solution.py:122
  253.0 1.2 gather_fusion.1
  254.3 0.8 multiply_reduce_fusion
  255.1 0.7 add_convert_fusion.1
  (65 shorter events, 2.0 us)
Async XLA Ops:
  6.5 190.6 %copy-start = (bf16[1,512,2048]{2,1,0:T(8,128)(2,1)S(1)}, bf16[1,512,2048]{2,1,0:T(8,128)(2,1)}, u32[]{:S(2)}) copy-start(bf16[1,512,2048]{2,1,0:T(8,128)(2,1)} %param.35) | copy-start | bytes 6291460
  6.5 32.1 %copy-start.5 = (bf16[128,128]{1,0:T(8,128)(2,1)S(1)}, bf16[128,128]{1,0:T(8,128)(2,1)}, u32[]{:S(2)}) copy-start(bf16[128,128]{1,0:T(8,128)(2,1)} %param.22) | copy-start | bytes 98308
  6.5 5.2 %copy-start.7 = (s32[128,2]{0,1:T(2,128)S(1)}, s32[128,2]{0,1:T(2,128)}, u32[]{:S(2)}) copy-start(s32[128,2]{0,1:T(2,128)} %param.31) | copy-start | bytes 3076
  6.5 6.4 %copy-start.4 = (bf16[128,1024]{1,0:T(8,128)(2,1)S(1)}, bf16[128,1024]{1,0:T(8,128)(2,1)}, u32[]{:S(2)}) copy-start(bf16[128,1024]{1,0:T(8,128)(2,1)} %param.21) | copy-start | bytes 786436
  6.5 32.1 %copy-start.6 = (bf16[128,128]{1,0:T(8,128)(2,1)S(1)}, bf16[128,128]{1,0:T(8,128)(2,1)}, u32[]{:S(2)}) copy-start(bf16[128,128]{1,0:T(8,128)(2,1)} %param.23) | copy-start | bytes 98308
  6.5 81.5 %all-gather.4.cloned.1.call-start = ((), (), s32[]{:S(2)}) async-start(), calls=%async_computation.5 | async-start | bytes 4718592 | tf_op jit(solution)/shard_map/all_gather | solution.py:9
  11.7 122.3 %all-reduce.2.cloned.1.call-start = ((), (), s32[]{:S(2)}) async-start(), calls=%async_computation.3 | async-start | bytes 1048576 | tf_op jit(solution)/shard_map/psum | solution.py:106
  89.6 2.4 copy-start.9
  89.6 2.6 copy-start.1
  92.3 41.8 %copy-start.3 = (bf16[128,2048]{1,0:T(8,128)(2,1)S(1)}, bf16[128,2048]{1,0:T(8,128)(2,1)}, u32[]{:S(2)}) copy-start(bf16[128,2048]{1,0:T(8,128)(2,1)} %param.19) | copy-start | bytes 1572868
  93.8 41.6 %copy-start.8 = (f32[2048]{0:T(1024)S(1)}, f32[2048]{0:T(1024)}, u32[]{:S(2)}) copy-start(f32[2048]{0:T(1024)} %param.30) | copy-start | bytes 24580
  93.9 139.2 %reduce-scatter.2.cloned.1.call-start = ((), (), s32[]{:S(2)}) async-start(), calls=%async_computation.4 | async-start | bytes 2621440 | tf_op jit(solution)/shard_map/reduce_scatter | solution.py:120
  135.6 3.4 %copy-start.11 = (pred[8,64]{1,0:T(8,128)(4,1)S(1)}, pred[8,64]{1,0:T(8,128)(4,1)}, u32[]{:S(2)}) copy-start(pred[8,64]{1,0:T(8,128)(4,1)} %broadcast_in_dim.65) | copy-start | bytes 1540
  140.7 54.1 %copy-start.12 = (bf16[1,2048,512]{2,1,0:T(8,128)(2,1)S(1)}, bf16[1,2048,512]{2,1,0:T(8,128)(2,1)}, u32[]{:S(2)}) copy-start(bf16[1,2048,512]{2,1,0:T(8,128)(2,1)} %param.33) | copy-start | bytes 6291460
  193.6 1.3 copy-start.2
  203.4 35.5 %copy-start.10 = (f32[128,2]{0,1:T(2,128)S(1)}, f32[128,2]{0,1:T(2,128)}, u32[]{:S(2)}) copy-start(f32[128,2]{0,1:T(2,128)} %param.32) | copy-start | bytes 3076
  233.0 20.0 %all-to-all-start.1 = ((bf16[8,64,512]{2,1,0:T(8,128)(2,1)}), bf16[8,64,512]{2,1,0:T(8,128)(2,1)S(1)}, u32[]{:S(2)}, u32[]{:S(2)}) async-start(bf16[8,64,512]{2,1,0:T(8,128)(2,1)} %bitcast.84), calls=%async_computation.2 | async-start | bytes 1048576 | tf_op jit(solution)/shard_map/all_to_all | solution.py:122
Sparse Core Ops, SparseCore 0:
  11.8 76.1 all-gather.3
  94.0 40.0 all-reduce.1
  203.5 29.4 reduce-scatter.1
where the time goes:
time: 263 us; the launch traced here: 262 us
  waiting for transfers between devices  133 us (51%)
  blocking collectives  75.1 us (29%)
  matrix products  15.9 us (6%)
  between operations  13.4 us (5%)
  local copies, waits for them, and re-layouts  13.2 us (5%)
  other arithmetic  6.09 us (2%)
  starting transfers between devices  5.64 us (2%)
    all_to_all x1, blocking collectives, body(): lax.all_to_all(outgoing, 'seq', split_axis=0, concat_axis=0, tiled=True)  52.8 us
    all_gather x1, waiting for transfers between devices, entering(): gathered = jax.tree.map(lambda a: lax.all_gather(a, axis), part)  49.2 us
    psum x1, waiting for transfers between devices, body(): lax.psum(partial_value.astype(jnp.bfloat16), 'tp').astype(jnp.float32)  40.1 us
    reduce_scatter x1, waiting for transfers between devices, body(): lax.psum_scatter(down_val.astype(jnp.bfloat16), 'tp', scatter_dimension=1...  29.6 us
    all_gather x1, blocking collectives, entering(): gathered = jax.tree.map(lambda a: lax.all_gather(a, axis), part)  22.3 us
    all_to_all x1, waiting for transfers between devices, body(): lax.all_to_all(results, 'seq', split_axis=0, concat_axis=0, tiled=True)  14 us
    dot_general x1, matrix products, body(): down_val = jnp.dot(act_vals, w_down[0], preferred_element_type=jnp.float32)  6.27 us
    all_to_all x1, starting transfers between devices, body(): lax.all_to_all(results, 'seq', split_axis=0, concat_axis=0, tiled=True)  5.52 us
  transfers between devices with their start and end apart: 4, of which 4 were waited for; matrix products, arithmetic and copies ran while one was open for 2% of the time, Pallas kernels for 0%

commit v1 on v0

v1 whole, which is shorter than its diff:
```python
import jax
import jax.numpy as jnp
from jax import lax
from jax.sharding import PartitionSpec as P

BF = jnp.bfloat16
F32 = jnp.float32


def swap(value, bit):
    count = lax.axis_size("tp")
    return lax.ppermute(value, "tp", [(i, i ^ bit) for i in range(count)])


def sum_share(part):
    place = lax.axis_index("tp")
    rows, width = part.shape
    share = width // 4
    quarters = [part[:, k * share : (k + 1) * share] for k in range(4)]
    low = (place & 1) == 0
    keep = [jnp.where(low, quarters[0], quarters[1]), jnp.where(low, quarters[2], quarters[3])]
    give = [jnp.where(low, quarters[1], quarters[0]), jnp.where(low, quarters[3], quarters[2])]
    got = swap(jnp.stack(give).astype(BF), 1)
    first = keep[0] + got[0].astype(F32)
    second = keep[1] + got[1].astype(F32)
    near = place < 2
    last = swap(jnp.where(near, second, first).astype(BF), 2)
    return jnp.where(near, first, second) + last.astype(F32)


def join_shares(own):
    place = lax.axis_index("tp")
    far = swap(own, 2)
    near = place < 2
    pair = jnp.stack([jnp.where(near, own, far), jnp.where(near, far, own)])
    other = swap(pair, 1)
    low = (place & 1) == 0
    return jnp.concatenate(
        [
            jnp.where(low, pair[0], other[0]),
            jnp.where(low, other[0], pair[0]),
            jnp.where(low, pair[1], other[1]),
            jnp.where(low, other[1], pair[1]),
        ],
        axis=1,
    )


def exchange(value):
    return lax.all_to_all(value, "seq", split_axis=0, concat_axis=0, tiled=True)


def entering_state(local_state, block_decay, init_state):
    count = lax.axis_size("seq")
    place = lax.axis_index("seq")
    rows, width = local_state.shape
    heads = block_decay.shape[0]
    part = rows // count
    if count <= heads:
        held = heads // count
        decays = block_decay.reshape(count, held)
    else:
        held = 1
        decays = jnp.repeat(block_decay, count // heads).reshape(count, 1)
    high = decays.astype(BF)
    low = (decays - high.astype(F32)).astype(BF)
    pad = ((0, 0), (0, 8 - held))
    extra = jnp.concatenate([jnp.pad(high, pad), jnp.pad(low, pad)], axis=1)
    extra = jnp.broadcast_to(extra[:, :, None], (count, 16, width))
    out = jnp.concatenate([local_state.astype(BF).reshape(count, part, width), extra], axis=1)
    got = exchange(out)
    states = got[:, :part].astype(F32).reshape(count, held, part // held, width)
    scale = got[:, part : part + held].astype(F32) + got[:, part + 8 : part + 8 + held].astype(F32)
    carry = lax.dynamic_slice_in_dim(init_state.reshape(rows, width), place * part, part, 0)
    carry = carry.reshape(held, part // held, width)
    entering = []
    for turn in range(count):
        entering.append(carry.astype(BF))
        carry = scale[turn][:, None, :] * carry + states[turn]
    back = jnp.stack(entering).reshape(count, part, width)
    return exchange(back).reshape(rows, width)


def body(
    tokens,
    input_heads,
    z_gate,
    b_proj,
    c_proj,
    step_size,
    decay_log,
    skip_gain,
    init_state,
    norm_gain,
    out_weight,
    moe_gain,
    routes,
    route_weights,
    w_gate,
    w_up,
    w_down,
):
    highest = lax.Precision.HIGHEST
    tok_rows = input_heads.shape[0]
    head_count = step_size.shape[1]
    head_size = init_state.shape[1]
    state_size = init_state.shape[2]
    x_heads = input_heads.reshape(tok_rows, head_count, head_size)
    x_wide = x_heads.astype(F32)
    positions = jnp.arange(tok_rows, dtype=jnp.int32)
    causal = positions[:, None] >= positions[None, :]
    cum_decay = jnp.dot(causal.astype(F32), decay_log, precision=highest)
    end_decay = cum_decay[-1]
    weighted = (jnp.exp(end_decay[None, :] - cum_decay) * step_size)[:, :, None] * x_wide
    weighted = weighted.astype(BF).reshape(tok_rows, head_count * head_size)
    local_state = lax.dot_general(
        weighted, b_proj, (((0,), (0,)), ((), ())), preferred_element_type=F32
    )
    arriving = entering_state(local_state, jnp.exp(end_decay), init_state)
    scores = jnp.einsum("in,jn->ij", c_proj, b_proj, preferred_element_type=F32)
    cum_heads = cum_decay.T
    log_gap = cum_heads[:, :, None] - cum_heads[:, None, :]
    decay_mat = jnp.where(causal, jnp.exp(jnp.where(causal, log_gap, 0.0)), 0.0)
    mix_weights = (decay_mat * scores[None] * step_size.T[:, None, :]).astype(BF)
    intra_part = jnp.einsum("hij,jhp->ihp", mix_weights, x_heads, preferred_element_type=F32)
    direct = intra_part + skip_gain[None, :, None] * x_wide
    inter = lax.dot_general(
        c_proj, arriving, (((1,), (1,)), ((), ())), preferred_element_type=F32
    ).reshape(tok_rows, head_count, head_size)
    ssd_out = direct + inter * jnp.exp(cum_decay)[:, :, None]
    z_wide = z_gate.astype(F32).reshape(tok_rows, head_count, head_size)
    gated_vals = ssd_out * jax.nn.silu(z_wide)
    gated_vals = gated_vals * lax.rsqrt(
        jnp.mean(gated_vals * gated_vals, axis=2, keepdims=True) + 1e-05
    )
    normed = (gated_vals.reshape(tok_rows, head_count * head_size) * norm_gain).astype(BF)
    partial_value = jnp.dot(normed, out_weight, preferred_element_type=F32)

    model_width = out_weight.shape[1]
    share = model_width // lax.axis_size("tp")
    seq_count = lax.axis_size("seq")
    expert_count = w_gate.shape[0] * seq_count
    slot_count = 4 * tok_rows // seq_count
    top_count = routes.shape[1]
    items = top_count * tok_rows
    slots = expert_count * slot_count
    flat_expert = routes.T.reshape(-1)
    onehot = flat_expert[:, None] == jnp.arange(expert_count, dtype=jnp.int32)[None, :]
    before = jnp.arange(items)[:, None] > jnp.arange(items)[None, :]
    earlier = jnp.dot(before.astype(BF), onehot.astype(BF), preferred_element_type=F32)
    rank = jnp.sum(jnp.where(onehot, earlier, 0.0), axis=1).astype(jnp.int32)
    placed = flat_expert * slot_count + rank
    spots = placed[:, None] == jnp.arange(slots, dtype=jnp.int32)[None, :]
    pick = spots.astype(BF)
    fill = jnp.any(spots.reshape(top_count, tok_rows, slots), axis=0).astype(BF)

    place = lax.axis_index("tp")
    own_tokens = lax.dynamic_slice_in_dim(tokens, place * share, share, 1)
    hidden = (own_tokens.astype(F32) + sum_share(partial_value)).astype(BF)
    outgoing = lax.dot_general(
        fill, hidden, (((0,), (0,)), ((), ())), preferred_element_type=F32
    ).astype(BF)
    arrived = exchange(outgoing.reshape(expert_count, slot_count, share))
    rows = join_shares(arrived.reshape(slots, share))
    wide = rows.astype(F32)
    mean_sq = jnp.mean(wide * wide, axis=-1, keepdims=True)
    moe_rows = (wide * lax.rsqrt(mean_sq + 1e-05) * moe_gain).astype(BF)
    gate_val = jnp.dot(moe_rows, w_gate[0], preferred_element_type=F32)
    up_val = jnp.dot(moe_rows, w_up[0], preferred_element_type=F32)
    act_vals = (jax.nn.silu(gate_val) * up_val).astype(BF)
    down_val = jnp.dot(act_vals, w_down[0], preferred_element_type=F32)
    results = sum_share(down_val).astype(BF)
    returned = exchange(results.reshape(expert_count, slot_count, share)).reshape(slots, share)
    chosen = jnp.dot(pick, returned, preferred_element_type=F32).reshape(
        top_count, tok_rows, share
    )
    mixed_out = hidden.astype(F32) + jnp.sum(route_weights.T[:, :, None] * chosen, axis=0)
    return mixed_out.astype(BF)


def solution(mesh):
    in_specs = (
        P("seq", None),
        P("seq", "tp"),
        P("seq", "tp"),
        P("seq", None),
        P("seq", None),
        P("seq", "tp"),
        P("seq", "tp"),
        P("tp"),
        P("tp", None, None),
        P("tp"),
        P("tp", None),
        P(),
        P("seq", None),
        P("seq", None),
        P("seq", None, "tp"),
        P("seq", None, "tp"),
        P("seq", "tp", None),
    )
    out_specs = P("seq", "tp")
    return jax.shard_map(body, mesh=mesh, in_specs=in_specs, out_specs=out_specs, check_vma=False)
```

time: 263 us -> 136 us (0.52)
  waiting for transfers between devices: 133 us -> 50.3 us
  blocking collectives: 75.1 us -> 35.6 us
  between operations: 13.4 us -> 0.32 us
  starting transfers between devices: 5.64 us -> 15.8 us
  other arithmetic: 6.09 us -> 14.7 us
  local copies, waits for them, and re-layouts: 13.2 us -> 4.69 us
    all_gather x1 -> x0, waiting for transfers between devices: 49.2 us -> none  [entering(): gathered = jax.tree.map(lambda a: lax.all_gather(a, axis), part)]
    psum x1 -> x0, waiting for transfers between devices: 40.1 us -> none  [body(): lax.psum(partial_value.astype(jnp.bfloat16), 'tp').astype(jnp.float32)]
    ppermute x0 -> x6, waiting for transfers between devices: none -> 33.9 us  [swap(): return lax.ppermute(value, 'tp', [(i, i ^ bit) for i in range(count)])]
    reduce_scatter x1 -> x0, waiting for transfers between devices: 29.6 us -> none  [body(): lax.psum_scatter(down_val.astype(jnp.bfloat16), 'tp', scatter_dimension=1...]
    all_gather x1 -> x0, blocking collectives: 22.3 us -> none  [entering(): gathered = jax.tree.map(lambda a: lax.all_gather(a, axis), part)]
    all_to_all x1 -> x2, blocking collectives: 52.8 us -> 35.6 us  [exchange(): return lax.all_to_all(value, 'seq', split_axis=0, concat_axis=0, tiled=True)]
    all_to_all x1 -> x2, starting transfers between devices: 5.52 us -> 10.8 us  [exchange(): return lax.all_to_all(value, 'seq', split_axis=0, concat_axis=0, tiled=True)]
    ppermute x0 -> x6, starting transfers between devices: none -> 4.98 us  [swap(): return lax.ppermute(value, 'tp', [(i, i ^ bit) for i in range(count)])]
  transfers between devices with their start and end apart: 4 -> 8, of which waited for: 4 -> 8; matrix products, arithmetic and copies ran while one was open for 2% -> 2% of each run, Pallas kernels for 0% -> 0%
where the time goes in v1:
time: 136 us; the launch traced here: 135 us
  waiting for transfers between devices  50.3 us (37%)
  blocking collectives  35.6 us (26%)
  starting transfers between devices  15.8 us (12%)
  other arithmetic  14.7 us (11%)
  matrix products  13.7 us (10%)
  local copies, waits for them, and re-layouts  4.69 us (3%)
    all_to_all x2, blocking collectives, exchange(): return lax.all_to_all(value, 'seq', split_axis=0, concat_axis=0, tiled=True)  35.6 us
    ppermute x6, waiting for transfers between devices, swap(): return lax.ppermute(value, 'tp', [(i, i ^ bit) for i in range(count)])  33.9 us
    all_to_all x2, waiting for transfers between devices, exchange(): return lax.all_to_all(value, 'seq', split_axis=0, concat_axis=0, tiled=True)  16.4 us
    all_to_all x2, starting transfers between devices, exchange(): return lax.all_to_all(value, 'seq', split_axis=0, concat_axis=0, tiled=True)  10.8 us
    dot_general x1, matrix products, body(): down_val = jnp.dot(act_vals, w_down[0], preferred_element_type=F32)  6.63 us
    ppermute x6, starting transfers between devices, swap(): return lax.ppermute(value, 'tp', [(i, i ^ bit) for i in range(count)])  4.98 us
    unnamed x6, other arithmetic  4.61 us
    unnamed x32, local copies, waits for them, and re-layouts  4.11 us
  transfers between devices with their start and end apart: 8, of which 8 were waited for; matrix products, arithmetic and copies ran while one was open for 2% of the time, Pallas kernels for 0%

profile of v1, /device:TPU:0, one launch (start us, length us, event | category | flops | bytes accessed | tf_op | source)
XLA Modules:
  0.0 135.1 jit_solution(12533577379640398472)
XLA Ops:
  0.0 1.0 fusion.46
  1.4 1.1 copy.24
  2.6 0.8 fusion.53
  3.4 1.0 convolution_convert_fusion.1
  4.5 0.7 pad_maximum_fusion.3
  5.2 7.3 %all-to-all-start = ((bf16[8,144,128]{2,1,0:T(8,128)(2,1)}), bf16[8,144,128]{2,1,0:T(8,128)(2,1)S(1)}, u32[]{:S(2)}, u32[]{:S(2)}) async-start(bf16[8,144,128]{2,1,0:T(8,128)(2,1)} %pad_maximum_fusion.3), calls=%async_computation | async-start | bytes 589824 | tf_op jit(solution)/shard_map/all_to_all | solution.py:50
  12.5 1.5 %fusion.44 = bf16[8,128,128]{2,1,0:T(8,128)(2,1)} fusion(f32[1024,128]{1,0:T(8,128)} %bitcast.224, s32[]{:T(128)S(6)} %select_n.108), kind=kLoop, calls=%fused_computation.96 | loop fusion | bytes 65540
  13.9 8.2 %all-to-all-done = bf16[8,144,128]{2,1,0:T(8,128)(2,1)S(1)} async-done(((bf16[8,144,128]{2,1,0:T(8,128)(2,1)}), bf16[8,144,128]{2,1,0:T(8,128)(2,1)S(1)}, u32[]{:S(2)}, u32[]{:S(2)}) %all-to-all-start) | async-done | bytes 294944 | tf_op jit(solution)/shard_map/all_to_all | solution.py:50
  22.2 1.5 %convert_dynamic-update-slice_fusion.5 = (bf16[8,128,128]{2,1,0:T(8,128)(2,1)}, f32[1,128,128]{2,1,0:T(8,128)S(1)}) fusion(bf16[8,128,128]{2,1,0:T(8,128)(2,1)} %fusion.44, f32[8,128,128]{2,1,0:T(8,128)S(1)} %slice_convert_fusion, f32[1024,128]{1,0:T(8,128)} %bitcast.225, s32[]{:T(128)S(6)} %select_n.108, f32[2,128]{1,0:T(2,128)S(1)} %get-tuple-element.33), kind=kLoop, calls=%fused_computation.103 | loop fusion | flops 49152 | bytes 230404
  27.4 3.6 %all-to-all-start.1 = ((bf16[8,128,128]{2,1,0:T(8,128)(2,1)}), bf16[8,128,128]{2,1,0:T(8,128)(2,1)S(1)}, u32[]{:S(2)}, u32[]{:S(2)}) async-start(bf16[8,128,128]{2,1,0:T(8,128)(2,1)} %fusion.45), calls=%async_computation.1 | async-start | bytes 524288 | tf_op jit(solution)/shard_map/all_to_all | solution.py:50
  31.4 8.2 %all-to-all-done.1 = bf16[8,128,128]{2,1,0:T(8,128)(2,1)S(1)} async-done(((bf16[8,128,128]{2,1,0:T(8,128)(2,1)}), bf16[8,128,128]{2,1,0:T(8,128)(2,1)S(1)}, u32[]{:S(2)}, u32[]{:S(2)}) %all-to-all-start.1) | async-done | bytes 262176 | tf_op jit(solution)/shard_map/all_to_all | solution.py:50
  39.8 0.7 multiply_reduce_fusion
  40.8 1.0 copy-done.2
  41.7 0.7 fusion.56
  42.5 0.7 pad_maximum_fusion.4
  43.5 1.5 %collective-permute-done = bf16[2,128,512]{2,1,0:T(8,128)(2,1)S(1)} collective-permute-done((bf16[2,128,512]{2,1,0:T(8,128)(2,1)}, bf16[2,128,512]{2,1,0:T(8,128)(2,1)S(1)}, u32[]{:S(2)}, u32[]{:S(2)}) %collective-permute-start) | collective-permute-done | bytes 262176 | tf_op jit(solution)/shard_map/ppermute | solution.py:12
  45.1 1.6 %collective-permute-start.1 = (bf16[128,512]{1,0:T(8,128)(2,1)S(1)}, bf16[128,512]{1,0:T(8,128)(2,1)}, u32[]{:S(2)}, u32[]{:S(2)}) collective-permute-start(bf16[128,512]{1,0:T(8,128)(2,1)S(1)} %select_convert_fusion.3), channel_id=1, source_target_pairs={{0,2},{1,3},{2,0},{3,1},{4,6},{5,7},{6,4},{7,5},{8,10},{9,11},{10,... | collective-permute-start | bytes 393224 | tf_op jit(solution)/shard_map/ppermute | solution.py:12
  46.9 4.0 %collective-permute-done.1 = bf16[128,512]{1,0:T(8,128)(2,1)} collective-permute-done((bf16[128,512]{1,0:T(8,128)(2,1)S(1)}, bf16[128,512]{1,0:T(8,128)(2,1)}, u32[]{:S(2)}, u32[]{:S(2)}) %collective-permute-start.1) | collective-permute-done | bytes 131104 | tf_op jit(solution)/shard_map/ppermute | solution.py:12
  50.9 1.1 add_convert_fusion.2
  52.3 17.3 %all_to_all.20 = bf16[8,64,512]{2,1,0:T(8,128)(2,1)S(1)} all-to-all(bf16[8,64,512]{2,1,0:T(8,128)(2,1)S(1)} %bitcast.206), channel_id=1, replica_groups=mesh['seq'=8,'tp'=4] {'seq'}, dimensions={0} | all-to-all | bytes 1048576 | tf_op jit(solution)/shard_map/all_to_all | solution.py:50
  69.7 1.5 %collective-permute-start.2 = (bf16[512,512]{1,0:T(8,128)(2,1)S(1)}, bf16[512,512]{1,0:T(8,128)(2,1)S(1)}, u32[]{:S(2)}, u32[]{:S(2)}) collective-permute-start(bf16[512,512]{1,0:T(8,128)(2,1)S(1)} %bitcast.205), channel_id=1, source_target_pairs={{0,2},{1,3},{2,0},{3,1},{4,6},{5,7},{6,4},{7,5},{8,10},{9,11},{10,... | collective-permute-start | bytes 1572872 | tf_op jit(solution)/shard_map/ppermute | solution.py:12
  71.2 10.8 %collective-permute-done.2 = bf16[512,512]{1,0:T(8,128)(2,1)S(1)} collective-permute-done((bf16[512,512]{1,0:T(8,128)(2,1)S(1)}, bf16[512,512]{1,0:T(8,128)(2,1)S(1)}, u32[]{:S(2)}, u32[]{:S(2)}) %collective-permute-start.2) | collective-permute-done | bytes 524320 | tf_op jit(solution)/shard_map/ppermute | solution.py:12
  82.3 2.6 %collective-permute-done.3 = bf16[2,512,512]{2,1,0:T(8,128)(2,1)S(1)} collective-permute-done((bf16[2,512,512]{2,1,0:T(8,128)(2,1)S(1)}, bf16[2,512,512]{2,1,0:T(8,128)(2,1)S(1)}, u32[]{:S(2)}, u32[]{:S(2)}) %collective-permute-start.3) | collective-permute-done | bytes 1048608 | tf_op jit(solution)/shard_map/ppermute | solution.py:12
  86.1 2.4 %fusion.7 = f32[512,512]{1,0:T(8,128)} fusion(bf16[1,2048,512]{2,1,0:T(8,128)(2,1)S(1)} %copy-done.11, f32[2048]{0:T(1024)S(1)} %copy-done.12, f32[512]{0:T(512)S(1)} %add_rsqrt_fusion.1, bf16[512,512]{1,0:T(8,128)(2,1)S(1)} %get-tuple-element.19, bf16[512,512]{1,0:T(8,128)(2,1)S(1)} %get-tuple-element.20, bf16[512,512]{1,0:T(8,128)(2,1)S(1)} %get-tuple-element.16, ...), kind=kOutput, calls=%fused_computation.10 | convolution fusion | flops 1085276160 | bytes 5253120 | tf_op jit(solution)/shard_map/dot_general | solution.py:168
  88.5 6.6 %fusion.3 = f32[512,2048]{1,0:T(8,128)} fusion(bf16[1,512,2048]{2,1,0:T(8,128)(2,1)S(1)} %copy-done, bf16[1,2048,512]{2,1,0:T(8,128)(2,1)} %param.32, f32[512,512]{1,0:T(8,128)} %fusion.7, f32[2048]{0:T(1024)S(1)} %copy-done.12, f32[512]{0:T(512)S(1)} %add_rsqrt_fusion.1, bf16[512,512]{1,0:T(8,128)(2,1)} %copy-done.3, bf16[512,512]{1,0:T(8,128)(2,1)} %copy-done.4, ...), kind=kOutput, calls=%fused_computation.6 | convolution fusion | flops 2160590848 | bytes 11544576 | tf_op jit(solution)/shard_map/dot_general | solution.py:171
  95.1 2.5 %fusion.25 = (bf16[1,512,512]{2,1,0:T(8,128)(2,1)S(1)}, bf16[1,512,512]{2,1,0:T(8,128)(2,1)S(1)}) fusion(f32[512,2048]{1,0:T(8,128)} %fusion.3, pred[]{:T(512)S(6)} %eq.56), kind=kLoop, calls=%fused_computation.33 | loop fusion | flops 524288 | bytes 3145729 | tf_op jit(solution)/shard_map/stack | solution.py:23
  98.0 2.5 %collective-permute-done.4 = bf16[2,512,512]{2,1,0:T(8,128)(2,1)S(1)} collective-permute-done((bf16[2,512,512]{2,1,0:T(8,128)(2,1)S(1)}, bf16[2,512,512]{2,1,0:T(8,128)(2,1)S(1)}, u32[]{:S(2)}, u32[]{:S(2)}) %collective-permute-start.4) | collective-permute-done | bytes 1048608 | tf_op jit(solution)/shard_map/ppermute | solution.py:12
  101.1 1.6 %collective-permute-start.5 = (bf16[512,512]{1,0:T(8,128)(2,1)S(1)}, bf16[512,512]{1,0:T(8,128)(2,1)S(1)}, u32[]{:S(2)}, u32[]{:S(2)}) collective-permute-start(bf16[512,512]{1,0:T(8,128)(2,1)S(1)} %select_convert_fusion), channel_id=1, source_target_pairs={{0,2},{1,3},{2,0},{3,1},{4,6},{5,7},{6,4},{7,5},{8,10},{9,11},{10,... | collective-permute-start | bytes 1572872 | tf_op jit(solution)/shard_map/ppermute | solution.py:12
  102.7 12.5 %collective-permute-done.5 = bf16[512,512]{1,0:T(8,128)(2,1)S(1)} collective-permute-done((bf16[512,512]{1,0:T(8,128)(2,1)S(1)}, bf16[512,512]{1,0:T(8,128)(2,1)S(1)}, u32[]{:S(2)}, u32[]{:S(2)}) %collective-permute-start.5) | collective-permute-done | bytes 524320 | tf_op jit(solution)/shard_map/ppermute | solution.py:12
  115.1 0.6 add_convert_fusion
  115.8 18.3 %all_to_all.21 = bf16[8,64,512]{2,1,0:T(8,128)(2,1)S(1)} all-to-all(bf16[8,64,512]{2,1,0:T(8,128)(2,1)S(1)} %bitcast.207), channel_id=1, replica_groups=mesh['seq'=8,'tp'=4] {'seq'}, dimensions={0} | all-to-all | bytes 1048576 | tf_op jit(solution)/shard_map/all_to_all | solution.py:50
  134.4 0.7 add_convert_fusion.1
  (74 shorter events, 8.7 us)
Async XLA Ops:
  0.0 88.5 %copy-start = (bf16[1,512,2048]{2,1,0:T(8,128)(2,1)S(1)}, bf16[1,512,2048]{2,1,0:T(8,128)(2,1)}, u32[]{:S(2)}) copy-start(bf16[1,512,2048]{2,1,0:T(8,128)(2,1)} %param.33) | copy-start | bytes 6291460
  0.0 31.2 %copy-start.6 = (bf16[128,128]{1,0:T(8,128)(2,1)S(1)}, bf16[128,128]{1,0:T(8,128)(2,1)}, u32[]{:S(2)}) copy-start(bf16[128,128]{1,0:T(8,128)(2,1)} %param.20) | copy-start | bytes 98308
  0.0 31.0 %copy-start.5 = (bf16[128,1024]{1,0:T(8,128)(2,1)S(1)}, bf16[128,1024]{1,0:T(8,128)(2,1)}, u32[]{:S(2)}) copy-start(bf16[128,1024]{1,0:T(8,128)(2,1)} %param.19) | copy-start | bytes 786436
  0.0 31.2 %copy-start.7 = (bf16[128,128]{1,0:T(8,128)(2,1)S(1)}, bf16[128,128]{1,0:T(8,128)(2,1)}, u32[]{:S(2)}) copy-start(bf16[128,128]{1,0:T(8,128)(2,1)} %param.21) | copy-start | bytes 98308
  1.3 38.4 %copy-start.8 = (f32[128,16]{0,1:T(8,128)S(1)}, f32[128,16]{0,1:T(8,128)}, u32[]{:S(2)}) copy-start(f32[128,16]{0,1:T(8,128)} %param.22) | copy-start | bytes 24580
  1.4 38.4 %copy-start.14 = (f32[16]{0:T(128)S(1)}, f32[16]{0:T(128)}, u32[]{:S(2)}) copy-start(f32[16]{0:T(128)} %param.24) | copy-start | bytes 196
  5.2 16.9 %all-to-all-start = ((bf16[8,144,128]{2,1,0:T(8,128)(2,1)}), bf16[8,144,128]{2,1,0:T(8,128)(2,1)S(1)}, u32[]{:S(2)}, u32[]{:S(2)}) async-start(bf16[8,144,128]{2,1,0:T(8,128)(2,1)} %pad_maximum_fusion.3), calls=%async_computation | async-start | bytes 589824 | tf_op jit(solution)/shard_map/all_to_all | solution.py:50
  27.4 12.1 %all-to-all-start.1 = ((bf16[8,128,128]{2,1,0:T(8,128)(2,1)}), bf16[8,128,128]{2,1,0:T(8,128)(2,1)S(1)}, u32[]{:S(2)}, u32[]{:S(2)}) async-start(bf16[8,128,128]{2,1,0:T(8,128)(2,1)} %fusion.45), calls=%async_computation.1 | async-start | bytes 524288 | tf_op jit(solution)/shard_map/all_to_all | solution.py:50
  31.0 9.5 %copy-start.9 = (f32[1024]{0:T(1024)S(1)}, f32[1024]{0:T(1024)}, u32[]{:S(2)}) copy-start(f32[1024]{0:T(1024)} %param.26) | copy-start | bytes 12292
  39.6 2.2 %copy-start.2 = (bf16[1024,2048]{1,0:T(8,128)(2,1)S(1)}, bf16[1024,2048]{1,0:T(8,128)(2,1)}, u32[]{:S(2)}) copy-start(bf16[1024,2048]{1,0:T(8,128)(2,1)} %param.27) | copy-start | bytes 12582916
  40.5 2.8 %copy-start.10 = (s32[128,2]{0,1:T(2,128)S(1)}, s32[128,2]{0,1:T(2,128)}, u32[]{:S(2)}) copy-start(s32[128,2]{0,1:T(2,128)} %param.29) | copy-start | bytes 3076
  43.3 1.7 %collective-permute-start = (bf16[2,128,512]{2,1,0:T(8,128)(2,1)}, bf16[2,128,512]{2,1,0:T(8,128)(2,1)S(1)}, u32[]{:S(2)}, u32[]{:S(2)}) collective-permute-start(bf16[2,128,512]{2,1,0:T(8,128)(2,1)} %pad_maximum_fusion.4), channel_id=1, source_target_pairs={{0,1},{1,0},{2,3},{3,2},{4,5},{5,4},{6,7},{7,6},{8,9},{9,8},{10,11... | collective-permute-start | bytes 786440 | tf_op jit(solution)/shard_map/ppermute | solution.py:12
  45.1 5.7 %collective-permute-start.1 = (bf16[128,512]{1,0:T(8,128)(2,1)S(1)}, bf16[128,512]{1,0:T(8,128)(2,1)}, u32[]{:S(2)}, u32[]{:S(2)}) collective-permute-start(bf16[128,512]{1,0:T(8,128)(2,1)S(1)} %select_convert_fusion.3), channel_id=1, source_target_pairs={{0,2},{1,3},{2,0},{3,1},{4,6},{5,7},{6,4},{7,5},{8,10},{9,11},{10,... | collective-permute-start | bytes 393224 | tf_op jit(solution)/shard_map/ppermute | solution.py:12
  69.7 12.3 %collective-permute-start.2 = (bf16[512,512]{1,0:T(8,128)(2,1)S(1)}, bf16[512,512]{1,0:T(8,128)(2,1)S(1)}, u32[]{:S(2)}, u32[]{:S(2)}) collective-permute-start(bf16[512,512]{1,0:T(8,128)(2,1)S(1)} %bitcast.205), channel_id=1, source_target_pairs={{0,2},{1,3},{2,0},{3,1},{4,6},{5,7},{6,4},{7,5},{8,10},{9,11},{10,... | collective-permute-start | bytes 1572872 | tf_op jit(solution)/shard_map/ppermute | solution.py:12
  82.1 4.0 %copy-start.11 = (bf16[1,2048,512]{2,1,0:T(8,128)(2,1)S(1)}, bf16[1,2048,512]{2,1,0:T(8,128)(2,1)}, u32[]{:S(2)}) copy-start(bf16[1,2048,512]{2,1,0:T(8,128)(2,1)} %param.31) | copy-start | bytes 6291460
  82.1 4.0 %copy-start.12 = (f32[2048]{0:T(1024)S(1)}, f32[2048]{0:T(1024)}, u32[]{:S(2)}) copy-start(f32[2048]{0:T(1024)} %param.28) | copy-start | bytes 24580
  82.2 2.7 %collective-permute-start.3 = (bf16[2,512,512]{2,1,0:T(8,128)(2,1)S(1)}, bf16[2,512,512]{2,1,0:T(8,128)(2,1)S(1)}, u32[]{:S(2)}, u32[]{:S(2)}) collective-permute-start(bf16[2,512,512]{2,1,0:T(8,128)(2,1)S(1)} %pad_maximum_fusion.1), channel_id=1, source_target_pairs={{0,1},{1,0},{2,3},{3,2},{4,5},{5,4},{6,7},{7,6},{8,9},{9,8},{10,11... | collective-permute-start | bytes 3145736 | tf_op jit(solution)/shard_map/ppermute | solution.py:12
  85.1 0.8 copy-start.3
  85.1 1.0 copy-start.4
  95.1 5.4 %copy-start.1 = (f32[512,2048]{1,0:T(8,128)S(1)}, f32[512,2048]{1,0:T(8,128)}, u32[]{:S(2)}) copy-start(f32[512,2048]{1,0:T(8,128)} %fusion.3) | copy-start | bytes 12582916
  97.8 2.7 %collective-permute-start.4 = (bf16[2,512,512]{2,1,0:T(8,128)(2,1)S(1)}, bf16[2,512,512]{2,1,0:T(8,128)(2,1)S(1)}, u32[]{:S(2)}, u32[]{:S(2)}) collective-permute-start(bf16[2,512,512]{2,1,0:T(8,128)(2,1)S(1)} %pad_maximum_fusion.2), channel_id=1, source_target_pairs={{0,1},{1,0},{2,3},{3,2},{4,5},{5,4},{6,7},{7,6},{8,9},{9,8},{10,11... | collective-permute-start | bytes 3145736 | tf_op jit(solution)/shard_map/ppermute | solution.py:12
  101.1 33.0 %copy-start.13 = (f32[128,2]{0,1:T(2,128)S(1)}, f32[128,2]{0,1:T(2,128)}, u32[]{:S(2)}) copy-start(f32[128,2]{0,1:T(2,128)} %param.30) | copy-start | bytes 3076
  101.1 14.0 %collective-permute-start.5 = (bf16[512,512]{1,0:T(8,128)(2,1)S(1)}, bf16[512,512]{1,0:T(8,128)(2,1)S(1)}, u32[]{:S(2)}, u32[]{:S(2)}) collective-permute-start(bf16[512,512]{1,0:T(8,128)(2,1)S(1)} %select_convert_fusion), channel_id=1, source_target_pairs={{0,2},{1,3},{2,0},{3,1},{4,6},{5,7},{6,4},{7,5},{8,10},{9,11},{10,... | collective-permute-start | bytes 1572872 | tf_op jit(solution)/shard_map/ppermute | solution.py:12

commit v2 on v1

--- a/solution.py
+++ b/solution.py
@@ -1,6 +1,8 @@
 import jax
 import jax.numpy as jnp
 from jax import lax
+from jax.experimental import pallas as pl
+from jax.experimental.pallas import tpu as pltpu
 from jax.sharding import PartitionSpec as P
 
 BF = jnp.bfloat16
@@ -26,24 +28,6 @@
     near = place < 2
     last = swap(jnp.where(near, second, first).astype(BF), 2)
     return jnp.where(near, first, second) + last.astype(F32)
-
-
-def join_shares(own):
-    place = lax.axis_index("tp")
-    far = swap(own, 2)
-    near = place < 2
-    pair = jnp.stack([jnp.where(near, own, far), jnp.where(near, far, own)])
-    other = swap(pair, 1)
-    low = (place & 1) == 0
-    return jnp.concatenate(
-        [
-            jnp.where(low, pair[0], other[0]),
-            jnp.where(low, other[0], pair[0]),
-            jnp.where(low, pair[1], other[1]),
-            jnp.where(low, other[1], pair[1]),
-        ],
-        axis=1,
-    )
 
 
 def exchange(value):
@@ -69,16 +53,106 @@
     extra = jnp.broadcast_to(extra[:, :, None], (count, 16, width))
     out = jnp.concatenate([local_state.astype(BF).reshape(count, part, width), extra], axis=1)
     got = exchange(out)
-    states = got[:, :part].astype(F32).reshape(count, held, part // held, width)
-    scale = got[:, part : part + held].astype(F32) + got[:, part + 8 : part + 8 + held].astype(F32)
-    carry = lax.dynamic_slice_in_dim(init_state.reshape(rows, width), place * part, part, 0)
-    carry = carry.reshape(held, part // held, width)
-    entering = []
-    for turn in range(count):
-        entering.append(carry.astype(BF))
-        carry = scale[turn][:, None, :] * carry + states[turn]
-    back = jnp.stack(entering).reshape(count, part, width)
+    start = lax.dynamic_slice_in_dim(init_state.reshape(rows, width), place * part, part, 0)
+
+    def prefix(got_ref, start_ref, back_ref):
+        group = part // held
+        carries = [start_ref[pl.ds(h * group, group), :] for h in range(held)]
+        for turn in range(count):
+            scale = got_ref[turn, pl.ds(part, 16), :].astype(F32)
+            scale = scale[:8] + scale[8:]
+            for h in range(held):
+                spot = pl.ds(h * group, group)
+                back_ref[turn, spot, :] = carries[h].astype(BF)
+                state = got_ref[turn, spot, :].astype(F32)
+                carries[h] = scale[h : h + 1] * carries[h] + state
+
+    back = pl.pallas_call(
+        prefix,
+        out_shape=jax.ShapeDtypeStruct((count, part, width), BF),
+        name="prefix",
+    )(got, start)
     return exchange(back).reshape(rows, width)
+
+
+def expert_kernel(place_ref, own, near, far, last, gain, wg, wu, wd, give, keep, rows, total):
+    place = place_ref[0]
+    step = pl.program_id(0)
+    share = own.shape[1]
+    spots = [pl.ds(pl.multiple_of((place ^ k) * share, share), share) for k in range(4)]
+    parts = [own, near, far, last]
+
+    @pl.when(step == 0)
+    def _():
+        wide = [p[...].astype(F32) for p in parts]
+        square = sum(jnp.sum(w * w, axis=1, keepdims=True) for w in wide)
+        scale = lax.rsqrt(square * (1.0 / (4 * share)) + 1e-05)
+        for k in range(4):
+            rows[k] = (wide[k] * scale * gain[:, spots[k]]).astype(BF)
+
+    gate = up = 0.0
+    for k in range(4):
+        gate += jnp.dot(rows[k], wg[spots[k], :], preferred_element_type=F32)
+        up += jnp.dot(rows[k], wu[spots[k], :], preferred_element_type=F32)
+    act = (gate * (1.0 / (1.0 + jnp.exp(-gate))) * up).astype(BF)
+    for k in range(4):
+        down = jnp.dot(act, wd[:, spots[k]], preferred_element_type=F32)
+
+        @pl.when(step == 0)
+        def _():
+            total[k] = down
+
+        @pl.when(step > 0)
+        def _():
+            total[k] += down
+
+    @pl.when(step == pl.num_programs(0) - 1)
+    def _():
+        give[0] = total[1].astype(BF)
+        give[1] = total[3].astype(BF)
+        keep[0] = total[0]
+        keep[1] = total[2]
+
+
+def run_expert(place, own, near, far, last, gain, wg, wu, wd):
+    rows, share = own.shape
+    width, inner = wg.shape
+    tile = inner // 2
+
+    def whole(j, _):
+        return (0, 0)
+
+    part = pl.BlockSpec((rows, share), whole)
+    return pl.pallas_call(
+        expert_kernel,
+        grid_spec=pltpu.PrefetchScalarGridSpec(
+            num_scalar_prefetch=1,
+            grid=(inner // tile,),
+            in_specs=[
+                part,
+                part,
+                part,
+                part,
+                pl.BlockSpec((1, width), whole),
+                pl.BlockSpec((width, tile), lambda j, _: (0, j)),
+                pl.BlockSpec((width, tile), lambda j, _: (0, j)),
+                pl.BlockSpec((tile, width), lambda j, _: (j, 0)),
+            ],
+            out_specs=[pl.BlockSpec((2, rows, share), lambda j, _: (0, 0, 0))] * 2,
+            scratch_shapes=[pltpu.VMEM((4, rows, share), BF), pltpu.VMEM((4, rows, share), F32)],
+        ),
+        out_shape=[
+            jax.ShapeDtypeStruct((2, rows, share), BF),
+            jax.ShapeDtypeStruct((2, rows, share), F32),
+        ],
+        compiler_params=pltpu.CompilerParams(vmem_limit_bytes=40 * 1024 * 1024),
+        cost_estimate=pl.CostEstimate(
+            flops=6 * rows * width * inner,
+            bytes_accessed=6 * width * inner + 14 * rows * width,
+            transcendentals=rows * inner,
+        ),
+        name="expert",
+    )(place.reshape(1), own, near, far, last, gain.reshape(1, width), wg, wu, wd)
 
 
 def body(
@@ -160,17 +234,23 @@
     outgoing = lax.dot_general(
         fill, hidden, (((0,), (0,)), ((), ())), preferred_element_type=F32
     ).astype(BF)
-    arrived = exchange(outgoing.reshape(expert_count, slot_count, share))
-    rows = join_shares(arrived.reshape(slots, share))
-    wide = rows.astype(F32)
-    mean_sq = jnp.mean(wide * wide, axis=-1, keepdims=True)
-    moe_rows = (wide * lax.rsqrt(mean_sq + 1e-05) * moe_gain).astype(BF)
-    gate_val = jnp.dot(moe_rows, w_gate[0], preferred_element_type=F32)
-    up_val = jnp.dot(moe_rows, w_up[0], preferred_element_type=F32)
-    act_vals = (jax.nn.silu(gate_val) * up_val).astype(BF)
-    down_val = jnp.dot(act_vals, w_down[0], preferred_element_type=F32)
-    results = sum_share(down_val).astype(BF)
-    returned = exchange(results.reshape(expert_count, slot_count, share)).reshape(slots, share)
+    outgoing = outgoing.reshape(expert_count, slot_count, share)
+    cuts = 2 if slot_count % 32 == 0 else 1
+    cut = slot_count // cuts
+    returned = []
+    for turn in range(cuts):
+        own = exchange(outgoing[:, turn * cut : (turn + 1) * cut]).reshape(-1, share)
+        far = swap(own, 2)
+        near = swap(own, 1)
+        last = swap(far, 1)
+        give, keep = run_expert(
+            place, own, near, far, last, moe_gain, w_gate[0], w_up[0], w_down[0]
+        )
+        got = swap(give, 1)
+        passing = swap((keep[1] + got[1].astype(F32)).astype(BF), 2)
+        result = (keep[0] + got[0].astype(F32) + passing.astype(F32)).astype(BF)
+        returned.append(exchange(result.reshape(expert_count, cut, share)))
+    returned = jnp.concatenate(returned, axis=1).reshape(slots, share)
     chosen = jnp.dot(pick, returned, preferred_element_type=F32).reshape(
         top_count, tok_rows, share
     )

time: 136 us -> 131 us (0.963)
  starting transfers between devices: 15.8 us -> 28.1 us
  blocking collectives: 35.6 us -> 23.6 us
  Pallas kernels: 0 us -> 10.2 us
  matrix products: 13.7 us -> 4.54 us
  other arithmetic: 14.7 us -> 7.65 us
  local copies, waits for them, and re-layouts: 4.69 us -> 8.99 us
  waiting for transfers between devices: 50.3 us -> 47 us
    ppermute x6 -> x12, waiting for transfers between devices: 33.9 us -> 15.5 us  [swap(): return lax.ppermute(value, 'tp', [(i, i ^ bit) for i in range(count)])]
    all_to_all x2 -> x4, waiting for transfers between devices: 16.4 us -> 31.5 us  [exchange(): return lax.all_to_all(value, 'seq', split_axis=0, concat_axis=0, tiled=True)]
    all_to_all x2, blocking collectives: 35.6 us -> 23.6 us  [exchange(): return lax.all_to_all(value, 'seq', split_axis=0, concat_axis=0, tiled=True)]
    pallas_call x0 -> x3, Pallas kernels: none -> 10.2 us  [the longest x2 8.5 us: run_expert(): pl.pallas_call(expert_kernel, grid_spec=pltpu.PrefetchScalarGridSpec(num_...]
    dot_general x2 -> x0, matrix products: 9.04 us -> none  [the longest x1 6.63 us: body(): down_val = jnp.dot(act_vals, w_down[0], preferred_element_type=F32)]
    all_to_all x2 -> x4, starting transfers between devices: 10.8 us -> 19 us  [exchange(): return lax.all_to_all(value, 'seq', split_axis=0, concat_axis=0, tiled=True)]
    unnamed x6 -> x0, other arithmetic: 4.61 us -> none
    ppermute x6 -> x12, starting transfers between devices: 4.98 us -> 9.08 us  [swap(): return lax.ppermute(value, 'tp', [(i, i ^ bit) for i in range(count)])]
  transfers between devices with their start and end apart: 8 -> 16, of which waited for: 8 -> 9; matrix products, arithmetic and copies ran while one was open for 2% -> 3% of each run, Pallas kernels for 0% -> 7%
where the time goes in v2:
time: 131 us; the launch traced here: 130 us
  waiting for transfers between devices  47 us (36%)
  starting transfers between devices  28.1 us (21%)
  blocking collectives  23.6 us (18%)
  Pallas kernels  10.2 us (8%)
  local copies, waits for them, and re-layouts  8.99 us (7%)
  other arithmetic  7.65 us (6%)
  matrix products  4.54 us (3%)
    all_to_all x4, waiting for transfers between devices, exchange(): return lax.all_to_all(value, 'seq', split_axis=0, concat_axis=0, tiled=True)  31.5 us
    all_to_all x2, blocking collectives, exchange(): return lax.all_to_all(value, 'seq', split_axis=0, concat_axis=0, tiled=True)  23.6 us
    all_to_all x4, starting transfers between devices, exchange(): return lax.all_to_all(value, 'seq', split_axis=0, concat_axis=0, tiled=True)  19 us
    ppermute x12, waiting for transfers between devices, swap(): return lax.ppermute(value, 'tp', [(i, i ^ bit) for i in range(count)])  15.5 us
    ppermute x12, starting transfers between devices, swap(): return lax.ppermute(value, 'tp', [(i, i ^ bit) for i in range(count)])  9.08 us
    pallas_call x2, Pallas kernels, run_expert(): pl.pallas_call(expert_kernel, grid_spec=pltpu.PrefetchScalarGridSpec(num_...  8.5 us
    unnamed x37, local copies, waits for them, and re-layouts  7.05 us
  transfers between devices with their start and end apart: 16, of which 9 were waited for; matrix products, arithmetic and copies ran while one was open for 3% of the time, Pallas kernels for 7%

profile of v2, /device:TPU:0, one launch (start us, length us, event | category | flops | bytes accessed | tf_op | source)
XLA Modules:
  0.0 130.5 jit_solution(15790278795061130447)
XLA Ops:
  0.0 0.9 fusion.23
  1.3 1.1 copy.24
  3.3 1.0 convolution_convert_fusion.1
  5.1 7.3 %all-to-all-start = ((bf16[8,144,128]{2,1,0:T(8,128)(2,1)}), bf16[8,144,128]{2,1,0:T(8,128)(2,1)S(1)}, u32[]{:S(2)}, u32[]{:S(2)}) async-start(bf16[8,144,128]{2,1,0:T(8,128)(2,1)} %pad_maximum_fusion.1), calls=%async_computation | async-start | bytes 589824 | tf_op jit(solution)/shard_map/all_to_all | solution.py:34
  13.1 9.0 %all-to-all-done.got_ref = bf16[8,144,128]{2,1,0:T(8,128)(2,1)S(1)} async-done(((bf16[8,144,128]{2,1,0:T(8,128)(2,1)}), bf16[8,144,128]{2,1,0:T(8,128)(2,1)S(1)}, u32[]{:S(2)}, u32[]{:S(2)}) %all-to-all-start) | async-done | bytes 294944 | tf_op jit(solution)/shard_map/all_to_all | solution.py:34
  22.8 1.7 %prefix.1 = bf16[8,128,128]{2,1,0:T(8,128)(2,1)} custom-call(bf16[8,144,128]{2,1,0:T(8,128)(2,1)} %copy-done.9, f32[128,128]{1,0:T(8,128)} %constant_dynamic-slice_fusion.start_ref), custom_call_target="tpu_custom_call" | custom-call | tf_op jit(solution)/shard_map/prefix/pallas_call | solution.py:70
  24.5 3.6 %all-to-all-start.1 = ((bf16[8,128,128]{2,1,0:T(8,128)(2,1)}), bf16[8,128,128]{2,1,0:T(8,128)(2,1)S(1)}, u32[]{:S(2)}, u32[]{:S(2)}) async-start(bf16[8,128,128]{2,1,0:T(8,128)(2,1)} %prefix.1), calls=%async_computation.1 | async-start | bytes 524288 | tf_op jit(solution)/shard_map/all_to_all | solution.py:34
  28.4 8.2 %all-to-all-done.1 = bf16[8,128,128]{2,1,0:T(8,128)(2,1)S(1)} async-done(((bf16[8,128,128]{2,1,0:T(8,128)(2,1)}), bf16[8,128,128]{2,1,0:T(8,128)(2,1)S(1)}, u32[]{:S(2)}, u32[]{:S(2)}) %all-to-all-start.1) | async-done | bytes 262176 | tf_op jit(solution)/shard_map/all_to_all | solution.py:34
  37.8 1.0 copy-done.8
  39.6 1.0 copy-done.7
  40.9 1.3 %collective-permute-done = bf16[2,128,512]{2,1,0:T(8,128)(2,1)S(1)} collective-permute-done((bf16[2,128,512]{2,1,0:T(8,128)(2,1)S(1)}, bf16[2,128,512]{2,1,0:T(8,128)(2,1)S(1)}, u32[]{:S(2)}, u32[]{:S(2)}) %collective-permute-start) | collective-permute-done | bytes 262176 | tf_op jit(solution)/shard_map/ppermute | solution.py:14
  42.3 1.3 %select_convert_fusion = bf16[128,512]{1,0:T(8,128)(2,1)S(1)} fusion(pred[]{:T(512)S(6)} %lt.10, bf16[2,128,512]{2,1,0:T(8,128)(2,1)S(1)} %collective-permute-done, f32[128,2048]{1,0:T(8,128)} %copy-done.7, pred[]{:T(512)S(6)} %eq.54), kind=kLoop, calls=%fused_computation.43 | loop fusion | flops 524288 | bytes 1441794 | tf_op jit(solution)/shard_map/convert_element_type | solution.py:29
  43.6 1.6 %collective-permute-start.1 = (bf16[128,512]{1,0:T(8,128)(2,1)S(1)}, bf16[128,512]{1,0:T(8,128)(2,1)S(1)}, u32[]{:S(2)}, u32[]{:S(2)}) collective-permute-start(bf16[128,512]{1,0:T(8,128)(2,1)S(1)} %select_convert_fusion), channel_id=1, source_target_pairs={{0,2},{1,3},{2,0},{3,1},{4,6},{5,7},{6,4},{7,5},{8,10},{9,11},{10,... | collective-permute-start | bytes 393224 | tf_op jit(solution)/shard_map/ppermute | solution.py:14
  45.3 3.9 %collective-permute-done.1 = bf16[128,512]{1,0:T(8,128)(2,1)S(1)} collective-permute-done((bf16[128,512]{1,0:T(8,128)(2,1)S(1)}, bf16[128,512]{1,0:T(8,128)(2,1)S(1)}, u32[]{:S(2)}, u32[]{:S(2)}) %collective-permute-start.1) | collective-permute-done | bytes 131104 | tf_op jit(solution)/shard_map/ppermute | solution.py:14
  49.2 1.4 %add_convert_fusion.3 = bf16[128,512]{1,0:T(8,128)(2,1)S(1)} fusion(bf16[128,512]{1,0:T(8,128)(2,1)S(1)} %collective-permute-done.1, bf16[128,2048]{1,0:T(8,128)(2,1)} %param.17, s32[]{:T(128)S(6)} %select_n.47, pred[]{:T(512)S(6)} %lt.10, bf16[2,128,512]{2,1,0:T(8,128)(2,1)S(1)} %collective-permute-done, f32[128,2048]{1,0:T(8,128)} %copy-done.7, pred[]{:T(512)S(6)} %eq.54), kind=kLoop, calls=%fused_computation.42 | loop fusion | flops 786432 | bytes 1703942 | tf_op jit(solution)/shard_map/convert_element_type | solution.py:233
  51.7 11.9 %all_to_all.30 = bf16[8,32,512]{2,1,0:T(8,128)(2,1)S(1)} all-to-all(bf16[8,32,512]{2,1,0:T(8,128)(2,1)S(1)} %get-tuple-element.19), channel_id=1, replica_groups=mesh['seq'=8,'tp'=4] {'seq'}, dimensions={0} | all-to-all | bytes 524288 | tf_op jit(solution)/shard_map/all_to_all | solution.py:34
  63.6 3.5 %all-to-all-start.4 = ((bf16[8,32,512]{2,1,0:T(8,128)(2,1)}), bf16[8,32,512]{2,1,0:T(8,128)(2,1)S(1)}, u32[]{:S(2)}, u32[]{:S(2)}) async-start(bf16[8,32,512]{2,1,0:T(8,128)(2,1)} %get-tuple-element.20), calls=%async_computation.4 | async-start | bytes 524288 | tf_op jit(solution)/shard_map/all_to_all | solution.py:34
  67.0 1.6 %collective-permute-start.3 = (bf16[256,512]{1,0:T(8,128)(2,1)S(1)}, bf16[256,512]{1,0:T(8,128)(2,1)S(1)}, u32[]{:S(2)}, u32[]{:S(2)}) collective-permute-start(bf16[256,512]{1,0:T(8,128)(2,1)S(1)} %bitcast.108), channel_id=1, source_target_pairs={{0,2},{1,3},{2,0},{3,1},{4,6},{5,7},{6,4},{7,5},{8,10},{9,11},{10,... | collective-permute-start | bytes 786440 | tf_op jit(solution)/shard_map/ppermute | solution.py:14
  68.6 7.0 %all-to-all-done.4 = bf16[8,32,512]{2,1,0:T(8,128)(2,1)S(1)} async-done(((bf16[8,32,512]{2,1,0:T(8,128)(2,1)}), bf16[8,32,512]{2,1,0:T(8,128)(2,1)S(1)}, u32[]{:S(2)}, u32[]{:S(2)}) %all-to-all-start.4) | async-done | bytes 262176 | tf_op jit(solution)/shard_map/all_to_all | solution.py:34
  75.6 1.5 %collective-permute-start.8 = (bf16[256,512]{1,0:T(8,128)(2,1)S(1)}, bf16[256,512]{1,0:T(8,128)(2,1)S(1)}, u32[]{:S(2)}, u32[]{:S(2)}) collective-permute-start(bf16[256,512]{1,0:T(8,128)(2,1)S(1)} %bitcast.105), channel_id=1, source_target_pairs={{0,2},{1,3},{2,0},{3,1},{4,6},{5,7},{6,4},{7,5},{8,10},{9,11},{10,... | collective-permute-start | bytes 786440 | tf_op jit(solution)/shard_map/ppermute | solution.py:14
  77.6 4.3 %collective-permute-done.8.far = bf16[256,512]{1,0:T(8,128)(2,1)S(1)} collective-permute-done((bf16[256,512]{1,0:T(8,128)(2,1)S(1)}, bf16[256,512]{1,0:T(8,128)(2,1)S(1)}, u32[]{:S(2)}, u32[]{:S(2)}) %collective-permute-start.8) | collective-permute-done | bytes 262176 | tf_op jit(solution)/shard_map/ppermute | solution.py:14
  82.0 1.6 %copy-done.2 = bf16[1,2048,512]{2,1,0:T(8,128)(2,1)S(1)} copy-done((bf16[1,2048,512]{2,1,0:T(8,128)(2,1)S(1)}, bf16[1,2048,512]{2,1,0:T(8,128)(2,1)}, u32[]{:S(2)}) %copy-start.2) | copy-done | bytes 2097176
  83.6 1.6 %copy-done.4 = bf16[1,512,2048]{2,1,0:T(8,128)(2,1)S(1)} copy-done((bf16[1,512,2048]{2,1,0:T(8,128)(2,1)S(1)}, bf16[1,512,2048]{2,1,0:T(8,128)(2,1)}, u32[]{:S(2)}) %copy-start.4) | copy-done | bytes 2097176
  85.2 4.2 %expert.2 = (bf16[2,256,512]{2,1,0:T(8,128)(2,1)S(1)}, f32[2,256,512]{2,1,0:T(8,128)S(1)}) custom-call(s32[1]{0:T(128)} %bitcast.21.place_ref, bf16[256,512]{1,0:T(8,128)(2,1)S(1)} %bitcast.110, bf16[256,512]{1,0:T(8,128)(2,1)S(1)} %collective-permute-done.2.near, bf16[256,512]{1,0:T(8,128)(2,1)S(1)} %collective-permute-done.3.far, ...), custom_call_target="tpu_custom_call" | custom-call | flops 1610612736 | bytes 13631488 | tf_op jit(solution)/shard_map/expert/pallas_call | solution.py:126
  90.0 4.3 %expert.3 = (bf16[2,256,512]{2,1,0:T(8,128)(2,1)S(1)}, f32[2,256,512]{2,1,0:T(8,128)S(1)}) custom-call(s32[1]{0:T(128)} %bitcast.21.place_ref, bf16[256,512]{1,0:T(8,128)(2,1)S(1)} %bitcast.107, bf16[256,512]{1,0:T(8,128)(2,1)S(1)} %collective-permute-done.7.near, bf16[256,512]{1,0:T(8,128)(2,1)S(1)} %collective-permute-done.8.far, ...), custom_call_target="tpu_custom_call" | custom-call | flops 1610612736 | bytes 13631488 | tf_op jit(solution)/shard_map/expert/pallas_call | solution.py:126
  94.4 1.6 %collective-permute-start.6 = (bf16[256,512]{1,0:T(8,128)(2,1)S(1)}, bf16[256,512]{1,0:T(8,128)(2,1)S(1)}, u32[]{:S(2)}, u32[]{:S(2)}) collective-permute-start(bf16[256,512]{1,0:T(8,128)(2,1)S(1)} %fusion.18), channel_id=1, source_target_pairs={{0,2},{1,3},{2,0},{3,1},{4,6},{5,7},{6,4},{7,5},{8,10},{9,11},{10,... | collective-permute-start | bytes 786440 | tf_op jit(solution)/shard_map/ppermute | solution.py:14
  96.3 1.6 %collective-permute-start.11 = (bf16[256,512]{1,0:T(8,128)(2,1)S(1)}, bf16[256,512]{1,0:T(8,128)(2,1)S(1)}, u32[]{:S(2)}, u32[]{:S(2)}) collective-permute-start(bf16[256,512]{1,0:T(8,128)(2,1)S(1)} %fusion.19), channel_id=1, source_target_pairs={{0,2},{1,3},{2,0},{3,1},{4,6},{5,7},{6,4},{7,5},{8,10},{9,11},{10,... | collective-permute-start | bytes 786440 | tf_op jit(solution)/shard_map/ppermute | solution.py:14
  97.9 5.7 %collective-permute-done.6 = bf16[256,512]{1,0:T(8,128)(2,1)S(1)} collective-permute-done((bf16[256,512]{1,0:T(8,128)(2,1)S(1)}, bf16[256,512]{1,0:T(8,128)(2,1)S(1)}, u32[]{:S(2)}, u32[]{:S(2)}) %collective-permute-start.6) | collective-permute-done | bytes 262176 | tf_op jit(solution)/shard_map/ppermute | solution.py:14
  104.4 4.7 %all-to-all-start.3 = ((bf16[8,32,512]{2,1,0:T(8,128)(2,1)}), bf16[8,32,512]{2,1,0:T(8,128)(2,1)S(1)}, u32[]{:S(2)}, u32[]{:S(2)}) async-start(bf16[8,32,512]{2,1,0:T(8,128)(2,1)} %bitcast.30), calls=%async_computation.3 | async-start | bytes 524288 | tf_op jit(solution)/shard_map/all_to_all | solution.py:34
  109.1 1.1 fusion.5
  110.2 7.4 %all-to-all-done.3 = bf16[8,32,512]{2,1,0:T(8,128)(2,1)S(1)} async-done(((bf16[8,32,512]{2,1,0:T(8,128)(2,1)}), bf16[8,32,512]{2,1,0:T(8,128)(2,1)S(1)}, u32[]{:S(2)}, u32[]{:S(2)}) %all-to-all-start.3) | async-done | bytes 262176 | tf_op jit(solution)/shard_map/all_to_all | solution.py:34
  117.6 11.8 %all_to_all.31 = bf16[8,32,512]{2,1,0:T(8,128)(2,1)S(1)} all-to-all(bf16[8,32,512]{2,1,0:T(8,128)(2,1)S(1)} %bitcast.115), channel_id=1, replica_groups=mesh['seq'=8,'tp'=4] {'seq'}, dimensions={0} | all-to-all | bytes 524288 | tf_op jit(solution)/shard_map/all_to_all | solution.py:34
  (78 shorter events, 10.6 us)
Async XLA Ops:
  0.0 12.4 %copy-start = (f32[16,64,128]{2,1,0:T(8,128)S(1)}, f32[16,64,128]{2,1,0:T(8,128)}, u32[]{:S(2)}) copy-start(f32[16,64,128]{2,1,0:T(8,128)} %param.25) | copy-start | bytes 1572868
  0.0 36.8 %copy-start.13 = (f32[128,16]{0,1:T(8,128)S(1)}, f32[128,16]{0,1:T(8,128)}, u32[]{:S(2)}) copy-start(f32[128,16]{0,1:T(8,128)} %param.22) | copy-start | bytes 24580
  0.0 28.3 %copy-start.11 = (bf16[128,128]{1,0:T(8,128)(2,1)S(1)}, bf16[128,128]{1,0:T(8,128)(2,1)}, u32[]{:S(2)}) copy-start(bf16[128,128]{1,0:T(8,128)(2,1)} %param.20) | copy-start | bytes 98308
  0.0 28.1 %copy-start.10 = (bf16[128,1024]{1,0:T(8,128)(2,1)S(1)}, bf16[128,1024]{1,0:T(8,128)(2,1)}, u32[]{:S(2)}) copy-start(bf16[128,1024]{1,0:T(8,128)(2,1)} %param.19) | copy-start | bytes 786436
  0.0 28.3 %copy-start.12 = (bf16[128,128]{1,0:T(8,128)(2,1)S(1)}, bf16[128,128]{1,0:T(8,128)(2,1)}, u32[]{:S(2)}) copy-start(bf16[128,128]{1,0:T(8,128)(2,1)} %param.21) | copy-start | bytes 98308
  0.0 36.8 %copy-start.17 = (f32[16]{0:T(128)S(1)}, f32[16]{0:T(128)}, u32[]{:S(2)}) copy-start(f32[16]{0:T(128)} %param.24) | copy-start | bytes 196
  5.1 16.9 %all-to-all-start = ((bf16[8,144,128]{2,1,0:T(8,128)(2,1)}), bf16[8,144,128]{2,1,0:T(8,128)(2,1)S(1)}, u32[]{:S(2)}, u32[]{:S(2)}) async-start(bf16[8,144,128]{2,1,0:T(8,128)(2,1)} %pad_maximum_fusion.1), calls=%async_computation | async-start | bytes 589824 | tf_op jit(solution)/shard_map/all_to_all | solution.py:34
  24.5 12.1 %all-to-all-start.1 = ((bf16[8,128,128]{2,1,0:T(8,128)(2,1)}), bf16[8,128,128]{2,1,0:T(8,128)(2,1)S(1)}, u32[]{:S(2)}, u32[]{:S(2)}) async-start(bf16[8,128,128]{2,1,0:T(8,128)(2,1)} %prefix.1), calls=%async_computation.1 | async-start | bytes 524288 | tf_op jit(solution)/shard_map/all_to_all | solution.py:34
  28.1 9.5 %copy-start.14 = (f32[1024]{0:T(1024)S(1)}, f32[1024]{0:T(1024)}, u32[]{:S(2)}) copy-start(f32[1024]{0:T(1024)} %param.26) | copy-start | bytes 12292
  36.6 2.2 %copy-start.8 = (bf16[1024,2048]{1,0:T(8,128)(2,1)S(1)}, bf16[1024,2048]{1,0:T(8,128)(2,1)}, u32[]{:S(2)}) copy-start(bf16[1024,2048]{1,0:T(8,128)(2,1)} %param.27) | copy-start | bytes 12582916
  37.6 3.2 %copy-start.15 = (s32[128,2]{0,1:T(2,128)S(1)}, s32[128,2]{0,1:T(2,128)}, u32[]{:S(2)}) copy-start(s32[128,2]{0,1:T(2,128)} %param.29) | copy-start | bytes 3076
  40.6 41.4 %copy-start.1 = (bf16[1,2048,512]{2,1,0:T(8,128)(2,1)S(1)}, bf16[1,2048,512]{2,1,0:T(8,128)(2,1)}, u32[]{:S(2)}) copy-start(bf16[1,2048,512]{2,1,0:T(8,128)(2,1)} %param.31) | copy-start | bytes 6291460
  40.6 41.4 %copy-start.6 = (f32[2048]{0:T(1024)S(1)}, f32[2048]{0:T(1024)}, u32[]{:S(2)}) copy-start(f32[2048]{0:T(1024)} %param.28) | copy-start | bytes 24580
  40.7 1.6 %collective-permute-start = (bf16[2,128,512]{2,1,0:T(8,128)(2,1)S(1)}, bf16[2,128,512]{2,1,0:T(8,128)(2,1)S(1)}, u32[]{:S(2)}, u32[]{:S(2)}) collective-permute-start(bf16[2,128,512]{2,1,0:T(8,128)(2,1)S(1)} %pad_maximum_fusion.2), channel_id=1, source_target_pairs={{0,1},{1,0},{2,3},{3,2},{4,5},{5,4},{6,7},{7,6},{8,9},{9,8},{10,11... | collective-permute-start | bytes 786440 | tf_op jit(solution)/shard_map/ppermute | solution.py:14
  43.6 5.6 %collective-permute-start.1 = (bf16[128,512]{1,0:T(8,128)(2,1)S(1)}, bf16[128,512]{1,0:T(8,128)(2,1)S(1)}, u32[]{:S(2)}, u32[]{:S(2)}) collective-permute-start(bf16[128,512]{1,0:T(8,128)(2,1)S(1)} %select_convert_fusion), channel_id=1, source_target_pairs={{0,2},{1,3},{2,0},{3,1},{4,6},{5,7},{6,4},{7,5},{8,10},{9,11},{10,... | collective-permute-start | bytes 393224 | tf_op jit(solution)/shard_map/ppermute | solution.py:14
  63.6 12.0 %all-to-all-start.4 = ((bf16[8,32,512]{2,1,0:T(8,128)(2,1)}), bf16[8,32,512]{2,1,0:T(8,128)(2,1)S(1)}, u32[]{:S(2)}, u32[]{:S(2)}) async-start(bf16[8,32,512]{2,1,0:T(8,128)(2,1)} %get-tuple-element.20), calls=%async_computation.4 | async-start | bytes 524288 | tf_op jit(solution)/shard_map/all_to_all | solution.py:34
  67.0 10.1 %collective-permute-start.3 = (bf16[256,512]{1,0:T(8,128)(2,1)S(1)}, bf16[256,512]{1,0:T(8,128)(2,1)S(1)}, u32[]{:S(2)}, u32[]{:S(2)}) collective-permute-start(bf16[256,512]{1,0:T(8,128)(2,1)S(1)} %bitcast.108), channel_id=1, source_target_pairs={{0,2},{1,3},{2,0},{3,1},{4,6},{5,7},{6,4},{7,5},{8,10},{9,11},{10,... | collective-permute-start | bytes 786440 | tf_op jit(solution)/shard_map/ppermute | solution.py:14
  75.6 6.4 %collective-permute-start.8 = (bf16[256,512]{1,0:T(8,128)(2,1)S(1)}, bf16[256,512]{1,0:T(8,128)(2,1)S(1)}, u32[]{:S(2)}, u32[]{:S(2)}) collective-permute-start(bf16[256,512]{1,0:T(8,128)(2,1)S(1)} %bitcast.105), channel_id=1, source_target_pairs={{0,2},{1,3},{2,0},{3,1},{4,6},{5,7},{6,4},{7,5},{8,10},{9,11},{10,... | collective-permute-start | bytes 786440 | tf_op jit(solution)/shard_map/ppermute | solution.py:14
  77.1 4.9 %collective-permute-start.2 = (bf16[256,512]{1,0:T(8,128)(2,1)S(1)}, bf16[256,512]{1,0:T(8,128)(2,1)S(1)}, u32[]{:S(2)}, u32[]{:S(2)}) collective-permute-start(bf16[256,512]{1,0:T(8,128)(2,1)S(1)} %bitcast.109), channel_id=1, source_target_pairs={{0,1},{1,0},{2,3},{3,2},{4,5},{5,4},{6,7},{7,6},{8,9},{9,8},{10,11... | collective-permute-start | bytes 786440 | tf_op jit(solution)/shard_map/ppermute | solution.py:14
  77.1 4.9 %collective-permute-start.4 = (bf16[256,512]{1,0:T(8,128)(2,1)S(1)}, bf16[256,512]{1,0:T(8,128)(2,1)S(1)}, u32[]{:S(2)}, u32[]{:S(2)}) collective-permute-start(bf16[256,512]{1,0:T(8,128)(2,1)S(1)} %collective-permute-done.3.far), channel_id=1, source_target_pairs={{0,1},{1,0},{2,3},{3,2},{4,5},{5,4},{6,7},{7,6},{8,9},{9,8},{10,11... | collective-permute-start | bytes 786440 | tf_op jit(solution)/shard_map/ppermute | solution.py:14
  77.6 12.4 %collective-permute-start.7 = (bf16[256,512]{1,0:T(8,128)(2,1)S(1)}, bf16[256,512]{1,0:T(8,128)(2,1)S(1)}, u32[]{:S(2)}, u32[]{:S(2)}) collective-permute-start(bf16[256,512]{1,0:T(8,128)(2,1)S(1)} %bitcast.106), channel_id=1, source_target_pairs={{0,1},{1,0},{2,3},{3,2},{4,5},{5,4},{6,7},{7,6},{8,9},{9,8},{10,11... | collective-permute-start | bytes 786440 | tf_op jit(solution)/shard_map/ppermute | solution.py:14
  81.9 8.0 %collective-permute-start.9 = (bf16[256,512]{1,0:T(8,128)(2,1)S(1)}, bf16[256,512]{1,0:T(8,128)(2,1)S(1)}, u32[]{:S(2)}, u32[]{:S(2)}) collective-permute-start(bf16[256,512]{1,0:T(8,128)(2,1)S(1)} %collective-permute-done.8.far), channel_id=1, source_target_pairs={{0,1},{1,0},{2,3},{3,2},{4,5},{5,4},{6,7},{7,6},{8,9},{9,8},{10,11... | collective-permute-start | bytes 786440 | tf_op jit(solution)/shard_map/ppermute | solution.py:14
  82.0 1.6 %copy-start.2 = (bf16[1,2048,512]{2,1,0:T(8,128)(2,1)S(1)}, bf16[1,2048,512]{2,1,0:T(8,128)(2,1)}, u32[]{:S(2)}) copy-start(bf16[1,2048,512]{2,1,0:T(8,128)(2,1)} %param.32) | copy-start | bytes 6291460
  83.6 1.6 %copy-start.4 = (bf16[1,512,2048]{2,1,0:T(8,128)(2,1)S(1)}, bf16[1,512,2048]{2,1,0:T(8,128)(2,1)}, u32[]{:S(2)}) copy-start(bf16[1,512,2048]{2,1,0:T(8,128)(2,1)} %param.33) | copy-start | bytes 6291460
  85.1 4.8 %copy-start.3 = (bf16[1,2048,512]{2,1,0:T(8,128)(2,1)S(1)}, bf16[1,2048,512]{2,1,0:T(8,128)(2,1)}, u32[]{:S(2)}) copy-start(bf16[1,2048,512]{2,1,0:T(8,128)(2,1)} %param.32) | copy-start | bytes 6291460
  89.4 4.9 %collective-permute-start.5 = (bf16[2,256,512]{2,1,0:T(8,128)(2,1)S(1)}, bf16[2,256,512]{2,1,0:T(8,128)(2,1)S(1)}, u32[]{:S(2)}, u32[]{:S(2)}) collective-permute-start(bf16[2,256,512]{2,1,0:T(8,128)(2,1)S(1)} %get-tuple-element.10), channel_id=1, source_target_pairs={{0,1},{1,0},{2,3},{3,2},{4,5},{5,4},{6,7},{7,6},{8,9},{9,8},{10,11... | collective-permute-start | bytes 1572872 | tf_op jit(solution)/shard_map/ppermute | solution.py:14
  94.2 10.2 %copy-start.5 = (f32[2,256,512]{2,1,0:T(8,128)}, f32[2,256,512]{2,1,0:T(8,128)S(1)}, u32[]{:S(2)}) copy-start(f32[2,256,512]{2,1,0:T(8,128)S(1)} %get-tuple-element.11) | copy-start | bytes 3145732
  94.2 35.2 %copy-start.16 = (f32[128,2]{0,1:T(2,128)S(1)}, f32[128,2]{0,1:T(2,128)}, u32[]{:S(2)}) copy-start(f32[128,2]{0,1:T(2,128)} %param.30) | copy-start | bytes 3076
  94.3 2.0 %collective-permute-start.10 = (bf16[2,256,512]{2,1,0:T(8,128)(2,1)S(1)}, bf16[2,256,512]{2,1,0:T(8,128)(2,1)S(1)}, u32[]{:S(2)}, u32[]{:S(2)}) collective-permute-start(bf16[2,256,512]{2,1,0:T(8,128)(2,1)S(1)} %get-tuple-element.12), channel_id=1, source_target_pairs={{0,1},{1,0},{2,3},{3,2},{4,5},{5,4},{6,7},{7,6},{8,9},{9,8},{10,11... | collective-permute-start | bytes 1572872 | tf_op jit(solution)/shard_map/ppermute | solution.py:14
  94.4 9.2 %collective-permute-start.6 = (bf16[256,512]{1,0:T(8,128)(2,1)S(1)}, bf16[256,512]{1,0:T(8,128)(2,1)S(1)}, u32[]{:S(2)}, u32[]{:S(2)}) collective-permute-start(bf16[256,512]{1,0:T(8,128)(2,1)S(1)} %fusion.18), channel_id=1, source_target_pairs={{0,2},{1,3},{2,0},{3,1},{4,6},{5,7},{6,4},{7,5},{8,10},{9,11},{10,... | collective-permute-start | bytes 786440 | tf_op jit(solution)/shard_map/ppermute | solution.py:14
  96.3 12.8 %collective-permute-start.11 = (bf16[256,512]{1,0:T(8,128)(2,1)S(1)}, bf16[256,512]{1,0:T(8,128)(2,1)S(1)}, u32[]{:S(2)}, u32[]{:S(2)}) collective-permute-start(bf16[256,512]{1,0:T(8,128)(2,1)S(1)} %fusion.19), channel_id=1, source_target_pairs={{0,2},{1,3},{2,0},{3,1},{4,6},{5,7},{6,4},{7,5},{8,10},{9,11},{10,... | collective-permute-start | bytes 786440 | tf_op jit(solution)/shard_map/ppermute | solution.py:14
  104.4 13.2 %all-to-all-start.3 = ((bf16[8,32,512]{2,1,0:T(8,128)(2,1)}), bf16[8,32,512]{2,1,0:T(8,128)(2,1)S(1)}, u32[]{:S(2)}, u32[]{:S(2)}) async-start(bf16[8,32,512]{2,1,0:T(8,128)(2,1)} %bitcast.30), calls=%async_computation.3 | async-start | bytes 524288 | tf_op jit(solution)/shard_map/all_to_all | solution.py:34
  (2 other events, 1.7 us)

commit v3 on v2

v3 whole, which is shorter than its diff:
```python
import jax
import jax.numpy as jnp
from jax import lax
from jax.experimental import pallas as pl
from jax.experimental.pallas import tpu as pltpu
from jax.sharding import PartitionSpec as P

BF = jnp.bfloat16
F32 = jnp.float32
MIB = 1024 * 1024
LANES = 128


def swap(value, bit):
    count = lax.axis_size("tp")
    return lax.ppermute(value, "tp", [(i, i ^ bit) for i in range(count)])


def exchange(value):
    return lax.all_to_all(value, "seq", split_axis=0, concat_axis=0, tiled=True)


def after(value, *others):
    return lax.optimization_barrier((value, *others))[0]


def params(mib):
    return pltpu.CompilerParams(vmem_limit_bytes=mib * MIB)


def whole(*shape):
    return pl.BlockSpec(shape, lambda *_: (0,) * len(shape))


def by_pair(left, right, size):
    lane = lax.broadcasted_iota(jnp.int32, (size, LANES), 1)
    return jnp.where(lane < LANES // 2, left, right)


def state_kernel(x, step_t, decay_t, b, out, cum_out):
    count, rows, _ = out.shape
    part = rows - 16
    heads, toks = decay_t.shape
    row = lax.broadcasted_iota(jnp.int32, (toks, toks), 0)
    col = lax.broadcasted_iota(jnp.int32, (toks, toks), 1)
    upper = (row <= col).astype(F32)
    cum_t = jnp.dot(
        decay_t[...], upper, precision=lax.Precision.HIGHEST, preferred_element_type=F32
    )
    cum_out[...] = cum_t
    end = cum_t[:, toks - 1 : toks]
    scale = (jnp.exp(end - cum_t) * step_t[...]).T
    decay = jnp.broadcast_to(jnp.exp(end), (heads, LANES))
    high = decay.astype(BF).astype(F32)
    extra = by_pair(high, decay - high, heads).astype(BF)
    for k in range(count):
        out[k, pl.ds(part, 16), :] = extra
    for p in range(heads // 2):
        pair = x[:, p * LANES : (p + 1) * LANES].astype(F32)
        factor = by_pair(scale[:, 2 * p : 2 * p + 1], scale[:, 2 * p + 1 : 2 * p + 2], toks)
        state = lax.dot_general(
            (pair * factor).astype(BF),
            b[...],
            (((0,), (0,)), ((), ())),
            preferred_element_type=F32,
        ).astype(BF)
        for k in range(LANES // part):
            out[p * (LANES // part) + k, pl.ds(0, part), :] = state[k * part : (k + 1) * part]


def own_state(x, step_t, decay_t, b, count):
    heads, toks = decay_t.shape
    part = x.shape[1] // count
    return pl.pallas_call(
        state_kernel,
        out_shape=[
            jax.ShapeDtypeStruct((count, part + 16, b.shape[1]), BF),
            jax.ShapeDtypeStruct((heads, toks), F32),
        ],
        compiler_params=params(8),
        name="own_state",
    )(x, step_t, decay_t, b)


def prefix_kernel(place_ref, got, start, back):
    count, part, _ = back.shape
    heads = 16
    held = max(1, heads // count)
    group = part // held
    first = place_ref[0] * heads // count
    row = lax.broadcasted_iota(jnp.int32, (heads, LANES), 0)
    carries = [start[pl.ds(h * group, group), :] for h in range(held)]
    for turn in range(count):
        extra = got[turn, pl.ds(part, 16), :].astype(F32)
        scale = extra[:, :1] + extra[:, LANES // 2 : LANES // 2 + 1]
        for h in range(held):
            spot = pl.ds(h * group, group)
            back[turn, spot, :] = carries[h].astype(BF)
            factor = jnp.sum(jnp.where(row == first + h, scale, 0.0), axis=0, keepdims=True)
            carries[h] = factor * carries[h] + got[turn, spot, :].astype(F32)


def entering_state(place, got, init_rows):
    count, rows, width = got.shape
    part = rows - 16
    return pl.pallas_call(
        prefix_kernel,
        grid_spec=pltpu.PrefetchScalarGridSpec(
            num_scalar_prefetch=1,
            grid=(1,),
            in_specs=[
                whole(count, rows, width),
                pl.BlockSpec((part, width), lambda _, place: (place[0], 0)),
            ],
            out_specs=whole(count, part, width),
        ),
        out_shape=jax.ShapeDtypeStruct((count, part, width), BF),
        compiler_params=params(8),
        name="prefix",
    )(place.reshape(1), got, init_rows)


def within_kernel(skip, x, step_t, cum_t, b, c, out):
    heads, toks = cum_t.shape
    row = lax.broadcasted_iota(jnp.int32, (toks, toks), 0)
    col = lax.broadcasted_iota(jnp.int32, (toks, toks), 1)
    causal = row >= col
    nt = (((1,), (1,)), ((), ()))
    scores = lax.dot_general(c[...], b[...], nt, preferred_element_type=F32)
    cum = cum_t[...].T
    for p in range(heads // 2):
        pair = x[:, p * LANES : (p + 1) * LANES]
        sums = []
        for h in (2 * p, 2 * p + 1):
            gap = cum[:, h : h + 1] - cum_t[h : h + 1, :]
            decay = jnp.where(causal, jnp.exp(jnp.where(causal, gap, 0.0)), 0.0)
            weights = (decay * scores * step_t[h : h + 1, :]).astype(BF)
            sums.append(jnp.dot(weights, pair, preferred_element_type=F32))
        gain = by_pair(skip[2 * p], skip[2 * p + 1], toks)
        out[:, p * LANES : (p + 1) * LANES] = (
            by_pair(sums[0], sums[1], toks) + gain * pair.astype(F32)
        )


def within_block(skip, x, step_t, cum_t, b, c):
    toks, inner = x.shape
    heads = cum_t.shape[0]
    vmem = pl.BlockSpec(memory_space=pltpu.VMEM)
    return pl.pallas_call(
        within_kernel,
        in_specs=[pl.BlockSpec(memory_space=pltpu.SMEM)] + [vmem] * 5,
        out_shape=jax.ShapeDtypeStruct((toks, inner), F32),
        compiler_params=params(8),
        cost_estimate=pl.CostEstimate(
            flops=4 * heads * toks * toks * LANES,
            bytes_accessed=6 * toks * inner,
            transcendentals=heads * toks * toks,
        ),
        name="within_block",
    )(skip, x, step_t, cum_t, b, c)


def tail_kernel(place_ref, c, arriving, cum_t, direct, z, gain, weight, give, keep, normed):
    step = pl.program_id(0)
    heads, toks = cum_t.shape

    @pl.when(step == 0)
    def _():
        grown = jnp.exp(cum_t[...]).T
        lane = lax.broadcasted_iota(jnp.int32, (toks, LANES), 1)
        left = lane < LANES // 2
        nt = (((1,), (1,)), ((), ()))
        for p in range(heads // 2):
            spot = pl.ds(p * LANES, LANES)
            inter = lax.dot_general(
                c[...], arriving[spot, :], nt, preferred_element_type=F32
            )
            factor = by_pair(grown[:, 2 * p : 2 * p + 1], grown[:, 2 * p + 1 : 2 * p + 2], toks)
            wide = z[:, spot].astype(F32)
            gated = (direct[:, spot] + inter * factor) * (wide * (1.0 / (1.0 + jnp.exp(-wide))))
            square = gated * gated
            first = jnp.sum(jnp.where(left, square, 0.0), axis=1, keepdims=True)
            second = jnp.sum(jnp.where(left, 0.0, square), axis=1, keepdims=True)
            mean = by_pair(first, second, toks) * (2.0 / LANES)
            normed[:, spot] = (gated * lax.rsqrt(mean + 1e-05) * gain[:, spot]).astype(BF)

    part = jnp.dot(normed[...], weight[...], preferred_element_type=F32)

    @pl.when(step < 2)
    def _():
        give[jnp.minimum(step, 1)] = part.astype(BF)

    @pl.when(step >= 2)
    def _():
        keep[jnp.maximum(step - 2, 0)] = part


def mixer_tail(place, c, arriving, cum_t, direct, z, gain, weight):
    heads, toks = cum_t.shape
    inner, width = weight.shape
    share = width // 4
    return pl.pallas_call(
        tail_kernel,
        grid_spec=pltpu.PrefetchScalarGridSpec(
            num_scalar_prefetch=1,
            grid=(4,),
            in_specs=[
                whole(*c.shape),
                whole(*arriving.shape),
                whole(heads, toks),
                whole(toks, inner),
                whole(toks, inner),
                whole(1, inner),
                pl.BlockSpec((inner, share), lambda j, place: (0, place[0] ^ ((2 * j + 1) % 5))),
            ],
            out_specs=[whole(2, toks, share)] * 2,
            scratch_shapes=[pltpu.VMEM((toks, inner), BF)],
        ),
        out_shape=[
            jax.ShapeDtypeStruct((2, toks, share), BF),
            jax.ShapeDtypeStruct((2, toks, share), F32),
        ],
        compiler_params=params(56),
        cost_estimate=pl.CostEstimate(
            flops=2 * toks * inner * width,
            bytes_accessed=2 * inner * width + 14 * toks * inner,
            transcendentals=toks * inner,
        ),
        name="mixer_tail",
    )(place.reshape(1), c, arriving, cum_t, direct, z, gain.reshape(1, inner), weight)


def expert_kernel(place_ref, own, near, far, last, gain, wg, wu, wd, give, keep, rows, total):
    place = place_ref[0]
    step = pl.program_id(0)
    share = own.shape[1]
    spots = [pl.ds(pl.multiple_of((place ^ k) * share, share), share) for k in range(4)]
    parts = [own, near, far, last]

    @pl.when(step == 0)
    def _():
        wide = [p[...].astype(F32) for p in parts]
        square = sum(jnp.sum(w * w, axis=1, keepdims=True) for w in wide)
        scale = lax.rsqrt(square * (1.0 / (4 * share)) + 1e-05)
        for k in range(4):
            rows[k] = (wide[k] * scale * gain[:, spots[k]]).astype(BF)

    gate = up = 0.0
    for k in range(4):
        gate += jnp.dot(rows[k], wg[spots[k], :], preferred_element_type=F32)
        up += jnp.dot(rows[k], wu[spots[k], :], preferred_element_type=F32)
    act = (gate * (1.0 / (1.0 + jnp.exp(-gate))) * up).astype(BF)
    for k in range(4):
        down = jnp.dot(act, wd[:, spots[k]], preferred_element_type=F32)

        @pl.when(step == 0)
        def _():
            total[k] = down

        @pl.when(step > 0)
        def _():
            total[k] += down

    @pl.when(step == pl.num_programs(0) - 1)
    def _():
        give[0] = total[1].astype(BF)
        give[1] = total[3].astype(BF)
        keep[0] = total[0]
        keep[1] = total[2]


def run_expert(place, own, near, far, last, gain, wg, wu, wd):
    rows, share = own.shape
    width, inner = wg.shape
    tile = inner // 2

    part = whole(rows, share)
    return pl.pallas_call(
        expert_kernel,
        grid_spec=pltpu.PrefetchScalarGridSpec(
            num_scalar_prefetch=1,
            grid=(inner // tile,),
            in_specs=[
                part,
                part,
                part,
                part,
                whole(1, width),
                pl.BlockSpec((width, tile), lambda j, _: (0, j)),
                pl.BlockSpec((width, tile), lambda j, _: (0, j)),
                pl.BlockSpec((tile, width), lambda j, _: (j, 0)),
            ],
            out_specs=[whole(2, rows, share)] * 2,
            scratch_shapes=[pltpu.VMEM((4, rows, share), BF), pltpu.VMEM((4, rows, share), F32)],
        ),
        out_shape=[
            jax.ShapeDtypeStruct((2, rows, share), BF),
            jax.ShapeDtypeStruct((2, rows, share), F32),
        ],
        compiler_params=params(56),
        cost_estimate=pl.CostEstimate(
            flops=6 * rows * width * inner,
            bytes_accessed=6 * width * inner + 14 * rows * width,
            transcendentals=rows * inner,
        ),
        name="expert",
    )(place.reshape(1), own, near, far, last, gain.reshape(1, width), wg, wu, wd)


def body(
    tokens,
    input_heads,
    z_gate,
    b_proj,
    c_proj,
    step_size,
    decay_log,
    skip_gain,
    init_state,
    norm_gain,
    out_weight,
    moe_gain,
    routes,
    route_weights,
    w_gate,
    w_up,
    w_down,
):
    tok_rows, inner = input_heads.shape
    state_size = init_state.shape[2]
    seq_count = lax.axis_size("seq")
    place = lax.axis_index("tp")
    step_t = step_size.T
    outgoing, cum_t = own_state(input_heads, step_t, decay_log.T, b_proj, seq_count)
    got = exchange(outgoing)
    direct = within_block(skip_gain, input_heads, step_t, cum_t, b_proj, c_proj)
    back = entering_state(lax.axis_index("seq"), got, init_state.reshape(inner, state_size))
    arriving = exchange(back).reshape(inner, state_size)
    give, keep = mixer_tail(
        place, c_proj, arriving, cum_t, direct, z_gate, norm_gain, out_weight
    )

    model_width = out_weight.shape[1]
    share = model_width // 4
    expert_count = w_gate.shape[0] * seq_count
    slot_count = 4 * tok_rows // seq_count
    top_count = routes.shape[1]
    items = top_count * tok_rows
    slots = expert_count * slot_count
    flat_expert = routes.T.reshape(-1)
    onehot = flat_expert[:, None] == jnp.arange(expert_count, dtype=jnp.int32)[None, :]
    before = jnp.arange(items)[:, None] > jnp.arange(items)[None, :]
    earlier = jnp.dot(before.astype(BF), onehot.astype(BF), preferred_element_type=F32)
    rank = jnp.sum(jnp.where(onehot, earlier, 0.0), axis=1).astype(jnp.int32)
    placed = flat_expert * slot_count + rank
    spots = placed[:, None] == jnp.arange(slots, dtype=jnp.int32)[None, :]
    pick = spots.astype(BF)
    fill = jnp.any(spots.reshape(top_count, tok_rows, slots), axis=0).astype(BF)

    got = swap(give, 1)
    passing = swap((keep[1] + got[1].astype(F32)).astype(BF), 2)
    own_tokens = lax.dynamic_slice_in_dim(tokens, place * share, share, 1)
    projected = keep[0] + got[0].astype(F32) + passing.astype(F32)
    hidden = (own_tokens.astype(F32) + projected).astype(BF)
    outgoing = lax.dot_general(
        fill, hidden, (((0,), (0,)), ((), ())), preferred_element_type=F32
    ).astype(BF)
    arrived = exchange(outgoing.reshape(expert_count, slot_count, share)).reshape(slots, share)

    cut = slots // 2
    own = [arrived[:cut], arrived[cut:]]
    far = [swap(own[0], 2), swap(own[1], 2)]
    near = [swap(own[0], 1), swap(own[1], 1)]
    weights = (moe_gain, w_gate[0], w_up[0], w_down[0])
    give0, keep0 = run_expert(place, own[0], near[0], far[0], swap(far[0], 1), *weights)
    pass_got0 = swap(give0[1], 1)
    last1 = swap(after(far[1], give0), 1)
    pass0 = (keep0[1] + pass_got0.astype(F32)).astype(BF)
    give1, keep1 = run_expert(
        place, after(own[1], pass0), near[1], far[1], last1, *weights
    )
    passed0 = swap(pass0, 2)
    kept_got0 = swap(give0[0], 1)
    pass_got1 = swap(give1[1], 1)
    kept_got1 = swap(give1[0], 1)
    passed1 = swap((keep1[1] + pass_got1.astype(F32)).astype(BF), 2)
    result0 = (keep0[0] + kept_got0.astype(F32) + passed0.astype(F32)).astype(BF)
    result1 = (keep1[0] + kept_got1.astype(F32) + passed1.astype(F32)).astype(BF)
    results = jnp.concatenate([result0, result1]).reshape(expert_count, slot_count, share)
    returned = exchange(results).reshape(slots, share)
    chosen = jnp.dot(pick, returned, preferred_element_type=F32).reshape(
        top_count, tok_rows, share
    )
    mixed_out = hidden.astype(F32) + jnp.sum(route_weights.T[:, :, None] * chosen, axis=0)
    return mixed_out.astype(BF)


def solution(mesh):
    in_specs = (
        P("seq", None),
        P("seq", "tp"),
        P("seq", "tp"),
        P("seq", None),
        P("seq", None),
        P("seq", "tp"),
        P("seq", "tp"),
        P("tp"),
        P("tp", None, None),
        P("tp"),
        P("tp", None),
        P(),
        P("seq", None),
        P("seq", None),
        P("seq", None, "tp"),
        P("seq", None, "tp"),
        P("seq", "tp", None),
    )
    out_specs = P("seq", "tp")
    return jax.shard_map(body, mesh=mesh, in_specs=in_specs, out_specs=out_specs, check_vma=False)
```

time: 131 us -> 135 us (1.031)
  Pallas kernels: 10.2 us -> 25 us
  blocking collectives: 23.6 us -> 35.8 us
  waiting for transfers between devices: 47 us -> 37.8 us
  starting transfers between devices: 28.1 us -> 19.4 us
  matrix products: 4.54 us -> 0.89 us
  other arithmetic: 7.65 us -> 5.33 us
    all_to_all x4 -> x2, waiting for transfers between devices: 31.5 us -> 16.1 us  [exchange(): return lax.all_to_all(value, 'seq', split_axis=0, concat_axis=0, tiled=True)]
    all_to_all x2, blocking collectives: 23.6 us -> 35.8 us  [exchange(): return lax.all_to_all(value, 'seq', split_axis=0, concat_axis=0, tiled=True)]
    pallas_call x1 -> x4, Pallas kernels: 1.74 us -> 9.93 us  [the longest x1 6.04 us: mixer_tail(): pl.pallas_call(tail_kernel, grid_spec=pltpu.PrefetchScalarGridSpec(num_sc...]
    all_to_all x4 -> x2, starting transfers between devices: 19 us -> 10.8 us  [exchange(): return lax.all_to_all(value, 'seq', split_axis=0, concat_axis=0, tiled=True)]
    pallas_call x2, Pallas kernels: 8.5 us -> 15.1 us  [run_expert(): pl.pallas_call(expert_kernel, grid_spec=pltpu.PrefetchScalarGridSpec(num_...]
    ppermute x12 -> x14, waiting for transfers between devices: 15.5 us -> 21.7 us  [swap(): return lax.ppermute(value, 'tp', [(i, i ^ bit) for i in range(count)])]
    dot_general x6 -> x0, matrix products: 3.65 us -> none  [the longest x1 0.96 us: body(): lax.dot_general(weighted, b_proj, (((0,), (0,)), ((), ())), preferred_ele...]
    squeeze x0 -> x2, local copies, waits for them, and re-layouts: none -> 2.28 us  [the longest x1 1.21 us: body(): kept_got1 = swap(give1[0], 1)]
  transfers between devices with their start and end apart: 16 -> 16, of which waited for: 9 -> 8; matrix products, arithmetic and copies ran while one was open for 3% -> 3% of each run, Pallas kernels for 7% -> 7%
where the time goes in v3:
time: 135 us
  waiting for transfers between devices  37.8 us (28%)
  blocking collectives  35.8 us (27%)
  Pallas kernels  25 us (19%)
  starting transfers between devices  19.4 us (14%)
  local copies, waits for them, and re-layouts  10.1 us (7%)
  other arithmetic  5.33 us (4%)
    all_to_all x2, blocking collectives, exchange(): return lax.all_to_all(value, 'seq', split_axis=0, concat_axis=0, tiled=True)  35.8 us
    ppermute x14, waiting for transfers between devices, swap(): return lax.ppermute(value, 'tp', [(i, i ^ bit) for i in range(count)])  21.7 us
    all_to_all x2, waiting for transfers between devices, exchange(): return lax.all_to_all(value, 'seq', split_axis=0, concat_axis=0, tiled=True)  16.1 us
    pallas_call x2, Pallas kernels, run_expert(): pl.pallas_call(expert_kernel, grid_spec=pltpu.PrefetchScalarGridSpec(num_...  15.1 us
    all_to_all x2, starting transfers between devices, exchange(): return lax.all_to_all(value, 'seq', split_axis=0, concat_axis=0, tiled=True)  10.8 us
    ppermute x14, starting transfers between devices, swap(): return lax.ppermute(value, 'tp', [(i, i ^ bit) for i in range(count)])  8.56 us
    unnamed x50, local copies, waits for them, and re-layouts  7.82 us
    pallas_call x1, Pallas kernels, mixer_tail(): pl.pallas_call(tail_kernel, grid_spec=pltpu.PrefetchScalarGridSpec(num_sc...  6.04 us
  transfers between devices with their start and end apart: 16, of which 8 were waited for; matrix products, arithmetic and copies ran while one was open for 3% of the time, Pallas kernels for 7%

profile of v3, /device:TPU:0, one launch (start us, length us, event | category | flops | bytes accessed | tf_op | source)
XLA Modules:
  0.0 134.6 jit_solution(13866994326157416879)
XLA Ops:
  0.0 1.0 copy-done.1
  3.1 1.8 %own_state.1 = (bf16[8,144,128]{2,1,0:T(8,128)(2,1)}, f32[16,128]{1,0:T(8,128)S(1)}) custom-call(bf16[128,1024]{1,0:T(8,128)(2,1)S(1)} %copy-done.1, f32[16,128]{1,0:T(8,128)S(1)} %bitcast.70, f32[16,128]{1,0:T(8,128)S(1)} %bitcast.72, bf16[128,128]{1,0:T(8,128)(2,1)S(1)} %copy-done.5), custom_call_target="tpu_custom_call" | custom-call | tf_op jit(solution)/shard_map/own_state/pallas_call | solution.py:74
  4.9 7.3 %all-to-all-start = ((bf16[8,144,128]{2,1,0:T(8,128)(2,1)}), bf16[8,144,128]{2,1,0:T(8,128)(2,1)S(1)}, u32[]{:S(2)}, u32[]{:S(2)}) async-start(bf16[8,144,128]{2,1,0:T(8,128)(2,1)} %get-tuple-element.15), calls=%async_computation | async-start | bytes 589824 | tf_op jit(solution)/shard_map/all_to_all | solution.py:20
  12.1 9.6 %all-to-all-done.got = bf16[8,144,128]{2,1,0:T(8,128)(2,1)S(1)} async-done(((bf16[8,144,128]{2,1,0:T(8,128)(2,1)}), bf16[8,144,128]{2,1,0:T(8,128)(2,1)S(1)}, u32[]{:S(2)}, u32[]{:S(2)}) %all-to-all-start) | async-done | bytes 294944 | tf_op jit(solution)/shard_map/all_to_all | solution.py:20
  21.8 1.0 copy-done.3
  22.8 0.9 prefix.1
  23.7 3.6 %all-to-all-start.1 = ((bf16[8,128,128]{2,1,0:T(8,128)(2,1)}), bf16[8,128,128]{2,1,0:T(8,128)(2,1)S(1)}, u32[]{:S(2)}, u32[]{:S(2)}) async-start(bf16[8,128,128]{2,1,0:T(8,128)(2,1)} %prefix.1), calls=%async_computation.1 | async-start | bytes 524288 | tf_op jit(solution)/shard_map/all_to_all | solution.py:20
  27.4 1.2 within_block.1.direct
  28.6 0.8 copy-done
  29.4 6.5 %all-to-all-done.1 = bf16[8,128,128]{2,1,0:T(8,128)(2,1)S(1)} async-done(((bf16[8,128,128]{2,1,0:T(8,128)(2,1)}), bf16[8,128,128]{2,1,0:T(8,128)(2,1)S(1)}, u32[]{:S(2)}, u32[]{:S(2)}) %all-to-all-start.1) | async-done | bytes 262176 | tf_op jit(solution)/shard_map/all_to_all | solution.py:20
  36.5 6.0 %mixer_tail.1 = (bf16[2,128,512]{2,1,0:T(8,128)(2,1)}, f32[2,128,512]{2,1,0:T(8,128)}) custom-call(s32[1]{0:T(128)} %bitcast.place_ref, bf16[128,128]{1,0:T(8,128)(2,1)} %c.3, bf16[1024,128]{1,0:T(8,128)(2,1)} %bitcast.81, f32[16,128]{1,0:T(8,128)} %copy-done.7, f32[128,1024]{1,0:T(8,128)} %copy-done, bf16[128,1024]{1,0:T(8,128)(2,1)} %z.1, ...), custom_call_target="tpu_custom_call" | custom-call | flops 536870912 | bytes 6029312 | tf_op jit(solution)/shard_map/mixer_tail/pallas_call | solution.py:202
  42.8 1.5 %collective-permute-done = bf16[2,128,512]{2,1,0:T(8,128)(2,1)S(1)} collective-permute-done((bf16[2,128,512]{2,1,0:T(8,128)(2,1)}, bf16[2,128,512]{2,1,0:T(8,128)(2,1)S(1)}, u32[]{:S(2)}, u32[]{:S(2)}) %collective-permute-start) | collective-permute-done | bytes 262176 | tf_op jit(solution)/shard_map/ppermute | solution.py:16
  44.3 1.0 fusion.14
  45.3 1.6 %collective-permute-start.1 = (bf16[128,512]{1,0:T(8,128)(2,1)S(1)}, bf16[128,512]{1,0:T(8,128)(2,1)S(1)}, u32[]{:S(2)}, u32[]{:S(2)}) collective-permute-start(bf16[128,512]{1,0:T(8,128)(2,1)S(1)} %fusion.14), channel_id=1, source_target_pairs={{0,2},{1,3},{2,0},{3,1},{4,6},{5,7},{6,4},{7,5},{8,10},{9,11},{10,... | collective-permute-start | bytes 393224 | tf_op jit(solution)/shard_map/ppermute | solution.py:16
  47.0 3.9 %collective-permute-done.1 = bf16[128,512]{1,0:T(8,128)(2,1)S(1)} collective-permute-done((bf16[128,512]{1,0:T(8,128)(2,1)S(1)}, bf16[128,512]{1,0:T(8,128)(2,1)S(1)}, u32[]{:S(2)}, u32[]{:S(2)}) %collective-permute-start.1) | collective-permute-done | bytes 131104 | tf_op jit(solution)/shard_map/ppermute | solution.py:16
  50.9 1.0 fusion.12
  52.3 17.3 %all_to_all.20 = bf16[8,64,512]{2,1,0:T(8,128)(2,1)S(1)} all-to-all(bf16[8,64,512]{2,1,0:T(8,128)(2,1)S(1)} %bitcast.80), channel_id=1, replica_groups=mesh['seq'=8,'tp'=4] {'seq'}, dimensions={0} | all-to-all | bytes 1048576 | tf_op jit(solution)/shard_map/all_to_all | solution.py:20
  69.7 1.6 %collective-permute-start.3 = (bf16[256,512]{1,0:T(8,128)(2,1)S(1)}, bf16[256,512]{1,0:T(8,128)(2,1)S(1)}, u32[]{:S(2)}, u32[]{:S(2)}) collective-permute-start(bf16[256,512]{1,0:T(8,128)(2,1)S(1)} %bitcast.85), channel_id=1, source_target_pairs={{0,2},{1,3},{2,0},{3,1},{4,6},{5,7},{6,4},{7,5},{8,10},{9,11},{10,... | collective-permute-start | bytes 786440 | tf_op jit(solution)/shard_map/ppermute | solution.py:16
  71.3 5.1 %collective-permute-done.3.far = bf16[256,512]{1,0:T(8,128)(2,1)S(1)} collective-permute-done((bf16[256,512]{1,0:T(8,128)(2,1)S(1)}, bf16[256,512]{1,0:T(8,128)(2,1)S(1)}, u32[]{:S(2)}, u32[]{:S(2)}) %collective-permute-start.3) | collective-permute-done | bytes 262176 | tf_op jit(solution)/shard_map/ppermute | solution.py:16
  76.4 1.5 %collective-permute-start.9 = (bf16[256,512]{1,0:T(8,128)(2,1)S(1)}, bf16[256,512]{1,0:T(8,128)(2,1)S(1)}, u32[]{:S(2)}, u32[]{:S(2)}) collective-permute-start(bf16[256,512]{1,0:T(8,128)(2,1)S(1)} %bitcast.82), channel_id=1, source_target_pairs={{0,2},{1,3},{2,0},{3,1},{4,6},{5,7},{6,4},{7,5},{8,10},{9,11},{10,... | collective-permute-start | bytes 786440 | tf_op jit(solution)/shard_map/ppermute | solution.py:16
  78.8 7.6 %expert.2 = (bf16[2,256,512]{2,1,0:T(8,128)(2,1)}, f32[2,256,512]{2,1,0:T(8,128)}) custom-call(s32[1]{0:T(128)} %bitcast.place_ref, bf16[256,512]{1,0:T(8,128)(2,1)} %bitcast.87, bf16[256,512]{1,0:T(8,128)(2,1)} %copy-done.20, bf16[256,512]{1,0:T(8,128)(2,1)} %copy-done.18, bf16[256,512]{1,0:T(8,128)(2,1)} %copy-done.22, f32[1,2048]{1,0:T(1,128)} %bitcast.89, ...), custom_call_target="tpu_custom_call" | custom-call | flops 1610612736 | bytes 13631488 | tf_op jit(solution)/shard_map/expert/pallas_call | solution.py:278
  86.4 1.1 slice_bitcast_fusion.3
  88.2 0.8 collective-permute-done.6
  89.0 1.1 fusion.5
  91.5 7.5 %expert.3 = (bf16[2,256,512]{2,1,0:T(8,128)(2,1)}, f32[2,256,512]{2,1,0:T(8,128)}) custom-call(s32[1]{0:T(128)} %bitcast.place_ref, bf16[256,512]{1,0:T(8,128)(2,1)} %bitcast.84, bf16[256,512]{1,0:T(8,128)(2,1)} %copy-done.19, bf16[256,512]{1,0:T(8,128)(2,1)} %copy-done.17, bf16[256,512]{1,0:T(8,128)(2,1)} %copy-done.21, f32[1,2048]{1,0:T(1,128)} %bitcast.90, ...), custom_call_target="tpu_custom_call" | custom-call | flops 1610612736 | bytes 13631488 | tf_op jit(solution)/shard_map/expert/pallas_call | solution.py:278
  99.1 1.2 slice_bitcast_fusion.1
  100.9 1.4 %collective-permute-start.7 = (bf16[256,512]{1,0:T(8,128)(2,1)S(1)}, bf16[256,512]{1,0:T(8,128)(2,1)S(1)}, u32[]{:S(2)}, u32[]{:S(2)}) collective-permute-start(bf16[256,512]{1,0:T(8,128)(2,1)S(1)} %fusion.5), channel_id=1, source_target_pairs={{0,2},{1,3},{2,0},{3,1},{4,6},{5,7},{6,4},{7,5},{8,10},{9,11},{10,... | collective-permute-start | bytes 786440 | tf_op jit(solution)/shard_map/ppermute | solution.py:16
  102.3 1.1 fusion.2
  103.4 1.1 collective-permute-start.13
  104.5 5.5 %collective-permute-done.7 = bf16[256,512]{1,0:T(8,128)(2,1)S(1)} collective-permute-done((bf16[256,512]{1,0:T(8,128)(2,1)S(1)}, bf16[256,512]{1,0:T(8,128)(2,1)S(1)}, u32[]{:S(2)}, u32[]{:S(2)}) %collective-permute-start.7) | collective-permute-done | bytes 262176 | tf_op jit(solution)/shard_map/ppermute | solution.py:16
  110.2 4.8 %collective-permute-done.13 = bf16[256,512]{1,0:T(8,128)(2,1)S(1)} collective-permute-done((bf16[256,512]{1,0:T(8,128)(2,1)S(1)}, bf16[256,512]{1,0:T(8,128)(2,1)S(1)}, u32[]{:S(2)}, u32[]{:S(2)}) %collective-permute-start.13) | collective-permute-done | bytes 262176 | tf_op jit(solution)/shard_map/ppermute | solution.py:16
  115.1 18.4 %all_to_all.21 = bf16[8,64,512]{2,1,0:T(8,128)(2,1)S(1)} all-to-all(bf16[8,64,512]{2,1,0:T(8,128)(2,1)S(1)} %bitcast.79), channel_id=1, replica_groups=mesh['seq'=8,'tp'=4] {'seq'}, dimensions={0} | all-to-all | bytes 1048576 | tf_op jit(solution)/shard_map/all_to_all | solution.py:20
  (74 shorter events, 8.5 us)
Async XLA Ops:
  0.0 27.3 %copy-start.11 = (f32[16]{0:T(128)S(1)}, f32[16]{0:T(128)}, u32[]{:S(2)}) copy-start(f32[16]{0:T(128)} %skip.1) | copy-start | bytes 196
  0.0 1.0 copy-start.1
  3.1 24.2 %copy-start.2 = (bf16[128,1024]{1,0:T(8,128)(2,1)S(1)}, bf16[128,1024]{1,0:T(8,128)(2,1)}, u32[]{:S(2)}) copy-start(bf16[128,1024]{1,0:T(8,128)(2,1)} %x.3) | copy-start | bytes 786436
  3.1 24.2 %copy-start.4 = (bf16[128,128]{1,0:T(8,128)(2,1)S(1)}, bf16[128,128]{1,0:T(8,128)(2,1)}, u32[]{:S(2)}) copy-start(bf16[128,128]{1,0:T(8,128)(2,1)} %c.3) | copy-start | bytes 98308
  3.1 24.2 %copy-start.6 = (bf16[128,128]{1,0:T(8,128)(2,1)S(1)}, bf16[128,128]{1,0:T(8,128)(2,1)}, u32[]{:S(2)}) copy-start(bf16[128,128]{1,0:T(8,128)(2,1)} %b.3) | copy-start | bytes 98308
  3.1 24.2 %copy-start.9 = (f32[128,16]{0,1:T(8,128)S(1)}, f32[128,16]{0,1:T(8,128)}, u32[]{:S(2)}) copy-start(f32[128,16]{0,1:T(8,128)} %param.22) | copy-start | bytes 24580
  4.9 31.0 %copy-start.7 = (f32[16,128]{1,0:T(8,128)}, f32[16,128]{1,0:T(8,128)S(1)}, u32[]{:S(2)}) copy-start(f32[16,128]{1,0:T(8,128)S(1)} %get-tuple-element.16.cum_t) | copy-start | bytes 24580
  4.9 16.9 %all-to-all-start = ((bf16[8,144,128]{2,1,0:T(8,128)(2,1)}), bf16[8,144,128]{2,1,0:T(8,128)(2,1)S(1)}, u32[]{:S(2)}, u32[]{:S(2)}) async-start(bf16[8,144,128]{2,1,0:T(8,128)(2,1)} %get-tuple-element.15), calls=%async_computation | async-start | bytes 589824 | tf_op jit(solution)/shard_map/all_to_all | solution.py:20
  21.8 1.0 copy-start.3
  23.7 12.1 %all-to-all-start.1 = ((bf16[8,128,128]{2,1,0:T(8,128)(2,1)}), bf16[8,128,128]{2,1,0:T(8,128)(2,1)S(1)}, u32[]{:S(2)}, u32[]{:S(2)}) async-start(bf16[8,128,128]{2,1,0:T(8,128)(2,1)} %prefix.1), calls=%async_computation.1 | async-start | bytes 524288 | tf_op jit(solution)/shard_map/all_to_all | solution.py:20
  36.5 6.0 %copy-start.23 = (s32[128,2]{0,1:T(2,128)S(1)}, s32[128,2]{0,1:T(2,128)}, u32[]{:S(2)}) copy-start(s32[128,2]{0,1:T(2,128)} %param.29) | copy-start | bytes 3076
  42.6 1.7 %collective-permute-start = (bf16[2,128,512]{2,1,0:T(8,128)(2,1)}, bf16[2,128,512]{2,1,0:T(8,128)(2,1)S(1)}, u32[]{:S(2)}, u32[]{:S(2)}) collective-permute-start(bf16[2,128,512]{2,1,0:T(8,128)(2,1)} %get-tuple-element.18), channel_id=1, source_target_pairs={{0,1},{1,0},{2,3},{3,2},{4,5},{5,4},{6,7},{7,6},{8,9},{9,8},{10,11... | collective-permute-start | bytes 786440 | tf_op jit(solution)/shard_map/ppermute | solution.py:16
  45.3 5.6 %collective-permute-start.1 = (bf16[128,512]{1,0:T(8,128)(2,1)S(1)}, bf16[128,512]{1,0:T(8,128)(2,1)S(1)}, u32[]{:S(2)}, u32[]{:S(2)}) collective-permute-start(bf16[128,512]{1,0:T(8,128)(2,1)S(1)} %fusion.14), channel_id=1, source_target_pairs={{0,2},{1,3},{2,0},{3,1},{4,6},{5,7},{6,4},{7,5},{8,10},{9,11},{10,... | collective-permute-start | bytes 393224 | tf_op jit(solution)/shard_map/ppermute | solution.py:16
  69.7 8.3 %copy-start.16 = (bf16[4,64,512]{2,1,0:T(8,128)(2,1)}, bf16[4,64,512]{2,1,0:T(8,128)(2,1)S(1)}, u32[]{:S(2)}) copy-start(bf16[4,64,512]{2,1,0:T(8,128)(2,1)S(1)} %get-tuple-element.29) | copy-start | bytes 786436
  69.7 18.0 %copy-start.15 = (bf16[4,64,512]{2,1,0:T(8,128)(2,1)}, bf16[4,64,512]{2,1,0:T(8,128)(2,1)S(1)}, u32[]{:S(2)}) copy-start(bf16[4,64,512]{2,1,0:T(8,128)(2,1)S(1)} %get-tuple-element.30) | copy-start | bytes 786436
  69.7 6.7 %collective-permute-start.3 = (bf16[256,512]{1,0:T(8,128)(2,1)S(1)}, bf16[256,512]{1,0:T(8,128)(2,1)S(1)}, u32[]{:S(2)}, u32[]{:S(2)}) collective-permute-start(bf16[256,512]{1,0:T(8,128)(2,1)S(1)} %bitcast.85), channel_id=1, source_target_pairs={{0,2},{1,3},{2,0},{3,1},{4,6},{5,7},{6,4},{7,5},{8,10},{9,11},{10,... | collective-permute-start | bytes 786440 | tf_op jit(solution)/shard_map/ppermute | solution.py:16
  71.3 6.7 %collective-permute-start.2 = (bf16[256,512]{1,0:T(8,128)(2,1)S(1)}, bf16[256,512]{1,0:T(8,128)(2,1)S(1)}, u32[]{:S(2)}, u32[]{:S(2)}) collective-permute-start(bf16[256,512]{1,0:T(8,128)(2,1)S(1)} %bitcast.86), channel_id=1, source_target_pairs={{0,1},{1,0},{2,3},{3,2},{4,5},{5,4},{6,7},{7,6},{8,9},{9,8},{10,11... | collective-permute-start | bytes 786440 | tf_op jit(solution)/shard_map/ppermute | solution.py:16
  76.4 1.6 %copy-start.18 = (bf16[256,512]{1,0:T(8,128)(2,1)}, bf16[256,512]{1,0:T(8,128)(2,1)S(1)}, u32[]{:S(2)}) copy-start(bf16[256,512]{1,0:T(8,128)(2,1)S(1)} %collective-permute-done.3.far) | copy-start | bytes 786436
  76.4 1.5 %collective-permute-start.4 = (bf16[256,512]{1,0:T(8,128)(2,1)S(1)}, bf16[256,512]{1,0:T(8,128)(2,1)S(1)}, u32[]{:S(2)}, u32[]{:S(2)}) collective-permute-start(bf16[256,512]{1,0:T(8,128)(2,1)S(1)} %collective-permute-done.3.far), channel_id=1, source_target_pairs={{0,1},{1,0},{2,3},{3,2},{4,5},{5,4},{6,7},{7,6},{8,9},{9,8},{10,11... | collective-permute-start | bytes 786440 | tf_op jit(solution)/shard_map/ppermute | solution.py:16
  76.4 11.6 %collective-permute-start.9 = (bf16[256,512]{1,0:T(8,128)(2,1)S(1)}, bf16[256,512]{1,0:T(8,128)(2,1)S(1)}, u32[]{:S(2)}, u32[]{:S(2)}) collective-permute-start(bf16[256,512]{1,0:T(8,128)(2,1)S(1)} %bitcast.82), channel_id=1, source_target_pairs={{0,2},{1,3},{2,0},{3,1},{4,6},{5,7},{6,4},{7,5},{8,10},{9,11},{10,... | collective-permute-start | bytes 786440 | tf_op jit(solution)/shard_map/ppermute | solution.py:16
  87.4 1.6 %collective-permute-start.6 = (bf16[256,512]{1,0:T(8,128)(2,1)S(1)}, bf16[256,512]{1,0:T(8,128)(2,1)S(1)}, u32[]{:S(2)}, u32[]{:S(2)}) collective-permute-start(bf16[256,512]{1,0:T(8,128)(2,1)S(1)} %get-tuple-element.26), channel_id=1, source_target_pairs={{0,1},{1,0},{2,3},{3,2},{4,5},{5,4},{6,7},{7,6},{8,9},{9,8},{10,11... | collective-permute-start | bytes 786440 | tf_op jit(solution)/shard_map/ppermute | solution.py:16
  87.7 2.4 %collective-permute-start.8 = (bf16[256,512]{1,0:T(8,128)(2,1)S(1)}, bf16[256,512]{1,0:T(8,128)(2,1)S(1)}, u32[]{:S(2)}, u32[]{:S(2)}) collective-permute-start(bf16[256,512]{1,0:T(8,128)(2,1)S(1)} %bitcast.83), channel_id=1, source_target_pairs={{0,1},{1,0},{2,3},{3,2},{4,5},{5,4},{6,7},{7,6},{8,9},{9,8},{10,11... | collective-permute-start | bytes 786440 | tf_op jit(solution)/shard_map/ppermute | solution.py:16
  88.0 2.2 %copy-start.17 = (bf16[256,512]{1,0:T(8,128)(2,1)}, bf16[256,512]{1,0:T(8,128)(2,1)S(1)}, u32[]{:S(2)}) copy-start(bf16[256,512]{1,0:T(8,128)(2,1)S(1)} %collective-permute-done.9.far) | copy-start | bytes 786436
  88.0 2.2 %collective-permute-start.10 = (bf16[256,512]{1,0:T(8,128)(2,1)S(1)}, bf16[256,512]{1,0:T(8,128)(2,1)S(1)}, u32[]{:S(2)}, u32[]{:S(2)}) collective-permute-start(bf16[256,512]{1,0:T(8,128)(2,1)S(1)} %collective-permute-done.9.far), channel_id=1, source_target_pairs={{0,1},{1,0},{2,3},{3,2},{4,5},{5,4},{6,7},{7,6},{8,9},{9,8},{10,11... | collective-permute-start | bytes 786440 | tf_op jit(solution)/shard_map/ppermute | solution.py:16
  99.1 10.9 %copy-start.13 = (f32[2,256,512]{2,1,0:T(8,128)S(1)}, f32[2,256,512]{2,1,0:T(8,128)}, u32[]{:S(2)}) copy-start(f32[2,256,512]{2,1,0:T(8,128)} %get-tuple-element.19) | copy-start | bytes 3145732
  99.1 15.9 %copy-start.14 = (f32[2,256,512]{2,1,0:T(8,128)S(1)}, f32[2,256,512]{2,1,0:T(8,128)}, u32[]{:S(2)}) copy-start(f32[2,256,512]{2,1,0:T(8,128)} %get-tuple-element.23) | copy-start | bytes 3145732
  100.3 2.0 %collective-permute-start.12 = (bf16[256,512]{1,0:T(8,128)(2,1)S(1)}, bf16[256,512]{1,0:T(8,128)(2,1)S(1)}, u32[]{:S(2)}, u32[]{:S(2)}) collective-permute-start(bf16[256,512]{1,0:T(8,128)(2,1)S(1)} %get-tuple-element.28), channel_id=1, source_target_pairs={{0,1},{1,0},{2,3},{3,2},{4,5},{5,4},{6,7},{7,6},{8,9},{9,8},{10,11... | collective-permute-start | bytes 786440 | tf_op jit(solution)/shard_map/ppermute | solution.py:16
  100.6 3.9 %collective-permute-start.5 = (bf16[256,512]{1,0:T(8,128)(2,1)S(1)}, bf16[256,512]{1,0:T(8,128)(2,1)S(1)}, u32[]{:S(2)}, u32[]{:S(2)}) collective-permute-start(bf16[256,512]{1,0:T(8,128)(2,1)S(1)} %get-tuple-element.25), channel_id=1, source_target_pairs={{0,1},{1,0},{2,3},{3,2},{4,5},{5,4},{6,7},{7,6},{8,9},{9,8},{10,11... | collective-permute-start | bytes 786440 | tf_op jit(solution)/shard_map/ppermute | solution.py:16
  100.9 9.1 %collective-permute-start.7 = (bf16[256,512]{1,0:T(8,128)(2,1)S(1)}, bf16[256,512]{1,0:T(8,128)(2,1)S(1)}, u32[]{:S(2)}, u32[]{:S(2)}) collective-permute-start(bf16[256,512]{1,0:T(8,128)(2,1)S(1)} %fusion.5), channel_id=1, source_target_pairs={{0,2},{1,3},{2,0},{3,1},{4,6},{5,7},{6,4},{7,5},{8,10},{9,11},{10,... | collective-permute-start | bytes 786440 | tf_op jit(solution)/shard_map/ppermute | solution.py:16
  102.3 7.9 %collective-permute-start.11 = (bf16[256,512]{1,0:T(8,128)(2,1)S(1)}, bf16[256,512]{1,0:T(8,128)(2,1)S(1)}, u32[]{:S(2)}, u32[]{:S(2)}) collective-permute-start(bf16[256,512]{1,0:T(8,128)(2,1)S(1)} %get-tuple-element.27), channel_id=1, source_target_pairs={{0,1},{1,0},{2,3},{3,2},{4,5},{5,4},{6,7},{7,6},{8,9},{9,8},{10,11... | collective-permute-start | bytes 786440 | tf_op jit(solution)/shard_map/ppermute | solution.py:16
  103.4 30.1 %copy-start.24 = (f32[128,2]{0,1:T(2,128)S(1)}, f32[128,2]{0,1:T(2,128)}, u32[]{:S(2)}) copy-start(f32[128,2]{0,1:T(2,128)} %param.30) | copy-start | bytes 3076
  103.4 11.5 %collective-permute-start.13 = (bf16[256,512]{1,0:T(8,128)(2,1)S(1)}, bf16[256,512]{1,0:T(8,128)(2,1)S(1)}, u32[]{:S(2)}, u32[]{:S(2)}) collective-permute-start(bf16[256,512]{1,0:T(8,128)(2,1)S(1)} %fusion.2), channel_id=1, source_target_pairs={{0,2},{1,3},{2,0},{3,1},{4,6},{5,7},{6,4},{7,5},{8,10},{9,11},{10,... | collective-permute-start | bytes 786440 | tf_op jit(solution)/shard_map/ppermute | solution.py:16
  (9 other events, 6.5 us)

commit v4 on v3

--- a/solution.py
+++ b/solution.py
@@ -18,10 +18,6 @@
 
 def exchange(value):
     return lax.all_to_all(value, "seq", split_axis=0, concat_axis=0, tiled=True)
-
-
-def after(value, *others):
-    return lax.optimization_barrier((value, *others))[0]
 
 
 def params(mib):
@@ -77,7 +73,7 @@
             jax.ShapeDtypeStruct((count, part + 16, b.shape[1]), BF),
             jax.ShapeDtypeStruct((heads, toks), F32),
         ],
-        compiler_params=params(8),
+        compiler_params=params(56),
         name="own_state",
     )(x, step_t, decay_t, b)
 
@@ -115,7 +111,7 @@
             out_specs=whole(count, part, width),
         ),
         out_shape=jax.ShapeDtypeStruct((count, part, width), BF),
-        compiler_params=params(8),
+        compiler_params=params(56),
         name="prefix",
     )(place.reshape(1), got, init_rows)
 
@@ -150,7 +146,7 @@
         within_kernel,
         in_specs=[pl.BlockSpec(memory_space=pltpu.SMEM)] + [vmem] * 5,
         out_shape=jax.ShapeDtypeStruct((toks, inner), F32),
-        compiler_params=params(8),
+        compiler_params=params(56),
         cost_estimate=pl.CostEstimate(
             flops=4 * heads * toks * toks * LANES,
             bytes_accessed=6 * toks * inner,
@@ -160,66 +156,76 @@
     )(skip, x, step_t, cum_t, b, c)
 
 
-def tail_kernel(place_ref, c, arriving, cum_t, direct, z, gain, weight, give, keep, normed):
-    step = pl.program_id(0)
+def fetch(sems, *pairs):
+    copies = [pltpu.make_async_copy(src, dst, sems.at[i]) for i, (src, dst) in enumerate(pairs)]
+    for copy in copies:
+        copy.start()
+    return copies
+
+
+def cuts_of(ref, count):
+    rows = ref.shape[0] // count
+    return [ref.at[pl.ds(k * rows, rows)] for k in range(count)]
+
+
+def quarters(place_ref, share):
+    return [pl.ds(pl.multiple_of((place_ref[0] ^ k) * share, share), share) for k in range(4)]
+
+
+def tail_kernel(
+    place_ref, c_in, cum_in, gain_in, arriving_in, direct_in, z_in, weight_in,
+    near, last, keep, passing,
+    c, cum_t, gain, arriving, direct, z, weight, normed, sems,
+):
     heads, toks = cum_t.shape
-
-    @pl.when(step == 0)
-    def _():
-        grown = jnp.exp(cum_t[...]).T
-        lane = lax.broadcasted_iota(jnp.int32, (toks, LANES), 1)
-        left = lane < LANES // 2
-        nt = (((1,), (1,)), ((), ()))
-        for p in range(heads // 2):
-            spot = pl.ds(p * LANES, LANES)
-            inter = lax.dot_general(
-                c[...], arriving[spot, :], nt, preferred_element_type=F32
-            )
-            factor = by_pair(grown[:, 2 * p : 2 * p + 1], grown[:, 2 * p + 1 : 2 * p + 2], toks)
-            wide = z[:, spot].astype(F32)
-            gated = (direct[:, spot] + inter * factor) * (wide * (1.0 / (1.0 + jnp.exp(-wide))))
-            square = gated * gated
-            first = jnp.sum(jnp.where(left, square, 0.0), axis=1, keepdims=True)
-            second = jnp.sum(jnp.where(left, 0.0, square), axis=1, keepdims=True)
-            mean = by_pair(first, second, toks) * (2.0 / LANES)
-            normed[:, spot] = (gated * lax.rsqrt(mean + 1e-05) * gain[:, spot]).astype(BF)
-
-    part = jnp.dot(normed[...], weight[...], preferred_element_type=F32)
-
-    @pl.when(step < 2)
-    def _():
-        give[jnp.minimum(step, 1)] = part.astype(BF)
-
-    @pl.when(step >= 2)
-    def _():
-        keep[jnp.maximum(step - 2, 0)] = part
+    share = near.shape[1]
+    copies = fetch(
+        sems,
+        (cum_in, cum_t),
+        (gain_in, gain),
+        (c_in, c),
+        (arriving_in, arriving),
+        (z_in, z),
+        (direct_in, direct),
+        *zip(cuts_of(weight_in, 8), cuts_of(weight, 8)),
+    )
+    for copy in copies[:6]:
+        copy.wait()
+    grown = jnp.exp(cum_t[...]).T
+    lane = lax.broadcasted_iota(jnp.int32, (toks, LANES), 1)
+    left = lane < LANES // 2
+    nt = (((1,), (1,)), ((), ()))
+    for p in range(heads // 2):
+        spot = pl.ds(p * LANES, LANES)
+        inter = lax.dot_general(c[...], arriving[spot, :], nt, preferred_element_type=F32)
+        factor = by_pair(grown[:, 2 * p : 2 * p + 1], grown[:, 2 * p + 1 : 2 * p + 2], toks)
+        wide = z[:, spot].astype(F32)
+        gated = (direct[:, spot] + inter * factor) * (wide * (1.0 / (1.0 + jnp.exp(-wide))))
+        square = gated * gated
+        first = jnp.sum(jnp.where(left, square, 0.0), axis=1, keepdims=True)
+        second = jnp.sum(jnp.where(left, 0.0, square), axis=1, keepdims=True)
+        mean = by_pair(first, second, toks) * (2.0 / LANES)
+        normed[:, spot] = (gated * lax.rsqrt(mean + 1e-05) * gain[:, spot]).astype(BF)
+    for copy in copies[6:]:
+        copy.wait()
+    spots = quarters(place_ref, share)
+    for k, out in ((3, last), (1, near), (2, passing), (0, keep)):
+        part = jnp.dot(normed[...], weight[:, spots[k]], preferred_element_type=F32)
+        out[...] = part.astype(out.dtype)
 
 
 def mixer_tail(place, c, arriving, cum_t, direct, z, gain, weight):
     heads, toks = cum_t.shape
     inner, width = weight.shape
     share = width // 4
+    operands = (c, cum_t, gain.reshape(1, inner), arriving, direct, z, weight)
     return pl.pallas_call(
         tail_kernel,
-        grid_spec=pltpu.PrefetchScalarGridSpec(
-            num_scalar_prefetch=1,
-            grid=(4,),
-            in_specs=[
-                whole(*c.shape),
-                whole(*arriving.shape),
-                whole(heads, toks),
-                whole(toks, inner),
-                whole(toks, inner),
-                whole(1, inner),
-                pl.BlockSpec((inner, share), lambda j, place: (0, place[0] ^ ((2 * j + 1) % 5))),
-            ],
-            out_specs=[whole(2, toks, share)] * 2,
-            scratch_shapes=[pltpu.VMEM((toks, inner), BF)],
-        ),
-        out_shape=[
-            jax.ShapeDtypeStruct((2, toks, share), BF),
-            jax.ShapeDtypeStruct((2, toks, share), F32),
-        ],
+        in_specs=[pl.BlockSpec(memory_space=pltpu.SMEM)]
+        + [pl.BlockSpec(memory_space=pl.ANY)] * len(operands),
+        out_shape=[jax.ShapeDtypeStruct((toks, share), kind) for kind in (BF, BF, F32, F32)],
+        scratch_shapes=[pltpu.VMEM(a.shape, a.dtype) for a in operands]
+        + [pltpu.VMEM((toks, inner), BF), pltpu.SemaphoreType.DMA((14,))],
         compiler_params=params(56),
         cost_estimate=pl.CostEstimate(
             flops=2 * toks * inner * width,
@@ -227,84 +233,89 @@
             transcendentals=toks * inner,
         ),
         name="mixer_tail",
-    )(place.reshape(1), c, arriving, cum_t, direct, z, gain.reshape(1, inner), weight)
-
-
-def expert_kernel(place_ref, own, near, far, last, gain, wg, wu, wd, give, keep, rows, total):
-    place = place_ref[0]
-    step = pl.program_id(0)
-    share = own.shape[1]
-    spots = [pl.ds(pl.multiple_of((place ^ k) * share, share), share) for k in range(4)]
-    parts = [own, near, far, last]
-
-    @pl.when(step == 0)
-    def _():
-        wide = [p[...].astype(F32) for p in parts]
+    )(place.reshape(1), *operands)
+
+
+def expert_kernel(
+    place_ref, gain_in, own_in, near_in, far_in, last_in, wg_in, wu_in, wd_in,
+    near_out, last_out, keep_out, pass_out,
+    gain, own, near, far, last, wg, wu, wd, rows, act, sems,
+):
+    count, share = own.shape
+    width = 4 * share
+    tile = min(count, 256)
+    copies = fetch(
+        sems,
+        (gain_in, gain),
+        (own_in, own),
+        (near_in, near),
+        (far_in, far),
+        (last_in, last),
+        *zip(cuts_of(wg_in, 4), cuts_of(wg, 4)),
+        *zip(cuts_of(wu_in, 4), cuts_of(wu, 4)),
+        *zip(cuts_of(wd_in, 4), cuts_of(wd, 4)),
+    )
+    spots = quarters(place_ref, share)
+    for copy in copies[:5]:
+        copy.wait()
+
+    @pl.loop(0, count, step=64)
+    def _(start):
+        spot = pl.ds(pl.multiple_of(start, 64), 64)
+        wide = [p[spot, :].astype(F32) for p in (own, near, far, last)]
         square = sum(jnp.sum(w * w, axis=1, keepdims=True) for w in wide)
-        scale = lax.rsqrt(square * (1.0 / (4 * share)) + 1e-05)
+        scale = lax.rsqrt(square * (1.0 / width) + 1e-05)
         for k in range(4):
-            rows[k] = (wide[k] * scale * gain[:, spots[k]]).astype(BF)
-
-    gate = up = 0.0
-    for k in range(4):
-        gate += jnp.dot(rows[k], wg[spots[k], :], preferred_element_type=F32)
-        up += jnp.dot(rows[k], wu[spots[k], :], preferred_element_type=F32)
-    act = (gate * (1.0 / (1.0 + jnp.exp(-gate))) * up).astype(BF)
-    for k in range(4):
-        down = jnp.dot(act, wd[:, spots[k]], preferred_element_type=F32)
-
-        @pl.when(step == 0)
-        def _():
-            total[k] = down
-
-        @pl.when(step > 0)
-        def _():
-            total[k] += down
-
-    @pl.when(step == pl.num_programs(0) - 1)
-    def _():
-        give[0] = total[1].astype(BF)
-        give[1] = total[3].astype(BF)
-        keep[0] = total[0]
-        keep[1] = total[2]
-
-
-def run_expert(place, own, near, far, last, gain, wg, wu, wd):
+            rows[k, spot, :] = (wide[k] * scale * gain[:, spots[k]]).astype(BF)
+
+    for copy in copies[5:13]:
+        copy.wait()
+
+    @pl.loop(0, count, step=tile)
+    def _(start):
+        spot = pl.ds(pl.multiple_of(start, tile), tile)
+        gate = up = 0.0
+        for k in range(4):
+            part = rows[k, spot, :]
+            gate += jnp.dot(part, wg[spots[k], :], preferred_element_type=F32)
+            up += jnp.dot(part, wu[spots[k], :], preferred_element_type=F32)
+        act[spot, :] = (gate * (1.0 / (1.0 + jnp.exp(-gate))) * up).astype(BF)
+
+    for copy in copies[13:]:
+        copy.wait()
+
+    @pl.loop(0, count, step=tile)
+    def _(start):
+        spot = pl.ds(pl.multiple_of(start, tile), tile)
+        part = act[spot, :]
+        for k, out in ((3, last_out), (1, near_out), (2, pass_out), (0, keep_out)):
+            down = jnp.dot(part, wd[:, spots[k]], preferred_element_type=F32)
+            out[spot, :] = down.astype(BF)
+
+
+def run_expert(place, gain, own, near, far, last, wg, wu, wd):
     rows, share = own.shape
     width, inner = wg.shape
-    tile = inner // 2
-
-    part = whole(rows, share)
+    operands = (gain.reshape(1, width), own, near, far, last, wg, wu, wd)
     return pl.pallas_call(
         expert_kernel,
-        grid_spec=pltpu.PrefetchScalarGridSpec(
-            num_scalar_prefetch=1,
-            grid=(inner // tile,),
-            in_specs=[
-                part,
-                part,
-                part,
-                part,
-                whole(1, width),
-                pl.BlockSpec((width, tile), lambda j, _: (0, j)),
-                pl.BlockSpec((width, tile), lambda j, _: (0, j)),
-                pl.BlockSpec((tile, width), lambda j, _: (j, 0)),
-            ],
-            out_specs=[whole(2, rows, share)] * 2,
-            scratch_shapes=[pltpu.VMEM((4, rows, share), BF), pltpu.VMEM((4, rows, share), F32)],
-        ),
-        out_shape=[
-            jax.ShapeDtypeStruct((2, rows, share), BF),
-            jax.ShapeDtypeStruct((2, rows, share), F32),
+        in_specs=[pl.BlockSpec(memory_space=pltpu.SMEM)]
+        + [pl.BlockSpec(memory_space=pl.ANY)] * len(operands),
+        out_shape=[jax.ShapeDtypeStruct((rows, share), BF)] * 4,
+        scratch_shapes=[pltpu.VMEM(a.shape, a.dtype) for a in operands]
+        + [
+            pltpu.VMEM((4, rows, share), BF),
+            pltpu.VMEM((rows, inner), BF),
+            pltpu.SemaphoreType.DMA((17,)),
         ],
         compiler_params=params(56),
         cost_estimate=pl.CostEstimate(
             flops=6 * rows * width * inner,
-            bytes_accessed=6 * width * inner + 14 * rows * width,
+            bytes_accessed=6 * width * inner + 4 * rows * width,
             transcendentals=rows * inner,
         ),
         name="expert",
-    )(place.reshape(1), own, near, far, last, gain.reshape(1, width), wg, wu, wd)
+    )(place.reshape(1), *operands)
 
 
 def body(
@@ -336,7 +347,7 @@
     direct = within_block(skip_gain, input_heads, step_t, cum_t, b_proj, c_proj)
     back = entering_state(lax.axis_index("seq"), got, init_state.reshape(inner, state_size))
     arriving = exchange(back).reshape(inner, state_size)
-    give, keep = mixer_tail(
+    to_near, to_last, keep, passing = mixer_tail(
         place, c_proj, arriving, cum_t, direct, z_gate, norm_gain, out_weight
     )
 
@@ -357,36 +368,28 @@
     pick = spots.astype(BF)
     fill = jnp.any(spots.reshape(top_count, tok_rows, slots), axis=0).astype(BF)
 
-    got = swap(give, 1)
-    passing = swap((keep[1] + got[1].astype(F32)).astype(BF), 2)
+    from_last = swap(to_last, 1)
+    from_near = swap(to_near, 1)
+    from_far = swap((passing + from_last.astype(F32)).astype(BF), 2)
     own_tokens = lax.dynamic_slice_in_dim(tokens, place * share, share, 1)
-    projected = keep[0] + got[0].astype(F32) + passing.astype(F32)
+    projected = keep + from_near.astype(F32) + from_far.astype(F32)
     hidden = (own_tokens.astype(F32) + projected).astype(BF)
     outgoing = lax.dot_general(
         fill, hidden, (((0,), (0,)), ((), ())), preferred_element_type=F32
     ).astype(BF)
     arrived = exchange(outgoing.reshape(expert_count, slot_count, share)).reshape(slots, share)
 
-    cut = slots // 2
-    own = [arrived[:cut], arrived[cut:]]
-    far = [swap(own[0], 2), swap(own[1], 2)]
-    near = [swap(own[0], 1), swap(own[1], 1)]
-    weights = (moe_gain, w_gate[0], w_up[0], w_down[0])
-    give0, keep0 = run_expert(place, own[0], near[0], far[0], swap(far[0], 1), *weights)
-    pass_got0 = swap(give0[1], 1)
-    last1 = swap(after(far[1], give0), 1)
-    pass0 = (keep0[1] + pass_got0.astype(F32)).astype(BF)
-    give1, keep1 = run_expert(
-        place, after(own[1], pass0), near[1], far[1], last1, *weights
-    )
-    passed0 = swap(pass0, 2)
-    kept_got0 = swap(give0[0], 1)
-    pass_got1 = swap(give1[1], 1)
-    kept_got1 = swap(give1[0], 1)
-    passed1 = swap((keep1[1] + pass_got1.astype(F32)).astype(BF), 2)
-    result0 = (keep0[0] + kept_got0.astype(F32) + passed0.astype(F32)).astype(BF)
-    result1 = (keep1[0] + kept_got1.astype(F32) + passed1.astype(F32)).astype(BF)
-    results = jnp.concatenate([result0, result1]).reshape(expert_count, slot_count, share)
+    far = swap(arrived, 2)
+    near = swap(arrived, 1)
+    last = swap(far, 1)
+    to_near, to_last, keep, passing = run_expert(
+        place, moe_gain, arrived, near, far, last, w_gate[0], w_up[0], w_down[0]
+    )
+    from_last = swap(to_last, 1)
+    from_near = swap(to_near, 1)
+    from_far = swap((passing.astype(F32) + from_last.astype(F32)).astype(BF), 2)
+    results = (keep.astype(F32) + from_near.astype(F32) + from_far.astype(F32)).astype(BF)
+    results = results.reshape(expert_count, slot_count, share)
     returned = exchange(results).reshape(slots, share)
     chosen = jnp.dot(pick, returned, preferred_element_type=F32).reshape(
         top_count, tok_rows, share

time: 135 us -> 128 us (0.948)
  waiting for transfers between devices: 37.8 us -> 47.1 us
  local copies, waits for them, and re-layouts: 10.1 us -> 2.23 us
  Pallas kernels: 25 us -> 19.1 us
  starting transfers between devices: 19.4 us -> 16.7 us
    ppermute x14 -> x9, waiting for transfers between devices: 21.7 us -> 31.4 us  [swap(): return lax.ppermute(value, 'tp', [(i, i ^ bit) for i in range(count)])]
    pallas_call x3 -> x2, Pallas kernels: 21.1 us -> 12 us  [the longest x1 7.9 us: run_expert(): pl.pallas_call(expert_kernel, in_specs=[pl.BlockSpec(memory_space=pltpu.S...]
    unnamed x50 -> x16, local copies, waits for them, and re-layouts: 7.82 us -> 2.23 us
    ppermute x14 -> x9, starting transfers between devices: 8.56 us -> 5.89 us  [swap(): return lax.ppermute(value, 'tp', [(i, i ^ bit) for i in range(count)])]
    squeeze x2 -> x0, local copies, waits for them, and re-layouts: 2.28 us -> none  [the longest x1 1.21 us: body(): kept_got1 = swap(give1[0], 1)]
    convert_element_type x5 -> x3, other arithmetic: 3.44 us -> 3.41 us  [the longest x1 1.24 us: body(): (keep.astype(F32) + from_near.astype(F32) + from_far.astype(F32)).astype(BF)]
  transfers between devices with their start and end apart: 16 -> 11, of which waited for: 8 -> 8; matrix products, arithmetic and copies ran while one was open for 3% -> 2% of each run, Pallas kernels for 7% -> 2%
where the time goes in v4:
time: 128 us; the launch traced here: 127 us
  waiting for transfers between devices  47.1 us (37%)
  blocking collectives  35.6 us (28%)
  Pallas kernels  19.1 us (15%)
  starting transfers between devices  16.7 us (13%)
  other arithmetic  5.26 us (4%)
  local copies, waits for them, and re-layouts  2.23 us (2%)
    all_to_all x2, blocking collectives, exchange(): return lax.all_to_all(value, 'seq', split_axis=0, concat_axis=0, tiled=True)  35.6 us
    ppermute x9, waiting for transfers between devices, swap(): return lax.ppermute(value, 'tp', [(i, i ^ bit) for i in range(count)])  31.4 us
    all_to_all x2, waiting for transfers between devices, exchange(): return lax.all_to_all(value, 'seq', split_axis=0, concat_axis=0, tiled=True)  15.7 us
    all_to_all x2, starting transfers between devices, exchange(): return lax.all_to_all(value, 'seq', split_axis=0, concat_axis=0, tiled=True)  10.8 us
    pallas_call x1, Pallas kernels, run_expert(): pl.pallas_call(expert_kernel, in_specs=[pl.BlockSpec(memory_space=pltpu.S...  7.9 us
    ppermute x9, starting transfers between devices, swap(): return lax.ppermute(value, 'tp', [(i, i ^ bit) for i in range(count)])  5.89 us
    pallas_call x1, Pallas kernels, mixer_tail(): pl.pallas_call(tail_kernel, in_specs=[pl.BlockSpec(memory_space=pltpu.SME...  4.12 us
    pallas_call x1, Pallas kernels, own_state(): pl.pallas_call(state_kernel, out_shape=[jax.ShapeDtypeStruct((count, part...  2.72 us
  transfers between devices with their start and end apart: 11, of which 8 were waited for; matrix products, arithmetic and copies ran while one was open for 2% of the time, Pallas kernels for 2%

profile of v4, /device:TPU:0, one launch (start us, length us, event | category | flops | bytes accessed | tf_op | source)
XLA Modules:
  0.0 127.0 jit_solution(5616389149140734736)
XLA Ops:
  0.0 2.7 %own_state.1 = (bf16[8,144,128]{2,1,0:T(8,128)(2,1)}, f32[16,128]{1,0:T(8,128)}) custom-call(bf16[128,1024]{1,0:T(8,128)(2,1)} %x.3, f32[16,128]{1,0:T(8,128)} %bitcast.40, f32[16,128]{1,0:T(8,128)} %bitcast.42, bf16[128,128]{1,0:T(8,128)(2,1)} %b.3), custom_call_target="tpu_custom_call" | custom-call | tf_op jit(solution)/shard_map/own_state/pallas_call | solution.py:70
  2.7 7.3 %all-to-all-start = ((bf16[8,144,128]{2,1,0:T(8,128)(2,1)}), bf16[8,144,128]{2,1,0:T(8,128)(2,1)S(1)}, u32[]{:S(2)}, u32[]{:S(2)}) async-start(bf16[8,144,128]{2,1,0:T(8,128)(2,1)} %get-tuple-element.16), calls=%async_computation | async-start | bytes 589824 | tf_op jit(solution)/shard_map/all_to_all | solution.py:20
  10.0 9.6 %all-to-all-done.got = bf16[8,144,128]{2,1,0:T(8,128)(2,1)S(1)} async-done(((bf16[8,144,128]{2,1,0:T(8,128)(2,1)}), bf16[8,144,128]{2,1,0:T(8,128)(2,1)S(1)}, u32[]{:S(2)}, u32[]{:S(2)}) %all-to-all-start) | async-done | bytes 294944 | tf_op jit(solution)/shard_map/all_to_all | solution.py:20
  19.6 0.7 copy-done
  20.3 1.9 %prefix.1 = bf16[8,128,128]{2,1,0:T(8,128)(2,1)} custom-call(s32[1]{0:T(128)} %bitcast.4.place_ref, bf16[8,144,128]{2,1,0:T(8,128)(2,1)} %copy-done, f32[1024,128]{1,0:T(8,128)} %bitcast.39), custom_call_target="tpu_custom_call" | custom-call | tf_op jit(solution)/shard_map/prefix/pallas_call | solution.py:102
  22.2 3.6 %all-to-all-start.1 = ((bf16[8,128,128]{2,1,0:T(8,128)(2,1)}), bf16[8,128,128]{2,1,0:T(8,128)(2,1)S(1)}, u32[]{:S(2)}, u32[]{:S(2)}) async-start(bf16[8,128,128]{2,1,0:T(8,128)(2,1)} %prefix.1), calls=%async_computation.1 | async-start | bytes 524288 | tf_op jit(solution)/shard_map/all_to_all | solution.py:20
  25.8 2.5 %within_block.1.direct_in = f32[128,1024]{1,0:T(8,128)} custom-call(f32[16]{0:T(128)} %skip.1, bf16[128,1024]{1,0:T(8,128)(2,1)} %x.3, f32[16,128]{1,0:T(8,128)} %bitcast.41, f32[16,128]{1,0:T(8,128)} %get-tuple-element.15.cum_t.cum_in, bf16[128,128]{1,0:T(8,128)(2,1)} %b.3, bf16[128,128]{1,0:T(8,128)(2,1)} %c_in.1), custom_call_target="tpu_custom_call" | custom-call | flops 134217728 | bytes 786432 | tf_op jit(solution)/shard_map/within_block/pallas_call | solution.py:145
  28.2 6.1 %all-to-all-done.1 = bf16[8,128,128]{2,1,0:T(8,128)(2,1)S(1)} async-done(((bf16[8,128,128]{2,1,0:T(8,128)(2,1)}), bf16[8,128,128]{2,1,0:T(8,128)(2,1)S(1)}, u32[]{:S(2)}, u32[]{:S(2)}) %all-to-all-start.1) | async-done | bytes 262176 | tf_op jit(solution)/shard_map/all_to_all | solution.py:20
  34.3 0.7 copy-done.1
  35.0 4.1 %mixer_tail.1 = (bf16[128,512]{1,0:T(8,128)(2,1)}, bf16[128,512]{1,0:T(8,128)(2,1)}, f32[128,512]{1,0:T(8,128)}, f32[128,512]{1,0:T(8,128)}) custom-call(s32[1]{0:T(128)} %bitcast.place_ref, bf16[128,128]{1,0:T(8,128)(2,1)} %c_in.1, f32[16,128]{1,0:T(8,128)} %get-tuple-element.15.cum_t.cum_in, f32[1,1024]{1,0:T(1,128)} %bitcast.43, ...), custom_call_target="tpu_custom_call" | custom-call | flops 536870912 | bytes 6029312 | tf_op jit(solution)/shard_map/mixer_tail/pallas_call | solution.py:222
  39.4 0.6 collective-permute-start
  40.0 0.8 collective-permute-done.1
  40.8 1.0 add_convert_fusion.4
  41.7 1.6 %collective-permute-start.2 = (bf16[128,512]{1,0:T(8,128)(2,1)S(1)}, bf16[128,512]{1,0:T(8,128)(2,1)S(1)}, u32[]{:S(2)}, u32[]{:S(2)}) collective-permute-start(bf16[128,512]{1,0:T(8,128)(2,1)S(1)} %add_convert_fusion.4), channel_id=1, source_target_pairs={{0,2},{1,3},{2,0},{3,1},{4,6},{5,7},{6,4},{7,5},{8,10},{9,11},{10,... | collective-permute-start | bytes 393224 | tf_op jit(solution)/shard_map/ppermute | solution.py:16
  43.5 3.9 %collective-permute-done.2 = bf16[128,512]{1,0:T(8,128)(2,1)S(1)} collective-permute-done((bf16[128,512]{1,0:T(8,128)(2,1)S(1)}, bf16[128,512]{1,0:T(8,128)(2,1)S(1)}, u32[]{:S(2)}, u32[]{:S(2)}) %collective-permute-start.2) | collective-permute-done | bytes 131104 | tf_op jit(solution)/shard_map/ppermute | solution.py:16
  47.4 1.0 add_convert_fusion.3
  48.4 0.3 convolution_convert_fusion
  48.8 17.3 %all_to_all.20 = bf16[8,64,512]{2,1,0:T(8,128)(2,1)S(1)} all-to-all(bf16[8,64,512]{2,1,0:T(8,128)(2,1)S(1)} %bitcast.32), channel_id=1, replica_groups=mesh['seq'=8,'tp'=4] {'seq'}, dimensions={0} | all-to-all | bytes 1048576 | tf_op jit(solution)/shard_map/all_to_all | solution.py:20
  66.1 1.5 %collective-permute-start.4 = (bf16[512,512]{1,0:T(8,128)(2,1)S(1)}, bf16[512,512]{1,0:T(8,128)(2,1)S(1)}, u32[]{:S(2)}, u32[]{:S(2)}) collective-permute-start(bf16[512,512]{1,0:T(8,128)(2,1)S(1)} %bitcast.35), channel_id=1, source_target_pairs={{0,2},{1,3},{2,0},{3,1},{4,6},{5,7},{6,4},{7,5},{8,10},{9,11},{10,... | collective-permute-start | bytes 1572872 | tf_op jit(solution)/shard_map/ppermute | solution.py:16
  67.6 10.8 %collective-permute-done.4.far_in = bf16[512,512]{1,0:T(8,128)(2,1)S(1)} collective-permute-done((bf16[512,512]{1,0:T(8,128)(2,1)S(1)}, bf16[512,512]{1,0:T(8,128)(2,1)S(1)}, u32[]{:S(2)}, u32[]{:S(2)}) %collective-permute-start.4) | collective-permute-done | bytes 524320 | tf_op jit(solution)/shard_map/ppermute | solution.py:16
  78.4 1.9 %collective-permute-done.5.last_in = bf16[512,512]{1,0:T(8,128)(2,1)S(1)} collective-permute-done((bf16[512,512]{1,0:T(8,128)(2,1)S(1)}, bf16[512,512]{1,0:T(8,128)(2,1)S(1)}, u32[]{:S(2)}, u32[]{:S(2)}) %collective-permute-start.5) | collective-permute-done | bytes 524320 | tf_op jit(solution)/shard_map/ppermute | solution.py:16
  80.3 0.8 copy-done.6
  81.1 7.9 %expert.1 = (bf16[512,512]{1,0:T(8,128)(2,1)}, bf16[512,512]{1,0:T(8,128)(2,1)}, bf16[512,512]{1,0:T(8,128)(2,1)}, bf16[512,512]{1,0:T(8,128)(2,1)}) custom-call(s32[1]{0:T(128)} %bitcast.place_ref, f32[1,2048]{1,0:T(1,128)} %bitcast.48, bf16[512,512]{1,0:T(8,128)(2,1)} %bitcast.37, bf16[512,512]{1,0:T(8,128)(2,1)} %copy-done.5, bf16[512,512]{1,0:T(8,128)(2,1)} %copy-done.4, ...), custom_call_target="tpu_custom_call" | custom-call | flops 3221225472 | bytes 10485760 | tf_op jit(solution)/shard_map/expert/pallas_call | solution.py:300
  89.2 0.4 collective-permute-start.6
  89.6 1.6 %collective-permute-done.7 = bf16[512,512]{1,0:T(8,128)(2,1)S(1)} collective-permute-done((bf16[512,512]{1,0:T(8,128)(2,1)}, bf16[512,512]{1,0:T(8,128)(2,1)S(1)}, u32[]{:S(2)}, u32[]{:S(2)}) %collective-permute-start.7) | collective-permute-done | bytes 524320 | tf_op jit(solution)/shard_map/ppermute | solution.py:16
  91.2 1.2 add_convert_fusion.1
  92.4 1.6 %collective-permute-start.8 = (bf16[512,512]{1,0:T(8,128)(2,1)S(1)}, bf16[512,512]{1,0:T(8,128)(2,1)S(1)}, u32[]{:S(2)}, u32[]{:S(2)}) collective-permute-start(bf16[512,512]{1,0:T(8,128)(2,1)S(1)} %add_convert_fusion.1), channel_id=1, source_target_pairs={{0,2},{1,3},{2,0},{3,1},{4,6},{5,7},{6,4},{7,5},{8,10},{9,11},{10,... | collective-permute-start | bytes 1572872 | tf_op jit(solution)/shard_map/ppermute | solution.py:16
  94.0 12.4 %collective-permute-done.8 = bf16[512,512]{1,0:T(8,128)(2,1)S(1)} collective-permute-done((bf16[512,512]{1,0:T(8,128)(2,1)S(1)}, bf16[512,512]{1,0:T(8,128)(2,1)S(1)}, u32[]{:S(2)}, u32[]{:S(2)}) %collective-permute-start.8) | collective-permute-done | bytes 524320 | tf_op jit(solution)/shard_map/ppermute | solution.py:16
  106.4 1.2 add_convert_fusion
  107.7 18.3 %all_to_all.21 = bf16[8,64,512]{2,1,0:T(8,128)(2,1)S(1)} all-to-all(bf16[8,64,512]{2,1,0:T(8,128)(2,1)S(1)} %bitcast.33), channel_id=1, replica_groups=mesh['seq'=8,'tp'=4] {'seq'}, dimensions={0} | all-to-all | bytes 1048576 | tf_op jit(solution)/shard_map/all_to_all | solution.py:20
  126.0 0.4 fusion
  126.3 0.7 add_convert_fusion.2
  (23 shorter events, 0.6 us)
Async XLA Ops:
  2.7 16.9 %all-to-all-start = ((bf16[8,144,128]{2,1,0:T(8,128)(2,1)}), bf16[8,144,128]{2,1,0:T(8,128)(2,1)S(1)}, u32[]{:S(2)}, u32[]{:S(2)}) async-start(bf16[8,144,128]{2,1,0:T(8,128)(2,1)} %get-tuple-element.16), calls=%async_computation | async-start | bytes 589824 | tf_op jit(solution)/shard_map/all_to_all | solution.py:20
  19.6 0.7 copy-start
  22.2 12.1 %all-to-all-start.1 = ((bf16[8,128,128]{2,1,0:T(8,128)(2,1)}), bf16[8,128,128]{2,1,0:T(8,128)(2,1)S(1)}, u32[]{:S(2)}, u32[]{:S(2)}) async-start(bf16[8,128,128]{2,1,0:T(8,128)(2,1)} %prefix.1), calls=%async_computation.1 | async-start | bytes 524288 | tf_op jit(solution)/shard_map/all_to_all | solution.py:20
  34.3 0.7 copy-start.1
  35.0 4.2 %copy-start.3 = (s32[128,2]{0,1:T(2,128)S(1)}, s32[128,2]{0,1:T(2,128)}, u32[]{:S(2)}) copy-start(s32[128,2]{0,1:T(2,128)} %param.29) | copy-start | bytes 3076
  39.1 1.6 %collective-permute-start.1 = (bf16[128,512]{1,0:T(8,128)(2,1)}, bf16[128,512]{1,0:T(8,128)(2,1)S(1)}, u32[]{:S(2)}, u32[]{:S(2)}) collective-permute-start(bf16[128,512]{1,0:T(8,128)(2,1)} %get-tuple-element.20), channel_id=1, source_target_pairs={{0,1},{1,0},{2,3},{3,2},{4,5},{5,4},{6,7},{7,6},{8,9},{9,8},{10,11... | collective-permute-start | bytes 393224 | tf_op jit(solution)/shard_map/ppermute | solution.py:16
  39.4 4.0 %collective-permute-start = (bf16[128,512]{1,0:T(8,128)(2,1)}, bf16[128,512]{1,0:T(8,128)(2,1)S(1)}, u32[]{:S(2)}, u32[]{:S(2)}) collective-permute-start(bf16[128,512]{1,0:T(8,128)(2,1)} %get-tuple-element.18), channel_id=1, source_target_pairs={{0,1},{1,0},{2,3},{3,2},{4,5},{5,4},{6,7},{7,6},{8,9},{9,8},{10,11... | collective-permute-start | bytes 393224 | tf_op jit(solution)/shard_map/ppermute | solution.py:16
  41.7 5.6 %collective-permute-start.2 = (bf16[128,512]{1,0:T(8,128)(2,1)S(1)}, bf16[128,512]{1,0:T(8,128)(2,1)S(1)}, u32[]{:S(2)}, u32[]{:S(2)}) collective-permute-start(bf16[128,512]{1,0:T(8,128)(2,1)S(1)} %add_convert_fusion.4), channel_id=1, source_target_pairs={{0,2},{1,3},{2,0},{3,1},{4,6},{5,7},{6,4},{7,5},{8,10},{9,11},{10,... | collective-permute-start | bytes 393224 | tf_op jit(solution)/shard_map/ppermute | solution.py:16
  66.1 14.2 %copy-start.2 = (bf16[8,64,512]{2,1,0:T(8,128)(2,1)}, bf16[8,64,512]{2,1,0:T(8,128)(2,1)S(1)}, u32[]{:S(2)}) copy-start(bf16[8,64,512]{2,1,0:T(8,128)(2,1)S(1)} %all_to_all.20) | copy-start | bytes 1572868
  66.1 12.3 %collective-permute-start.4 = (bf16[512,512]{1,0:T(8,128)(2,1)S(1)}, bf16[512,512]{1,0:T(8,128)(2,1)S(1)}, u32[]{:S(2)}, u32[]{:S(2)}) collective-permute-start(bf16[512,512]{1,0:T(8,128)(2,1)S(1)} %bitcast.35), channel_id=1, source_target_pairs={{0,2},{1,3},{2,0},{3,1},{4,6},{5,7},{6,4},{7,5},{8,10},{9,11},{10,... | collective-permute-start | bytes 1572872 | tf_op jit(solution)/shard_map/ppermute | solution.py:16
  67.6 10.8 %collective-permute-start.3 = (bf16[512,512]{1,0:T(8,128)(2,1)S(1)}, bf16[512,512]{1,0:T(8,128)(2,1)S(1)}, u32[]{:S(2)}, u32[]{:S(2)}) collective-permute-start(bf16[512,512]{1,0:T(8,128)(2,1)S(1)} %bitcast.36), channel_id=1, source_target_pairs={{0,1},{1,0},{2,3},{3,2},{4,5},{5,4},{6,7},{7,6},{8,9},{9,8},{10,11... | collective-permute-start | bytes 1572872 | tf_op jit(solution)/shard_map/ppermute | solution.py:16
  78.4 1.9 %copy-start.4 = (bf16[512,512]{1,0:T(8,128)(2,1)}, bf16[512,512]{1,0:T(8,128)(2,1)S(1)}, u32[]{:S(2)}) copy-start(bf16[512,512]{1,0:T(8,128)(2,1)S(1)} %collective-permute-done.4.far_in) | copy-start | bytes 1572868
  78.4 1.9 %collective-permute-start.5 = (bf16[512,512]{1,0:T(8,128)(2,1)S(1)}, bf16[512,512]{1,0:T(8,128)(2,1)S(1)}, u32[]{:S(2)}, u32[]{:S(2)}) collective-permute-start(bf16[512,512]{1,0:T(8,128)(2,1)S(1)} %collective-permute-done.4.far_in), channel_id=1, source_target_pairs={{0,1},{1,0},{2,3},{3,2},{4,5},{5,4},{6,7},{7,6},{8,9},{9,8},{10,11... | collective-permute-start | bytes 1572872 | tf_op jit(solution)/shard_map/ppermute | solution.py:16
  78.4 1.9 %copy-start.5 = (bf16[512,512]{1,0:T(8,128)(2,1)}, bf16[512,512]{1,0:T(8,128)(2,1)S(1)}, u32[]{:S(2)}) copy-start(bf16[512,512]{1,0:T(8,128)(2,1)S(1)} %collective-permute-done.3.near_in) | copy-start | bytes 1572868
  80.3 0.8 copy-start.6
  89.0 2.2 %collective-permute-start.7 = (bf16[512,512]{1,0:T(8,128)(2,1)}, bf16[512,512]{1,0:T(8,128)(2,1)S(1)}, u32[]{:S(2)}, u32[]{:S(2)}) collective-permute-start(bf16[512,512]{1,0:T(8,128)(2,1)} %get-tuple-element.24), channel_id=1, source_target_pairs={{0,1},{1,0},{2,3},{3,2},{4,5},{5,4},{6,7},{7,6},{8,9},{9,8},{10,11... | collective-permute-start | bytes 1572872 | tf_op jit(solution)/shard_map/ppermute | solution.py:16
  89.2 4.8 %collective-permute-start.6 = (bf16[512,512]{1,0:T(8,128)(2,1)}, bf16[512,512]{1,0:T(8,128)(2,1)S(1)}, u32[]{:S(2)}, u32[]{:S(2)}) collective-permute-start(bf16[512,512]{1,0:T(8,128)(2,1)} %get-tuple-element.22), channel_id=1, source_target_pairs={{0,1},{1,0},{2,3},{3,2},{4,5},{5,4},{6,7},{7,6},{8,9},{9,8},{10,11... | collective-permute-start | bytes 1572872 | tf_op jit(solution)/shard_map/ppermute | solution.py:16
  91.2 34.8 %copy-start.7 = (f32[128,2]{0,1:T(2,128)S(1)}, f32[128,2]{0,1:T(2,128)}, u32[]{:S(2)}) copy-start(f32[128,2]{0,1:T(2,128)} %param.30) | copy-start | bytes 3076
  92.4 14.0 %collective-permute-start.8 = (bf16[512,512]{1,0:T(8,128)(2,1)S(1)}, bf16[512,512]{1,0:T(8,128)(2,1)S(1)}, u32[]{:S(2)}, u32[]{:S(2)}) collective-permute-start(bf16[512,512]{1,0:T(8,128)(2,1)S(1)} %add_convert_fusion.1), channel_id=1, source_target_pairs={{0,2},{1,3},{2,0},{3,1},{4,6},{5,7},{6,4},{7,5},{8,10},{9,11},{10,... | collective-permute-start | bytes 1572872 | tf_op jit(solution)/shard_map/ppermute | solution.py:16

commit v5 on v4

--- a/solution.py
+++ b/solution.py
@@ -18,6 +18,14 @@
 
 def exchange(value):
     return lax.all_to_all(value, "seq", split_axis=0, concat_axis=0, tiled=True)
+
+
+def after(value, *others):
+    return lax.optimization_barrier((value, *others))[0]
+
+
+def in_hbm(value):
+    return pltpu.with_memory_space_constraint(value, pltpu.HBM)
 
 
 def params(mib):
@@ -73,9 +81,9 @@
             jax.ShapeDtypeStruct((count, part + 16, b.shape[1]), BF),
             jax.ShapeDtypeStruct((heads, toks), F32),
         ],
-        compiler_params=params(56),
+        compiler_params=params(24),
         name="own_state",
-    )(x, step_t, decay_t, b)
+    )(in_hbm(x), in_hbm(step_t), in_hbm(decay_t), in_hbm(b))
 
 
 def prefix_kernel(place_ref, got, start, back):
@@ -96,24 +104,19 @@
             carries[h] = factor * carries[h] + got[turn, spot, :].astype(F32)
 
 
-def entering_state(place, got, init_rows):
+def entering_state(got, init_rows):
     count, rows, width = got.shape
     part = rows - 16
+    place = lax.axis_index("seq")
+    start = lax.dynamic_slice_in_dim(init_rows, place * part, part, 0)
+    vmem = pl.BlockSpec(memory_space=pltpu.VMEM)
     return pl.pallas_call(
         prefix_kernel,
-        grid_spec=pltpu.PrefetchScalarGridSpec(
-            num_scalar_prefetch=1,
-            grid=(1,),
-            in_specs=[
-                whole(count, rows, width),
-                pl.BlockSpec((part, width), lambda _, place: (place[0], 0)),
-            ],
-            out_specs=whole(count, part, width),
-        ),
+        in_specs=[pl.BlockSpec(memory_space=pltpu.SMEM), vmem, vmem],
         out_shape=jax.ShapeDtypeStruct((count, part, width), BF),
-        compiler_params=params(56),
+        compiler_params=params(24),
         name="prefix",
-    )(place.reshape(1), got, init_rows)
+    )(place.reshape(1), got, start)
 
 
 def within_kernel(skip, x, step_t, cum_t, b, c, out):
@@ -146,14 +149,14 @@
         within_kernel,
         in_specs=[pl.BlockSpec(memory_space=pltpu.SMEM)] + [vmem] * 5,
         out_shape=jax.ShapeDtypeStruct((toks, inner), F32),
-        compiler_params=params(56),
+        compiler_params=params(24),
         cost_estimate=pl.CostEstimate(
             flops=4 * heads * toks * toks * LANES,
             bytes_accessed=6 * toks * inner,
             transcendentals=heads * toks * toks,
         ),
         name="within_block",
-    )(skip, x, step_t, cum_t, b, c)
+    )(skip, in_hbm(x), in_hbm(step_t), cum_t, in_hbm(b), in_hbm(c))
 
 
 def fetch(sems, *pairs):
@@ -219,6 +222,8 @@
     inner, width = weight.shape
     share = width // 4
     operands = (c, cum_t, gain.reshape(1, inner), arriving, direct, z, weight)
+    fixed = (0, 2, 5, 6)
+    operands = [in_hbm(a) if i in fixed else a for i, a in enumerate(operands)]
     return pl.pallas_call(
         tail_kernel,
         in_specs=[pl.BlockSpec(memory_space=pltpu.SMEM)]
@@ -226,7 +231,7 @@
         out_shape=[jax.ShapeDtypeStruct((toks, share), kind) for kind in (BF, BF, F32, F32)],
         scratch_shapes=[pltpu.VMEM(a.shape, a.dtype) for a in operands]
         + [pltpu.VMEM((toks, inner), BF), pltpu.SemaphoreType.DMA((14,))],
-        compiler_params=params(56),
+        compiler_params=params(24),
         cost_estimate=pl.CostEstimate(
             flops=2 * toks * inner * width,
             bytes_accessed=2 * inner * width + 14 * toks * inner,
@@ -239,11 +244,11 @@
 def expert_kernel(
     place_ref, gain_in, own_in, near_in, far_in, last_in, wg_in, wu_in, wd_in,
     near_out, last_out, keep_out, pass_out,
-    gain, own, near, far, last, wg, wu, wd, rows, act, sems,
+    gain, own, near, far, last, wg, wu, wd, rows, sems,
 ):
     count, share = own.shape
     width = 4 * share
-    tile = min(count, 256)
+    spots = quarters(place_ref, share)
     copies = fetch(
         sems,
         (gain_in, gain),
@@ -251,11 +256,9 @@
         (near_in, near),
         (far_in, far),
         (last_in, last),
-        *zip(cuts_of(wg_in, 4), cuts_of(wg, 4)),
-        *zip(cuts_of(wu_in, 4), cuts_of(wu, 4)),
+        *((w_in.at[s], w.at[s]) for s in spots for w_in, w in ((wg_in, wg), (wu_in, wu))),
         *zip(cuts_of(wd_in, 4), cuts_of(wd, 4)),
     )
-    spots = quarters(place_ref, share)
     for copy in copies[:5]:
         copy.wait()
 
@@ -268,35 +271,24 @@
         for k in range(4):
             rows[k, spot, :] = (wide[k] * scale * gain[:, spots[k]]).astype(BF)
 
-    for copy in copies[5:13]:
-        copy.wait()
-
-    @pl.loop(0, count, step=tile)
-    def _(start):
-        spot = pl.ds(pl.multiple_of(start, tile), tile)
-        gate = up = 0.0
-        for k in range(4):
-            part = rows[k, spot, :]
-            gate += jnp.dot(part, wg[spots[k], :], preferred_element_type=F32)
-            up += jnp.dot(part, wu[spots[k], :], preferred_element_type=F32)
-        act[spot, :] = (gate * (1.0 / (1.0 + jnp.exp(-gate))) * up).astype(BF)
-
+    gate = up = 0.0
+    for k in range(4):
+        copies[5 + 2 * k].wait()
+        gate += jnp.dot(rows[k], wg[spots[k], :], preferred_element_type=F32)
+        copies[6 + 2 * k].wait()
+        up += jnp.dot(rows[k], wu[spots[k], :], preferred_element_type=F32)
+    act = (gate * (1.0 / (1.0 + jnp.exp(-gate))) * up).astype(BF)
     for copy in copies[13:]:
         copy.wait()
-
-    @pl.loop(0, count, step=tile)
-    def _(start):
-        spot = pl.ds(pl.multiple_of(start, tile), tile)
-        part = act[spot, :]
-        for k, out in ((3, last_out), (1, near_out), (2, pass_out), (0, keep_out)):
-            down = jnp.dot(part, wd[:, spots[k]], preferred_element_type=F32)
-            out[spot, :] = down.astype(BF)
+    for k, out in ((3, last_out), (1, near_out), (2, pass_out), (0, keep_out)):
+        out[...] = jnp.dot(act, wd[:, spots[k]], preferred_element_type=F32).astype(BF)
 
 
 def run_expert(place, gain, own, near, far, last, wg, wu, wd):
     rows, share = own.shape
     width, inner = wg.shape
-    operands = (gain.reshape(1, width), own, near, far, last, wg, wu, wd)
+    weights = (in_hbm(wg), in_hbm(wu), in_hbm(wd))
+    operands = (in_hbm(gain.reshape(1, width)), own, near, far, last, *weights)
     return pl.pallas_call(
         expert_kernel,
         in_specs=[pl.BlockSpec(memory_space=pltpu.SMEM)]
@@ -305,10 +297,9 @@
         scratch_shapes=[pltpu.VMEM(a.shape, a.dtype) for a in operands]
         + [
             pltpu.VMEM((4, rows, share), BF),
-            pltpu.VMEM((rows, inner), BF),
             pltpu.SemaphoreType.DMA((17,)),
         ],
-        compiler_params=params(56),
+        compiler_params=params(24),
         cost_estimate=pl.CostEstimate(
             flops=6 * rows * width * inner,
             bytes_accessed=6 * width * inner + 4 * rows * width,
@@ -345,7 +336,7 @@
     outgoing, cum_t = own_state(input_heads, step_t, decay_log.T, b_proj, seq_count)
     got = exchange(outgoing)
     direct = within_block(skip_gain, input_heads, step_t, cum_t, b_proj, c_proj)
-    back = entering_state(lax.axis_index("seq"), got, init_state.reshape(inner, state_size))
+    back = entering_state(got, init_state.reshape(inner, state_size))
     arriving = exchange(back).reshape(inner, state_size)
     to_near, to_last, keep, passing = mixer_tail(
         place, c_proj, arriving, cum_t, direct, z_gate, norm_gain, out_weight
@@ -379,17 +370,34 @@
     ).astype(BF)
     arrived = exchange(outgoing.reshape(expert_count, slot_count, share)).reshape(slots, share)
 
-    far = swap(arrived, 2)
-    near = swap(arrived, 1)
-    last = swap(far, 1)
-    to_near, to_last, keep, passing = run_expert(
-        place, moe_gain, arrived, near, far, last, w_gate[0], w_up[0], w_down[0]
-    )
-    from_last = swap(to_last, 1)
-    from_near = swap(to_near, 1)
-    from_far = swap((passing.astype(F32) + from_last.astype(F32)).astype(BF), 2)
-    results = (keep.astype(F32) + from_near.astype(F32) + from_far.astype(F32)).astype(BF)
-    results = results.reshape(expert_count, slot_count, share)
+    cut = slots // 2
+    own = [arrived[:cut], arrived[cut:]]
+    far = [swap(part, 2) for part in own]
+    near = [swap(part, 1) for part in own]
+    weights = (w_gate[0], w_up[0], w_down[0])
+    last = swap(far[0], 1)
+    to_near0, to_last0, keep0, pass0 = run_expert(
+        place, moe_gain, own[0], near[0], far[0], last, *weights
+    )
+    from_last0 = swap(to_last0, 1)
+    last = swap(after(far[1], to_last0), 1)
+    pass0 = (pass0.astype(F32) + from_last0.astype(F32)).astype(BF)
+    from_far0 = swap(pass0, 2)
+    to_near1, to_last1, keep1, pass1 = run_expert(
+        place, moe_gain, after(own[1], pass0), near[1], far[1], last, *weights
+    )
+    from_near0 = swap(to_near0, 1)
+    from_last1 = swap(after(to_last1, from_far0), 1)
+    from_near1 = swap(to_near1, 1)
+    from_far1 = swap((pass1.astype(F32) + from_last1.astype(F32)).astype(BF), 2)
+    results = [
+        (keep.astype(F32) + from_near.astype(F32) + from_far.astype(F32)).astype(BF)
+        for keep, from_near, from_far in (
+            (keep0, from_near0, from_far0),
+            (keep1, from_near1, from_far1),
+        )
+    ]
+    results = jnp.concatenate(results).reshape(expert_count, slot_count, share)
     returned = exchange(results).reshape(slots, share)
     chosen = jnp.dot(pick, returned, preferred_element_type=F32).reshape(
         top_count, tok_rows, share

time: 128 us -> 116 us (0.906)
  waiting for transfers between devices: 47.1 us -> 39.6 us
  starting transfers between devices: 16.7 us -> 20.4 us
  other arithmetic: 5.26 us -> 2.18 us
  Pallas kernels: 19.1 us -> 16.5 us
  local copies, waits for them, and re-layouts: 2.23 us -> 0.07 us
    ppermute x9 -> x15, waiting for transfers between devices: 31.4 us -> 23.2 us  [swap(): return lax.ppermute(value, 'tp', [(i, i ^ bit) for i in range(count)])]
    ppermute x9 -> x15, starting transfers between devices: 5.89 us -> 9.59 us  [swap(): return lax.ppermute(value, 'tp', [(i, i ^ bit) for i in range(count)])]
    unnamed x16 -> x8, local copies, waits for them, and re-layouts: 2.23 us -> 0.02 us
    pallas_call x1 -> x2, Pallas kernels: 7.9 us -> 7.96 us  [run_expert(): pl.pallas_call(expert_kernel, in_specs=[pl.BlockSpec(memory_space=pltpu.S...]
  transfers between devices with their start and end apart: 11 -> 17, of which waited for: 8 -> 9; matrix products, arithmetic and copies ran while one was open for 2% -> 1% of each run, Pallas kernels for 2% -> 8%
where the time goes in v5:
time: 116 us; the launch traced here: 115 us
  waiting for transfers between devices  39.6 us (34%)
  blocking collectives  35.6 us (31%)
  starting transfers between devices  20.4 us (18%)
  Pallas kernels  16.5 us (14%)
  other arithmetic  2.18 us (2%)
    all_to_all x2, blocking collectives, exchange(): return lax.all_to_all(value, 'seq', split_axis=0, concat_axis=0, tiled=True)  35.6 us
    ppermute x15, waiting for transfers between devices, swap(): return lax.ppermute(value, 'tp', [(i, i ^ bit) for i in range(count)])  23.2 us
    all_to_all x2, waiting for transfers between devices, exchange(): return lax.all_to_all(value, 'seq', split_axis=0, concat_axis=0, tiled=True)  16.4 us
    all_to_all x2, starting transfers between devices, exchange(): return lax.all_to_all(value, 'seq', split_axis=0, concat_axis=0, tiled=True)  10.8 us
    ppermute x15, starting transfers between devices, swap(): return lax.ppermute(value, 'tp', [(i, i ^ bit) for i in range(count)])  9.59 us
    pallas_call x2, Pallas kernels, run_expert(): pl.pallas_call(expert_kernel, in_specs=[pl.BlockSpec(memory_space=pltpu.S...  7.96 us
    pallas_call x1, Pallas kernels, mixer_tail(): pl.pallas_call(tail_kernel, in_specs=[pl.BlockSpec(memory_space=pltpu.SME...  3.15 us
    pallas_call x1, Pallas kernels, own_state(): pl.pallas_call(state_kernel, out_shape=[jax.ShapeDtypeStruct((count, part...  2.78 us
  transfers between devices with their start and end apart: 17, of which 9 were waited for; matrix products, arithmetic and copies ran while one was open for 1% of the time, Pallas kernels for 8%

profile of v5, /device:TPU:0, one launch (start us, length us, event | category | flops | bytes accessed | tf_op | source)
XLA Modules:
  0.0 115.5 jit_solution(16025041171796515500)
XLA Ops:
  0.0 2.8 %own_state.1 = (bf16[8,144,128]{2,1,0:T(8,128)(2,1)}, f32[16,128]{1,0:T(8,128)S(1)}) custom-call(bf16[128,1024]{1,0:T(8,128)(2,1)} %x.3, f32[16,128]{1,0:T(8,128)} %bitcast.52, f32[16,128]{1,0:T(8,128)} %bitcast.54, bf16[128,128]{1,0:T(8,128)(2,1)} %b.3), custom_call_target="tpu_custom_call" | custom-call | tf_op jit(solution)/shard_map/own_state/pallas_call | solution.py:78
  2.8 7.3 %all-to-all-start = ((bf16[8,144,128]{2,1,0:T(8,128)(2,1)}), bf16[8,144,128]{2,1,0:T(8,128)(2,1)S(1)}, u32[]{:S(2)}, u32[]{:S(2)}) async-start(bf16[8,144,128]{2,1,0:T(8,128)(2,1)} %get-tuple-element.23), calls=%async_computation | async-start | bytes 589824 | tf_op jit(solution)/shard_map/all_to_all | solution.py:20
  10.1 9.6 %all-to-all-done.got = bf16[8,144,128]{2,1,0:T(8,128)(2,1)S(1)} async-done(((bf16[8,144,128]{2,1,0:T(8,128)(2,1)}), bf16[8,144,128]{2,1,0:T(8,128)(2,1)S(1)}, u32[]{:S(2)}, u32[]{:S(2)}) %all-to-all-start) | async-done | bytes 294944 | tf_op jit(solution)/shard_map/all_to_all | solution.py:20
  19.7 0.9 prefix.1
  20.6 3.6 %all-to-all-start.1 = ((bf16[8,128,128]{2,1,0:T(8,128)(2,1)}), bf16[8,128,128]{2,1,0:T(8,128)(2,1)S(1)}, u32[]{:S(2)}, u32[]{:S(2)}) async-start(bf16[8,128,128]{2,1,0:T(8,128)(2,1)} %prefix.1), calls=%async_computation.1 | async-start | bytes 524288 | tf_op jit(solution)/shard_map/all_to_all | solution.py:20
  24.2 1.7 %within_block.1.direct_in = f32[128,1024]{1,0:T(8,128)S(1)} custom-call(f32[16]{0:T(128)S(1)} %copy-done.1, bf16[128,1024]{1,0:T(8,128)(2,1)} %x.3, f32[16,128]{1,0:T(8,128)} %bitcast.53, f32[16,128]{1,0:T(8,128)S(1)} %get-tuple-element.22.cum_t.cum_in, bf16[128,128]{1,0:T(8,128)(2,1)} %b.3, bf16[128,128]{1,0:T(8,128)(2,1)} %c_in.1), custom_call_target="tpu_custom_call" | custom-call | flops 134217728 | bytes 786432 | tf_op jit(solution)/shard_map/within_block/pallas_call | solution.py:148
  25.8 6.9 %all-to-all-done.1 = bf16[8,128,128]{2,1,0:T(8,128)(2,1)S(1)} async-done(((bf16[8,128,128]{2,1,0:T(8,128)(2,1)}), bf16[8,128,128]{2,1,0:T(8,128)(2,1)S(1)}, u32[]{:S(2)}, u32[]{:S(2)}) %all-to-all-start.1) | async-done | bytes 262176 | tf_op jit(solution)/shard_map/all_to_all | solution.py:20
  32.7 3.1 %mixer_tail.1 = (bf16[128,512]{1,0:T(8,128)(2,1)S(1)}, bf16[128,512]{1,0:T(8,128)(2,1)S(1)}, f32[128,512]{1,0:T(8,128)S(1)}, f32[128,512]{1,0:T(8,128)S(1)}) custom-call(s32[1]{0:T(128)} %bitcast.place_ref, bf16[128,128]{1,0:T(8,128)(2,1)} %c_in.1, f32[16,128]{1,0:T(8,128)S(1)} %get-tuple-element.22.cum_t.cum_in, f32[1,1024]{1,0:T(1,128)} %bitcast.55, ...), custom_call_target="tpu_custom_call" | custom-call | flops 536870912 | bytes 6029312 | tf_op jit(solution)/shard_map/mixer_tail/pallas_call | solution.py:227
  36.1 0.6 collective-permute-start
  36.7 0.6 collective-permute-done.1
  37.3 1.6 %collective-permute-start.2 = (bf16[128,512]{1,0:T(8,128)(2,1)S(1)}, bf16[128,512]{1,0:T(8,128)(2,1)S(1)}, u32[]{:S(2)}, u32[]{:S(2)}) collective-permute-start(bf16[128,512]{1,0:T(8,128)(2,1)S(1)} %add_convert_fusion.6), channel_id=1, source_target_pairs={{0,2},{1,3},{2,0},{3,1},{4,6},{5,7},{6,4},{7,5},{8,10},{9,11},{10,... | collective-permute-start | bytes 393224 | tf_op jit(solution)/shard_map/ppermute | solution.py:16
  39.0 3.9 %collective-permute-done.2 = bf16[128,512]{1,0:T(8,128)(2,1)S(1)} collective-permute-done((bf16[128,512]{1,0:T(8,128)(2,1)S(1)}, bf16[128,512]{1,0:T(8,128)(2,1)S(1)}, u32[]{:S(2)}, u32[]{:S(2)}) %collective-permute-start.2) | collective-permute-done | bytes 131104 | tf_op jit(solution)/shard_map/ppermute | solution.py:16
  42.9 1.0 add_convert_fusion.5
  43.9 0.3 convolution_convert_fusion
  44.2 17.4 %all_to_all.20 = bf16[8,64,512]{2,1,0:T(8,128)(2,1)S(1)} all-to-all(bf16[8,64,512]{2,1,0:T(8,128)(2,1)S(1)} %bitcast.48), channel_id=1, replica_groups=mesh['seq'=8,'tp'=4] {'seq'}, dimensions={0} | all-to-all | bytes 1048576 | tf_op jit(solution)/shard_map/all_to_all | solution.py:20
  61.6 1.6 %collective-permute-start.4 = (bf16[256,512]{1,0:T(8,128)(2,1)S(1)}, bf16[256,512]{1,0:T(8,128)(2,1)S(1)}, u32[]{:S(2)}, u32[]{:S(2)}) collective-permute-start(bf16[256,512]{1,0:T(8,128)(2,1)S(1)} %bitcast.38), channel_id=1, source_target_pairs={{0,2},{1,3},{2,0},{3,1},{4,6},{5,7},{6,4},{7,5},{8,10},{9,11},{10,... | collective-permute-start | bytes 786440 | tf_op jit(solution)/shard_map/ppermute | solution.py:16
  63.2 5.2 %collective-permute-done.4.far_in = bf16[256,512]{1,0:T(8,128)(2,1)S(1)} collective-permute-done((bf16[256,512]{1,0:T(8,128)(2,1)S(1)}, bf16[256,512]{1,0:T(8,128)(2,1)S(1)}, u32[]{:S(2)}, u32[]{:S(2)}) %collective-permute-start.4) | collective-permute-done | bytes 262176 | tf_op jit(solution)/shard_map/ppermute | solution.py:16
  68.4 1.5 %collective-permute-start.10 = (bf16[256,512]{1,0:T(8,128)(2,1)S(1)}, bf16[256,512]{1,0:T(8,128)(2,1)S(1)}, u32[]{:S(2)}, u32[]{:S(2)}) collective-permute-start(bf16[256,512]{1,0:T(8,128)(2,1)S(1)} %bitcast.35), channel_id=1, source_target_pairs={{0,2},{1,3},{2,0},{3,1},{4,6},{5,7},{6,4},{7,5},{8,10},{9,11},{10,... | collective-permute-start | bytes 786440 | tf_op jit(solution)/shard_map/ppermute | solution.py:16
  69.9 4.0 %expert.2 = (bf16[256,512]{1,0:T(8,128)(2,1)S(1)}, bf16[256,512]{1,0:T(8,128)(2,1)S(1)}, bf16[256,512]{1,0:T(8,128)(2,1)S(1)}, bf16[256,512]{1,0:T(8,128)(2,1)S(1)}) custom-call(s32[1]{0:T(128)} %bitcast.place_ref, f32[1,2048]{1,0:T(1,128)} %bitcast.50, bf16[256,512]{1,0:T(8,128)(2,1)S(1)} %bitcast.40, bf16[256,512]{1,0:T(8,128)(2,1)S(1)} %collective-permute-done.3.near_in, ...), custom_call_target="tpu_custom_call" | custom-call | flops 1610612736 | bytes 8388608 | tf_op jit(solution)/shard_map/expert/pallas_call | solution.py:292
  73.9 0.3 collective-permute-start.7
  74.2 0.3 collective-permute-start.9
  74.5 2.6 %collective-permute-done.10.far_in = bf16[256,512]{1,0:T(8,128)(2,1)S(1)} collective-permute-done((bf16[256,512]{1,0:T(8,128)(2,1)S(1)}, bf16[256,512]{1,0:T(8,128)(2,1)S(1)}, u32[]{:S(2)}, u32[]{:S(2)}) %collective-permute-start.10) | collective-permute-done | bytes 262176 | tf_op jit(solution)/shard_map/ppermute | solution.py:16
  77.2 1.6 %collective-permute-start.8 = (bf16[256,512]{1,0:T(8,128)(2,1)S(1)}, bf16[256,512]{1,0:T(8,128)(2,1)S(1)}, u32[]{:S(2)}, u32[]{:S(2)}) collective-permute-start(bf16[256,512]{1,0:T(8,128)(2,1)S(1)} %add_convert_fusion.3), channel_id=1, source_target_pairs={{0,2},{1,3},{2,0},{3,1},{4,6},{5,7},{6,4},{7,5},{8,10},{9,11},{10,... | collective-permute-start | bytes 786440 | tf_op jit(solution)/shard_map/ppermute | solution.py:16
  78.8 4.0 %expert.3 = (bf16[256,512]{1,0:T(8,128)(2,1)S(1)}, bf16[256,512]{1,0:T(8,128)(2,1)S(1)}, bf16[256,512]{1,0:T(8,128)(2,1)S(1)}, bf16[256,512]{1,0:T(8,128)(2,1)S(1)}) custom-call(s32[1]{0:T(128)} %bitcast.place_ref, f32[1,2048]{1,0:T(1,128)} %bitcast.51, bf16[256,512]{1,0:T(8,128)(2,1)S(1)} %bitcast.37, bf16[256,512]{1,0:T(8,128)(2,1)S(1)} %collective-permute-done.9.near_in, ...), custom_call_target="tpu_custom_call" | custom-call | flops 1610612736 | bytes 8388608 | tf_op jit(solution)/shard_map/expert/pallas_call | solution.py:292
  82.8 3.2 %collective-permute-done.8 = bf16[256,512]{1,0:T(8,128)(2,1)S(1)} collective-permute-done((bf16[256,512]{1,0:T(8,128)(2,1)S(1)}, bf16[256,512]{1,0:T(8,128)(2,1)S(1)}, u32[]{:S(2)}, u32[]{:S(2)}) %collective-permute-start.8) | collective-permute-done | bytes 262176 | tf_op jit(solution)/shard_map/ppermute | solution.py:16
  86.0 0.5 collective-permute-start.6
  86.5 1.0 collective-permute-done.13
  87.6 1.6 %collective-permute-start.14 = (bf16[256,512]{1,0:T(8,128)(2,1)S(1)}, bf16[256,512]{1,0:T(8,128)(2,1)S(1)}, u32[]{:S(2)}, u32[]{:S(2)}) collective-permute-start(bf16[256,512]{1,0:T(8,128)(2,1)S(1)} %add_convert_fusion.1), channel_id=1, source_target_pairs={{0,2},{1,3},{2,0},{3,1},{4,6},{5,7},{6,4},{7,5},{8,10},{9,11},{10,... | collective-permute-start | bytes 786440 | tf_op jit(solution)/shard_map/ppermute | solution.py:16
  89.3 6.7 %collective-permute-done.14 = bf16[256,512]{1,0:T(8,128)(2,1)S(1)} collective-permute-done((bf16[256,512]{1,0:T(8,128)(2,1)S(1)}, bf16[256,512]{1,0:T(8,128)(2,1)S(1)}, u32[]{:S(2)}, u32[]{:S(2)}) %collective-permute-start.14) | collective-permute-done | bytes 262176 | tf_op jit(solution)/shard_map/ppermute | solution.py:16
  96.1 18.3 %all_to_all.21 = bf16[8,64,512]{2,1,0:T(8,128)(2,1)S(1)} all-to-all(bf16[8,64,512]{2,1,0:T(8,128)(2,1)S(1)} %bitcast.47), channel_id=1, replica_groups=mesh['seq'=8,'tp'=4] {'seq'}, dimensions={0} | all-to-all | bytes 1048576 | tf_op jit(solution)/shard_map/all_to_all | solution.py:20
  114.4 0.4 fusion
  114.8 0.7 add_convert_fusion.4
  (33 shorter events, 0.9 us)
Async XLA Ops:
  0.0 10.0 %copy-start = (f32[16,64,128]{2,1,0:T(8,128)S(1)}, f32[16,64,128]{2,1,0:T(8,128)}, u32[]{:S(2)}) copy-start(f32[16,64,128]{2,1,0:T(8,128)} %param.25) | copy-start | bytes 1572868
  0.0 24.1 %copy-start.1 = (f32[16]{0:T(128)S(1)}, f32[16]{0:T(128)}, u32[]{:S(2)}) copy-start(f32[16]{0:T(128)} %skip.1) | copy-start | bytes 196
  2.8 16.9 %all-to-all-start = ((bf16[8,144,128]{2,1,0:T(8,128)(2,1)}), bf16[8,144,128]{2,1,0:T(8,128)(2,1)S(1)}, u32[]{:S(2)}, u32[]{:S(2)}) async-start(bf16[8,144,128]{2,1,0:T(8,128)(2,1)} %get-tuple-element.23), calls=%async_computation | async-start | bytes 589824 | tf_op jit(solution)/shard_map/all_to_all | solution.py:20
  20.6 12.1 %all-to-all-start.1 = ((bf16[8,128,128]{2,1,0:T(8,128)(2,1)}), bf16[8,128,128]{2,1,0:T(8,128)(2,1)S(1)}, u32[]{:S(2)}, u32[]{:S(2)}) async-start(bf16[8,128,128]{2,1,0:T(8,128)(2,1)} %prefix.1), calls=%async_computation.1 | async-start | bytes 524288 | tf_op jit(solution)/shard_map/all_to_all | solution.py:20
  32.7 3.2 %copy-start.2 = (s32[128,2]{0,1:T(2,128)S(1)}, s32[128,2]{0,1:T(2,128)}, u32[]{:S(2)}) copy-start(s32[128,2]{0,1:T(2,128)} %param.29) | copy-start | bytes 3076
  35.8 1.4 %collective-permute-start.1 = (bf16[128,512]{1,0:T(8,128)(2,1)S(1)}, bf16[128,512]{1,0:T(8,128)(2,1)S(1)}, u32[]{:S(2)}, u32[]{:S(2)}) collective-permute-start(bf16[128,512]{1,0:T(8,128)(2,1)S(1)} %get-tuple-element.27), channel_id=1, source_target_pairs={{0,1},{1,0},{2,3},{3,2},{4,5},{5,4},{6,7},{7,6},{8,9},{9,8},{10,11... | collective-permute-start | bytes 393224 | tf_op jit(solution)/shard_map/ppermute | solution.py:16
  36.1 2.9 %collective-permute-start = (bf16[128,512]{1,0:T(8,128)(2,1)S(1)}, bf16[128,512]{1,0:T(8,128)(2,1)S(1)}, u32[]{:S(2)}, u32[]{:S(2)}) collective-permute-start(bf16[128,512]{1,0:T(8,128)(2,1)S(1)} %get-tuple-element.25), channel_id=1, source_target_pairs={{0,1},{1,0},{2,3},{3,2},{4,5},{5,4},{6,7},{7,6},{8,9},{9,8},{10,11... | collective-permute-start | bytes 393224 | tf_op jit(solution)/shard_map/ppermute | solution.py:16
  37.3 5.6 %collective-permute-start.2 = (bf16[128,512]{1,0:T(8,128)(2,1)S(1)}, bf16[128,512]{1,0:T(8,128)(2,1)S(1)}, u32[]{:S(2)}, u32[]{:S(2)}) collective-permute-start(bf16[128,512]{1,0:T(8,128)(2,1)S(1)} %add_convert_fusion.6), channel_id=1, source_target_pairs={{0,2},{1,3},{2,0},{3,1},{4,6},{5,7},{6,4},{7,5},{8,10},{9,11},{10,... | collective-permute-start | bytes 393224 | tf_op jit(solution)/shard_map/ppermute | solution.py:16
  61.6 6.7 %collective-permute-start.4 = (bf16[256,512]{1,0:T(8,128)(2,1)S(1)}, bf16[256,512]{1,0:T(8,128)(2,1)S(1)}, u32[]{:S(2)}, u32[]{:S(2)}) collective-permute-start(bf16[256,512]{1,0:T(8,128)(2,1)S(1)} %bitcast.38), channel_id=1, source_target_pairs={{0,2},{1,3},{2,0},{3,1},{4,6},{5,7},{6,4},{7,5},{8,10},{9,11},{10,... | collective-permute-start | bytes 786440 | tf_op jit(solution)/shard_map/ppermute | solution.py:16
  63.2 6.7 %collective-permute-start.3 = (bf16[256,512]{1,0:T(8,128)(2,1)S(1)}, bf16[256,512]{1,0:T(8,128)(2,1)S(1)}, u32[]{:S(2)}, u32[]{:S(2)}) collective-permute-start(bf16[256,512]{1,0:T(8,128)(2,1)S(1)} %bitcast.39), channel_id=1, source_target_pairs={{0,1},{1,0},{2,3},{3,2},{4,5},{5,4},{6,7},{7,6},{8,9},{9,8},{10,11... | collective-permute-start | bytes 786440 | tf_op jit(solution)/shard_map/ppermute | solution.py:16
  68.4 1.5 %collective-permute-start.5 = (bf16[256,512]{1,0:T(8,128)(2,1)S(1)}, bf16[256,512]{1,0:T(8,128)(2,1)S(1)}, u32[]{:S(2)}, u32[]{:S(2)}) collective-permute-start(bf16[256,512]{1,0:T(8,128)(2,1)S(1)} %collective-permute-done.4.far_in), channel_id=1, source_target_pairs={{0,1},{1,0},{2,3},{3,2},{4,5},{5,4},{6,7},{7,6},{8,9},{9,8},{10,11... | collective-permute-start | bytes 786440 | tf_op jit(solution)/shard_map/ppermute | solution.py:16
  68.4 8.7 %collective-permute-start.10 = (bf16[256,512]{1,0:T(8,128)(2,1)S(1)}, bf16[256,512]{1,0:T(8,128)(2,1)S(1)}, u32[]{:S(2)}, u32[]{:S(2)}) collective-permute-start(bf16[256,512]{1,0:T(8,128)(2,1)S(1)} %bitcast.35), channel_id=1, source_target_pairs={{0,2},{1,3},{2,0},{3,1},{4,6},{5,7},{6,4},{7,5},{8,10},{9,11},{10,... | collective-permute-start | bytes 786440 | tf_op jit(solution)/shard_map/ppermute | solution.py:16
  73.9 3.2 %collective-permute-start.7 = (bf16[256,512]{1,0:T(8,128)(2,1)S(1)}, bf16[256,512]{1,0:T(8,128)(2,1)S(1)}, u32[]{:S(2)}, u32[]{:S(2)}) collective-permute-start(bf16[256,512]{1,0:T(8,128)(2,1)S(1)} %get-tuple-element.31), channel_id=1, source_target_pairs={{0,1},{1,0},{2,3},{3,2},{4,5},{5,4},{6,7},{7,6},{8,9},{9,8},{10,11... | collective-permute-start | bytes 786440 | tf_op jit(solution)/shard_map/ppermute | solution.py:16
  74.2 4.6 %collective-permute-start.9 = (bf16[256,512]{1,0:T(8,128)(2,1)S(1)}, bf16[256,512]{1,0:T(8,128)(2,1)S(1)}, u32[]{:S(2)}, u32[]{:S(2)}) collective-permute-start(bf16[256,512]{1,0:T(8,128)(2,1)S(1)} %bitcast.36), channel_id=1, source_target_pairs={{0,1},{1,0},{2,3},{3,2},{4,5},{5,4},{6,7},{7,6},{8,9},{9,8},{10,11... | collective-permute-start | bytes 786440 | tf_op jit(solution)/shard_map/ppermute | solution.py:16
  77.1 1.7 %collective-permute-start.11 = (bf16[256,512]{1,0:T(8,128)(2,1)S(1)}, bf16[256,512]{1,0:T(8,128)(2,1)S(1)}, u32[]{:S(2)}, u32[]{:S(2)}) collective-permute-start(bf16[256,512]{1,0:T(8,128)(2,1)S(1)} %collective-permute-done.10.far_in), channel_id=1, source_target_pairs={{0,1},{1,0},{2,3},{3,2},{4,5},{5,4},{6,7},{7,6},{8,9},{9,8},{10,11... | collective-permute-start | bytes 786440 | tf_op jit(solution)/shard_map/ppermute | solution.py:16
  77.2 8.8 %collective-permute-start.8 = (bf16[256,512]{1,0:T(8,128)(2,1)S(1)}, bf16[256,512]{1,0:T(8,128)(2,1)S(1)}, u32[]{:S(2)}, u32[]{:S(2)}) collective-permute-start(bf16[256,512]{1,0:T(8,128)(2,1)S(1)} %add_convert_fusion.3), channel_id=1, source_target_pairs={{0,2},{1,3},{2,0},{3,1},{4,6},{5,7},{6,4},{7,5},{8,10},{9,11},{10,... | collective-permute-start | bytes 786440 | tf_op jit(solution)/shard_map/ppermute | solution.py:16
  86.0 1.5 %collective-permute-start.13 = (bf16[256,512]{1,0:T(8,128)(2,1)S(1)}, bf16[256,512]{1,0:T(8,128)(2,1)S(1)}, u32[]{:S(2)}, u32[]{:S(2)}) collective-permute-start(bf16[256,512]{1,0:T(8,128)(2,1)S(1)} %get-tuple-element.38), channel_id=1, source_target_pairs={{0,1},{1,0},{2,3},{3,2},{4,5},{5,4},{6,7},{7,6},{8,9},{9,8},{10,11... | collective-permute-start | bytes 786440 | tf_op jit(solution)/shard_map/ppermute | solution.py:16
  86.0 3.2 %collective-permute-start.6 = (bf16[256,512]{1,0:T(8,128)(2,1)S(1)}, bf16[256,512]{1,0:T(8,128)(2,1)S(1)}, u32[]{:S(2)}, u32[]{:S(2)}) collective-permute-start(bf16[256,512]{1,0:T(8,128)(2,1)S(1)} %get-tuple-element.29), channel_id=1, source_target_pairs={{0,1},{1,0},{2,3},{3,2},{4,5},{5,4},{6,7},{7,6},{8,9},{9,8},{10,11... | collective-permute-start | bytes 786440 | tf_op jit(solution)/shard_map/ppermute | solution.py:16
  86.5 2.8 %collective-permute-start.12 = (bf16[256,512]{1,0:T(8,128)(2,1)S(1)}, bf16[256,512]{1,0:T(8,128)(2,1)S(1)}, u32[]{:S(2)}, u32[]{:S(2)}) collective-permute-start(bf16[256,512]{1,0:T(8,128)(2,1)S(1)} %get-tuple-element.35), channel_id=1, source_target_pairs={{0,1},{1,0},{2,3},{3,2},{4,5},{5,4},{6,7},{7,6},{8,9},{9,8},{10,11... | collective-permute-start | bytes 786440 | tf_op jit(solution)/shard_map/ppermute | solution.py:16
  87.6 8.4 %collective-permute-start.14 = (bf16[256,512]{1,0:T(8,128)(2,1)S(1)}, bf16[256,512]{1,0:T(8,128)(2,1)S(1)}, u32[]{:S(2)}, u32[]{:S(2)}) collective-permute-start(bf16[256,512]{1,0:T(8,128)(2,1)S(1)} %add_convert_fusion.1), channel_id=1, source_target_pairs={{0,2},{1,3},{2,0},{3,1},{4,6},{5,7},{6,4},{7,5},{8,10},{9,11},{10,... | collective-permute-start | bytes 786440 | tf_op jit(solution)/shard_map/ppermute | solution.py:16
  89.2 25.2 %copy-start.3 = (f32[128,2]{0,1:T(2,128)S(1)}, f32[128,2]{0,1:T(2,128)}, u32[]{:S(2)}) copy-start(f32[128,2]{0,1:T(2,128)} %param.30) | copy-start | bytes 3076

commit v6 on v5

--- a/solution.py
+++ b/solution.py
@@ -176,12 +176,13 @@
 
 
 def tail_kernel(
-    place_ref, c_in, cum_in, gain_in, arriving_in, direct_in, z_in, weight_in,
+    place_ref, c_in, cum_in, gain_in, arriving_in, direct_in, z_in, weight_in, tokens_in,
     near, last, keep, passing,
-    c, cum_t, gain, arriving, direct, z, weight, normed, sems,
+    c, cum_t, gain, arriving, direct, z, weight, tokens, normed, sems,
 ):
     heads, toks = cum_t.shape
     share = near.shape[1]
+    spots = quarters(place_ref, share)
     copies = fetch(
         sems,
         (cum_in, cum_t),
@@ -191,6 +192,7 @@
         (z_in, z),
         (direct_in, direct),
         *zip(cuts_of(weight_in, 8), cuts_of(weight, 8)),
+        (tokens_in.at[:, spots[0]], tokens),
     )
     for copy in copies[:6]:
         copy.wait()
@@ -211,26 +213,31 @@
         normed[:, spot] = (gated * lax.rsqrt(mean + 1e-05) * gain[:, spot]).astype(BF)
     for copy in copies[6:]:
         copy.wait()
-    spots = quarters(place_ref, share)
     for k, out in ((3, last), (1, near), (2, passing), (0, keep)):
         part = jnp.dot(normed[...], weight[:, spots[k]], preferred_element_type=F32)
+        if k == 0:
+            part += tokens[...].astype(F32)
         out[...] = part.astype(out.dtype)
 
 
-def mixer_tail(place, c, arriving, cum_t, direct, z, gain, weight):
+def mixer_tail(place, c, arriving, cum_t, direct, z, gain, weight, tokens):
     heads, toks = cum_t.shape
     inner, width = weight.shape
     share = width // 4
-    operands = (c, cum_t, gain.reshape(1, inner), arriving, direct, z, weight)
-    fixed = (0, 2, 5, 6)
+    operands = (c, cum_t, gain.reshape(1, inner), arriving, direct, z, weight, tokens)
+    fixed = (0, 2, 5, 6, 7)
     operands = [in_hbm(a) if i in fixed else a for i, a in enumerate(operands)]
     return pl.pallas_call(
         tail_kernel,
         in_specs=[pl.BlockSpec(memory_space=pltpu.SMEM)]
         + [pl.BlockSpec(memory_space=pl.ANY)] * len(operands),
         out_shape=[jax.ShapeDtypeStruct((toks, share), kind) for kind in (BF, BF, F32, F32)],
-        scratch_shapes=[pltpu.VMEM(a.shape, a.dtype) for a in operands]
-        + [pltpu.VMEM((toks, inner), BF), pltpu.SemaphoreType.DMA((14,))],
+        scratch_shapes=[pltpu.VMEM(a.shape, a.dtype) for a in operands[:-1]]
+        + [
+            pltpu.VMEM((toks, share), BF),
+            pltpu.VMEM((toks, inner), BF),
+            pltpu.SemaphoreType.DMA((15,)),
+        ],
         compiler_params=params(24),
         cost_estimate=pl.CostEstimate(
             flops=2 * toks * inner * width,
@@ -339,7 +346,7 @@
     back = entering_state(got, init_state.reshape(inner, state_size))
     arriving = exchange(back).reshape(inner, state_size)
     to_near, to_last, keep, passing = mixer_tail(
-        place, c_proj, arriving, cum_t, direct, z_gate, norm_gain, out_weight
+        place, c_proj, arriving, cum_t, direct, z_gate, norm_gain, out_weight, tokens
     )
 
     model_width = out_weight.shape[1]
@@ -354,56 +361,66 @@
     before = jnp.arange(items)[:, None] > jnp.arange(items)[None, :]
     earlier = jnp.dot(before.astype(BF), onehot.astype(BF), preferred_element_type=F32)
     rank = jnp.sum(jnp.where(onehot, earlier, 0.0), axis=1).astype(jnp.int32)
-    placed = flat_expert * slot_count + rank
+    cut = slot_count // 2
+    half = slots // 2
+    late = (rank >= cut).astype(jnp.int32)
+    placed = late * half + flat_expert * cut + rank - late * cut
     spots = placed[:, None] == jnp.arange(slots, dtype=jnp.int32)[None, :]
-    pick = spots.astype(BF)
-    fill = jnp.any(spots.reshape(top_count, tok_rows, slots), axis=0).astype(BF)
+    spots = spots.reshape(top_count, tok_rows, slots)
+    fill = jnp.any(spots, axis=0).astype(BF)
+    combine = jnp.sum(jnp.where(spots, route_weights.T[:, :, None], 0.0), axis=0)
 
     from_last = swap(to_last, 1)
     from_near = swap(to_near, 1)
     from_far = swap((passing + from_last.astype(F32)).astype(BF), 2)
-    own_tokens = lax.dynamic_slice_in_dim(tokens, place * share, share, 1)
-    projected = keep + from_near.astype(F32) + from_far.astype(F32)
-    hidden = (own_tokens.astype(F32) + projected).astype(BF)
-    outgoing = lax.dot_general(
-        fill, hidden, (((0,), (0,)), ((), ())), preferred_element_type=F32
-    ).astype(BF)
-    arrived = exchange(outgoing.reshape(expert_count, slot_count, share)).reshape(slots, share)
-
-    cut = slots // 2
-    own = [arrived[:cut], arrived[cut:]]
-    far = [swap(part, 2) for part in own]
-    near = [swap(part, 1) for part in own]
+    hidden = (keep + from_near.astype(F32) + from_far.astype(F32)).astype(BF)
+
+    def dispatch(turn):
+        outgoing = lax.dot_general(
+            fill[:, turn * half : (turn + 1) * half],
+            hidden,
+            (((0,), (0,)), ((), ())),
+            preferred_element_type=F32,
+        ).astype(BF)
+        return outgoing.reshape(expert_count, cut, share)
+
+    def combined(turn, results):
+        returned = exchange(results.reshape(expert_count, cut, share)).reshape(half, share)
+        return jnp.dot(
+            combine[:, turn * half : (turn + 1) * half],
+            returned.astype(F32),
+            precision=lax.Precision.HIGHEST,
+            preferred_element_type=F32,
+        )
+
     weights = (w_gate[0], w_up[0], w_down[0])
-    last = swap(far[0], 1)
+    own0 = exchange(dispatch(0)).reshape(half, share)
+    far0 = swap(own0, 2)
+    near0 = swap(own0, 1)
+    own1 = exchange(after(dispatch(1), near0)).reshape(half, share)
+    last0 = swap(far0, 1)
     to_near0, to_last0, keep0, pass0 = run_expert(
-        place, moe_gain, own[0], near[0], far[0], last, *weights
-    )
+        place, moe_gain, own0, near0, far0, last0, *weights
+    )
+    own1 = after(own1, to_last0)
+    far1 = swap(own1, 2)
+    near1 = swap(own1, 1)
     from_last0 = swap(to_last0, 1)
-    last = swap(after(far[1], to_last0), 1)
+    from_near0 = swap(to_near0, 1)
     pass0 = (pass0.astype(F32) + from_last0.astype(F32)).astype(BF)
     from_far0 = swap(pass0, 2)
+    last1 = swap(far1, 1)
     to_near1, to_last1, keep1, pass1 = run_expert(
-        place, moe_gain, after(own[1], pass0), near[1], far[1], last, *weights
-    )
-    from_near0 = swap(to_near0, 1)
-    from_last1 = swap(after(to_last1, from_far0), 1)
+        place, moe_gain, after(own1, pass0), near1, far1, last1, *weights
+    )
+    result0 = (keep0.astype(F32) + from_near0.astype(F32) + from_far0.astype(F32)).astype(BF)
+    mixed = hidden.astype(F32) + combined(0, result0)
+    from_last1 = swap(to_last1, 1)
     from_near1 = swap(to_near1, 1)
     from_far1 = swap((pass1.astype(F32) + from_last1.astype(F32)).astype(BF), 2)
-    results = [
-        (keep.astype(F32) + from_near.astype(F32) + from_far.astype(F32)).astype(BF)
-        for keep, from_near, from_far in (
-            (keep0, from_near0, from_far0),
-            (keep1, from_near1, from_far1),
-        )
-    ]
-    results = jnp.concatenate(results).reshape(expert_count, slot_count, share)
-    returned = exchange(results).reshape(slots, share)
-    chosen = jnp.dot(pick, returned, preferred_element_type=F32).reshape(
-        top_count, tok_rows, share
-    )
-    mixed_out = hidden.astype(F32) + jnp.sum(route_weights.T[:, :, None] * chosen, axis=0)
-    return mixed_out.astype(BF)
+    result1 = (keep1.astype(F32) + from_near1.astype(F32) + from_far1.astype(F32)).astype(BF)
+    mixed = mixed + combined(1, result1)
+    return mixed.astype(BF)
 
 
 def solution(mesh):

time: 116 us -> 120 us (1.034)
  blocking collectives: 35.6 us -> 11.9 us
  waiting for transfers between devices: 39.6 us -> 55.6 us
  starting transfers between devices: 20.4 us -> 30.1 us
  matrix products: 0.89 us -> 2.67 us
    all_to_all x2 -> x1, blocking collectives: 35.6 us -> 11.9 us  [exchange(): return lax.all_to_all(value, 'seq', split_axis=0, concat_axis=0, tiled=True)]
    all_to_all x2 -> x5, waiting for transfers between devices: 16.4 us -> 32.8 us  [exchange(): return lax.all_to_all(value, 'seq', split_axis=0, concat_axis=0, tiled=True)]
    all_to_all x2 -> x5, starting transfers between devices: 10.8 us -> 22.2 us  [exchange(): return lax.all_to_all(value, 'seq', split_axis=0, concat_axis=0, tiled=True)]
    dot_general x2 -> x4, matrix products: 0.7 us -> 2.47 us  [the longest x2 1.25 us: dispatch(): lax.dot_general(fill[:, turn * half:(turn + 1) * half], hidden, (((0,), (...]
    ppermute x15, starting transfers between devices: 9.59 us -> 7.93 us  [swap(): return lax.ppermute(value, 'tp', [(i, i ^ bit) for i in range(count)])]
  transfers between devices with their start and end apart: 17 -> 20, of which waited for: 9 -> 12; matrix products, arithmetic and copies ran while one was open for 1% -> 3% of each run, Pallas kernels for 8% -> 5%
where the time goes in v6:
time: 120 us; the launch traced here: 119 us
  waiting for transfers between devices  55.6 us (46%)
  starting transfers between devices  30.1 us (25%)
  Pallas kernels  16.5 us (14%)
  blocking collectives  11.9 us (10%)
  matrix products  2.67 us (2%)
  other arithmetic  2.1 us (2%)
    all_to_all x5, waiting for transfers between devices, exchange(): return lax.all_to_all(value, 'seq', split_axis=0, concat_axis=0, tiled=True)  32.8 us
    ppermute x15, waiting for transfers between devices, swap(): return lax.ppermute(value, 'tp', [(i, i ^ bit) for i in range(count)])  22.9 us
    all_to_all x5, starting transfers between devices, exchange(): return lax.all_to_all(value, 'seq', split_axis=0, concat_axis=0, tiled=True)  22.2 us
    all_to_all x1, blocking collectives, exchange(): return lax.all_to_all(value, 'seq', split_axis=0, concat_axis=0, tiled=True)  11.9 us
    pallas_call x2, Pallas kernels, run_expert(): pl.pallas_call(expert_kernel, in_specs=[pl.BlockSpec(memory_space=pltpu.S...  7.96 us
    ppermute x15, starting transfers between devices, swap(): return lax.ppermute(value, 'tp', [(i, i ^ bit) for i in range(count)])  7.93 us
    pallas_call x1, Pallas kernels, mixer_tail(): pl.pallas_call(tail_kernel, in_specs=[pl.BlockSpec(memory_space=pltpu.SME...  3.18 us
    pallas_call x1, Pallas kernels, own_state(): pl.pallas_call(state_kernel, out_shape=[jax.ShapeDtypeStruct((count, part...  2.79 us
  transfers between devices with their start and end apart: 20, of which 12 were waited for; matrix products, arithmetic and copies ran while one was open for 3% of the time, Pallas kernels for 5%

profile of v6, /device:TPU:0, one launch (start us, length us, event | category | flops | bytes accessed | tf_op | source)
XLA Modules:
  0.0 119.2 jit_solution(13311072716278724279)
XLA Ops:
  0.0 2.8 %own_state.1 = (bf16[8,144,128]{2,1,0:T(8,128)(2,1)}, f32[16,128]{1,0:T(8,128)S(1)}) custom-call(bf16[128,1024]{1,0:T(8,128)(2,1)} %x.3, f32[16,128]{1,0:T(8,128)} %bitcast.58, f32[16,128]{1,0:T(8,128)} %bitcast.60, bf16[128,128]{1,0:T(8,128)(2,1)} %b.3), custom_call_target="tpu_custom_call" | custom-call | tf_op jit(solution)/shard_map/own_state/pallas_call | solution.py:78
  2.8 7.3 %all-to-all-start = ((bf16[8,144,128]{2,1,0:T(8,128)(2,1)}), bf16[8,144,128]{2,1,0:T(8,128)(2,1)S(1)}, u32[]{:S(2)}, u32[]{:S(2)}) async-start(bf16[8,144,128]{2,1,0:T(8,128)(2,1)} %get-tuple-element.23), calls=%async_computation | async-start | bytes 589824 | tf_op jit(solution)/shard_map/all_to_all | solution.py:20
  10.1 9.6 %all-to-all-done.got = bf16[8,144,128]{2,1,0:T(8,128)(2,1)S(1)} async-done(((bf16[8,144,128]{2,1,0:T(8,128)(2,1)}), bf16[8,144,128]{2,1,0:T(8,128)(2,1)S(1)}, u32[]{:S(2)}, u32[]{:S(2)}) %all-to-all-start) | async-done | bytes 294944 | tf_op jit(solution)/shard_map/all_to_all | solution.py:20
  19.7 0.9 prefix.1
  20.6 3.6 %all-to-all-start.1 = ((bf16[8,128,128]{2,1,0:T(8,128)(2,1)}), bf16[8,128,128]{2,1,0:T(8,128)(2,1)S(1)}, u32[]{:S(2)}, u32[]{:S(2)}) async-start(bf16[8,128,128]{2,1,0:T(8,128)(2,1)} %prefix.1), calls=%async_computation.1 | async-start | bytes 524288 | tf_op jit(solution)/shard_map/all_to_all | solution.py:20
  24.2 1.7 %within_block.1.direct_in = f32[128,1024]{1,0:T(8,128)S(1)} custom-call(f32[16]{0:T(128)S(1)} %copy-done.1, bf16[128,1024]{1,0:T(8,128)(2,1)} %x.3, f32[16,128]{1,0:T(8,128)} %bitcast.59, f32[16,128]{1,0:T(8,128)S(1)} %get-tuple-element.22.cum_t.cum_in, bf16[128,128]{1,0:T(8,128)(2,1)} %b.3, bf16[128,128]{1,0:T(8,128)(2,1)} %c_in.1), custom_call_target="tpu_custom_call" | custom-call | flops 134217728 | bytes 786432 | tf_op jit(solution)/shard_map/within_block/pallas_call | solution.py:148
  25.9 6.9 %all-to-all-done.1 = bf16[8,128,128]{2,1,0:T(8,128)(2,1)S(1)} async-done(((bf16[8,128,128]{2,1,0:T(8,128)(2,1)}), bf16[8,128,128]{2,1,0:T(8,128)(2,1)S(1)}, u32[]{:S(2)}, u32[]{:S(2)}) %all-to-all-start.1) | async-done | bytes 262176 | tf_op jit(solution)/shard_map/all_to_all | solution.py:20
  32.7 3.2 %mixer_tail.1 = (bf16[128,512]{1,0:T(8,128)(2,1)S(1)}, bf16[128,512]{1,0:T(8,128)(2,1)S(1)}, f32[128,512]{1,0:T(8,128)S(1)}, f32[128,512]{1,0:T(8,128)S(1)}) custom-call(s32[1]{0:T(128)} %bitcast.place_ref, bf16[128,128]{1,0:T(8,128)(2,1)} %c_in.1, f32[16,128]{1,0:T(8,128)S(1)} %get-tuple-element.22.cum_t.cum_in, f32[1,1024]{1,0:T(1,128)} %bitcast.61, ...), custom_call_target="tpu_custom_call" | custom-call | flops 536870912 | bytes 6029312 | tf_op jit(solution)/shard_map/mixer_tail/pallas_call | solution.py:230
  36.7 0.6 collective-permute-done.1
  37.3 1.6 %collective-permute-start.2 = (bf16[128,512]{1,0:T(8,128)(2,1)S(1)}, bf16[128,512]{1,0:T(8,128)(2,1)S(1)}, u32[]{:S(2)}, u32[]{:S(2)}) collective-permute-start(bf16[128,512]{1,0:T(8,128)(2,1)S(1)} %add_convert_fusion.6), channel_id=1, source_target_pairs={{0,2},{1,3},{2,0},{3,1},{4,6},{5,7},{6,4},{7,5},{8,10},{9,11},{10,... | collective-permute-start | bytes 393224 | tf_op jit(solution)/shard_map/ppermute | solution.py:16
  39.1 3.9 %collective-permute-done.2 = bf16[128,512]{1,0:T(8,128)(2,1)S(1)} collective-permute-done((bf16[128,512]{1,0:T(8,128)(2,1)S(1)}, bf16[128,512]{1,0:T(8,128)(2,1)S(1)}, u32[]{:S(2)}, u32[]{:S(2)}) %collective-permute-start.2) | collective-permute-done | bytes 131104 | tf_op jit(solution)/shard_map/ppermute | solution.py:16
  43.3 11.9 %all_to_all.30 = bf16[8,32,512]{2,1,0:T(8,128)(2,1)S(1)} all-to-all(bf16[8,32,512]{2,1,0:T(8,128)(2,1)S(1)} %bitcast.55), channel_id=1, replica_groups=mesh['seq'=8,'tp'=4] {'seq'}, dimensions={0} | all-to-all | bytes 524288 | tf_op jit(solution)/shard_map/all_to_all | solution.py:20
  55.2 1.5 %collective-permute-start.4 = (bf16[256,512]{1,0:T(8,128)(2,1)S(1)}, bf16[256,512]{1,0:T(8,128)(2,1)S(1)}, u32[]{:S(2)}, u32[]{:S(2)}) collective-permute-start(bf16[256,512]{1,0:T(8,128)(2,1)S(1)} %bitcast.44), channel_id=1, source_target_pairs={{0,2},{1,3},{2,0},{3,1},{4,6},{5,7},{6,4},{7,5},{8,10},{9,11},{10,... | collective-permute-start | bytes 786440 | tf_op jit(solution)/shard_map/ppermute | solution.py:16
  56.7 1.0 convolution_convert_fusion
  57.7 3.5 %all-to-all-start.4 = ((bf16[8,32,512]{2,1,0:T(8,128)(2,1)}), bf16[8,32,512]{2,1,0:T(8,128)(2,1)S(1)}, u32[]{:S(2)}, u32[]{:S(2)}) async-start(bf16[8,32,512]{2,1,0:T(8,128)(2,1)} %bitcast.19), calls=%async_computation.4 | async-start | bytes 524288 | tf_op jit(solution)/shard_map/all_to_all | solution.py:20
  61.2 2.8 %collective-permute-done.4.far_in = bf16[256,512]{1,0:T(8,128)(2,1)S(1)} collective-permute-done((bf16[256,512]{1,0:T(8,128)(2,1)S(1)}, bf16[256,512]{1,0:T(8,128)(2,1)S(1)}, u32[]{:S(2)}, u32[]{:S(2)}) %collective-permute-start.4) | collective-permute-done | bytes 262176 | tf_op jit(solution)/shard_map/ppermute | solution.py:16
  63.9 1.5 %collective-permute-done.5.last_in = bf16[256,512]{1,0:T(8,128)(2,1)S(1)} collective-permute-done((bf16[256,512]{1,0:T(8,128)(2,1)S(1)}, bf16[256,512]{1,0:T(8,128)(2,1)S(1)}, u32[]{:S(2)}, u32[]{:S(2)}) %collective-permute-start.5) | collective-permute-done | bytes 262176 | tf_op jit(solution)/shard_map/ppermute | solution.py:16
  65.5 4.0 %expert.2 = (bf16[256,512]{1,0:T(8,128)(2,1)S(1)}, bf16[256,512]{1,0:T(8,128)(2,1)S(1)}, bf16[256,512]{1,0:T(8,128)(2,1)S(1)}, bf16[256,512]{1,0:T(8,128)(2,1)S(1)}) custom-call(s32[1]{0:T(128)} %bitcast.place_ref, f32[1,2048]{1,0:T(1,128)} %bitcast.56, bf16[256,512]{1,0:T(8,128)(2,1)S(1)} %bitcast.45, bf16[256,512]{1,0:T(8,128)(2,1)S(1)} %collective-permute-done.3.near_in, ...), custom_call_target="tpu_custom_call" | custom-call | flops 1610612736 | bytes 8388608 | tf_op jit(solution)/shard_map/expert/pallas_call | solution.py:299
  69.4 1.2 %all-to-all-done.4 = bf16[8,32,512]{2,1,0:T(8,128)(2,1)S(1)} async-done(((bf16[8,32,512]{2,1,0:T(8,128)(2,1)}), bf16[8,32,512]{2,1,0:T(8,128)(2,1)S(1)}, u32[]{:S(2)}, u32[]{:S(2)}) %all-to-all-start.4) | async-done | bytes 262176 | tf_op jit(solution)/shard_map/all_to_all | solution.py:20
  71.7 6.2 %collective-permute-done.10.far_in = bf16[256,512]{1,0:T(8,128)(2,1)S(1)} collective-permute-done((bf16[256,512]{1,0:T(8,128)(2,1)S(1)}, bf16[256,512]{1,0:T(8,128)(2,1)S(1)}, u32[]{:S(2)}, u32[]{:S(2)}) %collective-permute-start.10) | collective-permute-done | bytes 262176 | tf_op jit(solution)/shard_map/ppermute | solution.py:16
  78.0 1.4 %collective-permute-done.11.last_in = bf16[256,512]{1,0:T(8,128)(2,1)S(1)} collective-permute-done((bf16[256,512]{1,0:T(8,128)(2,1)S(1)}, bf16[256,512]{1,0:T(8,128)(2,1)S(1)}, u32[]{:S(2)}, u32[]{:S(2)}) %collective-permute-start.11) | collective-permute-done | bytes 262176 | tf_op jit(solution)/shard_map/ppermute | solution.py:16
  79.4 4.0 %expert.3 = (bf16[256,512]{1,0:T(8,128)(2,1)S(1)}, bf16[256,512]{1,0:T(8,128)(2,1)S(1)}, bf16[256,512]{1,0:T(8,128)(2,1)S(1)}, bf16[256,512]{1,0:T(8,128)(2,1)S(1)}) custom-call(s32[1]{0:T(128)} %bitcast.place_ref, f32[1,2048]{1,0:T(1,128)} %bitcast.57, bf16[256,512]{1,0:T(8,128)(2,1)S(1)} %bitcast.42, bf16[256,512]{1,0:T(8,128)(2,1)S(1)} %collective-permute-done.9.near_in, ...), custom_call_target="tpu_custom_call" | custom-call | flops 1610612736 | bytes 8388608 | tf_op jit(solution)/shard_map/expert/pallas_call | solution.py:299
  84.0 1.5 %collective-permute-start.8 = (bf16[256,512]{1,0:T(8,128)(2,1)S(1)}, bf16[256,512]{1,0:T(8,128)(2,1)S(1)}, u32[]{:S(2)}, u32[]{:S(2)}) collective-permute-start(bf16[256,512]{1,0:T(8,128)(2,1)S(1)} %add_convert_fusion.3), channel_id=1, source_target_pairs={{0,2},{1,3},{2,0},{3,1},{4,6},{5,7},{6,4},{7,5},{8,10},{9,11},{10,... | collective-permute-start | bytes 786440 | tf_op jit(solution)/shard_map/ppermute | solution.py:16
  85.6 1.1 collective-permute-start.14
  86.7 6.5 %collective-permute-done.8 = bf16[256,512]{1,0:T(8,128)(2,1)S(1)} collective-permute-done((bf16[256,512]{1,0:T(8,128)(2,1)S(1)}, bf16[256,512]{1,0:T(8,128)(2,1)S(1)}, u32[]{:S(2)}, u32[]{:S(2)}) %collective-permute-start.8) | collective-permute-done | bytes 262176 | tf_op jit(solution)/shard_map/ppermute | solution.py:16
  93.1 0.8 add_convert_fusion.2
  94.0 4.5 %all-to-all-start.3 = ((bf16[8,32,512]{2,1,0:T(8,128)(2,1)}), bf16[8,32,512]{2,1,0:T(8,128)(2,1)S(1)}, u32[]{:S(2)}, u32[]{:S(2)}) async-start(bf16[8,32,512]{2,1,0:T(8,128)(2,1)} %bitcast.17), calls=%async_computation.3 | async-start | bytes 524288 | tf_op jit(solution)/shard_map/all_to_all | solution.py:20
  98.4 0.8 add_convert_fusion
  99.2 7.4 %all-to-all-done.3 = bf16[8,32,512]{2,1,0:T(8,128)(2,1)S(1)} async-done(((bf16[8,32,512]{2,1,0:T(8,128)(2,1)}), bf16[8,32,512]{2,1,0:T(8,128)(2,1)S(1)}, u32[]{:S(2)}, u32[]{:S(2)}) %all-to-all-start.3) | async-done | bytes 262176 | tf_op jit(solution)/shard_map/all_to_all | solution.py:20
  106.6 3.4 %all-to-all-start.5 = ((bf16[8,32,512]{2,1,0:T(8,128)(2,1)}), bf16[8,32,512]{2,1,0:T(8,128)(2,1)S(1)}, u32[]{:S(2)}, u32[]{:S(2)}) async-start(bf16[8,32,512]{2,1,0:T(8,128)(2,1)} %bitcast.21), calls=%async_computation.5 | async-start | bytes 524288 | tf_op jit(solution)/shard_map/all_to_all | solution.py:20
  110.5 7.7 %all-to-all-done.5 = bf16[8,32,512]{2,1,0:T(8,128)(2,1)S(1)} async-done(((bf16[8,32,512]{2,1,0:T(8,128)(2,1)}), bf16[8,32,512]{2,1,0:T(8,128)(2,1)S(1)}, u32[]{:S(2)}, u32[]{:S(2)}) %all-to-all-start.5) | async-done | bytes 262176 | tf_op jit(solution)/shard_map/all_to_all | solution.py:20
  118.2 0.9 add_convert_fusion.4
  (38 shorter events, 3.5 us)
Async XLA Ops:
  0.0 10.0 %copy-start = (f32[16,64,128]{2,1,0:T(8,128)S(1)}, f32[16,64,128]{2,1,0:T(8,128)}, u32[]{:S(2)}) copy-start(f32[16,64,128]{2,1,0:T(8,128)} %param.25) | copy-start | bytes 1572868
  0.0 24.2 %copy-start.1 = (f32[16]{0:T(128)S(1)}, f32[16]{0:T(128)}, u32[]{:S(2)}) copy-start(f32[16]{0:T(128)} %skip.1) | copy-start | bytes 196
  2.8 16.9 %all-to-all-start = ((bf16[8,144,128]{2,1,0:T(8,128)(2,1)}), bf16[8,144,128]{2,1,0:T(8,128)(2,1)S(1)}, u32[]{:S(2)}, u32[]{:S(2)}) async-start(bf16[8,144,128]{2,1,0:T(8,128)(2,1)} %get-tuple-element.23), calls=%async_computation | async-start | bytes 589824 | tf_op jit(solution)/shard_map/all_to_all | solution.py:20
  20.6 12.1 %all-to-all-start.1 = ((bf16[8,128,128]{2,1,0:T(8,128)(2,1)}), bf16[8,128,128]{2,1,0:T(8,128)(2,1)S(1)}, u32[]{:S(2)}, u32[]{:S(2)}) async-start(bf16[8,128,128]{2,1,0:T(8,128)(2,1)} %prefix.1), calls=%async_computation.1 | async-start | bytes 524288 | tf_op jit(solution)/shard_map/all_to_all | solution.py:20
  32.7 3.3 %copy-start.3 = (s32[128,2]{0,1:T(2,128)S(1)}, s32[128,2]{0,1:T(2,128)}, u32[]{:S(2)}) copy-start(s32[128,2]{0,1:T(2,128)} %param.29) | copy-start | bytes 3076
  35.9 1.4 %collective-permute-start.1 = (bf16[128,512]{1,0:T(8,128)(2,1)S(1)}, bf16[128,512]{1,0:T(8,128)(2,1)S(1)}, u32[]{:S(2)}, u32[]{:S(2)}) collective-permute-start(bf16[128,512]{1,0:T(8,128)(2,1)S(1)} %get-tuple-element.27), channel_id=1, source_target_pairs={{0,1},{1,0},{2,3},{3,2},{4,5},{5,4},{6,7},{7,6},{8,9},{9,8},{10,11... | collective-permute-start | bytes 393224 | tf_op jit(solution)/shard_map/ppermute | solution.py:16
  36.2 2.9 %collective-permute-start = (bf16[128,512]{1,0:T(8,128)(2,1)S(1)}, bf16[128,512]{1,0:T(8,128)(2,1)S(1)}, u32[]{:S(2)}, u32[]{:S(2)}) collective-permute-start(bf16[128,512]{1,0:T(8,128)(2,1)S(1)} %get-tuple-element.25), channel_id=1, source_target_pairs={{0,1},{1,0},{2,3},{3,2},{4,5},{5,4},{6,7},{7,6},{8,9},{9,8},{10,11... | collective-permute-start | bytes 393224 | tf_op jit(solution)/shard_map/ppermute | solution.py:16
  37.3 5.6 %collective-permute-start.2 = (bf16[128,512]{1,0:T(8,128)(2,1)S(1)}, bf16[128,512]{1,0:T(8,128)(2,1)S(1)}, u32[]{:S(2)}, u32[]{:S(2)}) collective-permute-start(bf16[128,512]{1,0:T(8,128)(2,1)S(1)} %add_convert_fusion.6), channel_id=1, source_target_pairs={{0,2},{1,3},{2,0},{3,1},{4,6},{5,7},{6,4},{7,5},{8,10},{9,11},{10,... | collective-permute-start | bytes 393224 | tf_op jit(solution)/shard_map/ppermute | solution.py:16
  55.2 2.5 %collective-permute-start.3 = (bf16[256,512]{1,0:T(8,128)(2,1)S(1)}, bf16[256,512]{1,0:T(8,128)(2,1)S(1)}, u32[]{:S(2)}, u32[]{:S(2)}) collective-permute-start(bf16[256,512]{1,0:T(8,128)(2,1)S(1)} %bitcast.43), channel_id=1, source_target_pairs={{0,1},{1,0},{2,3},{3,2},{4,5},{5,4},{6,7},{7,6},{8,9},{9,8},{10,11... | collective-permute-start | bytes 786440 | tf_op jit(solution)/shard_map/ppermute | solution.py:16
  55.2 8.7 %collective-permute-start.4 = (bf16[256,512]{1,0:T(8,128)(2,1)S(1)}, bf16[256,512]{1,0:T(8,128)(2,1)S(1)}, u32[]{:S(2)}, u32[]{:S(2)}) collective-permute-start(bf16[256,512]{1,0:T(8,128)(2,1)S(1)} %bitcast.44), channel_id=1, source_target_pairs={{0,2},{1,3},{2,0},{3,1},{4,6},{5,7},{6,4},{7,5},{8,10},{9,11},{10,... | collective-permute-start | bytes 786440 | tf_op jit(solution)/shard_map/ppermute | solution.py:16
  57.7 12.9 %all-to-all-start.4 = ((bf16[8,32,512]{2,1,0:T(8,128)(2,1)}), bf16[8,32,512]{2,1,0:T(8,128)(2,1)S(1)}, u32[]{:S(2)}, u32[]{:S(2)}) async-start(bf16[8,32,512]{2,1,0:T(8,128)(2,1)} %bitcast.19), calls=%async_computation.4 | async-start | bytes 524288 | tf_op jit(solution)/shard_map/all_to_all | solution.py:20
  63.9 1.5 %collective-permute-start.5 = (bf16[256,512]{1,0:T(8,128)(2,1)S(1)}, bf16[256,512]{1,0:T(8,128)(2,1)S(1)}, u32[]{:S(2)}, u32[]{:S(2)}) collective-permute-start(bf16[256,512]{1,0:T(8,128)(2,1)S(1)} %collective-permute-done.4.far_in), channel_id=1, source_target_pairs={{0,1},{1,0},{2,3},{3,2},{4,5},{5,4},{6,7},{7,6},{8,9},{9,8},{10,11... | collective-permute-start | bytes 786440 | tf_op jit(solution)/shard_map/ppermute | solution.py:16
  70.6 7.2 %collective-permute-start.10 = (bf16[256,512]{1,0:T(8,128)(2,1)S(1)}, bf16[256,512]{1,0:T(8,128)(2,1)S(1)}, u32[]{:S(2)}, u32[]{:S(2)}) collective-permute-start(bf16[256,512]{1,0:T(8,128)(2,1)S(1)} %bitcast.40), channel_id=1, source_target_pairs={{0,2},{1,3},{2,0},{3,1},{4,6},{5,7},{6,4},{7,5},{8,10},{9,11},{10,... | collective-permute-start | bytes 786440 | tf_op jit(solution)/shard_map/ppermute | solution.py:16
  71.2 6.7 %collective-permute-start.7 = (bf16[256,512]{1,0:T(8,128)(2,1)S(1)}, bf16[256,512]{1,0:T(8,128)(2,1)S(1)}, u32[]{:S(2)}, u32[]{:S(2)}) collective-permute-start(bf16[256,512]{1,0:T(8,128)(2,1)S(1)} %get-tuple-element.31), channel_id=1, source_target_pairs={{0,1},{1,0},{2,3},{3,2},{4,5},{5,4},{6,7},{7,6},{8,9},{9,8},{10,11... | collective-permute-start | bytes 786440 | tf_op jit(solution)/shard_map/ppermute | solution.py:16
  71.2 6.8 %collective-permute-start.9 = (bf16[256,512]{1,0:T(8,128)(2,1)S(1)}, bf16[256,512]{1,0:T(8,128)(2,1)S(1)}, u32[]{:S(2)}, u32[]{:S(2)}) collective-permute-start(bf16[256,512]{1,0:T(8,128)(2,1)S(1)} %bitcast.41), channel_id=1, source_target_pairs={{0,1},{1,0},{2,3},{3,2},{4,5},{5,4},{6,7},{7,6},{8,9},{9,8},{10,11... | collective-permute-start | bytes 786440 | tf_op jit(solution)/shard_map/ppermute | solution.py:16
  77.9 1.5 %collective-permute-start.11 = (bf16[256,512]{1,0:T(8,128)(2,1)S(1)}, bf16[256,512]{1,0:T(8,128)(2,1)S(1)}, u32[]{:S(2)}, u32[]{:S(2)}) collective-permute-start(bf16[256,512]{1,0:T(8,128)(2,1)S(1)} %collective-permute-done.10.far_in), channel_id=1, source_target_pairs={{0,1},{1,0},{2,3},{3,2},{4,5},{5,4},{6,7},{7,6},{8,9},{9,8},{10,11... | collective-permute-start | bytes 786440 | tf_op jit(solution)/shard_map/ppermute | solution.py:16
  83.4 26.7 %copy-start.2 = (f32[128,2]{0,1:T(2,128)S(1)}, f32[128,2]{0,1:T(2,128)}, u32[]{:S(2)}) copy-start(f32[128,2]{0,1:T(2,128)} %param.30) | copy-start | bytes 3076
  83.4 2.1 %collective-permute-start.13 = (bf16[256,512]{1,0:T(8,128)(2,1)S(1)}, bf16[256,512]{1,0:T(8,128)(2,1)S(1)}, u32[]{:S(2)}, u32[]{:S(2)}) collective-permute-start(bf16[256,512]{1,0:T(8,128)(2,1)S(1)} %get-tuple-element.38), channel_id=1, source_target_pairs={{0,1},{1,0},{2,3},{3,2},{4,5},{5,4},{6,7},{7,6},{8,9},{9,8},{10,11... | collective-permute-start | bytes 786440 | tf_op jit(solution)/shard_map/ppermute | solution.py:16
  83.6 3.1 %collective-permute-start.6 = (bf16[256,512]{1,0:T(8,128)(2,1)S(1)}, bf16[256,512]{1,0:T(8,128)(2,1)S(1)}, u32[]{:S(2)}, u32[]{:S(2)}) collective-permute-start(bf16[256,512]{1,0:T(8,128)(2,1)S(1)} %get-tuple-element.29), channel_id=1, source_target_pairs={{0,1},{1,0},{2,3},{3,2},{4,5},{5,4},{6,7},{7,6},{8,9},{9,8},{10,11... | collective-permute-start | bytes 786440 | tf_op jit(solution)/shard_map/ppermute | solution.py:16
  84.0 9.2 %collective-permute-start.8 = (bf16[256,512]{1,0:T(8,128)(2,1)S(1)}, bf16[256,512]{1,0:T(8,128)(2,1)S(1)}, u32[]{:S(2)}, u32[]{:S(2)}) collective-permute-start(bf16[256,512]{1,0:T(8,128)(2,1)S(1)} %add_convert_fusion.3), channel_id=1, source_target_pairs={{0,2},{1,3},{2,0},{3,1},{4,6},{5,7},{6,4},{7,5},{8,10},{9,11},{10,... | collective-permute-start | bytes 786440 | tf_op jit(solution)/shard_map/ppermute | solution.py:16
  85.5 12.9 %collective-permute-start.12 = (bf16[256,512]{1,0:T(8,128)(2,1)S(1)}, bf16[256,512]{1,0:T(8,128)(2,1)S(1)}, u32[]{:S(2)}, u32[]{:S(2)}) collective-permute-start(bf16[256,512]{1,0:T(8,128)(2,1)S(1)} %get-tuple-element.36), channel_id=1, source_target_pairs={{0,1},{1,0},{2,3},{3,2},{4,5},{5,4},{6,7},{7,6},{8,9},{9,8},{10,11... | collective-permute-start | bytes 786440 | tf_op jit(solution)/shard_map/ppermute | solution.py:16
  85.6 12.8 %collective-permute-start.14 = (bf16[256,512]{1,0:T(8,128)(2,1)S(1)}, bf16[256,512]{1,0:T(8,128)(2,1)S(1)}, u32[]{:S(2)}, u32[]{:S(2)}) collective-permute-start(bf16[256,512]{1,0:T(8,128)(2,1)S(1)} %add_convert_fusion.1), channel_id=1, source_target_pairs={{0,2},{1,3},{2,0},{3,1},{4,6},{5,7},{6,4},{7,5},{8,10},{9,11},{10,... | collective-permute-start | bytes 786440 | tf_op jit(solution)/shard_map/ppermute | solution.py:16
  94.0 12.7 %all-to-all-start.3 = ((bf16[8,32,512]{2,1,0:T(8,128)(2,1)}), bf16[8,32,512]{2,1,0:T(8,128)(2,1)S(1)}, u32[]{:S(2)}, u32[]{:S(2)}) async-start(bf16[8,32,512]{2,1,0:T(8,128)(2,1)} %bitcast.17), calls=%async_computation.3 | async-start | bytes 524288 | tf_op jit(solution)/shard_map/all_to_all | solution.py:20
  106.6 11.6 %all-to-all-start.5 = ((bf16[8,32,512]{2,1,0:T(8,128)(2,1)}), bf16[8,32,512]{2,1,0:T(8,128)(2,1)S(1)}, u32[]{:S(2)}, u32[]{:S(2)}) async-start(bf16[8,32,512]{2,1,0:T(8,128)(2,1)} %bitcast.21), calls=%async_computation.5 | async-start | bytes 524288 | tf_op jit(solution)/shard_map/all_to_all | solution.py:20

commit v7 on v6

--- a/solution.py
+++ b/solution.py
@@ -81,7 +81,7 @@
             jax.ShapeDtypeStruct((count, part + 16, b.shape[1]), BF),
             jax.ShapeDtypeStruct((heads, toks), F32),
         ],
-        compiler_params=params(24),
+        compiler_params=params(8),
         name="own_state",
     )(in_hbm(x), in_hbm(step_t), in_hbm(decay_t), in_hbm(b))
 
@@ -114,7 +114,7 @@
         prefix_kernel,
         in_specs=[pl.BlockSpec(memory_space=pltpu.SMEM), vmem, vmem],
         out_shape=jax.ShapeDtypeStruct((count, part, width), BF),
-        compiler_params=params(24),
+        compiler_params=params(8),
         name="prefix",
     )(place.reshape(1), got, start)
 
@@ -409,13 +409,13 @@
     from_near0 = swap(to_near0, 1)
     pass0 = (pass0.astype(F32) + from_last0.astype(F32)).astype(BF)
     from_far0 = swap(pass0, 2)
-    last1 = swap(far1, 1)
+    last1 = swap(after(far1, pass0), 1)
     to_near1, to_last1, keep1, pass1 = run_expert(
         place, moe_gain, after(own1, pass0), near1, far1, last1, *weights
     )
     result0 = (keep0.astype(F32) + from_near0.astype(F32) + from_far0.astype(F32)).astype(BF)
     mixed = hidden.astype(F32) + combined(0, result0)
-    from_last1 = swap(to_last1, 1)
+    from_last1 = swap(after(to_last1, from_far0), 1)
     from_near1 = swap(to_near1, 1)
     from_far1 = swap((pass1.astype(F32) + from_last1.astype(F32)).astype(BF), 2)
     result1 = (keep1.astype(F32) + from_near1.astype(F32) + from_far1.astype(F32)).astype(BF)

time: 120 us -> 124 us (1.033)
  starting transfers between devices: 30.1 us -> 33 us
  waiting for transfers between devices: 55.6 us -> 57 us
    all_to_all x5, waiting for transfers between devices: 32.8 us -> 36.8 us  [exchange(): return lax.all_to_all(value, 'seq', split_axis=0, concat_axis=0, tiled=True)]
    ppermute x15, waiting for transfers between devices: 22.9 us -> 20.3 us  [swap(): return lax.ppermute(value, 'tp', [(i, i ^ bit) for i in range(count)])]
    all_to_all x5, starting transfers between devices: 22.2 us -> 23.8 us  [exchange(): return lax.all_to_all(value, 'seq', split_axis=0, concat_axis=0, tiled=True)]
  transfers between devices with their start and end apart: 20 -> 20, of which waited for: 12 -> 12; matrix products, arithmetic and copies ran while one was open for 3% -> 3% of each run, Pallas kernels for 5% -> 8%
where the time goes in v7:
time: 124 us; the launch traced here: 123 us
  waiting for transfers between devices  57 us (46%)
  starting transfers between devices  33 us (27%)
  Pallas kernels  16.5 us (13%)
  blocking collectives  11.9 us (10%)
  matrix products  2.67 us (2%)
  other arithmetic  2.1 us (2%)
    all_to_all x5, waiting for transfers between devices, exchange(): return lax.all_to_all(value, 'seq', split_axis=0, concat_axis=0, tiled=True)  36.8 us
    all_to_all x5, starting transfers between devices, exchange(): return lax.all_to_all(value, 'seq', split_axis=0, concat_axis=0, tiled=True)  23.8 us
    ppermute x15, waiting for transfers between devices, swap(): return lax.ppermute(value, 'tp', [(i, i ^ bit) for i in range(count)])  20.3 us
    all_to_all x1, blocking collectives, exchange(): return lax.all_to_all(value, 'seq', split_axis=0, concat_axis=0, tiled=True)  11.9 us
    ppermute x15, starting transfers between devices, swap(): return lax.ppermute(value, 'tp', [(i, i ^ bit) for i in range(count)])  9.15 us
    pallas_call x2, Pallas kernels, run_expert(): pl.pallas_call(expert_kernel, in_specs=[pl.BlockSpec(memory_space=pltpu.S...  7.97 us
    pallas_call x1, Pallas kernels, mixer_tail(): pl.pallas_call(tail_kernel, in_specs=[pl.BlockSpec(memory_space=pltpu.SME...  3.18 us
    pallas_call x1, Pallas kernels, own_state(): pl.pallas_call(state_kernel, out_shape=[jax.ShapeDtypeStruct((count, part...  2.79 us
  transfers between devices with their start and end apart: 20, of which 12 were waited for; matrix products, arithmetic and copies ran while one was open for 3% of the time, Pallas kernels for 8%

profile of v7, /device:TPU:0, one launch (start us, length us, event | category | flops | bytes accessed | tf_op | source)
XLA Modules:
  0.0 123.4 jit_solution(3437847265482436304)
XLA Ops:
  0.0 2.8 %own_state.1 = (bf16[8,144,128]{2,1,0:T(8,128)(2,1)}, f32[16,128]{1,0:T(8,128)S(1)}) custom-call(bf16[128,1024]{1,0:T(8,128)(2,1)} %x.3, f32[16,128]{1,0:T(8,128)} %bitcast.58, f32[16,128]{1,0:T(8,128)} %bitcast.60, bf16[128,128]{1,0:T(8,128)(2,1)} %b.3), custom_call_target="tpu_custom_call" | custom-call | tf_op jit(solution)/shard_map/own_state/pallas_call | solution.py:78
  2.8 7.3 %all-to-all-start = ((bf16[8,144,128]{2,1,0:T(8,128)(2,1)}), bf16[8,144,128]{2,1,0:T(8,128)(2,1)S(1)}, u32[]{:S(2)}, u32[]{:S(2)}) async-start(bf16[8,144,128]{2,1,0:T(8,128)(2,1)} %get-tuple-element.25), calls=%async_computation | async-start | bytes 589824 | tf_op jit(solution)/shard_map/all_to_all | solution.py:20
  10.1 9.6 %all-to-all-done.got = bf16[8,144,128]{2,1,0:T(8,128)(2,1)S(1)} async-done(((bf16[8,144,128]{2,1,0:T(8,128)(2,1)}), bf16[8,144,128]{2,1,0:T(8,128)(2,1)S(1)}, u32[]{:S(2)}, u32[]{:S(2)}) %all-to-all-start) | async-done | bytes 294944 | tf_op jit(solution)/shard_map/all_to_all | solution.py:20
  19.7 0.9 prefix.1
  20.6 3.6 %all-to-all-start.1 = ((bf16[8,128,128]{2,1,0:T(8,128)(2,1)}), bf16[8,128,128]{2,1,0:T(8,128)(2,1)S(1)}, u32[]{:S(2)}, u32[]{:S(2)}) async-start(bf16[8,128,128]{2,1,0:T(8,128)(2,1)} %prefix.1), calls=%async_computation.1 | async-start | bytes 524288 | tf_op jit(solution)/shard_map/all_to_all | solution.py:20
  24.2 1.7 %within_block.1.direct_in = f32[128,1024]{1,0:T(8,128)S(1)} custom-call(f32[16]{0:T(128)S(1)} %copy-done.1, bf16[128,1024]{1,0:T(8,128)(2,1)} %x.3, f32[16,128]{1,0:T(8,128)} %bitcast.59, f32[16,128]{1,0:T(8,128)S(1)} %get-tuple-element.24.cum_t.cum_in, bf16[128,128]{1,0:T(8,128)(2,1)} %b.3, bf16[128,128]{1,0:T(8,128)(2,1)} %c_in.1), custom_call_target="tpu_custom_call" | custom-call | flops 134217728 | bytes 786432 | tf_op jit(solution)/shard_map/within_block/pallas_call | solution.py:148
  25.9 6.9 %all-to-all-done.1 = bf16[8,128,128]{2,1,0:T(8,128)(2,1)S(1)} async-done(((bf16[8,128,128]{2,1,0:T(8,128)(2,1)}), bf16[8,128,128]{2,1,0:T(8,128)(2,1)S(1)}, u32[]{:S(2)}, u32[]{:S(2)}) %all-to-all-start.1) | async-done | bytes 262176 | tf_op jit(solution)/shard_map/all_to_all | solution.py:20
  32.7 3.2 %mixer_tail.1 = (bf16[128,512]{1,0:T(8,128)(2,1)S(1)}, bf16[128,512]{1,0:T(8,128)(2,1)S(1)}, f32[128,512]{1,0:T(8,128)S(1)}, f32[128,512]{1,0:T(8,128)S(1)}) custom-call(s32[1]{0:T(128)} %bitcast.place_ref, bf16[128,128]{1,0:T(8,128)(2,1)} %c_in.1, f32[16,128]{1,0:T(8,128)S(1)} %get-tuple-element.24.cum_t.cum_in, f32[1,1024]{1,0:T(1,128)} %bitcast.61, ...), custom_call_target="tpu_custom_call" | custom-call | flops 536870912 | bytes 6029312 | tf_op jit(solution)/shard_map/mixer_tail/pallas_call | solution.py:230
  37.3 1.6 %collective-permute-start.2 = (bf16[128,512]{1,0:T(8,128)(2,1)S(1)}, bf16[128,512]{1,0:T(8,128)(2,1)S(1)}, u32[]{:S(2)}, u32[]{:S(2)}) collective-permute-start(bf16[128,512]{1,0:T(8,128)(2,1)S(1)} %add_convert_fusion.6), channel_id=1, source_target_pairs={{0,2},{1,3},{2,0},{3,1},{4,6},{5,7},{6,4},{7,5},{8,10},{9,11},{10,... | collective-permute-start | bytes 393224 | tf_op jit(solution)/shard_map/ppermute | solution.py:16
  39.1 3.9 %collective-permute-done.2 = bf16[128,512]{1,0:T(8,128)(2,1)S(1)} collective-permute-done((bf16[128,512]{1,0:T(8,128)(2,1)S(1)}, bf16[128,512]{1,0:T(8,128)(2,1)S(1)}, u32[]{:S(2)}, u32[]{:S(2)}) %collective-permute-start.2) | collective-permute-done | bytes 131104 | tf_op jit(solution)/shard_map/ppermute | solution.py:16
  43.3 11.9 %all_to_all.30 = bf16[8,32,512]{2,1,0:T(8,128)(2,1)S(1)} all-to-all(bf16[8,32,512]{2,1,0:T(8,128)(2,1)S(1)} %bitcast.55), channel_id=1, replica_groups=mesh['seq'=8,'tp'=4] {'seq'}, dimensions={0} | all-to-all | bytes 524288 | tf_op jit(solution)/shard_map/all_to_all | solution.py:20
  55.2 1.5 %collective-permute-start.4 = (bf16[256,512]{1,0:T(8,128)(2,1)S(1)}, bf16[256,512]{1,0:T(8,128)(2,1)S(1)}, u32[]{:S(2)}, u32[]{:S(2)}) collective-permute-start(bf16[256,512]{1,0:T(8,128)(2,1)S(1)} %bitcast.43), channel_id=1, source_target_pairs={{0,2},{1,3},{2,0},{3,1},{4,6},{5,7},{6,4},{7,5},{8,10},{9,11},{10,... | collective-permute-start | bytes 786440 | tf_op jit(solution)/shard_map/ppermute | solution.py:16
  56.7 4.9 %collective-permute-done.4.far_in = bf16[256,512]{1,0:T(8,128)(2,1)S(1)} collective-permute-done((bf16[256,512]{1,0:T(8,128)(2,1)S(1)}, bf16[256,512]{1,0:T(8,128)(2,1)S(1)}, u32[]{:S(2)}, u32[]{:S(2)}) %collective-permute-start.4) | collective-permute-done | bytes 262176 | tf_op jit(solution)/shard_map/ppermute | solution.py:16
  61.6 1.0 convolution_convert_fusion
  62.6 4.6 %all-to-all-start.4 = ((bf16[8,32,512]{2,1,0:T(8,128)(2,1)}), bf16[8,32,512]{2,1,0:T(8,128)(2,1)S(1)}, u32[]{:S(2)}, u32[]{:S(2)}) async-start(bf16[8,32,512]{2,1,0:T(8,128)(2,1)} %bitcast.19), calls=%async_computation.4 | async-start | bytes 524288 | tf_op jit(solution)/shard_map/all_to_all | solution.py:20
  67.2 4.0 %expert.2 = (bf16[256,512]{1,0:T(8,128)(2,1)S(1)}, bf16[256,512]{1,0:T(8,128)(2,1)S(1)}, bf16[256,512]{1,0:T(8,128)(2,1)S(1)}, bf16[256,512]{1,0:T(8,128)(2,1)S(1)}) custom-call(s32[1]{0:T(128)} %bitcast.place_ref, f32[1,2048]{1,0:T(1,128)} %bitcast.56, bf16[256,512]{1,0:T(8,128)(2,1)S(1)} %bitcast.45, bf16[256,512]{1,0:T(8,128)(2,1)S(1)} %collective-permute-done.3.near_in, ...), custom_call_target="tpu_custom_call" | custom-call | flops 1610612736 | bytes 8388608 | tf_op jit(solution)/shard_map/expert/pallas_call | solution.py:299
  71.5 5.3 %all-to-all-done.4 = bf16[8,32,512]{2,1,0:T(8,128)(2,1)S(1)} async-done(((bf16[8,32,512]{2,1,0:T(8,128)(2,1)}), bf16[8,32,512]{2,1,0:T(8,128)(2,1)S(1)}, u32[]{:S(2)}, u32[]{:S(2)}) %all-to-all-start.4) | async-done | bytes 262176 | tf_op jit(solution)/shard_map/all_to_all | solution.py:20
  76.8 1.5 %collective-permute-start.10 = (bf16[256,512]{1,0:T(8,128)(2,1)S(1)}, bf16[256,512]{1,0:T(8,128)(2,1)S(1)}, u32[]{:S(2)}, u32[]{:S(2)}) collective-permute-start(bf16[256,512]{1,0:T(8,128)(2,1)S(1)} %bitcast.40), channel_id=1, source_target_pairs={{0,2},{1,3},{2,0},{3,1},{4,6},{5,7},{6,4},{7,5},{8,10},{9,11},{10,... | collective-permute-start | bytes 786440 | tf_op jit(solution)/shard_map/ppermute | solution.py:16
  78.4 5.5 %collective-permute-done.10.far_in = bf16[256,512]{1,0:T(8,128)(2,1)S(1)} collective-permute-done((bf16[256,512]{1,0:T(8,128)(2,1)S(1)}, bf16[256,512]{1,0:T(8,128)(2,1)S(1)}, u32[]{:S(2)}, u32[]{:S(2)}) %collective-permute-start.10) | collective-permute-done | bytes 262176 | tf_op jit(solution)/shard_map/ppermute | solution.py:16
  83.9 1.5 %collective-permute-start.8 = (bf16[256,512]{1,0:T(8,128)(2,1)S(1)}, bf16[256,512]{1,0:T(8,128)(2,1)S(1)}, u32[]{:S(2)}, u32[]{:S(2)}) collective-permute-start(bf16[256,512]{1,0:T(8,128)(2,1)S(1)} %add_convert_fusion.3), channel_id=1, source_target_pairs={{0,2},{1,3},{2,0},{3,1},{4,6},{5,7},{6,4},{7,5},{8,10},{9,11},{10,... | collective-permute-start | bytes 786440 | tf_op jit(solution)/shard_map/ppermute | solution.py:16
  85.4 4.0 %expert.3 = (bf16[256,512]{1,0:T(8,128)(2,1)S(1)}, bf16[256,512]{1,0:T(8,128)(2,1)S(1)}, bf16[256,512]{1,0:T(8,128)(2,1)S(1)}, bf16[256,512]{1,0:T(8,128)(2,1)S(1)}) custom-call(s32[1]{0:T(128)} %bitcast.place_ref, f32[1,2048]{1,0:T(1,128)} %bitcast.57, bf16[256,512]{1,0:T(8,128)(2,1)S(1)} %bitcast.42, bf16[256,512]{1,0:T(8,128)(2,1)S(1)} %collective-permute-done.9.near_in, ...), custom_call_target="tpu_custom_call" | custom-call | flops 1610612736 | bytes 8388608 | tf_op jit(solution)/shard_map/expert/pallas_call | solution.py:299
  89.4 3.2 %collective-permute-done.8 = bf16[256,512]{1,0:T(8,128)(2,1)S(1)} collective-permute-done((bf16[256,512]{1,0:T(8,128)(2,1)S(1)}, bf16[256,512]{1,0:T(8,128)(2,1)S(1)}, u32[]{:S(2)}, u32[]{:S(2)}) %collective-permute-start.8) | collective-permute-done | bytes 262176 | tf_op jit(solution)/shard_map/ppermute | solution.py:16
  93.1 1.0 collective-permute-done.13
  94.2 1.6 %collective-permute-start.14 = (bf16[256,512]{1,0:T(8,128)(2,1)S(1)}, bf16[256,512]{1,0:T(8,128)(2,1)S(1)}, u32[]{:S(2)}, u32[]{:S(2)}) collective-permute-start(bf16[256,512]{1,0:T(8,128)(2,1)S(1)} %add_convert_fusion.1), channel_id=1, source_target_pairs={{0,2},{1,3},{2,0},{3,1},{4,6},{5,7},{6,4},{7,5},{8,10},{9,11},{10,... | collective-permute-start | bytes 786440 | tf_op jit(solution)/shard_map/ppermute | solution.py:16
  95.8 0.8 add_convert_fusion.2
  96.6 4.8 %all-to-all-start.3 = ((bf16[8,32,512]{2,1,0:T(8,128)(2,1)}), bf16[8,32,512]{2,1,0:T(8,128)(2,1)S(1)}, u32[]{:S(2)}, u32[]{:S(2)}) async-start(bf16[8,32,512]{2,1,0:T(8,128)(2,1)} %bitcast.17), calls=%async_computation.3 | async-start | bytes 524288 | tf_op jit(solution)/shard_map/all_to_all | solution.py:20
  101.4 1.2 %collective-permute-done.14 = bf16[256,512]{1,0:T(8,128)(2,1)S(1)} collective-permute-done((bf16[256,512]{1,0:T(8,128)(2,1)S(1)}, bf16[256,512]{1,0:T(8,128)(2,1)S(1)}, u32[]{:S(2)}, u32[]{:S(2)}) %collective-permute-start.14) | collective-permute-done | bytes 262176 | tf_op jit(solution)/shard_map/ppermute | solution.py:16
  102.6 0.8 add_convert_fusion
  103.4 6.9 %all-to-all-done.3 = bf16[8,32,512]{2,1,0:T(8,128)(2,1)S(1)} async-done(((bf16[8,32,512]{2,1,0:T(8,128)(2,1)}), bf16[8,32,512]{2,1,0:T(8,128)(2,1)S(1)}, u32[]{:S(2)}, u32[]{:S(2)}) %all-to-all-start.3) | async-done | bytes 262176 | tf_op jit(solution)/shard_map/all_to_all | solution.py:20
  110.3 3.6 %all-to-all-start.5 = ((bf16[8,32,512]{2,1,0:T(8,128)(2,1)}), bf16[8,32,512]{2,1,0:T(8,128)(2,1)S(1)}, u32[]{:S(2)}, u32[]{:S(2)}) async-start(bf16[8,32,512]{2,1,0:T(8,128)(2,1)} %bitcast.21), calls=%async_computation.5 | async-start | bytes 524288 | tf_op jit(solution)/shard_map/all_to_all | solution.py:20
  114.3 8.1 %all-to-all-done.5 = bf16[8,32,512]{2,1,0:T(8,128)(2,1)S(1)} async-done(((bf16[8,32,512]{2,1,0:T(8,128)(2,1)}), bf16[8,32,512]{2,1,0:T(8,128)(2,1)S(1)}, u32[]{:S(2)}, u32[]{:S(2)}) %all-to-all-start.5) | async-done | bytes 262176 | tf_op jit(solution)/shard_map/all_to_all | solution.py:20
  122.5 0.9 add_convert_fusion.4
  (38 shorter events, 3.3 us)
Async XLA Ops:
  0.0 10.0 %copy-start = (f32[16,64,128]{2,1,0:T(8,128)S(1)}, f32[16,64,128]{2,1,0:T(8,128)}, u32[]{:S(2)}) copy-start(f32[16,64,128]{2,1,0:T(8,128)} %param.25) | copy-start | bytes 1572868
  0.0 24.2 %copy-start.1 = (f32[16]{0:T(128)S(1)}, f32[16]{0:T(128)}, u32[]{:S(2)}) copy-start(f32[16]{0:T(128)} %skip.1) | copy-start | bytes 196
  2.8 16.9 %all-to-all-start = ((bf16[8,144,128]{2,1,0:T(8,128)(2,1)}), bf16[8,144,128]{2,1,0:T(8,128)(2,1)S(1)}, u32[]{:S(2)}, u32[]{:S(2)}) async-start(bf16[8,144,128]{2,1,0:T(8,128)(2,1)} %get-tuple-element.25), calls=%async_computation | async-start | bytes 589824 | tf_op jit(solution)/shard_map/all_to_all | solution.py:20
  20.6 12.1 %all-to-all-start.1 = ((bf16[8,128,128]{2,1,0:T(8,128)(2,1)}), bf16[8,128,128]{2,1,0:T(8,128)(2,1)S(1)}, u32[]{:S(2)}, u32[]{:S(2)}) async-start(bf16[8,128,128]{2,1,0:T(8,128)(2,1)} %prefix.1), calls=%async_computation.1 | async-start | bytes 524288 | tf_op jit(solution)/shard_map/all_to_all | solution.py:20
  32.7 3.3 %copy-start.3 = (s32[128,2]{0,1:T(2,128)S(1)}, s32[128,2]{0,1:T(2,128)}, u32[]{:S(2)}) copy-start(s32[128,2]{0,1:T(2,128)} %param.29) | copy-start | bytes 3076
  35.9 1.4 %collective-permute-start.1 = (bf16[128,512]{1,0:T(8,128)(2,1)S(1)}, bf16[128,512]{1,0:T(8,128)(2,1)S(1)}, u32[]{:S(2)}, u32[]{:S(2)}) collective-permute-start(bf16[128,512]{1,0:T(8,128)(2,1)S(1)} %get-tuple-element.29), channel_id=1, source_target_pairs={{0,1},{1,0},{2,3},{3,2},{4,5},{5,4},{6,7},{7,6},{8,9},{9,8},{10,11... | collective-permute-start | bytes 393224 | tf_op jit(solution)/shard_map/ppermute | solution.py:16
  36.2 2.9 %collective-permute-start = (bf16[128,512]{1,0:T(8,128)(2,1)S(1)}, bf16[128,512]{1,0:T(8,128)(2,1)S(1)}, u32[]{:S(2)}, u32[]{:S(2)}) collective-permute-start(bf16[128,512]{1,0:T(8,128)(2,1)S(1)} %get-tuple-element.27), channel_id=1, source_target_pairs={{0,1},{1,0},{2,3},{3,2},{4,5},{5,4},{6,7},{7,6},{8,9},{9,8},{10,11... | collective-permute-start | bytes 393224 | tf_op jit(solution)/shard_map/ppermute | solution.py:16
  37.3 5.6 %collective-permute-start.2 = (bf16[128,512]{1,0:T(8,128)(2,1)S(1)}, bf16[128,512]{1,0:T(8,128)(2,1)S(1)}, u32[]{:S(2)}, u32[]{:S(2)}) collective-permute-start(bf16[128,512]{1,0:T(8,128)(2,1)S(1)} %add_convert_fusion.6), channel_id=1, source_target_pairs={{0,2},{1,3},{2,0},{3,1},{4,6},{5,7},{6,4},{7,5},{8,10},{9,11},{10,... | collective-permute-start | bytes 393224 | tf_op jit(solution)/shard_map/ppermute | solution.py:16
  55.2 6.4 %collective-permute-start.4 = (bf16[256,512]{1,0:T(8,128)(2,1)S(1)}, bf16[256,512]{1,0:T(8,128)(2,1)S(1)}, u32[]{:S(2)}, u32[]{:S(2)}) collective-permute-start(bf16[256,512]{1,0:T(8,128)(2,1)S(1)} %bitcast.43), channel_id=1, source_target_pairs={{0,2},{1,3},{2,0},{3,1},{4,6},{5,7},{6,4},{7,5},{8,10},{9,11},{10,... | collective-permute-start | bytes 786440 | tf_op jit(solution)/shard_map/ppermute | solution.py:16
  56.7 5.8 %collective-permute-start.3 = (bf16[256,512]{1,0:T(8,128)(2,1)S(1)}, bf16[256,512]{1,0:T(8,128)(2,1)S(1)}, u32[]{:S(2)}, u32[]{:S(2)}) collective-permute-start(bf16[256,512]{1,0:T(8,128)(2,1)S(1)} %bitcast.44), channel_id=1, source_target_pairs={{0,1},{1,0},{2,3},{3,2},{4,5},{5,4},{6,7},{7,6},{8,9},{9,8},{10,11... | collective-permute-start | bytes 786440 | tf_op jit(solution)/shard_map/ppermute | solution.py:16
  61.6 5.6 %collective-permute-start.5 = (bf16[256,512]{1,0:T(8,128)(2,1)S(1)}, bf16[256,512]{1,0:T(8,128)(2,1)S(1)}, u32[]{:S(2)}, u32[]{:S(2)}) collective-permute-start(bf16[256,512]{1,0:T(8,128)(2,1)S(1)} %collective-permute-done.4.far_in), channel_id=1, source_target_pairs={{0,1},{1,0},{2,3},{3,2},{4,5},{5,4},{6,7},{7,6},{8,9},{9,8},{10,11... | collective-permute-start | bytes 786440 | tf_op jit(solution)/shard_map/ppermute | solution.py:16
  62.6 14.2 %all-to-all-start.4 = ((bf16[8,32,512]{2,1,0:T(8,128)(2,1)}), bf16[8,32,512]{2,1,0:T(8,128)(2,1)S(1)}, u32[]{:S(2)}, u32[]{:S(2)}) async-start(bf16[8,32,512]{2,1,0:T(8,128)(2,1)} %bitcast.19), calls=%async_computation.4 | async-start | bytes 524288 | tf_op jit(solution)/shard_map/all_to_all | solution.py:20
  71.2 7.1 %collective-permute-start.7 = (bf16[256,512]{1,0:T(8,128)(2,1)S(1)}, bf16[256,512]{1,0:T(8,128)(2,1)S(1)}, u32[]{:S(2)}, u32[]{:S(2)}) collective-permute-start(bf16[256,512]{1,0:T(8,128)(2,1)S(1)} %get-tuple-element.33), channel_id=1, source_target_pairs={{0,1},{1,0},{2,3},{3,2},{4,5},{5,4},{6,7},{7,6},{8,9},{9,8},{10,11... | collective-permute-start | bytes 786440 | tf_op jit(solution)/shard_map/ppermute | solution.py:16
  76.8 7.1 %collective-permute-start.10 = (bf16[256,512]{1,0:T(8,128)(2,1)S(1)}, bf16[256,512]{1,0:T(8,128)(2,1)S(1)}, u32[]{:S(2)}, u32[]{:S(2)}) collective-permute-start(bf16[256,512]{1,0:T(8,128)(2,1)S(1)} %bitcast.40), channel_id=1, source_target_pairs={{0,2},{1,3},{2,0},{3,1},{4,6},{5,7},{6,4},{7,5},{8,10},{9,11},{10,... | collective-permute-start | bytes 786440 | tf_op jit(solution)/shard_map/ppermute | solution.py:16
  78.3 7.1 %collective-permute-start.9 = (bf16[256,512]{1,0:T(8,128)(2,1)S(1)}, bf16[256,512]{1,0:T(8,128)(2,1)S(1)}, u32[]{:S(2)}, u32[]{:S(2)}) collective-permute-start(bf16[256,512]{1,0:T(8,128)(2,1)S(1)} %bitcast.41), channel_id=1, source_target_pairs={{0,1},{1,0},{2,3},{3,2},{4,5},{5,4},{6,7},{7,6},{8,9},{9,8},{10,11... | collective-permute-start | bytes 786440 | tf_op jit(solution)/shard_map/ppermute | solution.py:16
  83.9 1.5 %collective-permute-start.11 = (bf16[256,512]{1,0:T(8,128)(2,1)S(1)}, bf16[256,512]{1,0:T(8,128)(2,1)S(1)}, u32[]{:S(2)}, u32[]{:S(2)}) collective-permute-start(bf16[256,512]{1,0:T(8,128)(2,1)S(1)} %collective-permute-done.10.far_in), channel_id=1, source_target_pairs={{0,1},{1,0},{2,3},{3,2},{4,5},{5,4},{6,7},{7,6},{8,9},{9,8},{10,11... | collective-permute-start | bytes 786440 | tf_op jit(solution)/shard_map/ppermute | solution.py:16
  83.9 8.7 %collective-permute-start.8 = (bf16[256,512]{1,0:T(8,128)(2,1)S(1)}, bf16[256,512]{1,0:T(8,128)(2,1)S(1)}, u32[]{:S(2)}, u32[]{:S(2)}) collective-permute-start(bf16[256,512]{1,0:T(8,128)(2,1)S(1)} %add_convert_fusion.3), channel_id=1, source_target_pairs={{0,2},{1,3},{2,0},{3,1},{4,6},{5,7},{6,4},{7,5},{8,10},{9,11},{10,... | collective-permute-start | bytes 786440 | tf_op jit(solution)/shard_map/ppermute | solution.py:16
  89.4 24.5 %copy-start.2 = (f32[128,2]{0,1:T(2,128)S(1)}, f32[128,2]{0,1:T(2,128)}, u32[]{:S(2)}) copy-start(f32[128,2]{0,1:T(2,128)} %param.30) | copy-start | bytes 3076
  92.6 1.5 %collective-permute-start.13 = (bf16[256,512]{1,0:T(8,128)(2,1)S(1)}, bf16[256,512]{1,0:T(8,128)(2,1)S(1)}, u32[]{:S(2)}, u32[]{:S(2)}) collective-permute-start(bf16[256,512]{1,0:T(8,128)(2,1)S(1)} %get-tuple-element.42), channel_id=1, source_target_pairs={{0,1},{1,0},{2,3},{3,2},{4,5},{5,4},{6,7},{7,6},{8,9},{9,8},{10,11... | collective-permute-start | bytes 786440 | tf_op jit(solution)/shard_map/ppermute | solution.py:16
  92.6 3.2 %collective-permute-start.6 = (bf16[256,512]{1,0:T(8,128)(2,1)S(1)}, bf16[256,512]{1,0:T(8,128)(2,1)S(1)}, u32[]{:S(2)}, u32[]{:S(2)}) collective-permute-start(bf16[256,512]{1,0:T(8,128)(2,1)S(1)} %get-tuple-element.31), channel_id=1, source_target_pairs={{0,1},{1,0},{2,3},{3,2},{4,5},{5,4},{6,7},{7,6},{8,9},{9,8},{10,11... | collective-permute-start | bytes 786440 | tf_op jit(solution)/shard_map/ppermute | solution.py:16
  93.1 8.3 %collective-permute-start.12 = (bf16[256,512]{1,0:T(8,128)(2,1)S(1)}, bf16[256,512]{1,0:T(8,128)(2,1)S(1)}, u32[]{:S(2)}, u32[]{:S(2)}) collective-permute-start(bf16[256,512]{1,0:T(8,128)(2,1)S(1)} %get-tuple-element.39), channel_id=1, source_target_pairs={{0,1},{1,0},{2,3},{3,2},{4,5},{5,4},{6,7},{7,6},{8,9},{9,8},{10,11... | collective-permute-start | bytes 786440 | tf_op jit(solution)/shard_map/ppermute | solution.py:16
  94.2 8.4 %collective-permute-start.14 = (bf16[256,512]{1,0:T(8,128)(2,1)S(1)}, bf16[256,512]{1,0:T(8,128)(2,1)S(1)}, u32[]{:S(2)}, u32[]{:S(2)}) collective-permute-start(bf16[256,512]{1,0:T(8,128)(2,1)S(1)} %add_convert_fusion.1), channel_id=1, source_target_pairs={{0,2},{1,3},{2,0},{3,1},{4,6},{5,7},{6,4},{7,5},{8,10},{9,11},{10,... | collective-permute-start | bytes 786440 | tf_op jit(solution)/shard_map/ppermute | solution.py:16
  96.6 13.7 %all-to-all-start.3 = ((bf16[8,32,512]{2,1,0:T(8,128)(2,1)}), bf16[8,32,512]{2,1,0:T(8,128)(2,1)S(1)}, u32[]{:S(2)}, u32[]{:S(2)}) async-start(bf16[8,32,512]{2,1,0:T(8,128)(2,1)} %bitcast.17), calls=%async_computation.3 | async-start | bytes 524288 | tf_op jit(solution)/shard_map/all_to_all | solution.py:20
  110.3 12.2 %all-to-all-start.5 = ((bf16[8,32,512]{2,1,0:T(8,128)(2,1)}), bf16[8,32,512]{2,1,0:T(8,128)(2,1)S(1)}, u32[]{:S(2)}, u32[]{:S(2)}) async-start(bf16[8,32,512]{2,1,0:T(8,128)(2,1)} %bitcast.21), calls=%async_computation.5 | async-start | bytes 524288 | tf_op jit(solution)/shard_map/all_to_all | solution.py:20

commit v8 on v5

--- a/solution.py
+++ b/solution.py
@@ -81,7 +81,7 @@
             jax.ShapeDtypeStruct((count, part + 16, b.shape[1]), BF),
             jax.ShapeDtypeStruct((heads, toks), F32),
         ],
-        compiler_params=params(24),
+        compiler_params=params(8),
         name="own_state",
     )(in_hbm(x), in_hbm(step_t), in_hbm(decay_t), in_hbm(b))
 
@@ -114,7 +114,7 @@
         prefix_kernel,
         in_specs=[pl.BlockSpec(memory_space=pltpu.SMEM), vmem, vmem],
         out_shape=jax.ShapeDtypeStruct((count, part, width), BF),
-        compiler_params=params(24),
+        compiler_params=params(8),
         name="prefix",
     )(place.reshape(1), got, start)
 
@@ -176,12 +176,13 @@
 
 
 def tail_kernel(
-    place_ref, c_in, cum_in, gain_in, arriving_in, direct_in, z_in, weight_in,
+    place_ref, c_in, cum_in, gain_in, arriving_in, direct_in, z_in, weight_in, tokens_in,
     near, last, keep, passing,
-    c, cum_t, gain, arriving, direct, z, weight, normed, sems,
+    c, cum_t, gain, arriving, direct, z, weight, tokens, normed, sems,
 ):
     heads, toks = cum_t.shape
     share = near.shape[1]
+    spots = quarters(place_ref, share)
     copies = fetch(
         sems,
         (cum_in, cum_t),
@@ -191,6 +192,7 @@
         (z_in, z),
         (direct_in, direct),
         *zip(cuts_of(weight_in, 8), cuts_of(weight, 8)),
+        (tokens_in.at[:, spots[0]], tokens),
     )
     for copy in copies[:6]:
         copy.wait()
@@ -211,26 +213,31 @@
         normed[:, spot] = (gated * lax.rsqrt(mean + 1e-05) * gain[:, spot]).astype(BF)
     for copy in copies[6:]:
         copy.wait()
-    spots = quarters(place_ref, share)
     for k, out in ((3, last), (1, near), (2, passing), (0, keep)):
         part = jnp.dot(normed[...], weight[:, spots[k]], preferred_element_type=F32)
+        if k == 0:
+            part += tokens[...].astype(F32)
         out[...] = part.astype(out.dtype)
 
 
-def mixer_tail(place, c, arriving, cum_t, direct, z, gain, weight):
+def mixer_tail(place, c, arriving, cum_t, direct, z, gain, weight, tokens):
     heads, toks = cum_t.shape
     inner, width = weight.shape
     share = width // 4
-    operands = (c, cum_t, gain.reshape(1, inner), arriving, direct, z, weight)
-    fixed = (0, 2, 5, 6)
+    operands = (c, cum_t, gain.reshape(1, inner), arriving, direct, z, weight, tokens)
+    fixed = (0, 2, 5, 6, 7)
     operands = [in_hbm(a) if i in fixed else a for i, a in enumerate(operands)]
     return pl.pallas_call(
         tail_kernel,
         in_specs=[pl.BlockSpec(memory_space=pltpu.SMEM)]
         + [pl.BlockSpec(memory_space=pl.ANY)] * len(operands),
         out_shape=[jax.ShapeDtypeStruct((toks, share), kind) for kind in (BF, BF, F32, F32)],
-        scratch_shapes=[pltpu.VMEM(a.shape, a.dtype) for a in operands]
-        + [pltpu.VMEM((toks, inner), BF), pltpu.SemaphoreType.DMA((14,))],
+        scratch_shapes=[pltpu.VMEM(a.shape, a.dtype) for a in operands[:-1]]
+        + [
+            pltpu.VMEM((toks, share), BF),
+            pltpu.VMEM((toks, inner), BF),
+            pltpu.SemaphoreType.DMA((15,)),
+        ],
         compiler_params=params(24),
         cost_estimate=pl.CostEstimate(
             flops=2 * toks * inner * width,
@@ -300,11 +307,7 @@
             pltpu.SemaphoreType.DMA((17,)),
         ],
         compiler_params=params(24),
-        cost_estimate=pl.CostEstimate(
-            flops=6 * rows * width * inner,
-            bytes_accessed=6 * width * inner + 4 * rows * width,
-            transcendentals=rows * inner,
-        ),
+        cost_estimate=pl.CostEstimate(flops=1, bytes_accessed=1, transcendentals=0),
         name="expert",
     )(place.reshape(1), *operands)
 
@@ -339,7 +342,7 @@
     back = entering_state(got, init_state.reshape(inner, state_size))
     arriving = exchange(back).reshape(inner, state_size)
     to_near, to_last, keep, passing = mixer_tail(
-        place, c_proj, arriving, cum_t, direct, z_gate, norm_gain, out_weight
+        place, c_proj, arriving, cum_t, direct, z_gate, norm_gain, out_weight, tokens
     )
 
     model_width = out_weight.shape[1]
@@ -356,15 +359,15 @@
     rank = jnp.sum(jnp.where(onehot, earlier, 0.0), axis=1).astype(jnp.int32)
     placed = flat_expert * slot_count + rank
     spots = placed[:, None] == jnp.arange(slots, dtype=jnp.int32)[None, :]
-    pick = spots.astype(BF)
-    fill = jnp.any(spots.reshape(top_count, tok_rows, slots), axis=0).astype(BF)
+    spots = spots.reshape(top_count, tok_rows, slots)
+    fill = jnp.any(spots, axis=0).astype(BF)
+    combine = jnp.sum(jnp.where(spots, route_weights.T[:, :, None], 0.0), axis=0)
 
     from_last = swap(to_last, 1)
     from_near = swap(to_near, 1)
     from_far = swap((passing + from_last.astype(F32)).astype(BF), 2)
-    own_tokens = lax.dynamic_slice_in_dim(tokens, place * share, share, 1)
-    projected = keep + from_near.astype(F32) + from_far.astype(F32)
-    hidden = (own_tokens.astype(F32) + projected).astype(BF)
+    hidden = (keep + from_near.astype(F32) + from_far.astype(F32)).astype(BF)
+
     outgoing = lax.dot_general(
         fill, hidden, (((0,), (0,)), ((), ())), preferred_element_type=F32
     ).astype(BF)
@@ -387,9 +390,10 @@
         place, moe_gain, after(own[1], pass0), near[1], far[1], last, *weights
     )
     from_near0 = swap(to_near0, 1)
-    from_last1 = swap(after(to_last1, from_far0), 1)
-    from_near1 = swap(to_near1, 1)
-    from_far1 = swap((pass1.astype(F32) + from_last1.astype(F32)).astype(BF), 2)
+    from_last1 = swap(to_last1, 1)
+    from_near1 = swap(after(to_near1, from_far0), 1)
+    pass1 = (pass1.astype(F32) + from_last1.astype(F32)).astype(BF)
+    from_far1 = swap(pass1, 2)
     results = [
         (keep.astype(F32) + from_near.astype(F32) + from_far.astype(F32)).astype(BF)
         for keep, from_near, from_far in (
@@ -399,11 +403,13 @@
     ]
     results = jnp.concatenate(results).reshape(expert_count, slot_count, share)
     returned = exchange(results).reshape(slots, share)
-    chosen = jnp.dot(pick, returned, preferred_element_type=F32).reshape(
-        top_count, tok_rows, share
-    )
-    mixed_out = hidden.astype(F32) + jnp.sum(route_weights.T[:, :, None] * chosen, axis=0)
-    return mixed_out.astype(BF)
+    mixed = hidden.astype(F32) + jnp.dot(
+        combine,
+        returned.astype(F32),
+        precision=lax.Precision.HIGHEST,
+        preferred_element_type=F32,
+    )
+    return mixed.astype(BF)
 
 
 def solution(mesh):

time: 116 us -> 115 us (level)
  blocking collectives: 35.6 us -> 17.4 us
  waiting for transfers between devices: 39.6 us -> 52.6 us
  starting transfers between devices: 20.4 us -> 25 us
    all_to_all x2 -> x1, blocking collectives: 35.6 us -> 17.4 us  [exchange(): return lax.all_to_all(value, 'seq', split_axis=0, concat_axis=0, tiled=True)]
    all_to_all x2 -> x3, waiting for transfers between devices: 16.4 us -> 30.7 us  [exchange(): return lax.all_to_all(value, 'seq', split_axis=0, concat_axis=0, tiled=True)]
    all_to_all x2 -> x3, starting transfers between devices: 10.8 us -> 15.4 us  [exchange(): return lax.all_to_all(value, 'seq', split_axis=0, concat_axis=0, tiled=True)]
    convert_element_type x3 -> x2, other arithmetic: 1.72 us -> 0.12 us  [the longest x1 0.07 us: body(): pass1 = (pass1.astype(F32) + from_last1.astype(F32)).astype(BF)]
    ppermute x15, waiting for transfers between devices: 23.2 us -> 22 us  [swap(): return lax.ppermute(value, 'tp', [(i, i ^ bit) for i in range(count)])]
  transfers between devices with their start and end apart: 17 -> 18, of which waited for: 9 -> 9; matrix products, arithmetic and copies ran while one was open for 1% -> 1% of each run, Pallas kernels for 8% -> 8%
where the time goes in v8:
time: 115 us
  waiting for transfers between devices  52.6 us (46%)
  starting transfers between devices  25 us (22%)
  blocking collectives  17.4 us (15%)
  Pallas kernels  16.5 us (14%)
  matrix products  1.57 us (1%)
  other arithmetic  1.52 us (1%)
    all_to_all x3, waiting for transfers between devices, exchange(): return lax.all_to_all(value, 'seq', split_axis=0, concat_axis=0, tiled=True)  30.7 us
    ppermute x15, waiting for transfers between devices, swap(): return lax.ppermute(value, 'tp', [(i, i ^ bit) for i in range(count)])  22 us
    all_to_all x1, blocking collectives, exchange(): return lax.all_to_all(value, 'seq', split_axis=0, concat_axis=0, tiled=True)  17.4 us
    all_to_all x3, starting transfers between devices, exchange(): return lax.all_to_all(value, 'seq', split_axis=0, concat_axis=0, tiled=True)  15.4 us
    ppermute x15, starting transfers between devices, swap(): return lax.ppermute(value, 'tp', [(i, i ^ bit) for i in range(count)])  9.65 us
    pallas_call x2, Pallas kernels, run_expert(): pl.pallas_call(expert_kernel, in_specs=[pl.BlockSpec(memory_space=pltpu.S...  7.96 us
    pallas_call x1, Pallas kernels, mixer_tail(): pl.pallas_call(tail_kernel, in_specs=[pl.BlockSpec(memory_space=pltpu.SME...  3.18 us
    pallas_call x1, Pallas kernels, own_state(): pl.pallas_call(state_kernel, out_shape=[jax.ShapeDtypeStruct((count, part...  2.79 us
  transfers between devices with their start and end apart: 18, of which 9 were waited for; matrix products, arithmetic and copies ran while one was open for 1% of the time, Pallas kernels for 8%

profile of v8, /device:TPU:0, one launch (start us, length us, event | category | flops | bytes accessed | tf_op | source)
XLA Modules:
  0.0 114.8 jit_solution(8537178018593796198)
XLA Ops:
  0.0 2.8 %own_state.1 = (bf16[8,144,128]{2,1,0:T(8,128)(2,1)}, f32[16,128]{1,0:T(8,128)S(1)}) custom-call(bf16[128,1024]{1,0:T(8,128)(2,1)} %x.3, f32[16,128]{1,0:T(8,128)} %bitcast.47, f32[16,128]{1,0:T(8,128)} %bitcast.49, bf16[128,128]{1,0:T(8,128)(2,1)} %b.3), custom_call_target="tpu_custom_call" | custom-call | tf_op jit(solution)/shard_map/own_state/pallas_call | solution.py:78
  2.8 7.3 %all-to-all-start = ((bf16[8,144,128]{2,1,0:T(8,128)(2,1)}), bf16[8,144,128]{2,1,0:T(8,128)(2,1)S(1)}, u32[]{:S(2)}, u32[]{:S(2)}) async-start(bf16[8,144,128]{2,1,0:T(8,128)(2,1)} %get-tuple-element.23), calls=%async_computation | async-start | bytes 589824 | tf_op jit(solution)/shard_map/all_to_all | solution.py:20
  10.1 9.6 %all-to-all-done.got = bf16[8,144,128]{2,1,0:T(8,128)(2,1)S(1)} async-done(((bf16[8,144,128]{2,1,0:T(8,128)(2,1)}), bf16[8,144,128]{2,1,0:T(8,128)(2,1)S(1)}, u32[]{:S(2)}, u32[]{:S(2)}) %all-to-all-start) | async-done | bytes 294944 | tf_op jit(solution)/shard_map/all_to_all | solution.py:20
  19.7 0.9 prefix.1
  20.6 3.6 %all-to-all-start.1 = ((bf16[8,128,128]{2,1,0:T(8,128)(2,1)}), bf16[8,128,128]{2,1,0:T(8,128)(2,1)S(1)}, u32[]{:S(2)}, u32[]{:S(2)}) async-start(bf16[8,128,128]{2,1,0:T(8,128)(2,1)} %prefix.1), calls=%async_computation.1 | async-start | bytes 524288 | tf_op jit(solution)/shard_map/all_to_all | solution.py:20
  24.2 1.7 %within_block.1.direct_in = f32[128,1024]{1,0:T(8,128)S(1)} custom-call(f32[16]{0:T(128)S(1)} %copy-done.1, bf16[128,1024]{1,0:T(8,128)(2,1)} %x.3, f32[16,128]{1,0:T(8,128)} %bitcast.48, f32[16,128]{1,0:T(8,128)S(1)} %get-tuple-element.22.cum_t.cum_in, bf16[128,128]{1,0:T(8,128)(2,1)} %b.3, bf16[128,128]{1,0:T(8,128)(2,1)} %c_in.1), custom_call_target="tpu_custom_call" | custom-call | flops 134217728 | bytes 786432 | tf_op jit(solution)/shard_map/within_block/pallas_call | solution.py:148
  25.8 6.9 %all-to-all-done.1 = bf16[8,128,128]{2,1,0:T(8,128)(2,1)S(1)} async-done(((bf16[8,128,128]{2,1,0:T(8,128)(2,1)}), bf16[8,128,128]{2,1,0:T(8,128)(2,1)S(1)}, u32[]{:S(2)}, u32[]{:S(2)}) %all-to-all-start.1) | async-done | bytes 262176 | tf_op jit(solution)/shard_map/all_to_all | solution.py:20
  32.7 3.2 %mixer_tail.1 = (bf16[128,512]{1,0:T(8,128)(2,1)S(1)}, bf16[128,512]{1,0:T(8,128)(2,1)S(1)}, f32[128,512]{1,0:T(8,128)S(1)}, f32[128,512]{1,0:T(8,128)S(1)}) custom-call(s32[1]{0:T(128)} %bitcast.place_ref, bf16[128,128]{1,0:T(8,128)(2,1)} %c_in.1, f32[16,128]{1,0:T(8,128)S(1)} %get-tuple-element.22.cum_t.cum_in, f32[1,1024]{1,0:T(1,128)} %bitcast.50, ...), custom_call_target="tpu_custom_call" | custom-call | flops 536870912 | bytes 6029312 | tf_op jit(solution)/shard_map/mixer_tail/pallas_call | solution.py:230
  36.2 0.6 collective-permute-start
  36.7 0.6 collective-permute-done.1
  37.3 1.6 %collective-permute-start.2 = (bf16[128,512]{1,0:T(8,128)(2,1)S(1)}, bf16[128,512]{1,0:T(8,128)(2,1)S(1)}, u32[]{:S(2)}, u32[]{:S(2)}) collective-permute-start(bf16[128,512]{1,0:T(8,128)(2,1)S(1)} %add_convert_fusion.6), channel_id=1, source_target_pairs={{0,2},{1,3},{2,0},{3,1},{4,6},{5,7},{6,4},{7,5},{8,10},{9,11},{10,... | collective-permute-start | bytes 393224 | tf_op jit(solution)/shard_map/ppermute | solution.py:16
  39.0 3.9 %collective-permute-done.2 = bf16[128,512]{1,0:T(8,128)(2,1)S(1)} collective-permute-done((bf16[128,512]{1,0:T(8,128)(2,1)S(1)}, bf16[128,512]{1,0:T(8,128)(2,1)S(1)}, u32[]{:S(2)}, u32[]{:S(2)}) %collective-permute-start.2) | collective-permute-done | bytes 131104 | tf_op jit(solution)/shard_map/ppermute | solution.py:16
  43.0 0.3 convolution_convert_fusion
  43.3 17.4 %all_to_all.20 = bf16[8,64,512]{2,1,0:T(8,128)(2,1)S(1)} all-to-all(bf16[8,64,512]{2,1,0:T(8,128)(2,1)S(1)} %bitcast.44), channel_id=1, replica_groups=mesh['seq'=8,'tp'=4] {'seq'}, dimensions={0} | all-to-all | bytes 1048576 | tf_op jit(solution)/shard_map/all_to_all | solution.py:20
  60.8 1.6 %collective-permute-start.4 = (bf16[256,512]{1,0:T(8,128)(2,1)S(1)}, bf16[256,512]{1,0:T(8,128)(2,1)S(1)}, u32[]{:S(2)}, u32[]{:S(2)}) collective-permute-start(bf16[256,512]{1,0:T(8,128)(2,1)S(1)} %bitcast.33), channel_id=1, source_target_pairs={{0,2},{1,3},{2,0},{3,1},{4,6},{5,7},{6,4},{7,5},{8,10},{9,11},{10,... | collective-permute-start | bytes 786440 | tf_op jit(solution)/shard_map/ppermute | solution.py:16
  62.3 5.2 %collective-permute-done.4.far_in = bf16[256,512]{1,0:T(8,128)(2,1)S(1)} collective-permute-done((bf16[256,512]{1,0:T(8,128)(2,1)S(1)}, bf16[256,512]{1,0:T(8,128)(2,1)S(1)}, u32[]{:S(2)}, u32[]{:S(2)}) %collective-permute-start.4) | collective-permute-done | bytes 262176 | tf_op jit(solution)/shard_map/ppermute | solution.py:16
  67.5 1.5 %collective-permute-start.10 = (bf16[256,512]{1,0:T(8,128)(2,1)S(1)}, bf16[256,512]{1,0:T(8,128)(2,1)S(1)}, u32[]{:S(2)}, u32[]{:S(2)}) collective-permute-start(bf16[256,512]{1,0:T(8,128)(2,1)S(1)} %bitcast.30), channel_id=1, source_target_pairs={{0,2},{1,3},{2,0},{3,1},{4,6},{5,7},{6,4},{7,5},{8,10},{9,11},{10,... | collective-permute-start | bytes 786440 | tf_op jit(solution)/shard_map/ppermute | solution.py:16
  69.0 4.0 %expert.2 = (bf16[256,512]{1,0:T(8,128)(2,1)S(1)}, bf16[256,512]{1,0:T(8,128)(2,1)S(1)}, bf16[256,512]{1,0:T(8,128)(2,1)S(1)}, bf16[256,512]{1,0:T(8,128)(2,1)S(1)}) custom-call(s32[1]{0:T(128)} %bitcast.place_ref, f32[1,2048]{1,0:T(1,128)} %bitcast.45, bf16[256,512]{1,0:T(8,128)(2,1)S(1)} %bitcast.35, bf16[256,512]{1,0:T(8,128)(2,1)S(1)} %collective-permute-done.3.near_in, ...), custom_call_target="tpu_custom_call" | custom-call | flops 1 | bytes 1 | tf_op jit(solution)/shard_map/expert/pallas_call | solution.py:299
  73.0 0.3 collective-permute-start.7
  73.3 0.3 collective-permute-start.9
  73.6 2.6 %collective-permute-done.10.far_in = bf16[256,512]{1,0:T(8,128)(2,1)S(1)} collective-permute-done((bf16[256,512]{1,0:T(8,128)(2,1)S(1)}, bf16[256,512]{1,0:T(8,128)(2,1)S(1)}, u32[]{:S(2)}, u32[]{:S(2)}) %collective-permute-start.10) | collective-permute-done | bytes 262176 | tf_op jit(solution)/shard_map/ppermute | solution.py:16
  76.3 1.6 %collective-permute-start.8 = (bf16[256,512]{1,0:T(8,128)(2,1)S(1)}, bf16[256,512]{1,0:T(8,128)(2,1)S(1)}, u32[]{:S(2)}, u32[]{:S(2)}) collective-permute-start(bf16[256,512]{1,0:T(8,128)(2,1)S(1)} %add_convert_fusion.3), channel_id=1, source_target_pairs={{0,2},{1,3},{2,0},{3,1},{4,6},{5,7},{6,4},{7,5},{8,10},{9,11},{10,... | collective-permute-start | bytes 786440 | tf_op jit(solution)/shard_map/ppermute | solution.py:16
  77.9 4.0 %expert.3 = (bf16[256,512]{1,0:T(8,128)(2,1)S(1)}, bf16[256,512]{1,0:T(8,128)(2,1)S(1)}, bf16[256,512]{1,0:T(8,128)(2,1)S(1)}, bf16[256,512]{1,0:T(8,128)(2,1)S(1)}) custom-call(s32[1]{0:T(128)} %bitcast.place_ref, f32[1,2048]{1,0:T(1,128)} %bitcast.46, bf16[256,512]{1,0:T(8,128)(2,1)S(1)} %bitcast.32, bf16[256,512]{1,0:T(8,128)(2,1)S(1)} %collective-permute-done.9.near_in, ...), custom_call_target="tpu_custom_call" | custom-call | flops 1 | bytes 1 | tf_op jit(solution)/shard_map/expert/pallas_call | solution.py:299
  81.9 0.3 collective-permute-start.13
  82.2 0.3 collective-permute-start.6
  82.5 2.6 %collective-permute-done.8 = bf16[256,512]{1,0:T(8,128)(2,1)S(1)} collective-permute-done((bf16[256,512]{1,0:T(8,128)(2,1)S(1)}, bf16[256,512]{1,0:T(8,128)(2,1)S(1)}, u32[]{:S(2)}, u32[]{:S(2)}) %collective-permute-start.8) | collective-permute-done | bytes 262176 | tf_op jit(solution)/shard_map/ppermute | solution.py:16
  85.2 1.6 %collective-permute-start.14 = (bf16[256,512]{1,0:T(8,128)(2,1)S(1)}, bf16[256,512]{1,0:T(8,128)(2,1)S(1)}, u32[]{:S(2)}, u32[]{:S(2)}) collective-permute-start(bf16[256,512]{1,0:T(8,128)(2,1)S(1)} %add_convert_fusion.1), channel_id=1, source_target_pairs={{0,2},{1,3},{2,0},{3,1},{4,6},{5,7},{6,4},{7,5},{8,10},{9,11},{10,... | collective-permute-start | bytes 786440 | tf_op jit(solution)/shard_map/ppermute | solution.py:16
  86.9 7.1 %collective-permute-done.14 = bf16[256,512]{1,0:T(8,128)(2,1)S(1)} collective-permute-done((bf16[256,512]{1,0:T(8,128)(2,1)S(1)}, bf16[256,512]{1,0:T(8,128)(2,1)S(1)}, u32[]{:S(2)}, u32[]{:S(2)}) %collective-permute-start.14) | collective-permute-done | bytes 262176 | tf_op jit(solution)/shard_map/ppermute | solution.py:16
  94.1 0.8 pad_maximum_fusion
  94.9 4.5 %all-to-all-start.3 = ((bf16[8,64,512]{2,1,0:T(8,128)(2,1)}), bf16[8,64,512]{2,1,0:T(8,128)(2,1)S(1)}, u32[]{:S(2)}, u32[]{:S(2)}) async-start(bf16[8,64,512]{2,1,0:T(8,128)(2,1)} %bitcast.18), calls=%async_computation.3 | async-start | bytes 1048576 | tf_op jit(solution)/shard_map/all_to_all | solution.py:20
  99.6 14.2 %all-to-all-done.3 = bf16[8,64,512]{2,1,0:T(8,128)(2,1)S(1)} async-done(((bf16[8,64,512]{2,1,0:T(8,128)(2,1)}), bf16[8,64,512]{2,1,0:T(8,128)(2,1)S(1)}, u32[]{:S(2)}, u32[]{:S(2)}) %all-to-all-start.3) | async-done | bytes 524320 | tf_op jit(solution)/shard_map/all_to_all | solution.py:20
  113.8 1.0 add_convert_fusion.4
  (34 shorter events, 1.1 us)
Async XLA Ops:
  0.0 10.0 %copy-start = (f32[16,64,128]{2,1,0:T(8,128)S(1)}, f32[16,64,128]{2,1,0:T(8,128)}, u32[]{:S(2)}) copy-start(f32[16,64,128]{2,1,0:T(8,128)} %param.25) | copy-start | bytes 1572868
  0.0 24.2 %copy-start.1 = (f32[16]{0:T(128)S(1)}, f32[16]{0:T(128)}, u32[]{:S(2)}) copy-start(f32[16]{0:T(128)} %skip.1) | copy-start | bytes 196
  2.8 16.9 %all-to-all-start = ((bf16[8,144,128]{2,1,0:T(8,128)(2,1)}), bf16[8,144,128]{2,1,0:T(8,128)(2,1)S(1)}, u32[]{:S(2)}, u32[]{:S(2)}) async-start(bf16[8,144,128]{2,1,0:T(8,128)(2,1)} %get-tuple-element.23), calls=%async_computation | async-start | bytes 589824 | tf_op jit(solution)/shard_map/all_to_all | solution.py:20
  20.6 12.1 %all-to-all-start.1 = ((bf16[8,128,128]{2,1,0:T(8,128)(2,1)}), bf16[8,128,128]{2,1,0:T(8,128)(2,1)S(1)}, u32[]{:S(2)}, u32[]{:S(2)}) async-start(bf16[8,128,128]{2,1,0:T(8,128)(2,1)} %prefix.1), calls=%async_computation.1 | async-start | bytes 524288 | tf_op jit(solution)/shard_map/all_to_all | solution.py:20
  32.7 3.3 %copy-start.3 = (s32[128,2]{0,1:T(2,128)S(1)}, s32[128,2]{0,1:T(2,128)}, u32[]{:S(2)}) copy-start(s32[128,2]{0,1:T(2,128)} %param.29) | copy-start | bytes 3076
  35.9 1.4 %collective-permute-start.1 = (bf16[128,512]{1,0:T(8,128)(2,1)S(1)}, bf16[128,512]{1,0:T(8,128)(2,1)S(1)}, u32[]{:S(2)}, u32[]{:S(2)}) collective-permute-start(bf16[128,512]{1,0:T(8,128)(2,1)S(1)} %get-tuple-element.27), channel_id=1, source_target_pairs={{0,1},{1,0},{2,3},{3,2},{4,5},{5,4},{6,7},{7,6},{8,9},{9,8},{10,11... | collective-permute-start | bytes 393224 | tf_op jit(solution)/shard_map/ppermute | solution.py:16
  36.2 2.9 %collective-permute-start = (bf16[128,512]{1,0:T(8,128)(2,1)S(1)}, bf16[128,512]{1,0:T(8,128)(2,1)S(1)}, u32[]{:S(2)}, u32[]{:S(2)}) collective-permute-start(bf16[128,512]{1,0:T(8,128)(2,1)S(1)} %get-tuple-element.25), channel_id=1, source_target_pairs={{0,1},{1,0},{2,3},{3,2},{4,5},{5,4},{6,7},{7,6},{8,9},{9,8},{10,11... | collective-permute-start | bytes 393224 | tf_op jit(solution)/shard_map/ppermute | solution.py:16
  37.3 5.6 %collective-permute-start.2 = (bf16[128,512]{1,0:T(8,128)(2,1)S(1)}, bf16[128,512]{1,0:T(8,128)(2,1)S(1)}, u32[]{:S(2)}, u32[]{:S(2)}) collective-permute-start(bf16[128,512]{1,0:T(8,128)(2,1)S(1)} %add_convert_fusion.6), channel_id=1, source_target_pairs={{0,2},{1,3},{2,0},{3,1},{4,6},{5,7},{6,4},{7,5},{8,10},{9,11},{10,... | collective-permute-start | bytes 393224 | tf_op jit(solution)/shard_map/ppermute | solution.py:16
  60.8 6.7 %collective-permute-start.4 = (bf16[256,512]{1,0:T(8,128)(2,1)S(1)}, bf16[256,512]{1,0:T(8,128)(2,1)S(1)}, u32[]{:S(2)}, u32[]{:S(2)}) collective-permute-start(bf16[256,512]{1,0:T(8,128)(2,1)S(1)} %bitcast.33), channel_id=1, source_target_pairs={{0,2},{1,3},{2,0},{3,1},{4,6},{5,7},{6,4},{7,5},{8,10},{9,11},{10,... | collective-permute-start | bytes 786440 | tf_op jit(solution)/shard_map/ppermute | solution.py:16
  62.3 6.7 %collective-permute-start.3 = (bf16[256,512]{1,0:T(8,128)(2,1)S(1)}, bf16[256,512]{1,0:T(8,128)(2,1)S(1)}, u32[]{:S(2)}, u32[]{:S(2)}) collective-permute-start(bf16[256,512]{1,0:T(8,128)(2,1)S(1)} %bitcast.34), channel_id=1, source_target_pairs={{0,1},{1,0},{2,3},{3,2},{4,5},{5,4},{6,7},{7,6},{8,9},{9,8},{10,11... | collective-permute-start | bytes 786440 | tf_op jit(solution)/shard_map/ppermute | solution.py:16
  67.5 1.5 %collective-permute-start.5 = (bf16[256,512]{1,0:T(8,128)(2,1)S(1)}, bf16[256,512]{1,0:T(8,128)(2,1)S(1)}, u32[]{:S(2)}, u32[]{:S(2)}) collective-permute-start(bf16[256,512]{1,0:T(8,128)(2,1)S(1)} %collective-permute-done.4.far_in), channel_id=1, source_target_pairs={{0,1},{1,0},{2,3},{3,2},{4,5},{5,4},{6,7},{7,6},{8,9},{9,8},{10,11... | collective-permute-start | bytes 786440 | tf_op jit(solution)/shard_map/ppermute | solution.py:16
  67.5 8.7 %collective-permute-start.10 = (bf16[256,512]{1,0:T(8,128)(2,1)S(1)}, bf16[256,512]{1,0:T(8,128)(2,1)S(1)}, u32[]{:S(2)}, u32[]{:S(2)}) collective-permute-start(bf16[256,512]{1,0:T(8,128)(2,1)S(1)} %bitcast.30), channel_id=1, source_target_pairs={{0,2},{1,3},{2,0},{3,1},{4,6},{5,7},{6,4},{7,5},{8,10},{9,11},{10,... | collective-permute-start | bytes 786440 | tf_op jit(solution)/shard_map/ppermute | solution.py:16
  73.0 3.2 %collective-permute-start.7 = (bf16[256,512]{1,0:T(8,128)(2,1)S(1)}, bf16[256,512]{1,0:T(8,128)(2,1)S(1)}, u32[]{:S(2)}, u32[]{:S(2)}) collective-permute-start(bf16[256,512]{1,0:T(8,128)(2,1)S(1)} %get-tuple-element.31), channel_id=1, source_target_pairs={{0,1},{1,0},{2,3},{3,2},{4,5},{5,4},{6,7},{7,6},{8,9},{9,8},{10,11... | collective-permute-start | bytes 786440 | tf_op jit(solution)/shard_map/ppermute | solution.py:16
  73.3 4.6 %collective-permute-start.9 = (bf16[256,512]{1,0:T(8,128)(2,1)S(1)}, bf16[256,512]{1,0:T(8,128)(2,1)S(1)}, u32[]{:S(2)}, u32[]{:S(2)}) collective-permute-start(bf16[256,512]{1,0:T(8,128)(2,1)S(1)} %bitcast.31), channel_id=1, source_target_pairs={{0,1},{1,0},{2,3},{3,2},{4,5},{5,4},{6,7},{7,6},{8,9},{9,8},{10,11... | collective-permute-start | bytes 786440 | tf_op jit(solution)/shard_map/ppermute | solution.py:16
  76.2 1.7 %collective-permute-start.11 = (bf16[256,512]{1,0:T(8,128)(2,1)S(1)}, bf16[256,512]{1,0:T(8,128)(2,1)S(1)}, u32[]{:S(2)}, u32[]{:S(2)}) collective-permute-start(bf16[256,512]{1,0:T(8,128)(2,1)S(1)} %collective-permute-done.10.far_in), channel_id=1, source_target_pairs={{0,1},{1,0},{2,3},{3,2},{4,5},{5,4},{6,7},{7,6},{8,9},{9,8},{10,11... | collective-permute-start | bytes 786440 | tf_op jit(solution)/shard_map/ppermute | solution.py:16
  76.3 8.8 %collective-permute-start.8 = (bf16[256,512]{1,0:T(8,128)(2,1)S(1)}, bf16[256,512]{1,0:T(8,128)(2,1)S(1)}, u32[]{:S(2)}, u32[]{:S(2)}) collective-permute-start(bf16[256,512]{1,0:T(8,128)(2,1)S(1)} %add_convert_fusion.3), channel_id=1, source_target_pairs={{0,2},{1,3},{2,0},{3,1},{4,6},{5,7},{6,4},{7,5},{8,10},{9,11},{10,... | collective-permute-start | bytes 786440 | tf_op jit(solution)/shard_map/ppermute | solution.py:16
  81.9 3.2 %collective-permute-start.13 = (bf16[256,512]{1,0:T(8,128)(2,1)S(1)}, bf16[256,512]{1,0:T(8,128)(2,1)S(1)}, u32[]{:S(2)}, u32[]{:S(2)}) collective-permute-start(bf16[256,512]{1,0:T(8,128)(2,1)S(1)} %get-tuple-element.38), channel_id=1, source_target_pairs={{0,1},{1,0},{2,3},{3,2},{4,5},{5,4},{6,7},{7,6},{8,9},{9,8},{10,11... | collective-permute-start | bytes 786440 | tf_op jit(solution)/shard_map/ppermute | solution.py:16
  82.2 4.6 %collective-permute-start.6 = (bf16[256,512]{1,0:T(8,128)(2,1)S(1)}, bf16[256,512]{1,0:T(8,128)(2,1)S(1)}, u32[]{:S(2)}, u32[]{:S(2)}) collective-permute-start(bf16[256,512]{1,0:T(8,128)(2,1)S(1)} %get-tuple-element.29), channel_id=1, source_target_pairs={{0,1},{1,0},{2,3},{3,2},{4,5},{5,4},{6,7},{7,6},{8,9},{9,8},{10,11... | collective-permute-start | bytes 786440 | tf_op jit(solution)/shard_map/ppermute | solution.py:16
  85.1 1.8 %collective-permute-start.12 = (bf16[256,512]{1,0:T(8,128)(2,1)S(1)}, bf16[256,512]{1,0:T(8,128)(2,1)S(1)}, u32[]{:S(2)}, u32[]{:S(2)}) collective-permute-start(bf16[256,512]{1,0:T(8,128)(2,1)S(1)} %get-tuple-element.36), channel_id=1, source_target_pairs={{0,1},{1,0},{2,3},{3,2},{4,5},{5,4},{6,7},{7,6},{8,9},{9,8},{10,11... | collective-permute-start | bytes 786440 | tf_op jit(solution)/shard_map/ppermute | solution.py:16
  85.2 8.8 %collective-permute-start.14 = (bf16[256,512]{1,0:T(8,128)(2,1)S(1)}, bf16[256,512]{1,0:T(8,128)(2,1)S(1)}, u32[]{:S(2)}, u32[]{:S(2)}) collective-permute-start(bf16[256,512]{1,0:T(8,128)(2,1)S(1)} %add_convert_fusion.1), channel_id=1, source_target_pairs={{0,2},{1,3},{2,0},{3,1},{4,6},{5,7},{6,4},{7,5},{8,10},{9,11},{10,... | collective-permute-start | bytes 786440 | tf_op jit(solution)/shard_map/ppermute | solution.py:16
  86.8 12.7 %copy-start.2 = (f32[128,2]{0,1:T(2,128)S(1)}, f32[128,2]{0,1:T(2,128)}, u32[]{:S(2)}) copy-start(f32[128,2]{0,1:T(2,128)} %param.30) | copy-start | bytes 3076
  94.9 18.9 %all-to-all-start.3 = ((bf16[8,64,512]{2,1,0:T(8,128)(2,1)}), bf16[8,64,512]{2,1,0:T(8,128)(2,1)S(1)}, u32[]{:S(2)}, u32[]{:S(2)}) async-start(bf16[8,64,512]{2,1,0:T(8,128)(2,1)} %bitcast.18), calls=%async_computation.3 | async-start | bytes 1048576 | tf_op jit(solution)/shard_map/all_to_all | solution.py:20

commit v9 on v8

--- a/solution.py
+++ b/solution.py
@@ -149,7 +149,7 @@
         within_kernel,
         in_specs=[pl.BlockSpec(memory_space=pltpu.SMEM)] + [vmem] * 5,
         out_shape=jax.ShapeDtypeStruct((toks, inner), F32),
-        compiler_params=params(24),
+        compiler_params=params(8),
         cost_estimate=pl.CostEstimate(
             flops=4 * heads * toks * toks * LANES,
             bytes_accessed=6 * toks * inner,
@@ -238,7 +238,7 @@
             pltpu.VMEM((toks, inner), BF),
             pltpu.SemaphoreType.DMA((15,)),
         ],
-        compiler_params=params(24),
+        compiler_params=params(12),
         cost_estimate=pl.CostEstimate(
             flops=2 * toks * inner * width,
             bytes_accessed=2 * inner * width + 14 * toks * inner,
@@ -306,7 +306,7 @@
             pltpu.VMEM((4, rows, share), BF),
             pltpu.SemaphoreType.DMA((17,)),
         ],
-        compiler_params=params(24),
+        compiler_params=params(16),
         cost_estimate=pl.CostEstimate(flops=1, bytes_accessed=1, transcendentals=0),
         name="expert",
     )(place.reshape(1), *operands)
@@ -389,11 +389,11 @@
     to_near1, to_last1, keep1, pass1 = run_expert(
         place, moe_gain, after(own[1], pass0), near[1], far[1], last, *weights
     )
-    from_near0 = swap(to_near0, 1)
     from_last1 = swap(to_last1, 1)
-    from_near1 = swap(after(to_near1, from_far0), 1)
+    from_near0 = swap(after(to_near0, from_far0), 1)
     pass1 = (pass1.astype(F32) + from_last1.astype(F32)).astype(BF)
     from_far1 = swap(pass1, 2)
+    from_near1 = swap(after(to_near1, pass1), 1)
     results = [
         (keep.astype(F32) + from_near.astype(F32) + from_far.astype(F32)).astype(BF)
         for keep, from_near, from_far in (

time: 115 us -> 115 us (level)
  no operation moved by 1% of the time
where the time goes in v9:
time: 115 us; the launch traced here: 114 us
  waiting for transfers between devices  52.1 us (45%)
  starting transfers between devices  25.2 us (22%)
  blocking collectives  17.4 us (15%)
  Pallas kernels  16.5 us (14%)
  matrix products  1.58 us (1%)
  other arithmetic  1.52 us (1%)
    all_to_all x3, waiting for transfers between devices, exchange(): return lax.all_to_all(value, 'seq', split_axis=0, concat_axis=0, tiled=True)  30.2 us
    ppermute x15, waiting for transfers between devices, swap(): return lax.ppermute(value, 'tp', [(i, i ^ bit) for i in range(count)])  21.8 us
    all_to_all x1, blocking collectives, exchange(): return lax.all_to_all(value, 'seq', split_axis=0, concat_axis=0, tiled=True)  17.4 us
    all_to_all x3, starting transfers between devices, exchange(): return lax.all_to_all(value, 'seq', split_axis=0, concat_axis=0, tiled=True)  15.4 us
    ppermute x15, starting transfers between devices, swap(): return lax.ppermute(value, 'tp', [(i, i ^ bit) for i in range(count)])  9.88 us
    pallas_call x2, Pallas kernels, run_expert(): pl.pallas_call(expert_kernel, in_specs=[pl.BlockSpec(memory_space=pltpu.S...  7.96 us
    pallas_call x1, Pallas kernels, mixer_tail(): pl.pallas_call(tail_kernel, in_specs=[pl.BlockSpec(memory_space=pltpu.SME...  3.18 us
    pallas_call x1, Pallas kernels, own_state(): pl.pallas_call(state_kernel, out_shape=[jax.ShapeDtypeStruct((count, part...  2.79 us
  transfers between devices with their start and end apart: 18, of which 9 were waited for; matrix products, arithmetic and copies ran while one was open for 1% of the time, Pallas kernels for 8%

profile of v9, /device:TPU:0, one launch (start us, length us, event | category | flops | bytes accessed | tf_op | source)
XLA Modules:
  0.0 114.5 jit_solution(14396655830182963633)
XLA Ops:
  0.0 2.8 %own_state.1 = (bf16[8,144,128]{2,1,0:T(8,128)(2,1)}, f32[16,128]{1,0:T(8,128)S(1)}) custom-call(bf16[128,1024]{1,0:T(8,128)(2,1)} %x.3, f32[16,128]{1,0:T(8,128)} %bitcast.47, f32[16,128]{1,0:T(8,128)} %bitcast.49, bf16[128,128]{1,0:T(8,128)(2,1)} %b.3), custom_call_target="tpu_custom_call" | custom-call | tf_op jit(solution)/shard_map/own_state/pallas_call | solution.py:78
  2.8 7.3 %all-to-all-start = ((bf16[8,144,128]{2,1,0:T(8,128)(2,1)}), bf16[8,144,128]{2,1,0:T(8,128)(2,1)S(1)}, u32[]{:S(2)}, u32[]{:S(2)}) async-start(bf16[8,144,128]{2,1,0:T(8,128)(2,1)} %get-tuple-element.24), calls=%async_computation | async-start | bytes 589824 | tf_op jit(solution)/shard_map/all_to_all | solution.py:20
  10.1 9.6 %all-to-all-done.got = bf16[8,144,128]{2,1,0:T(8,128)(2,1)S(1)} async-done(((bf16[8,144,128]{2,1,0:T(8,128)(2,1)}), bf16[8,144,128]{2,1,0:T(8,128)(2,1)S(1)}, u32[]{:S(2)}, u32[]{:S(2)}) %all-to-all-start) | async-done | bytes 294944 | tf_op jit(solution)/shard_map/all_to_all | solution.py:20
  19.7 0.9 prefix.1
  20.6 3.6 %all-to-all-start.1 = ((bf16[8,128,128]{2,1,0:T(8,128)(2,1)}), bf16[8,128,128]{2,1,0:T(8,128)(2,1)S(1)}, u32[]{:S(2)}, u32[]{:S(2)}) async-start(bf16[8,128,128]{2,1,0:T(8,128)(2,1)} %prefix.1), calls=%async_computation.1 | async-start | bytes 524288 | tf_op jit(solution)/shard_map/all_to_all | solution.py:20
  24.2 1.7 %within_block.1.direct_in = f32[128,1024]{1,0:T(8,128)S(1)} custom-call(f32[16]{0:T(128)S(1)} %copy-done.1, bf16[128,1024]{1,0:T(8,128)(2,1)} %x.3, f32[16,128]{1,0:T(8,128)} %bitcast.48, f32[16,128]{1,0:T(8,128)S(1)} %get-tuple-element.23.cum_t.cum_in, bf16[128,128]{1,0:T(8,128)(2,1)} %b.3, bf16[128,128]{1,0:T(8,128)(2,1)} %c_in.1), custom_call_target="tpu_custom_call" | custom-call | flops 134217728 | bytes 786432 | tf_op jit(solution)/shard_map/within_block/pallas_call | solution.py:148
  25.8 6.9 %all-to-all-done.1 = bf16[8,128,128]{2,1,0:T(8,128)(2,1)S(1)} async-done(((bf16[8,128,128]{2,1,0:T(8,128)(2,1)}), bf16[8,128,128]{2,1,0:T(8,128)(2,1)S(1)}, u32[]{:S(2)}, u32[]{:S(2)}) %all-to-all-start.1) | async-done | bytes 262176 | tf_op jit(solution)/shard_map/all_to_all | solution.py:20
  32.7 3.2 %mixer_tail.1 = (bf16[128,512]{1,0:T(8,128)(2,1)S(1)}, bf16[128,512]{1,0:T(8,128)(2,1)S(1)}, f32[128,512]{1,0:T(8,128)S(1)}, f32[128,512]{1,0:T(8,128)S(1)}) custom-call(s32[1]{0:T(128)} %bitcast.place_ref, bf16[128,128]{1,0:T(8,128)(2,1)} %c_in.1, f32[16,128]{1,0:T(8,128)S(1)} %get-tuple-element.23.cum_t.cum_in, f32[1,1024]{1,0:T(1,128)} %bitcast.50, ...), custom_call_target="tpu_custom_call" | custom-call | flops 536870912 | bytes 6029312 | tf_op jit(solution)/shard_map/mixer_tail/pallas_call | solution.py:230
  36.2 0.6 collective-permute-start
  36.7 0.6 collective-permute-done.1
  37.3 1.6 %collective-permute-start.2 = (bf16[128,512]{1,0:T(8,128)(2,1)S(1)}, bf16[128,512]{1,0:T(8,128)(2,1)S(1)}, u32[]{:S(2)}, u32[]{:S(2)}) collective-permute-start(bf16[128,512]{1,0:T(8,128)(2,1)S(1)} %add_convert_fusion.6), channel_id=1, source_target_pairs={{0,2},{1,3},{2,0},{3,1},{4,6},{5,7},{6,4},{7,5},{8,10},{9,11},{10,... | collective-permute-start | bytes 393224 | tf_op jit(solution)/shard_map/ppermute | solution.py:16
  39.0 3.9 %collective-permute-done.2 = bf16[128,512]{1,0:T(8,128)(2,1)S(1)} collective-permute-done((bf16[128,512]{1,0:T(8,128)(2,1)S(1)}, bf16[128,512]{1,0:T(8,128)(2,1)S(1)}, u32[]{:S(2)}, u32[]{:S(2)}) %collective-permute-start.2) | collective-permute-done | bytes 131104 | tf_op jit(solution)/shard_map/ppermute | solution.py:16
  43.0 0.3 convolution_convert_fusion
  43.4 17.4 %all_to_all.20 = bf16[8,64,512]{2,1,0:T(8,128)(2,1)S(1)} all-to-all(bf16[8,64,512]{2,1,0:T(8,128)(2,1)S(1)} %bitcast.44), channel_id=1, replica_groups=mesh['seq'=8,'tp'=4] {'seq'}, dimensions={0} | all-to-all | bytes 1048576 | tf_op jit(solution)/shard_map/all_to_all | solution.py:20
  60.8 1.6 %collective-permute-start.4 = (bf16[256,512]{1,0:T(8,128)(2,1)S(1)}, bf16[256,512]{1,0:T(8,128)(2,1)S(1)}, u32[]{:S(2)}, u32[]{:S(2)}) collective-permute-start(bf16[256,512]{1,0:T(8,128)(2,1)S(1)} %bitcast.33), channel_id=1, source_target_pairs={{0,2},{1,3},{2,0},{3,1},{4,6},{5,7},{6,4},{7,5},{8,10},{9,11},{10,... | collective-permute-start | bytes 786440 | tf_op jit(solution)/shard_map/ppermute | solution.py:16
  62.3 5.2 %collective-permute-done.4.far_in = bf16[256,512]{1,0:T(8,128)(2,1)S(1)} collective-permute-done((bf16[256,512]{1,0:T(8,128)(2,1)S(1)}, bf16[256,512]{1,0:T(8,128)(2,1)S(1)}, u32[]{:S(2)}, u32[]{:S(2)}) %collective-permute-start.4) | collective-permute-done | bytes 262176 | tf_op jit(solution)/shard_map/ppermute | solution.py:16
  67.5 1.5 %collective-permute-start.10 = (bf16[256,512]{1,0:T(8,128)(2,1)S(1)}, bf16[256,512]{1,0:T(8,128)(2,1)S(1)}, u32[]{:S(2)}, u32[]{:S(2)}) collective-permute-start(bf16[256,512]{1,0:T(8,128)(2,1)S(1)} %bitcast.30), channel_id=1, source_target_pairs={{0,2},{1,3},{2,0},{3,1},{4,6},{5,7},{6,4},{7,5},{8,10},{9,11},{10,... | collective-permute-start | bytes 786440 | tf_op jit(solution)/shard_map/ppermute | solution.py:16
  69.0 4.0 %expert.2 = (bf16[256,512]{1,0:T(8,128)(2,1)S(1)}, bf16[256,512]{1,0:T(8,128)(2,1)S(1)}, bf16[256,512]{1,0:T(8,128)(2,1)S(1)}, bf16[256,512]{1,0:T(8,128)(2,1)S(1)}) custom-call(s32[1]{0:T(128)} %bitcast.place_ref, f32[1,2048]{1,0:T(1,128)} %bitcast.45, bf16[256,512]{1,0:T(8,128)(2,1)S(1)} %bitcast.35, bf16[256,512]{1,0:T(8,128)(2,1)S(1)} %collective-permute-done.3.near_in, ...), custom_call_target="tpu_custom_call" | custom-call | flops 1 | bytes 1 | tf_op jit(solution)/shard_map/expert/pallas_call | solution.py:299
  73.0 0.3 collective-permute-start.6
  73.3 0.3 collective-permute-start.9
  73.6 2.6 %collective-permute-done.10.far_in = bf16[256,512]{1,0:T(8,128)(2,1)S(1)} collective-permute-done((bf16[256,512]{1,0:T(8,128)(2,1)S(1)}, bf16[256,512]{1,0:T(8,128)(2,1)S(1)}, u32[]{:S(2)}, u32[]{:S(2)}) %collective-permute-start.10) | collective-permute-done | bytes 262176 | tf_op jit(solution)/shard_map/ppermute | solution.py:16
  76.3 1.6 %collective-permute-start.7 = (bf16[256,512]{1,0:T(8,128)(2,1)S(1)}, bf16[256,512]{1,0:T(8,128)(2,1)S(1)}, u32[]{:S(2)}, u32[]{:S(2)}) collective-permute-start(bf16[256,512]{1,0:T(8,128)(2,1)S(1)} %add_convert_fusion.3), channel_id=1, source_target_pairs={{0,2},{1,3},{2,0},{3,1},{4,6},{5,7},{6,4},{7,5},{8,10},{9,11},{10,... | collective-permute-start | bytes 786440 | tf_op jit(solution)/shard_map/ppermute | solution.py:16
  77.9 4.0 %expert.3 = (bf16[256,512]{1,0:T(8,128)(2,1)S(1)}, bf16[256,512]{1,0:T(8,128)(2,1)S(1)}, bf16[256,512]{1,0:T(8,128)(2,1)S(1)}, bf16[256,512]{1,0:T(8,128)(2,1)S(1)}) custom-call(s32[1]{0:T(128)} %bitcast.place_ref, f32[1,2048]{1,0:T(1,128)} %bitcast.46, bf16[256,512]{1,0:T(8,128)(2,1)S(1)} %bitcast.32, bf16[256,512]{1,0:T(8,128)(2,1)S(1)} %collective-permute-done.9.near_in, ...), custom_call_target="tpu_custom_call" | custom-call | flops 1 | bytes 1 | tf_op jit(solution)/shard_map/expert/pallas_call | solution.py:299
  81.9 0.3 collective-permute-start.12
  82.2 2.9 %collective-permute-done.7 = bf16[256,512]{1,0:T(8,128)(2,1)S(1)} collective-permute-done((bf16[256,512]{1,0:T(8,128)(2,1)S(1)}, bf16[256,512]{1,0:T(8,128)(2,1)S(1)}, u32[]{:S(2)}, u32[]{:S(2)}) %collective-permute-start.7) | collective-permute-done | bytes 262176 | tf_op jit(solution)/shard_map/ppermute | solution.py:16
  85.2 0.6 collective-permute-start.13
  85.7 1.5 %collective-permute-start.14 = (bf16[256,512]{1,0:T(8,128)(2,1)S(1)}, bf16[256,512]{1,0:T(8,128)(2,1)S(1)}, u32[]{:S(2)}, u32[]{:S(2)}) collective-permute-start(bf16[256,512]{1,0:T(8,128)(2,1)S(1)} %add_convert_fusion.1), channel_id=1, source_target_pairs={{0,2},{1,3},{2,0},{3,1},{4,6},{5,7},{6,4},{7,5},{8,10},{9,11},{10,... | collective-permute-start | bytes 786440 | tf_op jit(solution)/shard_map/ppermute | solution.py:16
  87.4 6.6 %collective-permute-done.14 = bf16[256,512]{1,0:T(8,128)(2,1)S(1)} collective-permute-done((bf16[256,512]{1,0:T(8,128)(2,1)S(1)}, bf16[256,512]{1,0:T(8,128)(2,1)S(1)}, u32[]{:S(2)}, u32[]{:S(2)}) %collective-permute-start.14) | collective-permute-done | bytes 262176 | tf_op jit(solution)/shard_map/ppermute | solution.py:16
  94.1 0.8 pad_maximum_fusion
  95.0 4.5 %all-to-all-start.3 = ((bf16[8,64,512]{2,1,0:T(8,128)(2,1)}), bf16[8,64,512]{2,1,0:T(8,128)(2,1)S(1)}, u32[]{:S(2)}, u32[]{:S(2)}) async-start(bf16[8,64,512]{2,1,0:T(8,128)(2,1)} %bitcast.18), calls=%async_computation.3 | async-start | bytes 1048576 | tf_op jit(solution)/shard_map/all_to_all | solution.py:20
  99.6 13.8 %all-to-all-done.3 = bf16[8,64,512]{2,1,0:T(8,128)(2,1)S(1)} async-done(((bf16[8,64,512]{2,1,0:T(8,128)(2,1)}), bf16[8,64,512]{2,1,0:T(8,128)(2,1)S(1)}, u32[]{:S(2)}, u32[]{:S(2)}) %all-to-all-start.3) | async-done | bytes 524320 | tf_op jit(solution)/shard_map/all_to_all | solution.py:20
  113.4 1.0 add_convert_fusion.4
  (34 shorter events, 1.1 us)
Async XLA Ops:
  0.0 10.0 %copy-start = (f32[16,64,128]{2,1,0:T(8,128)S(1)}, f32[16,64,128]{2,1,0:T(8,128)}, u32[]{:S(2)}) copy-start(f32[16,64,128]{2,1,0:T(8,128)} %param.25) | copy-start | bytes 1572868
  0.0 24.2 %copy-start.1 = (f32[16]{0:T(128)S(1)}, f32[16]{0:T(128)}, u32[]{:S(2)}) copy-start(f32[16]{0:T(128)} %skip.1) | copy-start | bytes 196
  2.8 16.9 %all-to-all-start = ((bf16[8,144,128]{2,1,0:T(8,128)(2,1)}), bf16[8,144,128]{2,1,0:T(8,128)(2,1)S(1)}, u32[]{:S(2)}, u32[]{:S(2)}) async-start(bf16[8,144,128]{2,1,0:T(8,128)(2,1)} %get-tuple-element.24), calls=%async_computation | async-start | bytes 589824 | tf_op jit(solution)/shard_map/all_to_all | solution.py:20
  20.6 12.1 %all-to-all-start.1 = ((bf16[8,128,128]{2,1,0:T(8,128)(2,1)}), bf16[8,128,128]{2,1,0:T(8,128)(2,1)S(1)}, u32[]{:S(2)}, u32[]{:S(2)}) async-start(bf16[8,128,128]{2,1,0:T(8,128)(2,1)} %prefix.1), calls=%async_computation.1 | async-start | bytes 524288 | tf_op jit(solution)/shard_map/all_to_all | solution.py:20
  32.7 3.3 %copy-start.3 = (s32[128,2]{0,1:T(2,128)S(1)}, s32[128,2]{0,1:T(2,128)}, u32[]{:S(2)}) copy-start(s32[128,2]{0,1:T(2,128)} %param.29) | copy-start | bytes 3076
  35.9 1.4 %collective-permute-start.1 = (bf16[128,512]{1,0:T(8,128)(2,1)S(1)}, bf16[128,512]{1,0:T(8,128)(2,1)S(1)}, u32[]{:S(2)}, u32[]{:S(2)}) collective-permute-start(bf16[128,512]{1,0:T(8,128)(2,1)S(1)} %get-tuple-element.28), channel_id=1, source_target_pairs={{0,1},{1,0},{2,3},{3,2},{4,5},{5,4},{6,7},{7,6},{8,9},{9,8},{10,11... | collective-permute-start | bytes 393224 | tf_op jit(solution)/shard_map/ppermute | solution.py:16
  36.2 2.9 %collective-permute-start = (bf16[128,512]{1,0:T(8,128)(2,1)S(1)}, bf16[128,512]{1,0:T(8,128)(2,1)S(1)}, u32[]{:S(2)}, u32[]{:S(2)}) collective-permute-start(bf16[128,512]{1,0:T(8,128)(2,1)S(1)} %get-tuple-element.26), channel_id=1, source_target_pairs={{0,1},{1,0},{2,3},{3,2},{4,5},{5,4},{6,7},{7,6},{8,9},{9,8},{10,11... | collective-permute-start | bytes 393224 | tf_op jit(solution)/shard_map/ppermute | solution.py:16
  37.3 5.6 %collective-permute-start.2 = (bf16[128,512]{1,0:T(8,128)(2,1)S(1)}, bf16[128,512]{1,0:T(8,128)(2,1)S(1)}, u32[]{:S(2)}, u32[]{:S(2)}) collective-permute-start(bf16[128,512]{1,0:T(8,128)(2,1)S(1)} %add_convert_fusion.6), channel_id=1, source_target_pairs={{0,2},{1,3},{2,0},{3,1},{4,6},{5,7},{6,4},{7,5},{8,10},{9,11},{10,... | collective-permute-start | bytes 393224 | tf_op jit(solution)/shard_map/ppermute | solution.py:16
  60.8 6.7 %collective-permute-start.4 = (bf16[256,512]{1,0:T(8,128)(2,1)S(1)}, bf16[256,512]{1,0:T(8,128)(2,1)S(1)}, u32[]{:S(2)}, u32[]{:S(2)}) collective-permute-start(bf16[256,512]{1,0:T(8,128)(2,1)S(1)} %bitcast.33), channel_id=1, source_target_pairs={{0,2},{1,3},{2,0},{3,1},{4,6},{5,7},{6,4},{7,5},{8,10},{9,11},{10,... | collective-permute-start | bytes 786440 | tf_op jit(solution)/shard_map/ppermute | solution.py:16
  62.3 6.7 %collective-permute-start.3 = (bf16[256,512]{1,0:T(8,128)(2,1)S(1)}, bf16[256,512]{1,0:T(8,128)(2,1)S(1)}, u32[]{:S(2)}, u32[]{:S(2)}) collective-permute-start(bf16[256,512]{1,0:T(8,128)(2,1)S(1)} %bitcast.34), channel_id=1, source_target_pairs={{0,1},{1,0},{2,3},{3,2},{4,5},{5,4},{6,7},{7,6},{8,9},{9,8},{10,11... | collective-permute-start | bytes 786440 | tf_op jit(solution)/shard_map/ppermute | solution.py:16
  67.5 1.5 %collective-permute-start.5 = (bf16[256,512]{1,0:T(8,128)(2,1)S(1)}, bf16[256,512]{1,0:T(8,128)(2,1)S(1)}, u32[]{:S(2)}, u32[]{:S(2)}) collective-permute-start(bf16[256,512]{1,0:T(8,128)(2,1)S(1)} %collective-permute-done.4.far_in), channel_id=1, source_target_pairs={{0,1},{1,0},{2,3},{3,2},{4,5},{5,4},{6,7},{7,6},{8,9},{9,8},{10,11... | collective-permute-start | bytes 786440 | tf_op jit(solution)/shard_map/ppermute | solution.py:16
  67.5 8.7 %collective-permute-start.10 = (bf16[256,512]{1,0:T(8,128)(2,1)S(1)}, bf16[256,512]{1,0:T(8,128)(2,1)S(1)}, u32[]{:S(2)}, u32[]{:S(2)}) collective-permute-start(bf16[256,512]{1,0:T(8,128)(2,1)S(1)} %bitcast.30), channel_id=1, source_target_pairs={{0,2},{1,3},{2,0},{3,1},{4,6},{5,7},{6,4},{7,5},{8,10},{9,11},{10,... | collective-permute-start | bytes 786440 | tf_op jit(solution)/shard_map/ppermute | solution.py:16
  73.0 3.2 %collective-permute-start.6 = (bf16[256,512]{1,0:T(8,128)(2,1)S(1)}, bf16[256,512]{1,0:T(8,128)(2,1)S(1)}, u32[]{:S(2)}, u32[]{:S(2)}) collective-permute-start(bf16[256,512]{1,0:T(8,128)(2,1)S(1)} %get-tuple-element.32), channel_id=1, source_target_pairs={{0,1},{1,0},{2,3},{3,2},{4,5},{5,4},{6,7},{7,6},{8,9},{9,8},{10,11... | collective-permute-start | bytes 786440 | tf_op jit(solution)/shard_map/ppermute | solution.py:16
  73.3 4.6 %collective-permute-start.9 = (bf16[256,512]{1,0:T(8,128)(2,1)S(1)}, bf16[256,512]{1,0:T(8,128)(2,1)S(1)}, u32[]{:S(2)}, u32[]{:S(2)}) collective-permute-start(bf16[256,512]{1,0:T(8,128)(2,1)S(1)} %bitcast.31), channel_id=1, source_target_pairs={{0,1},{1,0},{2,3},{3,2},{4,5},{5,4},{6,7},{7,6},{8,9},{9,8},{10,11... | collective-permute-start | bytes 786440 | tf_op jit(solution)/shard_map/ppermute | solution.py:16
  76.2 1.7 %collective-permute-start.11 = (bf16[256,512]{1,0:T(8,128)(2,1)S(1)}, bf16[256,512]{1,0:T(8,128)(2,1)S(1)}, u32[]{:S(2)}, u32[]{:S(2)}) collective-permute-start(bf16[256,512]{1,0:T(8,128)(2,1)S(1)} %collective-permute-done.10.far_in), channel_id=1, source_target_pairs={{0,1},{1,0},{2,3},{3,2},{4,5},{5,4},{6,7},{7,6},{8,9},{9,8},{10,11... | collective-permute-start | bytes 786440 | tf_op jit(solution)/shard_map/ppermute | solution.py:16
  76.3 8.8 %collective-permute-start.7 = (bf16[256,512]{1,0:T(8,128)(2,1)S(1)}, bf16[256,512]{1,0:T(8,128)(2,1)S(1)}, u32[]{:S(2)}, u32[]{:S(2)}) collective-permute-start(bf16[256,512]{1,0:T(8,128)(2,1)S(1)} %add_convert_fusion.3), channel_id=1, source_target_pairs={{0,2},{1,3},{2,0},{3,1},{4,6},{5,7},{6,4},{7,5},{8,10},{9,11},{10,... | collective-permute-start | bytes 786440 | tf_op jit(solution)/shard_map/ppermute | solution.py:16
  81.9 3.2 %collective-permute-start.12 = (bf16[256,512]{1,0:T(8,128)(2,1)S(1)}, bf16[256,512]{1,0:T(8,128)(2,1)S(1)}, u32[]{:S(2)}, u32[]{:S(2)}) collective-permute-start(bf16[256,512]{1,0:T(8,128)(2,1)S(1)} %get-tuple-element.39), channel_id=1, source_target_pairs={{0,1},{1,0},{2,3},{3,2},{4,5},{5,4},{6,7},{7,6},{8,9},{9,8},{10,11... | collective-permute-start | bytes 786440 | tf_op jit(solution)/shard_map/ppermute | solution.py:16
  85.1 2.2 %collective-permute-start.8 = (bf16[256,512]{1,0:T(8,128)(2,1)S(1)}, bf16[256,512]{1,0:T(8,128)(2,1)S(1)}, u32[]{:S(2)}, u32[]{:S(2)}) collective-permute-start(bf16[256,512]{1,0:T(8,128)(2,1)S(1)} %get-tuple-element.33), channel_id=1, source_target_pairs={{0,1},{1,0},{2,3},{3,2},{4,5},{5,4},{6,7},{7,6},{8,9},{9,8},{10,11... | collective-permute-start | bytes 786440 | tf_op jit(solution)/shard_map/ppermute | solution.py:16
  85.2 2.2 %collective-permute-start.13 = (bf16[256,512]{1,0:T(8,128)(2,1)S(1)}, bf16[256,512]{1,0:T(8,128)(2,1)S(1)}, u32[]{:S(2)}, u32[]{:S(2)}) collective-permute-start(bf16[256,512]{1,0:T(8,128)(2,1)S(1)} %get-tuple-element.40), channel_id=1, source_target_pairs={{0,1},{1,0},{2,3},{3,2},{4,5},{5,4},{6,7},{7,6},{8,9},{9,8},{10,11... | collective-permute-start | bytes 786440 | tf_op jit(solution)/shard_map/ppermute | solution.py:16
  85.7 8.3 %collective-permute-start.14 = (bf16[256,512]{1,0:T(8,128)(2,1)S(1)}, bf16[256,512]{1,0:T(8,128)(2,1)S(1)}, u32[]{:S(2)}, u32[]{:S(2)}) collective-permute-start(bf16[256,512]{1,0:T(8,128)(2,1)S(1)} %add_convert_fusion.1), channel_id=1, source_target_pairs={{0,2},{1,3},{2,0},{3,1},{4,6},{5,7},{6,4},{7,5},{8,10},{9,11},{10,... | collective-permute-start | bytes 786440 | tf_op jit(solution)/shard_map/ppermute | solution.py:16
  87.3 12.2 %copy-start.2 = (f32[128,2]{0,1:T(2,128)S(1)}, f32[128,2]{0,1:T(2,128)}, u32[]{:S(2)}) copy-start(f32[128,2]{0,1:T(2,128)} %param.30) | copy-start | bytes 3076
  95.0 18.5 %all-to-all-start.3 = ((bf16[8,64,512]{2,1,0:T(8,128)(2,1)}), bf16[8,64,512]{2,1,0:T(8,128)(2,1)S(1)}, u32[]{:S(2)}, u32[]{:S(2)}) async-start(bf16[8,64,512]{2,1,0:T(8,128)(2,1)} %bitcast.18), calls=%async_computation.3 | async-start | bytes 1048576 | tf_op jit(solution)/shard_map/all_to_all | solution.py:20

commit v10 on v9

--- a/solution.py
+++ b/solution.py
@@ -102,6 +102,20 @@
             back[turn, spot, :] = carries[h].astype(BF)
             factor = jnp.sum(jnp.where(row == first + h, scale, 0.0), axis=0, keepdims=True)
             carries[h] = factor * carries[h] + got[turn, spot, :].astype(F32)
+
+
+def exchange_halves(pieces):
+    count = lax.axis_size("seq")
+    halves = []
+    for turn in range(2):
+        got = []
+        for k in range(turn * count // 2, (turn + 1) * count // 2):
+            piece = pieces[turn][k - turn * count // 2]
+            if k > 0:
+                piece = lax.ppermute(piece, "seq", [(i, i ^ k) for i in range(count)])
+            got.append(piece)
+        halves.append(jnp.concatenate(got))
+    return halves
 
 
 def entering_state(got, init_rows):
@@ -341,10 +355,6 @@
     direct = within_block(skip_gain, input_heads, step_t, cum_t, b_proj, c_proj)
     back = entering_state(got, init_state.reshape(inner, state_size))
     arriving = exchange(back).reshape(inner, state_size)
-    to_near, to_last, keep, passing = mixer_tail(
-        place, c_proj, arriving, cum_t, direct, z_gate, norm_gain, out_weight, tokens
-    )
-
     model_width = out_weight.shape[1]
     share = model_width // 4
     expert_count = w_gate.shape[0] * seq_count
@@ -357,11 +367,18 @@
     before = jnp.arange(items)[:, None] > jnp.arange(items)[None, :]
     earlier = jnp.dot(before.astype(BF), onehot.astype(BF), preferred_element_type=F32)
     rank = jnp.sum(jnp.where(onehot, earlier, 0.0), axis=1).astype(jnp.int32)
-    placed = flat_expert * slot_count + rank
+    few = seq_count <= 8
+    layout = flat_expert ^ lax.axis_index("seq") if few else flat_expert
+    placed = layout * slot_count + rank
     spots = placed[:, None] == jnp.arange(slots, dtype=jnp.int32)[None, :]
     spots = spots.reshape(top_count, tok_rows, slots)
     fill = jnp.any(spots, axis=0).astype(BF)
     combine = jnp.sum(jnp.where(spots, route_weights.T[:, :, None], 0.0), axis=0)
+    direct = after(direct, fill, combine)
+
+    to_near, to_last, keep, passing = mixer_tail(
+        place, c_proj, arriving, cum_t, direct, z_gate, norm_gain, out_weight, tokens
+    )
 
     from_last = swap(to_last, 1)
     from_near = swap(to_near, 1)
@@ -371,10 +388,15 @@
     outgoing = lax.dot_general(
         fill, hidden, (((0,), (0,)), ((), ())), preferred_element_type=F32
     ).astype(BF)
-    arrived = exchange(outgoing.reshape(expert_count, slot_count, share)).reshape(slots, share)
+    outgoing = outgoing.reshape(expert_count, slot_count, share)
 
     cut = slots // 2
-    own = [arrived[:cut], arrived[cut:]]
+    middle = expert_count // 2
+    if few:
+        own = exchange_halves((outgoing[:middle], outgoing[middle:]))
+    else:
+        arrived = exchange(outgoing).reshape(slots, share)
+        own = [arrived[:cut], arrived[cut:]]
     far = [swap(part, 2) for part in own]
     near = [swap(part, 1) for part in own]
     weights = (w_gate[0], w_up[0], w_down[0])
@@ -401,8 +423,12 @@
             (keep1, from_near1, from_far1),
         )
     ]
-    results = jnp.concatenate(results).reshape(expert_count, slot_count, share)
-    returned = exchange(results).reshape(slots, share)
+    if few:
+        results = [part.reshape(middle, slot_count, share) for part in results]
+        returned = jnp.concatenate(exchange_halves(results))
+    else:
+        results = jnp.concatenate(results).reshape(expert_count, slot_count, share)
+        returned = exchange(results).reshape(slots, share)
     mixed = hidden.astype(F32) + jnp.dot(
         combine,
         returned.astype(F32),

time: 115 us -> 103 us (0.90)
  blocking collectives: 17.4 us -> 0 us
  starting transfers between devices: 25.2 us -> 41.6 us
  waiting for transfers between devices: 52.1 us -> 41 us
    ppermute x0 -> x14, starting transfers between devices: none -> 22.6 us  [exchange_halves(): piece = lax.ppermute(piece, 'seq', [(i, i ^ k) for i in range(count)])]
    all_to_all x1 -> x0, blocking collectives: 17.4 us -> none  [exchange(): return lax.all_to_all(value, 'seq', split_axis=0, concat_axis=0, tiled=True)]
    all_to_all x3 -> x2, waiting for transfers between devices: 30.2 us -> 15.4 us  [exchange(): return lax.all_to_all(value, 'seq', split_axis=0, concat_axis=0, tiled=True)]
    ppermute x0 -> x14, waiting for transfers between devices: none -> 12.3 us  [exchange_halves(): piece = lax.ppermute(piece, 'seq', [(i, i ^ k) for i in range(count)])]
    ppermute x15, waiting for transfers between devices: 21.8 us -> 13.2 us  [swap(): return lax.ppermute(value, 'tp', [(i, i ^ bit) for i in range(count)])]
    all_to_all x3 -> x2, starting transfers between devices: 15.4 us -> 10.8 us  [exchange(): return lax.all_to_all(value, 'seq', split_axis=0, concat_axis=0, tiled=True)]
    ppermute x15, starting transfers between devices: 9.88 us -> 8.12 us  [swap(): return lax.ppermute(value, 'tp', [(i, i ^ bit) for i in range(count)])]
  transfers between devices with their start and end apart: 18 -> 31, of which waited for: 9 -> 16; matrix products, arithmetic and copies ran while one was open for 1% -> 1% of each run, Pallas kernels for 8% -> 9%
where the time goes in v10:
time: 103 us; the launch traced here: 102 us
  starting transfers between devices  41.6 us (40%)
  waiting for transfers between devices  41 us (40%)
  Pallas kernels  16.5 us (16%)
  matrix products  1.58 us (2%)
    ppermute x14, starting transfers between devices, exchange_halves(): piece = lax.ppermute(piece, 'seq', [(i, i ^ k) for i in range(count)])  22.6 us
    all_to_all x2, waiting for transfers between devices, exchange(): return lax.all_to_all(value, 'seq', split_axis=0, concat_axis=0, tiled=True)  15.4 us
    ppermute x15, waiting for transfers between devices, swap(): return lax.ppermute(value, 'tp', [(i, i ^ bit) for i in range(count)])  13.2 us
    ppermute x14, waiting for transfers between devices, exchange_halves(): piece = lax.ppermute(piece, 'seq', [(i, i ^ k) for i in range(count)])  12.3 us
    all_to_all x2, starting transfers between devices, exchange(): return lax.all_to_all(value, 'seq', split_axis=0, concat_axis=0, tiled=True)  10.8 us
    ppermute x15, starting transfers between devices, swap(): return lax.ppermute(value, 'tp', [(i, i ^ bit) for i in range(count)])  8.12 us
    pallas_call x2, Pallas kernels, run_expert(): pl.pallas_call(expert_kernel, in_specs=[pl.BlockSpec(memory_space=pltpu.S...  7.97 us
    pallas_call x1, Pallas kernels, mixer_tail(): pl.pallas_call(tail_kernel, in_specs=[pl.BlockSpec(memory_space=pltpu.SME...  3.17 us
  transfers between devices with their start and end apart: 31, of which 16 were waited for; matrix products, arithmetic and copies ran while one was open for 1% of the time, Pallas kernels for 9%

profile of v10, /device:TPU:0, one launch (start us, length us, event | category | flops | bytes accessed | tf_op | source)
XLA Modules:
  0.0 102.4 jit_solution(3229742380522897078)
XLA Ops:
  0.0 2.8 %own_state.1 = (bf16[8,144,128]{2,1,0:T(8,128)(2,1)}, f32[16,128]{1,0:T(8,128)S(1)}) custom-call(bf16[128,1024]{1,0:T(8,128)(2,1)} %x.3, f32[16,128]{1,0:T(8,128)} %bitcast.36, f32[16,128]{1,0:T(8,128)} %bitcast.38, bf16[128,128]{1,0:T(8,128)(2,1)} %b.3), custom_call_target="tpu_custom_call" | custom-call | tf_op jit(solution)/shard_map/own_state/pallas_call | solution.py:78
  2.8 7.3 %all-to-all-start = ((bf16[8,144,128]{2,1,0:T(8,128)(2,1)}), bf16[8,144,128]{2,1,0:T(8,128)(2,1)S(1)}, u32[]{:S(2)}, u32[]{:S(2)}) async-start(bf16[8,144,128]{2,1,0:T(8,128)(2,1)} %get-tuple-element.25), calls=%async_computation | async-start | bytes 589824 | tf_op jit(solution)/shard_map/all_to_all | solution.py:20
  10.7 1.7 %within_block.1.direct_in = f32[128,1024]{1,0:T(8,128)S(1)} custom-call(f32[16]{0:T(128)S(1)} %copy-done.1, bf16[128,1024]{1,0:T(8,128)(2,1)} %x.3, f32[16,128]{1,0:T(8,128)} %bitcast.37, f32[16,128]{1,0:T(8,128)S(1)} %get-tuple-element.24.cum_t.cum_in, bf16[128,128]{1,0:T(8,128)(2,1)} %b.3, bf16[128,128]{1,0:T(8,128)(2,1)} %c_in.1), custom_call_target="tpu_custom_call" | custom-call | flops 134217728 | bytes 786432 | tf_op jit(solution)/shard_map/within_block/pallas_call | solution.py:162
  12.4 7.3 %all-to-all-done.got = bf16[8,144,128]{2,1,0:T(8,128)(2,1)S(1)} async-done(((bf16[8,144,128]{2,1,0:T(8,128)(2,1)}), bf16[8,144,128]{2,1,0:T(8,128)(2,1)S(1)}, u32[]{:S(2)}, u32[]{:S(2)}) %all-to-all-start) | async-done | bytes 294944 | tf_op jit(solution)/shard_map/all_to_all | solution.py:20
  20.6 3.6 %all-to-all-start.1 = ((bf16[8,128,128]{2,1,0:T(8,128)(2,1)}), bf16[8,128,128]{2,1,0:T(8,128)(2,1)S(1)}, u32[]{:S(2)}, u32[]{:S(2)}) async-start(bf16[8,128,128]{2,1,0:T(8,128)(2,1)} %prefix.1), calls=%async_computation.1 | async-start | bytes 524288 | tf_op jit(solution)/shard_map/all_to_all | solution.py:20
  24.5 8.2 %all-to-all-done.1 = bf16[8,128,128]{2,1,0:T(8,128)(2,1)S(1)} async-done(((bf16[8,128,128]{2,1,0:T(8,128)(2,1)}), bf16[8,128,128]{2,1,0:T(8,128)(2,1)S(1)}, u32[]{:S(2)}, u32[]{:S(2)}) %all-to-all-start.1) | async-done | bytes 262176 | tf_op jit(solution)/shard_map/all_to_all | solution.py:20
  32.7 3.2 %mixer_tail.1 = (bf16[128,512]{1,0:T(8,128)(2,1)S(1)}, bf16[128,512]{1,0:T(8,128)(2,1)S(1)}, f32[128,512]{1,0:T(8,128)S(1)}, f32[128,512]{1,0:T(8,128)S(1)}) custom-call(s32[1]{0:T(128)} %bitcast.place_ref, bf16[128,128]{1,0:T(8,128)(2,1)} %c_in.1, f32[16,128]{1,0:T(8,128)S(1)} %get-tuple-element.24.cum_t.cum_in, f32[1,1024]{1,0:T(1,128)} %bitcast.39, ...), custom_call_target="tpu_custom_call" | custom-call | flops 536870912 | bytes 6029312 | tf_op jit(solution)/shard_map/mixer_tail/pallas_call | solution.py:244
  37.3 1.6 %collective-permute-start.2 = (bf16[128,512]{1,0:T(8,128)(2,1)S(1)}, bf16[128,512]{1,0:T(8,128)(2,1)S(1)}, u32[]{:S(2)}, u32[]{:S(2)}) collective-permute-start(bf16[128,512]{1,0:T(8,128)(2,1)S(1)} %add_convert_fusion.6), channel_id=1, source_target_pairs={{0,2},{1,3},{2,0},{3,1},{4,6},{5,7},{6,4},{7,5},{8,10},{9,11},{10,... | collective-permute-start | bytes 393224 | tf_op jit(solution)/shard_map/ppermute | solution.py:16
  39.0 3.9 %collective-permute-done.2 = bf16[128,512]{1,0:T(8,128)(2,1)S(1)} collective-permute-done((bf16[128,512]{1,0:T(8,128)(2,1)S(1)}, bf16[128,512]{1,0:T(8,128)(2,1)S(1)}, u32[]{:S(2)}, u32[]{:S(2)}) %collective-permute-start.2) | collective-permute-done | bytes 131104 | tf_op jit(solution)/shard_map/ppermute | solution.py:16
  43.4 1.0 collective-permute-start.5
  44.4 2.0 %collective-permute-start.4 = (bf16[64,512]{1,0:T(8,128)(2,1)S(1)}, bf16[64,512]{1,0:T(8,128)(2,1)S(1)}, u32[]{:S(2)}, u32[]{:S(2)}) collective-permute-start(bf16[64,512]{1,0:T(8,128)(2,1)S(1)} %get-tuple-element.48), channel_id=1, source_target_pairs={{0,8},{4,12},{8,0},{12,4},{16,24},{20,28},{24,16},{28,20},{1,9},{5... | collective-permute-start | bytes 196616 | tf_op jit(solution)/shard_map/ppermute | solution.py:115
  46.9 1.8 %collective-permute-done.5 = bf16[64,512]{1,0:T(8,128)(2,1)S(1)} collective-permute-done((bf16[64,512]{1,0:T(8,128)(2,1)S(1)}, bf16[64,512]{1,0:T(8,128)(2,1)S(1)}, u32[]{:S(2)}, u32[]{:S(2)}) %collective-permute-start.5) | collective-permute-done | bytes 65568 | tf_op jit(solution)/shard_map/ppermute | solution.py:115
  49.3 1.3 %collective-permute-done.3 = bf16[64,512]{1,0:T(8,128)(2,1)S(1)} collective-permute-done((bf16[64,512]{1,0:T(8,128)(2,1)S(1)}, bf16[64,512]{1,0:T(8,128)(2,1)S(1)}, u32[]{:S(2)}, u32[]{:S(2)}) %collective-permute-start.3) | collective-permute-done | bytes 65568 | tf_op jit(solution)/shard_map/ppermute | solution.py:115
  50.7 1.6 %collective-permute-start.7 = (bf16[256,512]{1,0:T(8,128)(2,1)S(1)}, bf16[256,512]{1,0:T(8,128)(2,1)S(1)}, u32[]{:S(2)}, u32[]{:S(2)}) collective-permute-start(bf16[256,512]{1,0:T(8,128)(2,1)S(1)} %pad_maximum_fusion.own_in), channel_id=1, source_target_pairs={{0,2},{1,3},{2,0},{3,1},{4,6},{5,7},{6,4},{7,5},{8,10},{9,11},{10,... | collective-permute-start | bytes 786440 | tf_op jit(solution)/shard_map/ppermute | solution.py:16
  52.3 2.9 %collective-permute-start.16 = (bf16[64,512]{1,0:T(8,128)(2,1)S(1)}, bf16[64,512]{1,0:T(8,128)(2,1)S(1)}, u32[]{:S(2)}, u32[]{:S(2)}) collective-permute-start(bf16[64,512]{1,0:T(8,128)(2,1)S(1)} %get-tuple-element.45), channel_id=1, source_target_pairs={{0,20},{4,16},{8,28},{12,24},{16,4},{20,0},{24,12},{28,8},{1,21},{... | collective-permute-start | bytes 196616 | tf_op jit(solution)/shard_map/ppermute | solution.py:115
  55.2 1.1 %collective-permute-start.17 = (bf16[64,512]{1,0:T(8,128)(2,1)S(1)}, bf16[64,512]{1,0:T(8,128)(2,1)S(1)}, u32[]{:S(2)}, u32[]{:S(2)}) collective-permute-start(bf16[64,512]{1,0:T(8,128)(2,1)S(1)} %get-tuple-element.44), channel_id=1, source_target_pairs={{0,24},{4,28},{8,16},{12,20},{16,8},{20,12},{24,0},{28,4},{1,25},{... | collective-permute-start | bytes 196616 | tf_op jit(solution)/shard_map/ppermute | solution.py:115
  56.3 3.6 %collective-permute-start.18 = (bf16[64,512]{1,0:T(8,128)(2,1)S(1)}, bf16[64,512]{1,0:T(8,128)(2,1)S(1)}, u32[]{:S(2)}, u32[]{:S(2)}) collective-permute-start(bf16[64,512]{1,0:T(8,128)(2,1)S(1)} %get-tuple-element.43), channel_id=1, source_target_pairs={{0,28},{4,24},{8,20},{12,16},{16,12},{20,8},{24,4},{28,0},{1,29},{... | collective-permute-start | bytes 196616 | tf_op jit(solution)/shard_map/ppermute | solution.py:115
  61.1 2.6 %collective-permute-done.16 = bf16[64,512]{1,0:T(8,128)(2,1)S(1)} collective-permute-done((bf16[64,512]{1,0:T(8,128)(2,1)S(1)}, bf16[64,512]{1,0:T(8,128)(2,1)S(1)}, u32[]{:S(2)}, u32[]{:S(2)}) %collective-permute-start.16) | collective-permute-done | bytes 65568 | tf_op jit(solution)/shard_map/ppermute | solution.py:115
  64.4 4.0 %expert.2 = (bf16[256,512]{1,0:T(8,128)(2,1)S(1)}, bf16[256,512]{1,0:T(8,128)(2,1)S(1)}, bf16[256,512]{1,0:T(8,128)(2,1)S(1)}, bf16[256,512]{1,0:T(8,128)(2,1)S(1)}) custom-call(s32[1]{0:T(128)} %bitcast.place_ref, f32[1,2048]{1,0:T(1,128)} %bitcast.34, bf16[256,512]{1,0:T(8,128)(2,1)S(1)} %pad_maximum_fusion.own_in, ...), custom_call_target="tpu_custom_call" | custom-call | flops 1 | bytes 1 | tf_op jit(solution)/shard_map/expert/pallas_call | solution.py:313
  68.9 1.3 %collective-permute-done.20.far_in = bf16[256,512]{1,0:T(8,128)(2,1)S(1)} collective-permute-done((bf16[256,512]{1,0:T(8,128)(2,1)S(1)}, bf16[256,512]{1,0:T(8,128)(2,1)S(1)}, u32[]{:S(2)}, u32[]{:S(2)}) %collective-permute-start.20) | collective-permute-done | bytes 262176 | tf_op jit(solution)/shard_map/ppermute | solution.py:16
  70.3 1.3 %collective-permute-start.10 = (bf16[256,512]{1,0:T(8,128)(2,1)S(1)}, bf16[256,512]{1,0:T(8,128)(2,1)S(1)}, u32[]{:S(2)}, u32[]{:S(2)}) collective-permute-start(bf16[256,512]{1,0:T(8,128)(2,1)S(1)} %add_convert_fusion.3), channel_id=1, source_target_pairs={{0,2},{1,3},{2,0},{3,1},{4,6},{5,7},{6,4},{7,5},{8,10},{9,11},{10,... | collective-permute-start | bytes 786440 | tf_op jit(solution)/shard_map/ppermute | solution.py:16
  71.8 4.0 %expert.3 = (bf16[256,512]{1,0:T(8,128)(2,1)S(1)}, bf16[256,512]{1,0:T(8,128)(2,1)S(1)}, bf16[256,512]{1,0:T(8,128)(2,1)S(1)}, bf16[256,512]{1,0:T(8,128)(2,1)S(1)}) custom-call(s32[1]{0:T(128)} %bitcast.place_ref, f32[1,2048]{1,0:T(1,128)} %bitcast.35, bf16[256,512]{1,0:T(8,128)(2,1)S(1)} %constant_dynamic-update-slice_fusion.own_in, ...), custom_call_target="tpu_custom_call" | custom-call | flops 1 | bytes 1 | tf_op jit(solution)/shard_map/expert/pallas_call | solution.py:313
  76.0 3.1 %collective-permute-done.10 = bf16[256,512]{1,0:T(8,128)(2,1)S(1)} collective-permute-done((bf16[256,512]{1,0:T(8,128)(2,1)S(1)}, bf16[256,512]{1,0:T(8,128)(2,1)S(1)}, u32[]{:S(2)}, u32[]{:S(2)}) %collective-permute-start.10) | collective-permute-done | bytes 262176 | tf_op jit(solution)/shard_map/ppermute | solution.py:16
  80.8 1.3 %collective-permute-start.12 = (bf16[64,512]{1,0:T(8,128)(2,1)S(1)}, bf16[64,512]{1,0:T(8,128)(2,1)S(1)}, u32[]{:S(2)}, u32[]{:S(2)}) collective-permute-start(bf16[64,512]{1,0:T(8,128)(2,1)S(1)} %get-tuple-element.57), channel_id=1, source_target_pairs={{0,4},{4,0},{8,12},{12,8},{16,20},{20,16},{24,28},{28,24},{1,5},{5... | collective-permute-start | bytes 196616 | tf_op jit(solution)/shard_map/ppermute | solution.py:115
  82.1 2.3 %collective-permute-start.13 = (bf16[64,512]{1,0:T(8,128)(2,1)S(1)}, bf16[64,512]{1,0:T(8,128)(2,1)S(1)}, u32[]{:S(2)}, u32[]{:S(2)}) collective-permute-start(bf16[64,512]{1,0:T(8,128)(2,1)S(1)} %get-tuple-element.56), channel_id=1, source_target_pairs={{0,8},{4,12},{8,0},{12,4},{16,24},{20,28},{24,16},{28,20},{1,9},{5... | collective-permute-start | bytes 196616 | tf_op jit(solution)/shard_map/ppermute | solution.py:115
  84.4 3.6 %collective-permute-done.24 = bf16[256,512]{1,0:T(8,128)(2,1)S(1)} collective-permute-done((bf16[256,512]{1,0:T(8,128)(2,1)S(1)}, bf16[256,512]{1,0:T(8,128)(2,1)S(1)}, u32[]{:S(2)}, u32[]{:S(2)}) %collective-permute-start.24) | collective-permute-done | bytes 262176 | tf_op jit(solution)/shard_map/ppermute | solution.py:16
  88.1 2.4 %collective-permute-start.25 = (bf16[64,512]{1,0:T(8,128)(2,1)S(1)}, bf16[64,512]{1,0:T(8,128)(2,1)S(1)}, u32[]{:S(2)}, u32[]{:S(2)}) collective-permute-start(bf16[64,512]{1,0:T(8,128)(2,1)S(1)} %get-tuple-element.54), channel_id=1, source_target_pairs={{0,16},{4,20},{8,24},{12,28},{16,0},{20,4},{24,8},{28,12},{1,17},{... | collective-permute-start | bytes 196616 | tf_op jit(solution)/shard_map/ppermute | solution.py:115
  90.5 1.3 %collective-permute-start.26 = (bf16[64,512]{1,0:T(8,128)(2,1)S(1)}, bf16[64,512]{1,0:T(8,128)(2,1)S(1)}, u32[]{:S(2)}, u32[]{:S(2)}) collective-permute-start(bf16[64,512]{1,0:T(8,128)(2,1)S(1)} %get-tuple-element.53), channel_id=1, source_target_pairs={{0,20},{4,16},{8,28},{12,24},{16,4},{20,0},{24,12},{28,8},{1,21},{... | collective-permute-start | bytes 196616 | tf_op jit(solution)/shard_map/ppermute | solution.py:115
  91.8 2.4 %collective-permute-start.27 = (bf16[64,512]{1,0:T(8,128)(2,1)S(1)}, bf16[64,512]{1,0:T(8,128)(2,1)S(1)}, u32[]{:S(2)}, u32[]{:S(2)}) collective-permute-start(bf16[64,512]{1,0:T(8,128)(2,1)S(1)} %get-tuple-element.52), channel_id=1, source_target_pairs={{0,24},{4,28},{8,16},{12,20},{16,8},{20,12},{24,0},{28,4},{1,25},{... | collective-permute-start | bytes 196616 | tf_op jit(solution)/shard_map/ppermute | solution.py:115
  94.2 1.7 %collective-permute-start.28 = (bf16[64,512]{1,0:T(8,128)(2,1)S(1)}, bf16[64,512]{1,0:T(8,128)(2,1)S(1)}, u32[]{:S(2)}, u32[]{:S(2)}) collective-permute-start(bf16[64,512]{1,0:T(8,128)(2,1)S(1)} %get-tuple-element.51), channel_id=1, source_target_pairs={{0,28},{4,24},{8,20},{12,16},{16,12},{20,8},{24,4},{28,0},{1,29},{... | collective-permute-start | bytes 196616 | tf_op jit(solution)/shard_map/ppermute | solution.py:115
  95.9 4.5 %collective-permute-done.26 = bf16[64,512]{1,0:T(8,128)(2,1)S(1)} collective-permute-done((bf16[64,512]{1,0:T(8,128)(2,1)S(1)}, bf16[64,512]{1,0:T(8,128)(2,1)S(1)}, u32[]{:S(2)}, u32[]{:S(2)}) %collective-permute-start.26) | collective-permute-done | bytes 65568 | tf_op jit(solution)/shard_map/ppermute | solution.py:115
  101.3 1.0 %add_convert_fusion.4 = bf16[128,512]{1,0:T(8,128)(2,1)} fusion(bf16[128,512]{1,0:T(8,128)(2,1)S(1)} %add_convert_fusion.5, f32[128,512]{1,0:T(8,128)S(1)} %select_reduce_fusion, bf16[512,512]{1,0:T(8,128)(2,1)S(1)} %constant_dynamic-update-slice_fusion.4), kind=kOutput, calls=%fused_computation.11 | convolution fusion | flops 402849792 | bytes 1048576 | tf_op jit(solution)/shard_map/dot_general | solution.py:432
  (72 shorter events, 10.6 us)
Async XLA Ops:
  0.0 24.4 %copy-start.2 = (f32[128,2]{0,1:T(2,128)S(1)}, f32[128,2]{0,1:T(2,128)}, u32[]{:S(2)}) copy-start(f32[128,2]{0,1:T(2,128)} %param.30) | copy-start | bytes 3076
  2.8 16.9 %all-to-all-start = ((bf16[8,144,128]{2,1,0:T(8,128)(2,1)}), bf16[8,144,128]{2,1,0:T(8,128)(2,1)S(1)}, u32[]{:S(2)}, u32[]{:S(2)}) async-start(bf16[8,144,128]{2,1,0:T(8,128)(2,1)} %get-tuple-element.25), calls=%async_computation | async-start | bytes 589824 | tf_op jit(solution)/shard_map/all_to_all | solution.py:20
  20.6 12.1 %all-to-all-start.1 = ((bf16[8,128,128]{2,1,0:T(8,128)(2,1)}), bf16[8,128,128]{2,1,0:T(8,128)(2,1)S(1)}, u32[]{:S(2)}, u32[]{:S(2)}) async-start(bf16[8,128,128]{2,1,0:T(8,128)(2,1)} %prefix.1), calls=%async_computation.1 | async-start | bytes 524288 | tf_op jit(solution)/shard_map/all_to_all | solution.py:20
  35.9 1.4 %collective-permute-start.1 = (bf16[128,512]{1,0:T(8,128)(2,1)S(1)}, bf16[128,512]{1,0:T(8,128)(2,1)S(1)}, u32[]{:S(2)}, u32[]{:S(2)}) collective-permute-start(bf16[128,512]{1,0:T(8,128)(2,1)S(1)} %get-tuple-element.30), channel_id=1, source_target_pairs={{0,1},{1,0},{2,3},{3,2},{4,5},{5,4},{6,7},{7,6},{8,9},{9,8},{10,11... | collective-permute-start | bytes 393224 | tf_op jit(solution)/shard_map/ppermute | solution.py:16
  35.9 3.1 %collective-permute-start = (bf16[128,512]{1,0:T(8,128)(2,1)S(1)}, bf16[128,512]{1,0:T(8,128)(2,1)S(1)}, u32[]{:S(2)}, u32[]{:S(2)}) collective-permute-start(bf16[128,512]{1,0:T(8,128)(2,1)S(1)} %get-tuple-element.28), channel_id=1, source_target_pairs={{0,1},{1,0},{2,3},{3,2},{4,5},{5,4},{6,7},{7,6},{8,9},{9,8},{10,11... | collective-permute-start | bytes 393224 | tf_op jit(solution)/shard_map/ppermute | solution.py:16
  37.3 5.6 %collective-permute-start.2 = (bf16[128,512]{1,0:T(8,128)(2,1)S(1)}, bf16[128,512]{1,0:T(8,128)(2,1)S(1)}, u32[]{:S(2)}, u32[]{:S(2)}) collective-permute-start(bf16[128,512]{1,0:T(8,128)(2,1)S(1)} %add_convert_fusion.6), channel_id=1, source_target_pairs={{0,2},{1,3},{2,0},{3,1},{4,6},{5,7},{6,4},{7,5},{8,10},{9,11},{10,... | collective-permute-start | bytes 393224 | tf_op jit(solution)/shard_map/ppermute | solution.py:16
  43.4 5.3 %collective-permute-start.5 = (bf16[64,512]{1,0:T(8,128)(2,1)S(1)}, bf16[64,512]{1,0:T(8,128)(2,1)S(1)}, u32[]{:S(2)}, u32[]{:S(2)}) collective-permute-start(bf16[64,512]{1,0:T(8,128)(2,1)S(1)} %get-tuple-element.47), channel_id=1, source_target_pairs={{0,12},{4,8},{8,4},{12,0},{16,28},{20,24},{24,20},{28,16},{1,13},{... | collective-permute-start | bytes 196616 | tf_op jit(solution)/shard_map/ppermute | solution.py:115
  44.4 5.0 %collective-permute-start.4 = (bf16[64,512]{1,0:T(8,128)(2,1)S(1)}, bf16[64,512]{1,0:T(8,128)(2,1)S(1)}, u32[]{:S(2)}, u32[]{:S(2)}) collective-permute-start(bf16[64,512]{1,0:T(8,128)(2,1)S(1)} %get-tuple-element.48), channel_id=1, source_target_pairs={{0,8},{4,12},{8,0},{12,4},{16,24},{20,28},{24,16},{28,20},{1,9},{5... | collective-permute-start | bytes 196616 | tf_op jit(solution)/shard_map/ppermute | solution.py:115
  46.4 4.3 %collective-permute-start.3 = (bf16[64,512]{1,0:T(8,128)(2,1)S(1)}, bf16[64,512]{1,0:T(8,128)(2,1)S(1)}, u32[]{:S(2)}, u32[]{:S(2)}) collective-permute-start(bf16[64,512]{1,0:T(8,128)(2,1)S(1)} %get-tuple-element.49), channel_id=1, source_target_pairs={{0,4},{4,0},{8,12},{12,8},{16,20},{20,16},{24,28},{28,24},{1,5},{5... | collective-permute-start | bytes 196616 | tf_op jit(solution)/shard_map/ppermute | solution.py:115
  50.7 9.9 %collective-permute-start.7 = (bf16[256,512]{1,0:T(8,128)(2,1)S(1)}, bf16[256,512]{1,0:T(8,128)(2,1)S(1)}, u32[]{:S(2)}, u32[]{:S(2)}) collective-permute-start(bf16[256,512]{1,0:T(8,128)(2,1)S(1)} %pad_maximum_fusion.own_in), channel_id=1, source_target_pairs={{0,2},{1,3},{2,0},{3,1},{4,6},{5,7},{6,4},{7,5},{8,10},{9,11},{10,... | collective-permute-start | bytes 786440 | tf_op jit(solution)/shard_map/ppermute | solution.py:16
  52.2 8.3 %collective-permute-start.15 = (bf16[64,512]{1,0:T(8,128)(2,1)S(1)}, bf16[64,512]{1,0:T(8,128)(2,1)S(1)}, u32[]{:S(2)}, u32[]{:S(2)}) collective-permute-start(bf16[64,512]{1,0:T(8,128)(2,1)S(1)} %get-tuple-element.46), channel_id=1, source_target_pairs={{0,16},{4,20},{8,24},{12,28},{16,0},{20,4},{24,8},{28,12},{1,17},{... | collective-permute-start | bytes 196616 | tf_op jit(solution)/shard_map/ppermute | solution.py:115
  52.3 11.5 %collective-permute-start.16 = (bf16[64,512]{1,0:T(8,128)(2,1)S(1)}, bf16[64,512]{1,0:T(8,128)(2,1)S(1)}, u32[]{:S(2)}, u32[]{:S(2)}) collective-permute-start(bf16[64,512]{1,0:T(8,128)(2,1)S(1)} %get-tuple-element.45), channel_id=1, source_target_pairs={{0,20},{4,16},{8,28},{12,24},{16,4},{20,0},{24,12},{28,8},{1,21},{... | collective-permute-start | bytes 196616 | tf_op jit(solution)/shard_map/ppermute | solution.py:115
  55.2 8.6 %collective-permute-start.17 = (bf16[64,512]{1,0:T(8,128)(2,1)S(1)}, bf16[64,512]{1,0:T(8,128)(2,1)S(1)}, u32[]{:S(2)}, u32[]{:S(2)}) collective-permute-start(bf16[64,512]{1,0:T(8,128)(2,1)S(1)} %get-tuple-element.44), channel_id=1, source_target_pairs={{0,24},{4,28},{8,16},{12,20},{16,8},{20,12},{24,0},{28,4},{1,25},{... | collective-permute-start | bytes 196616 | tf_op jit(solution)/shard_map/ppermute | solution.py:115
  56.3 7.5 %collective-permute-start.18 = (bf16[64,512]{1,0:T(8,128)(2,1)S(1)}, bf16[64,512]{1,0:T(8,128)(2,1)S(1)}, u32[]{:S(2)}, u32[]{:S(2)}) collective-permute-start(bf16[64,512]{1,0:T(8,128)(2,1)S(1)} %get-tuple-element.43), channel_id=1, source_target_pairs={{0,28},{4,24},{8,20},{12,16},{16,12},{20,8},{24,4},{28,0},{1,29},{... | collective-permute-start | bytes 196616 | tf_op jit(solution)/shard_map/ppermute | solution.py:115
  60.5 3.8 %collective-permute-start.6 = (bf16[256,512]{1,0:T(8,128)(2,1)S(1)}, bf16[256,512]{1,0:T(8,128)(2,1)S(1)}, u32[]{:S(2)}, u32[]{:S(2)}) collective-permute-start(bf16[256,512]{1,0:T(8,128)(2,1)S(1)} %pad_maximum_fusion.own_in), channel_id=1, source_target_pairs={{0,1},{1,0},{2,3},{3,2},{4,5},{5,4},{6,7},{7,6},{8,9},{9,8},{10,11... | collective-permute-start | bytes 786440 | tf_op jit(solution)/shard_map/ppermute | solution.py:16
  60.6 3.8 %collective-permute-start.8 = (bf16[256,512]{1,0:T(8,128)(2,1)S(1)}, bf16[256,512]{1,0:T(8,128)(2,1)S(1)}, u32[]{:S(2)}, u32[]{:S(2)}) collective-permute-start(bf16[256,512]{1,0:T(8,128)(2,1)S(1)} %collective-permute-done.7.far_in), channel_id=1, source_target_pairs={{0,1},{1,0},{2,3},{3,2},{4,5},{5,4},{6,7},{7,6},{8,9},{9,8},{10,11... | collective-permute-start | bytes 786440 | tf_op jit(solution)/shard_map/ppermute | solution.py:16
  63.8 6.4 %collective-permute-start.20 = (bf16[256,512]{1,0:T(8,128)(2,1)S(1)}, bf16[256,512]{1,0:T(8,128)(2,1)S(1)}, u32[]{:S(2)}, u32[]{:S(2)}) collective-permute-start(bf16[256,512]{1,0:T(8,128)(2,1)S(1)} %constant_dynamic-update-slice_fusion.own_in), channel_id=1, source_target_pairs={{0,2},{1,3},{2,0},{3,1},{4,6},{5,7},{6,4},{7,5},{8,10},{9,11},{10,... | collective-permute-start | bytes 786440 | tf_op jit(solution)/shard_map/ppermute | solution.py:16
  68.4 1.9 %collective-permute-start.9 = (bf16[256,512]{1,0:T(8,128)(2,1)S(1)}, bf16[256,512]{1,0:T(8,128)(2,1)S(1)}, u32[]{:S(2)}, u32[]{:S(2)}) collective-permute-start(bf16[256,512]{1,0:T(8,128)(2,1)S(1)} %get-tuple-element.34), channel_id=1, source_target_pairs={{0,1},{1,0},{2,3},{3,2},{4,5},{5,4},{6,7},{7,6},{8,9},{9,8},{10,11... | collective-permute-start | bytes 786440 | tf_op jit(solution)/shard_map/ppermute | solution.py:16
  68.5 3.2 %collective-permute-start.19 = (bf16[256,512]{1,0:T(8,128)(2,1)S(1)}, bf16[256,512]{1,0:T(8,128)(2,1)S(1)}, u32[]{:S(2)}, u32[]{:S(2)}) collective-permute-start(bf16[256,512]{1,0:T(8,128)(2,1)S(1)} %constant_dynamic-update-slice_fusion.own_in), channel_id=1, source_target_pairs={{0,1},{1,0},{2,3},{3,2},{4,5},{5,4},{6,7},{7,6},{8,9},{9,8},{10,11... | collective-permute-start | bytes 786440 | tf_op jit(solution)/shard_map/ppermute | solution.py:16
  70.2 1.5 %collective-permute-start.21 = (bf16[256,512]{1,0:T(8,128)(2,1)S(1)}, bf16[256,512]{1,0:T(8,128)(2,1)S(1)}, u32[]{:S(2)}, u32[]{:S(2)}) collective-permute-start(bf16[256,512]{1,0:T(8,128)(2,1)S(1)} %collective-permute-done.20.far_in), channel_id=1, source_target_pairs={{0,1},{1,0},{2,3},{3,2},{4,5},{5,4},{6,7},{7,6},{8,9},{9,8},{10,11... | collective-permute-start | bytes 786440 | tf_op jit(solution)/shard_map/ppermute | solution.py:16
  70.3 8.8 %collective-permute-start.10 = (bf16[256,512]{1,0:T(8,128)(2,1)S(1)}, bf16[256,512]{1,0:T(8,128)(2,1)S(1)}, u32[]{:S(2)}, u32[]{:S(2)}) collective-permute-start(bf16[256,512]{1,0:T(8,128)(2,1)S(1)} %add_convert_fusion.3), channel_id=1, source_target_pairs={{0,2},{1,3},{2,0},{3,1},{4,6},{5,7},{6,4},{7,5},{8,10},{9,11},{10,... | collective-permute-start | bytes 786440 | tf_op jit(solution)/shard_map/ppermute | solution.py:16
  75.8 3.3 %collective-permute-start.22 = (bf16[256,512]{1,0:T(8,128)(2,1)S(1)}, bf16[256,512]{1,0:T(8,128)(2,1)S(1)}, u32[]{:S(2)}, u32[]{:S(2)}) collective-permute-start(bf16[256,512]{1,0:T(8,128)(2,1)S(1)} %get-tuple-element.41), channel_id=1, source_target_pairs={{0,1},{1,0},{2,3},{3,2},{4,5},{5,4},{6,7},{7,6},{8,9},{9,8},{10,11... | collective-permute-start | bytes 786440 | tf_op jit(solution)/shard_map/ppermute | solution.py:16
  79.1 1.5 %collective-permute-start.11 = (bf16[256,512]{1,0:T(8,128)(2,1)S(1)}, bf16[256,512]{1,0:T(8,128)(2,1)S(1)}, u32[]{:S(2)}, u32[]{:S(2)}) collective-permute-start(bf16[256,512]{1,0:T(8,128)(2,1)S(1)} %get-tuple-element.35), channel_id=1, source_target_pairs={{0,1},{1,0},{2,3},{3,2},{4,5},{5,4},{6,7},{7,6},{8,9},{9,8},{10,11... | collective-permute-start | bytes 786440 | tf_op jit(solution)/shard_map/ppermute | solution.py:16
  79.2 8.8 %collective-permute-start.24 = (bf16[256,512]{1,0:T(8,128)(2,1)S(1)}, bf16[256,512]{1,0:T(8,128)(2,1)S(1)}, u32[]{:S(2)}, u32[]{:S(2)}) collective-permute-start(bf16[256,512]{1,0:T(8,128)(2,1)S(1)} %add_convert_fusion.1), channel_id=1, source_target_pairs={{0,2},{1,3},{2,0},{3,1},{4,6},{5,7},{6,4},{7,5},{8,10},{9,11},{10,... | collective-permute-start | bytes 786440 | tf_op jit(solution)/shard_map/ppermute | solution.py:16
  80.1 7.8 %collective-permute-start.23 = (bf16[256,512]{1,0:T(8,128)(2,1)S(1)}, bf16[256,512]{1,0:T(8,128)(2,1)S(1)}, u32[]{:S(2)}, u32[]{:S(2)}) collective-permute-start(bf16[256,512]{1,0:T(8,128)(2,1)S(1)} %get-tuple-element.42), channel_id=1, source_target_pairs={{0,1},{1,0},{2,3},{3,2},{4,5},{5,4},{6,7},{7,6},{8,9},{9,8},{10,11... | collective-permute-start | bytes 786440 | tf_op jit(solution)/shard_map/ppermute | solution.py:16
  80.8 11.0 %collective-permute-start.12 = (bf16[64,512]{1,0:T(8,128)(2,1)S(1)}, bf16[64,512]{1,0:T(8,128)(2,1)S(1)}, u32[]{:S(2)}, u32[]{:S(2)}) collective-permute-start(bf16[64,512]{1,0:T(8,128)(2,1)S(1)} %get-tuple-element.57), channel_id=1, source_target_pairs={{0,4},{4,0},{8,12},{12,8},{16,20},{20,16},{24,28},{28,24},{1,5},{5... | collective-permute-start | bytes 196616 | tf_op jit(solution)/shard_map/ppermute | solution.py:115
  82.1 12.1 %collective-permute-start.13 = (bf16[64,512]{1,0:T(8,128)(2,1)S(1)}, bf16[64,512]{1,0:T(8,128)(2,1)S(1)}, u32[]{:S(2)}, u32[]{:S(2)}) collective-permute-start(bf16[64,512]{1,0:T(8,128)(2,1)S(1)} %get-tuple-element.56), channel_id=1, source_target_pairs={{0,8},{4,12},{8,0},{12,4},{16,24},{20,28},{24,16},{28,20},{1,9},{5... | collective-permute-start | bytes 196616 | tf_op jit(solution)/shard_map/ppermute | solution.py:115
  84.4 11.5 %collective-permute-start.14 = (bf16[64,512]{1,0:T(8,128)(2,1)S(1)}, bf16[64,512]{1,0:T(8,128)(2,1)S(1)}, u32[]{:S(2)}, u32[]{:S(2)}) collective-permute-start(bf16[64,512]{1,0:T(8,128)(2,1)S(1)} %get-tuple-element.55), channel_id=1, source_target_pairs={{0,12},{4,8},{8,4},{12,0},{16,28},{20,24},{24,20},{28,16},{1,13},{... | collective-permute-start | bytes 196616 | tf_op jit(solution)/shard_map/ppermute | solution.py:115
  88.1 7.8 %collective-permute-start.25 = (bf16[64,512]{1,0:T(8,128)(2,1)S(1)}, bf16[64,512]{1,0:T(8,128)(2,1)S(1)}, u32[]{:S(2)}, u32[]{:S(2)}) collective-permute-start(bf16[64,512]{1,0:T(8,128)(2,1)S(1)} %get-tuple-element.54), channel_id=1, source_target_pairs={{0,16},{4,20},{8,24},{12,28},{16,0},{20,4},{24,8},{28,12},{1,17},{... | collective-permute-start | bytes 196616 | tf_op jit(solution)/shard_map/ppermute | solution.py:115
  90.5 10.0 %collective-permute-start.26 = (bf16[64,512]{1,0:T(8,128)(2,1)S(1)}, bf16[64,512]{1,0:T(8,128)(2,1)S(1)}, u32[]{:S(2)}, u32[]{:S(2)}) collective-permute-start(bf16[64,512]{1,0:T(8,128)(2,1)S(1)} %get-tuple-element.53), channel_id=1, source_target_pairs={{0,20},{4,16},{8,28},{12,24},{16,4},{20,0},{24,12},{28,8},{1,21},{... | collective-permute-start | bytes 196616 | tf_op jit(solution)/shard_map/ppermute | solution.py:115
  91.8 8.7 %collective-permute-start.27 = (bf16[64,512]{1,0:T(8,128)(2,1)S(1)}, bf16[64,512]{1,0:T(8,128)(2,1)S(1)}, u32[]{:S(2)}, u32[]{:S(2)}) collective-permute-start(bf16[64,512]{1,0:T(8,128)(2,1)S(1)} %get-tuple-element.52), channel_id=1, source_target_pairs={{0,24},{4,28},{8,16},{12,20},{16,8},{20,12},{24,0},{28,4},{1,25},{... | collective-permute-start | bytes 196616 | tf_op jit(solution)/shard_map/ppermute | solution.py:115
  94.2 7.1 %collective-permute-start.28 = (bf16[64,512]{1,0:T(8,128)(2,1)S(1)}, bf16[64,512]{1,0:T(8,128)(2,1)S(1)}, u32[]{:S(2)}, u32[]{:S(2)}) collective-permute-start(bf16[64,512]{1,0:T(8,128)(2,1)S(1)} %get-tuple-element.51), channel_id=1, source_target_pairs={{0,28},{4,24},{8,20},{12,16},{16,12},{20,8},{24,4},{28,0},{1,29},{... | collective-permute-start | bytes 196616 | tf_op jit(solution)/shard_map/ppermute | solution.py:115
  (3 other events, 37.2 us)

commit v11 on v10

--- a/solution.py
+++ b/solution.py
@@ -104,15 +104,17 @@
             carries[h] = factor * carries[h] + got[turn, spot, :].astype(F32)
 
 
+HALVES = ((0, 1, 4, 5), (2, 3, 6, 7))
+
+
 def exchange_halves(pieces):
-    count = lax.axis_size("seq")
     halves = []
-    for turn in range(2):
+    for order, part in zip(HALVES, pieces):
         got = []
-        for k in range(turn * count // 2, (turn + 1) * count // 2):
-            piece = pieces[turn][k - turn * count // 2]
+        for spot, k in enumerate(order):
+            piece = part[spot]
             if k > 0:
-                piece = lax.ppermute(piece, "seq", [(i, i ^ k) for i in range(count)])
+                piece = lax.ppermute(piece, "seq", [(i, i ^ k) for i in range(8)])
             got.append(piece)
         halves.append(jnp.concatenate(got))
     return halves
@@ -367,8 +369,11 @@
     before = jnp.arange(items)[:, None] > jnp.arange(items)[None, :]
     earlier = jnp.dot(before.astype(BF), onehot.astype(BF), preferred_element_type=F32)
     rank = jnp.sum(jnp.where(onehot, earlier, 0.0), axis=1).astype(jnp.int32)
-    few = seq_count <= 8
-    layout = flat_expert ^ lax.axis_index("seq") if few else flat_expert
+    few = seq_count == 8
+    layout = flat_expert
+    if few:
+        layout = flat_expert ^ lax.axis_index("seq")
+        layout = (layout & 1) | ((layout & 2) << 1) | ((layout & 4) >> 1)
     placed = layout * slot_count + rank
     spots = placed[:, None] == jnp.arange(slots, dtype=jnp.int32)[None, :]
     spots = spots.reshape(top_count, tok_rows, slots)

time: 103 us -> 102 us (level)
  transfers between devices with their start and end apart: 31 -> 31, of which waited for: 16 -> 15; matrix products, arithmetic and copies ran while one was open for 1% -> 1% of each run, Pallas kernels for 9% -> 9%
where the time goes in v11:
time: 102 us
  starting transfers between devices  41.4 us (41%)
  waiting for transfers between devices  40.7 us (40%)
  Pallas kernels  16.5 us (16%)
  matrix products  1.58 us (2%)
    ppermute x14, starting transfers between devices, exchange_halves(): piece = lax.ppermute(piece, 'seq', [(i, i ^ k) for i in range(8)])  22.5 us
    all_to_all x2, waiting for transfers between devices, exchange(): return lax.all_to_all(value, 'seq', split_axis=0, concat_axis=0, tiled=True)  15.4 us
    ppermute x14, waiting for transfers between devices, exchange_halves(): piece = lax.ppermute(piece, 'seq', [(i, i ^ k) for i in range(8)])  12.9 us
    ppermute x15, waiting for transfers between devices, swap(): return lax.ppermute(value, 'tp', [(i, i ^ bit) for i in range(count)])  12.4 us
    all_to_all x2, starting transfers between devices, exchange(): return lax.all_to_all(value, 'seq', split_axis=0, concat_axis=0, tiled=True)  10.8 us
    ppermute x15, starting transfers between devices, swap(): return lax.ppermute(value, 'tp', [(i, i ^ bit) for i in range(count)])  8.06 us
    pallas_call x2, Pallas kernels, run_expert(): pl.pallas_call(expert_kernel, in_specs=[pl.BlockSpec(memory_space=pltpu.S...  7.96 us
    pallas_call x1, Pallas kernels, mixer_tail(): pl.pallas_call(tail_kernel, in_specs=[pl.BlockSpec(memory_space=pltpu.SME...  3.17 us
  transfers between devices with their start and end apart: 31, of which 15 were waited for; matrix products, arithmetic and copies ran while one was open for 1% of the time, Pallas kernels for 9%

profile of v11, /device:TPU:0, one launch (start us, length us, event | category | flops | bytes accessed | tf_op | source)
XLA Modules:
  0.0 102.0 jit_solution(12727270869772769199)
XLA Ops:
  0.0 2.8 %own_state.1 = (bf16[8,144,128]{2,1,0:T(8,128)(2,1)}, f32[16,128]{1,0:T(8,128)S(1)}) custom-call(bf16[128,1024]{1,0:T(8,128)(2,1)} %x.3, f32[16,128]{1,0:T(8,128)} %bitcast.34, f32[16,128]{1,0:T(8,128)} %bitcast.36, bf16[128,128]{1,0:T(8,128)(2,1)} %b.3), custom_call_target="tpu_custom_call" | custom-call | tf_op jit(solution)/shard_map/own_state/pallas_call | solution.py:78
  2.8 7.3 %all-to-all-start = ((bf16[8,144,128]{2,1,0:T(8,128)(2,1)}), bf16[8,144,128]{2,1,0:T(8,128)(2,1)S(1)}, u32[]{:S(2)}, u32[]{:S(2)}) async-start(bf16[8,144,128]{2,1,0:T(8,128)(2,1)} %get-tuple-element.25), calls=%async_computation | async-start | bytes 589824 | tf_op jit(solution)/shard_map/all_to_all | solution.py:20
  10.7 1.7 %within_block.1.direct_in = f32[128,1024]{1,0:T(8,128)S(1)} custom-call(f32[16]{0:T(128)S(1)} %copy-done.1, bf16[128,1024]{1,0:T(8,128)(2,1)} %x.3, f32[16,128]{1,0:T(8,128)} %bitcast.35, f32[16,128]{1,0:T(8,128)S(1)} %get-tuple-element.24.cum_t.cum_in, bf16[128,128]{1,0:T(8,128)(2,1)} %b.3, bf16[128,128]{1,0:T(8,128)(2,1)} %c_in.1), custom_call_target="tpu_custom_call" | custom-call | flops 134217728 | bytes 786432 | tf_op jit(solution)/shard_map/within_block/pallas_call | solution.py:164
  12.4 7.3 %all-to-all-done.got = bf16[8,144,128]{2,1,0:T(8,128)(2,1)S(1)} async-done(((bf16[8,144,128]{2,1,0:T(8,128)(2,1)}), bf16[8,144,128]{2,1,0:T(8,128)(2,1)S(1)}, u32[]{:S(2)}, u32[]{:S(2)}) %all-to-all-start) | async-done | bytes 294944 | tf_op jit(solution)/shard_map/all_to_all | solution.py:20
  19.7 0.9 prefix.1
  20.6 3.6 %all-to-all-start.1 = ((bf16[8,128,128]{2,1,0:T(8,128)(2,1)}), bf16[8,128,128]{2,1,0:T(8,128)(2,1)S(1)}, u32[]{:S(2)}, u32[]{:S(2)}) async-start(bf16[8,128,128]{2,1,0:T(8,128)(2,1)} %prefix.1), calls=%async_computation.1 | async-start | bytes 524288 | tf_op jit(solution)/shard_map/all_to_all | solution.py:20
  24.5 8.2 %all-to-all-done.1 = bf16[8,128,128]{2,1,0:T(8,128)(2,1)S(1)} async-done(((bf16[8,128,128]{2,1,0:T(8,128)(2,1)}), bf16[8,128,128]{2,1,0:T(8,128)(2,1)S(1)}, u32[]{:S(2)}, u32[]{:S(2)}) %all-to-all-start.1) | async-done | bytes 262176 | tf_op jit(solution)/shard_map/all_to_all | solution.py:20
  32.7 3.2 %mixer_tail.1 = (bf16[128,512]{1,0:T(8,128)(2,1)S(1)}, bf16[128,512]{1,0:T(8,128)(2,1)S(1)}, f32[128,512]{1,0:T(8,128)S(1)}, f32[128,512]{1,0:T(8,128)S(1)}) custom-call(s32[1]{0:T(128)} %bitcast.place_ref, bf16[128,128]{1,0:T(8,128)(2,1)} %c_in.1, f32[16,128]{1,0:T(8,128)S(1)} %get-tuple-element.24.cum_t.cum_in, f32[1,1024]{1,0:T(1,128)} %bitcast.37, ...), custom_call_target="tpu_custom_call" | custom-call | flops 536870912 | bytes 6029312 | tf_op jit(solution)/shard_map/mixer_tail/pallas_call | solution.py:246
  37.3 1.6 %collective-permute-start.2 = (bf16[128,512]{1,0:T(8,128)(2,1)S(1)}, bf16[128,512]{1,0:T(8,128)(2,1)S(1)}, u32[]{:S(2)}, u32[]{:S(2)}) collective-permute-start(bf16[128,512]{1,0:T(8,128)(2,1)S(1)} %add_convert_fusion.6), channel_id=1, source_target_pairs={{0,2},{1,3},{2,0},{3,1},{4,6},{5,7},{6,4},{7,5},{8,10},{9,11},{10,... | collective-permute-start | bytes 393224 | tf_op jit(solution)/shard_map/ppermute | solution.py:16
  39.0 3.9 %collective-permute-done.2 = bf16[128,512]{1,0:T(8,128)(2,1)S(1)} collective-permute-done((bf16[128,512]{1,0:T(8,128)(2,1)S(1)}, bf16[128,512]{1,0:T(8,128)(2,1)S(1)}, u32[]{:S(2)}, u32[]{:S(2)}) %collective-permute-start.2) | collective-permute-done | bytes 131104 | tf_op jit(solution)/shard_map/ppermute | solution.py:16
  44.2 3.1 %collective-permute-start.4 = (bf16[64,512]{1,0:T(8,128)(2,1)S(1)}, bf16[64,512]{1,0:T(8,128)(2,1)S(1)}, u32[]{:S(2)}, u32[]{:S(2)}) collective-permute-start(bf16[64,512]{1,0:T(8,128)(2,1)S(1)} %get-tuple-element.48), channel_id=1, source_target_pairs={{0,16},{4,20},{8,24},{12,28},{16,0},{20,4},{24,8},{28,12},{1,17},{... | collective-permute-start | bytes 196616 | tf_op jit(solution)/shard_map/ppermute | solution.py:117
  47.8 4.2 %collective-permute-done.5 = bf16[64,512]{1,0:T(8,128)(2,1)S(1)} collective-permute-done((bf16[64,512]{1,0:T(8,128)(2,1)S(1)}, bf16[64,512]{1,0:T(8,128)(2,1)S(1)}, u32[]{:S(2)}, u32[]{:S(2)}) %collective-permute-start.5) | collective-permute-done | bytes 65568 | tf_op jit(solution)/shard_map/ppermute | solution.py:117
  52.3 1.6 %collective-permute-start.7 = (bf16[256,512]{1,0:T(8,128)(2,1)S(1)}, bf16[256,512]{1,0:T(8,128)(2,1)S(1)}, u32[]{:S(2)}, u32[]{:S(2)}) collective-permute-start(bf16[256,512]{1,0:T(8,128)(2,1)S(1)} %pad_maximum_fusion.own_in), channel_id=1, source_target_pairs={{0,2},{1,3},{2,0},{3,1},{4,6},{5,7},{6,4},{7,5},{8,10},{9,11},{10,... | collective-permute-start | bytes 786440 | tf_op jit(solution)/shard_map/ppermute | solution.py:16
  53.8 2.6 %collective-permute-start.16 = (bf16[64,512]{1,0:T(8,128)(2,1)S(1)}, bf16[64,512]{1,0:T(8,128)(2,1)S(1)}, u32[]{:S(2)}, u32[]{:S(2)}) collective-permute-start(bf16[64,512]{1,0:T(8,128)(2,1)S(1)} %get-tuple-element.45), channel_id=1, source_target_pairs={{0,12},{4,8},{8,4},{12,0},{16,28},{20,24},{24,20},{28,16},{1,13},{... | collective-permute-start | bytes 196616 | tf_op jit(solution)/shard_map/ppermute | solution.py:117
  56.4 1.4 %collective-permute-start.17 = (bf16[64,512]{1,0:T(8,128)(2,1)S(1)}, bf16[64,512]{1,0:T(8,128)(2,1)S(1)}, u32[]{:S(2)}, u32[]{:S(2)}) collective-permute-start(bf16[64,512]{1,0:T(8,128)(2,1)S(1)} %get-tuple-element.44), channel_id=1, source_target_pairs={{0,24},{4,28},{8,16},{12,20},{16,8},{20,12},{24,0},{28,4},{1,25},{... | collective-permute-start | bytes 196616 | tf_op jit(solution)/shard_map/ppermute | solution.py:117
  57.8 2.8 %collective-permute-start.18 = (bf16[64,512]{1,0:T(8,128)(2,1)S(1)}, bf16[64,512]{1,0:T(8,128)(2,1)S(1)}, u32[]{:S(2)}, u32[]{:S(2)}) collective-permute-start(bf16[64,512]{1,0:T(8,128)(2,1)S(1)} %get-tuple-element.43), channel_id=1, source_target_pairs={{0,28},{4,24},{8,20},{12,16},{16,12},{20,8},{24,4},{28,0},{1,29},{... | collective-permute-start | bytes 196616 | tf_op jit(solution)/shard_map/ppermute | solution.py:117
  61.2 1.3 %collective-permute-done.17 = bf16[64,512]{1,0:T(8,128)(2,1)S(1)} collective-permute-done((bf16[64,512]{1,0:T(8,128)(2,1)S(1)}, bf16[64,512]{1,0:T(8,128)(2,1)S(1)}, u32[]{:S(2)}, u32[]{:S(2)}) %collective-permute-start.17) | collective-permute-done | bytes 65568 | tf_op jit(solution)/shard_map/ppermute | solution.py:117
  62.5 2.3 %collective-permute-done.18 = bf16[64,512]{1,0:T(8,128)(2,1)S(1)} collective-permute-done((bf16[64,512]{1,0:T(8,128)(2,1)S(1)}, bf16[64,512]{1,0:T(8,128)(2,1)S(1)}, u32[]{:S(2)}, u32[]{:S(2)}) %collective-permute-start.18) | collective-permute-done | bytes 65568 | tf_op jit(solution)/shard_map/ppermute | solution.py:117
  65.3 4.0 %expert.2 = (bf16[256,512]{1,0:T(8,128)(2,1)S(1)}, bf16[256,512]{1,0:T(8,128)(2,1)S(1)}, bf16[256,512]{1,0:T(8,128)(2,1)S(1)}, bf16[256,512]{1,0:T(8,128)(2,1)S(1)}) custom-call(s32[1]{0:T(128)} %bitcast.place_ref, f32[1,2048]{1,0:T(1,128)} %bitcast.32, bf16[256,512]{1,0:T(8,128)(2,1)S(1)} %pad_maximum_fusion.own_in, ...), custom_call_target="tpu_custom_call" | custom-call | flops 1 | bytes 1 | tf_op jit(solution)/shard_map/expert/pallas_call | solution.py:315
  69.8 1.3 %collective-permute-done.20.far_in = bf16[256,512]{1,0:T(8,128)(2,1)S(1)} collective-permute-done((bf16[256,512]{1,0:T(8,128)(2,1)S(1)}, bf16[256,512]{1,0:T(8,128)(2,1)S(1)}, u32[]{:S(2)}, u32[]{:S(2)}) %collective-permute-start.20) | collective-permute-done | bytes 262176 | tf_op jit(solution)/shard_map/ppermute | solution.py:16
  71.2 1.3 %collective-permute-start.10 = (bf16[256,512]{1,0:T(8,128)(2,1)S(1)}, bf16[256,512]{1,0:T(8,128)(2,1)S(1)}, u32[]{:S(2)}, u32[]{:S(2)}) collective-permute-start(bf16[256,512]{1,0:T(8,128)(2,1)S(1)} %add_convert_fusion.3), channel_id=1, source_target_pairs={{0,2},{1,3},{2,0},{3,1},{4,6},{5,7},{6,4},{7,5},{8,10},{9,11},{10,... | collective-permute-start | bytes 786440 | tf_op jit(solution)/shard_map/ppermute | solution.py:16
  72.7 4.0 %expert.3 = (bf16[256,512]{1,0:T(8,128)(2,1)S(1)}, bf16[256,512]{1,0:T(8,128)(2,1)S(1)}, bf16[256,512]{1,0:T(8,128)(2,1)S(1)}, bf16[256,512]{1,0:T(8,128)(2,1)S(1)}) custom-call(s32[1]{0:T(128)} %bitcast.place_ref, f32[1,2048]{1,0:T(1,128)} %bitcast.33, bf16[256,512]{1,0:T(8,128)(2,1)S(1)} %constant_dynamic-update-slice_fusion.own_in, ...), custom_call_target="tpu_custom_call" | custom-call | flops 1 | bytes 1 | tf_op jit(solution)/shard_map/expert/pallas_call | solution.py:315
  76.9 3.1 %collective-permute-done.10 = bf16[256,512]{1,0:T(8,128)(2,1)S(1)} collective-permute-done((bf16[256,512]{1,0:T(8,128)(2,1)S(1)}, bf16[256,512]{1,0:T(8,128)(2,1)S(1)}, u32[]{:S(2)}, u32[]{:S(2)}) %collective-permute-start.10) | collective-permute-done | bytes 262176 | tf_op jit(solution)/shard_map/ppermute | solution.py:16
  80.1 0.9 collective-permute-start.24
  82.5 3.6 %collective-permute-start.14 = (bf16[64,512]{1,0:T(8,128)(2,1)S(1)}, bf16[64,512]{1,0:T(8,128)(2,1)S(1)}, u32[]{:S(2)}, u32[]{:S(2)}) collective-permute-start(bf16[64,512]{1,0:T(8,128)(2,1)S(1)} %get-tuple-element.55), channel_id=1, source_target_pairs={{0,20},{4,16},{8,28},{12,24},{16,4},{20,0},{24,12},{28,8},{1,21},{... | collective-permute-start | bytes 196616 | tf_op jit(solution)/shard_map/ppermute | solution.py:117
  86.1 2.7 %collective-permute-done.24 = bf16[256,512]{1,0:T(8,128)(2,1)S(1)} collective-permute-done((bf16[256,512]{1,0:T(8,128)(2,1)S(1)}, bf16[256,512]{1,0:T(8,128)(2,1)S(1)}, u32[]{:S(2)}, u32[]{:S(2)}) %collective-permute-start.24) | collective-permute-done | bytes 262176 | tf_op jit(solution)/shard_map/ppermute | solution.py:16
  89.1 2.2 %collective-permute-start.26 = (bf16[64,512]{1,0:T(8,128)(2,1)S(1)}, bf16[64,512]{1,0:T(8,128)(2,1)S(1)}, u32[]{:S(2)}, u32[]{:S(2)}) collective-permute-start(bf16[64,512]{1,0:T(8,128)(2,1)S(1)} %get-tuple-element.53), channel_id=1, source_target_pairs={{0,12},{4,8},{8,4},{12,0},{16,28},{20,24},{24,20},{28,16},{1,13},{... | collective-permute-start | bytes 196616 | tf_op jit(solution)/shard_map/ppermute | solution.py:117
  91.3 2.6 %collective-permute-start.27 = (bf16[64,512]{1,0:T(8,128)(2,1)S(1)}, bf16[64,512]{1,0:T(8,128)(2,1)S(1)}, u32[]{:S(2)}, u32[]{:S(2)}) collective-permute-start(bf16[64,512]{1,0:T(8,128)(2,1)S(1)} %get-tuple-element.52), channel_id=1, source_target_pairs={{0,24},{4,28},{8,16},{12,20},{16,8},{20,12},{24,0},{28,4},{1,25},{... | collective-permute-start | bytes 196616 | tf_op jit(solution)/shard_map/ppermute | solution.py:117
  93.9 2.0 %collective-permute-start.28 = (bf16[64,512]{1,0:T(8,128)(2,1)S(1)}, bf16[64,512]{1,0:T(8,128)(2,1)S(1)}, u32[]{:S(2)}, u32[]{:S(2)}) collective-permute-start(bf16[64,512]{1,0:T(8,128)(2,1)S(1)} %get-tuple-element.51), channel_id=1, source_target_pairs={{0,28},{4,24},{8,20},{12,16},{16,12},{20,8},{24,4},{28,0},{1,29},{... | collective-permute-start | bytes 196616 | tf_op jit(solution)/shard_map/ppermute | solution.py:117
  96.0 1.5 %collective-permute-done.27 = bf16[64,512]{1,0:T(8,128)(2,1)S(1)} collective-permute-done((bf16[64,512]{1,0:T(8,128)(2,1)S(1)}, bf16[64,512]{1,0:T(8,128)(2,1)S(1)}, u32[]{:S(2)}, u32[]{:S(2)}) %collective-permute-start.27) | collective-permute-done | bytes 65568 | tf_op jit(solution)/shard_map/ppermute | solution.py:117
  97.5 3.5 %collective-permute-done.28 = bf16[64,512]{1,0:T(8,128)(2,1)S(1)} collective-permute-done((bf16[64,512]{1,0:T(8,128)(2,1)S(1)}, bf16[64,512]{1,0:T(8,128)(2,1)S(1)}, u32[]{:S(2)}, u32[]{:S(2)}) %collective-permute-start.28) | collective-permute-done | bytes 65568 | tf_op jit(solution)/shard_map/ppermute | solution.py:117
  100.9 1.0 %add_convert_fusion.4 = bf16[128,512]{1,0:T(8,128)(2,1)} fusion(bf16[128,512]{1,0:T(8,128)(2,1)S(1)} %add_convert_fusion.5, f32[128,512]{1,0:T(8,128)S(1)} %select_reduce_fusion, bf16[512,512]{1,0:T(8,128)(2,1)S(1)} %constant_dynamic-update-slice_fusion.4), kind=kOutput, calls=%fused_computation.11 | convolution fusion | flops 402849792 | bytes 1048576 | tf_op jit(solution)/shard_map/dot_general | solution.py:437
  (72 shorter events, 8.5 us)
Async XLA Ops:
  0.0 24.4 %copy-start.2 = (f32[128,2]{0,1:T(2,128)S(1)}, f32[128,2]{0,1:T(2,128)}, u32[]{:S(2)}) copy-start(f32[128,2]{0,1:T(2,128)} %param.30) | copy-start | bytes 3076
  2.8 16.9 %all-to-all-start = ((bf16[8,144,128]{2,1,0:T(8,128)(2,1)}), bf16[8,144,128]{2,1,0:T(8,128)(2,1)S(1)}, u32[]{:S(2)}, u32[]{:S(2)}) async-start(bf16[8,144,128]{2,1,0:T(8,128)(2,1)} %get-tuple-element.25), calls=%async_computation | async-start | bytes 589824 | tf_op jit(solution)/shard_map/all_to_all | solution.py:20
  20.6 12.1 %all-to-all-start.1 = ((bf16[8,128,128]{2,1,0:T(8,128)(2,1)}), bf16[8,128,128]{2,1,0:T(8,128)(2,1)S(1)}, u32[]{:S(2)}, u32[]{:S(2)}) async-start(bf16[8,128,128]{2,1,0:T(8,128)(2,1)} %prefix.1), calls=%async_computation.1 | async-start | bytes 524288 | tf_op jit(solution)/shard_map/all_to_all | solution.py:20
  35.9 1.4 %collective-permute-start.1 = (bf16[128,512]{1,0:T(8,128)(2,1)S(1)}, bf16[128,512]{1,0:T(8,128)(2,1)S(1)}, u32[]{:S(2)}, u32[]{:S(2)}) collective-permute-start(bf16[128,512]{1,0:T(8,128)(2,1)S(1)} %get-tuple-element.30), channel_id=1, source_target_pairs={{0,1},{1,0},{2,3},{3,2},{4,5},{5,4},{6,7},{7,6},{8,9},{9,8},{10,11... | collective-permute-start | bytes 393224 | tf_op jit(solution)/shard_map/ppermute | solution.py:16
  35.9 3.1 %collective-permute-start = (bf16[128,512]{1,0:T(8,128)(2,1)S(1)}, bf16[128,512]{1,0:T(8,128)(2,1)S(1)}, u32[]{:S(2)}, u32[]{:S(2)}) collective-permute-start(bf16[128,512]{1,0:T(8,128)(2,1)S(1)} %get-tuple-element.28), channel_id=1, source_target_pairs={{0,1},{1,0},{2,3},{3,2},{4,5},{5,4},{6,7},{7,6},{8,9},{9,8},{10,11... | collective-permute-start | bytes 393224 | tf_op jit(solution)/shard_map/ppermute | solution.py:16
  37.3 5.6 %collective-permute-start.2 = (bf16[128,512]{1,0:T(8,128)(2,1)S(1)}, bf16[128,512]{1,0:T(8,128)(2,1)S(1)}, u32[]{:S(2)}, u32[]{:S(2)}) collective-permute-start(bf16[128,512]{1,0:T(8,128)(2,1)S(1)} %add_convert_fusion.6), channel_id=1, source_target_pairs={{0,2},{1,3},{2,0},{3,1},{4,6},{5,7},{6,4},{7,5},{8,10},{9,11},{10,... | collective-permute-start | bytes 393224 | tf_op jit(solution)/shard_map/ppermute | solution.py:16
  43.4 8.7 %collective-permute-start.5 = (bf16[64,512]{1,0:T(8,128)(2,1)S(1)}, bf16[64,512]{1,0:T(8,128)(2,1)S(1)}, u32[]{:S(2)}, u32[]{:S(2)}) collective-permute-start(bf16[64,512]{1,0:T(8,128)(2,1)S(1)} %get-tuple-element.47), channel_id=1, source_target_pairs={{0,20},{4,16},{8,28},{12,24},{16,4},{20,0},{24,12},{28,8},{1,21},{... | collective-permute-start | bytes 196616 | tf_op jit(solution)/shard_map/ppermute | solution.py:117
  44.2 8.1 %collective-permute-start.4 = (bf16[64,512]{1,0:T(8,128)(2,1)S(1)}, bf16[64,512]{1,0:T(8,128)(2,1)S(1)}, u32[]{:S(2)}, u32[]{:S(2)}) collective-permute-start(bf16[64,512]{1,0:T(8,128)(2,1)S(1)} %get-tuple-element.48), channel_id=1, source_target_pairs={{0,16},{4,20},{8,24},{12,28},{16,0},{20,4},{24,8},{28,12},{1,17},{... | collective-permute-start | bytes 196616 | tf_op jit(solution)/shard_map/ppermute | solution.py:117
  47.3 5.0 %collective-permute-start.3 = (bf16[64,512]{1,0:T(8,128)(2,1)S(1)}, bf16[64,512]{1,0:T(8,128)(2,1)S(1)}, u32[]{:S(2)}, u32[]{:S(2)}) collective-permute-start(bf16[64,512]{1,0:T(8,128)(2,1)S(1)} %get-tuple-element.49), channel_id=1, source_target_pairs={{0,4},{4,0},{8,12},{12,8},{16,20},{20,16},{24,28},{28,24},{1,5},{5... | collective-permute-start | bytes 196616 | tf_op jit(solution)/shard_map/ppermute | solution.py:117
  52.3 8.3 %collective-permute-start.7 = (bf16[256,512]{1,0:T(8,128)(2,1)S(1)}, bf16[256,512]{1,0:T(8,128)(2,1)S(1)}, u32[]{:S(2)}, u32[]{:S(2)}) collective-permute-start(bf16[256,512]{1,0:T(8,128)(2,1)S(1)} %pad_maximum_fusion.own_in), channel_id=1, source_target_pairs={{0,2},{1,3},{2,0},{3,1},{4,6},{5,7},{6,4},{7,5},{8,10},{9,11},{10,... | collective-permute-start | bytes 786440 | tf_op jit(solution)/shard_map/ppermute | solution.py:16
  53.8 6.8 %collective-permute-start.15 = (bf16[64,512]{1,0:T(8,128)(2,1)S(1)}, bf16[64,512]{1,0:T(8,128)(2,1)S(1)}, u32[]{:S(2)}, u32[]{:S(2)}) collective-permute-start(bf16[64,512]{1,0:T(8,128)(2,1)S(1)} %get-tuple-element.46), channel_id=1, source_target_pairs={{0,8},{4,12},{8,0},{12,4},{16,24},{20,28},{24,16},{28,20},{1,9},{5... | collective-permute-start | bytes 196616 | tf_op jit(solution)/shard_map/ppermute | solution.py:117
  53.8 7.3 %collective-permute-start.16 = (bf16[64,512]{1,0:T(8,128)(2,1)S(1)}, bf16[64,512]{1,0:T(8,128)(2,1)S(1)}, u32[]{:S(2)}, u32[]{:S(2)}) collective-permute-start(bf16[64,512]{1,0:T(8,128)(2,1)S(1)} %get-tuple-element.45), channel_id=1, source_target_pairs={{0,12},{4,8},{8,4},{12,0},{16,28},{20,24},{24,20},{28,16},{1,13},{... | collective-permute-start | bytes 196616 | tf_op jit(solution)/shard_map/ppermute | solution.py:117
  56.4 6.1 %collective-permute-start.17 = (bf16[64,512]{1,0:T(8,128)(2,1)S(1)}, bf16[64,512]{1,0:T(8,128)(2,1)S(1)}, u32[]{:S(2)}, u32[]{:S(2)}) collective-permute-start(bf16[64,512]{1,0:T(8,128)(2,1)S(1)} %get-tuple-element.44), channel_id=1, source_target_pairs={{0,24},{4,28},{8,16},{12,20},{16,8},{20,12},{24,0},{28,4},{1,25},{... | collective-permute-start | bytes 196616 | tf_op jit(solution)/shard_map/ppermute | solution.py:117
  57.8 7.0 %collective-permute-start.18 = (bf16[64,512]{1,0:T(8,128)(2,1)S(1)}, bf16[64,512]{1,0:T(8,128)(2,1)S(1)}, u32[]{:S(2)}, u32[]{:S(2)}) collective-permute-start(bf16[64,512]{1,0:T(8,128)(2,1)S(1)} %get-tuple-element.43), channel_id=1, source_target_pairs={{0,28},{4,24},{8,20},{12,16},{16,12},{20,8},{24,4},{28,0},{1,29},{... | collective-permute-start | bytes 196616 | tf_op jit(solution)/shard_map/ppermute | solution.py:117
  60.6 4.7 %collective-permute-start.6 = (bf16[256,512]{1,0:T(8,128)(2,1)S(1)}, bf16[256,512]{1,0:T(8,128)(2,1)S(1)}, u32[]{:S(2)}, u32[]{:S(2)}) collective-permute-start(bf16[256,512]{1,0:T(8,128)(2,1)S(1)} %pad_maximum_fusion.own_in), channel_id=1, source_target_pairs={{0,1},{1,0},{2,3},{3,2},{4,5},{5,4},{6,7},{7,6},{8,9},{9,8},{10,11... | collective-permute-start | bytes 786440 | tf_op jit(solution)/shard_map/ppermute | solution.py:16
  60.6 4.7 %collective-permute-start.8 = (bf16[256,512]{1,0:T(8,128)(2,1)S(1)}, bf16[256,512]{1,0:T(8,128)(2,1)S(1)}, u32[]{:S(2)}, u32[]{:S(2)}) collective-permute-start(bf16[256,512]{1,0:T(8,128)(2,1)S(1)} %collective-permute-done.7.far_in), channel_id=1, source_target_pairs={{0,1},{1,0},{2,3},{3,2},{4,5},{5,4},{6,7},{7,6},{8,9},{9,8},{10,11... | collective-permute-start | bytes 786440 | tf_op jit(solution)/shard_map/ppermute | solution.py:16
  64.8 6.4 %collective-permute-start.20 = (bf16[256,512]{1,0:T(8,128)(2,1)S(1)}, bf16[256,512]{1,0:T(8,128)(2,1)S(1)}, u32[]{:S(2)}, u32[]{:S(2)}) collective-permute-start(bf16[256,512]{1,0:T(8,128)(2,1)S(1)} %constant_dynamic-update-slice_fusion.own_in), channel_id=1, source_target_pairs={{0,2},{1,3},{2,0},{3,1},{4,6},{5,7},{6,4},{7,5},{8,10},{9,11},{10,... | collective-permute-start | bytes 786440 | tf_op jit(solution)/shard_map/ppermute | solution.py:16
  69.3 1.9 %collective-permute-start.9 = (bf16[256,512]{1,0:T(8,128)(2,1)S(1)}, bf16[256,512]{1,0:T(8,128)(2,1)S(1)}, u32[]{:S(2)}, u32[]{:S(2)}) collective-permute-start(bf16[256,512]{1,0:T(8,128)(2,1)S(1)} %get-tuple-element.34), channel_id=1, source_target_pairs={{0,1},{1,0},{2,3},{3,2},{4,5},{5,4},{6,7},{7,6},{8,9},{9,8},{10,11... | collective-permute-start | bytes 786440 | tf_op jit(solution)/shard_map/ppermute | solution.py:16
  69.4 3.2 %collective-permute-start.19 = (bf16[256,512]{1,0:T(8,128)(2,1)S(1)}, bf16[256,512]{1,0:T(8,128)(2,1)S(1)}, u32[]{:S(2)}, u32[]{:S(2)}) collective-permute-start(bf16[256,512]{1,0:T(8,128)(2,1)S(1)} %constant_dynamic-update-slice_fusion.own_in), channel_id=1, source_target_pairs={{0,1},{1,0},{2,3},{3,2},{4,5},{5,4},{6,7},{7,6},{8,9},{9,8},{10,11... | collective-permute-start | bytes 786440 | tf_op jit(solution)/shard_map/ppermute | solution.py:16
  71.1 1.5 %collective-permute-start.21 = (bf16[256,512]{1,0:T(8,128)(2,1)S(1)}, bf16[256,512]{1,0:T(8,128)(2,1)S(1)}, u32[]{:S(2)}, u32[]{:S(2)}) collective-permute-start(bf16[256,512]{1,0:T(8,128)(2,1)S(1)} %collective-permute-done.20.far_in), channel_id=1, source_target_pairs={{0,1},{1,0},{2,3},{3,2},{4,5},{5,4},{6,7},{7,6},{8,9},{9,8},{10,11... | collective-permute-start | bytes 786440 | tf_op jit(solution)/shard_map/ppermute | solution.py:16
  71.2 8.8 %collective-permute-start.10 = (bf16[256,512]{1,0:T(8,128)(2,1)S(1)}, bf16[256,512]{1,0:T(8,128)(2,1)S(1)}, u32[]{:S(2)}, u32[]{:S(2)}) collective-permute-start(bf16[256,512]{1,0:T(8,128)(2,1)S(1)} %add_convert_fusion.3), channel_id=1, source_target_pairs={{0,2},{1,3},{2,0},{3,1},{4,6},{5,7},{6,4},{7,5},{8,10},{9,11},{10,... | collective-permute-start | bytes 786440 | tf_op jit(solution)/shard_map/ppermute | solution.py:16
  76.7 3.3 %collective-permute-start.22 = (bf16[256,512]{1,0:T(8,128)(2,1)S(1)}, bf16[256,512]{1,0:T(8,128)(2,1)S(1)}, u32[]{:S(2)}, u32[]{:S(2)}) collective-permute-start(bf16[256,512]{1,0:T(8,128)(2,1)S(1)} %get-tuple-element.41), channel_id=1, source_target_pairs={{0,1},{1,0},{2,3},{3,2},{4,5},{5,4},{6,7},{7,6},{8,9},{9,8},{10,11... | collective-permute-start | bytes 786440 | tf_op jit(solution)/shard_map/ppermute | solution.py:16
  80.0 1.5 %collective-permute-start.11 = (bf16[256,512]{1,0:T(8,128)(2,1)S(1)}, bf16[256,512]{1,0:T(8,128)(2,1)S(1)}, u32[]{:S(2)}, u32[]{:S(2)}) collective-permute-start(bf16[256,512]{1,0:T(8,128)(2,1)S(1)} %get-tuple-element.35), channel_id=1, source_target_pairs={{0,1},{1,0},{2,3},{3,2},{4,5},{5,4},{6,7},{7,6},{8,9},{9,8},{10,11... | collective-permute-start | bytes 786440 | tf_op jit(solution)/shard_map/ppermute | solution.py:16
  80.1 8.8 %collective-permute-start.24 = (bf16[256,512]{1,0:T(8,128)(2,1)S(1)}, bf16[256,512]{1,0:T(8,128)(2,1)S(1)}, u32[]{:S(2)}, u32[]{:S(2)}) collective-permute-start(bf16[256,512]{1,0:T(8,128)(2,1)S(1)} %add_convert_fusion.1), channel_id=1, source_target_pairs={{0,2},{1,3},{2,0},{3,1},{4,6},{5,7},{6,4},{7,5},{8,10},{9,11},{10,... | collective-permute-start | bytes 786440 | tf_op jit(solution)/shard_map/ppermute | solution.py:16
  81.0 7.8 %collective-permute-start.23 = (bf16[256,512]{1,0:T(8,128)(2,1)S(1)}, bf16[256,512]{1,0:T(8,128)(2,1)S(1)}, u32[]{:S(2)}, u32[]{:S(2)}) collective-permute-start(bf16[256,512]{1,0:T(8,128)(2,1)S(1)} %get-tuple-element.42), channel_id=1, source_target_pairs={{0,1},{1,0},{2,3},{3,2},{4,5},{5,4},{6,7},{7,6},{8,9},{9,8},{10,11... | collective-permute-start | bytes 786440 | tf_op jit(solution)/shard_map/ppermute | solution.py:16
  81.7 9.7 %collective-permute-start.12 = (bf16[64,512]{1,0:T(8,128)(2,1)S(1)}, bf16[64,512]{1,0:T(8,128)(2,1)S(1)}, u32[]{:S(2)}, u32[]{:S(2)}) collective-permute-start(bf16[64,512]{1,0:T(8,128)(2,1)S(1)} %get-tuple-element.57), channel_id=1, source_target_pairs={{0,4},{4,0},{8,12},{12,8},{16,20},{20,16},{24,28},{28,24},{1,5},{5... | collective-permute-start | bytes 196616 | tf_op jit(solution)/shard_map/ppermute | solution.py:117
  82.5 11.4 %collective-permute-start.13 = (bf16[64,512]{1,0:T(8,128)(2,1)S(1)}, bf16[64,512]{1,0:T(8,128)(2,1)S(1)}, u32[]{:S(2)}, u32[]{:S(2)}) collective-permute-start(bf16[64,512]{1,0:T(8,128)(2,1)S(1)} %get-tuple-element.56), channel_id=1, source_target_pairs={{0,16},{4,20},{8,24},{12,28},{16,0},{20,4},{24,8},{28,12},{1,17},{... | collective-permute-start | bytes 196616 | tf_op jit(solution)/shard_map/ppermute | solution.py:117
  82.5 13.4 %collective-permute-start.14 = (bf16[64,512]{1,0:T(8,128)(2,1)S(1)}, bf16[64,512]{1,0:T(8,128)(2,1)S(1)}, u32[]{:S(2)}, u32[]{:S(2)}) collective-permute-start(bf16[64,512]{1,0:T(8,128)(2,1)S(1)} %get-tuple-element.55), channel_id=1, source_target_pairs={{0,20},{4,16},{8,28},{12,24},{16,4},{20,0},{24,12},{28,8},{1,21},{... | collective-permute-start | bytes 196616 | tf_op jit(solution)/shard_map/ppermute | solution.py:117
  89.0 6.9 %collective-permute-start.25 = (bf16[64,512]{1,0:T(8,128)(2,1)S(1)}, bf16[64,512]{1,0:T(8,128)(2,1)S(1)}, u32[]{:S(2)}, u32[]{:S(2)}) collective-permute-start(bf16[64,512]{1,0:T(8,128)(2,1)S(1)} %get-tuple-element.54), channel_id=1, source_target_pairs={{0,8},{4,12},{8,0},{12,4},{16,24},{20,28},{24,16},{28,20},{1,9},{5... | collective-permute-start | bytes 196616 | tf_op jit(solution)/shard_map/ppermute | solution.py:117
  89.1 6.9 %collective-permute-start.26 = (bf16[64,512]{1,0:T(8,128)(2,1)S(1)}, bf16[64,512]{1,0:T(8,128)(2,1)S(1)}, u32[]{:S(2)}, u32[]{:S(2)}) collective-permute-start(bf16[64,512]{1,0:T(8,128)(2,1)S(1)} %get-tuple-element.53), channel_id=1, source_target_pairs={{0,12},{4,8},{8,4},{12,0},{16,28},{20,24},{24,20},{28,16},{1,13},{... | collective-permute-start | bytes 196616 | tf_op jit(solution)/shard_map/ppermute | solution.py:117
  91.3 6.1 %collective-permute-start.27 = (bf16[64,512]{1,0:T(8,128)(2,1)S(1)}, bf16[64,512]{1,0:T(8,128)(2,1)S(1)}, u32[]{:S(2)}, u32[]{:S(2)}) collective-permute-start(bf16[64,512]{1,0:T(8,128)(2,1)S(1)} %get-tuple-element.52), channel_id=1, source_target_pairs={{0,24},{4,28},{8,16},{12,20},{16,8},{20,12},{24,0},{28,4},{1,25},{... | collective-permute-start | bytes 196616 | tf_op jit(solution)/shard_map/ppermute | solution.py:117
  93.9 7.0 %collective-permute-start.28 = (bf16[64,512]{1,0:T(8,128)(2,1)S(1)}, bf16[64,512]{1,0:T(8,128)(2,1)S(1)}, u32[]{:S(2)}, u32[]{:S(2)}) collective-permute-start(bf16[64,512]{1,0:T(8,128)(2,1)S(1)} %get-tuple-element.51), channel_id=1, source_target_pairs={{0,28},{4,24},{8,20},{12,16},{16,12},{20,8},{24,4},{28,0},{1,29},{... | collective-permute-start | bytes 196616 | tf_op jit(solution)/shard_map/ppermute | solution.py:117
  (3 other events, 37.2 us)

commit v12 on v11

--- a/solution.py
+++ b/solution.py
@@ -104,20 +104,20 @@
             carries[h] = factor * carries[h] + got[turn, spot, :].astype(F32)
 
 
-HALVES = ((0, 1, 4, 5), (2, 3, 6, 7))
-
-
-def exchange_halves(pieces):
-    halves = []
-    for order, part in zip(HALVES, pieces):
+PARTS = ((2, 3, 5, 6, 7), (0, 1, 4))
+
+
+def exchange_parts(pieces):
+    parts = []
+    for order, part in zip(PARTS, pieces):
         got = []
         for spot, k in enumerate(order):
             piece = part[spot]
             if k > 0:
                 piece = lax.ppermute(piece, "seq", [(i, i ^ k) for i in range(8)])
             got.append(piece)
-        halves.append(jnp.concatenate(got))
-    return halves
+        parts.append(jnp.concatenate(got))
+    return parts
 
 
 def entering_state(got, init_rows):
@@ -372,8 +372,9 @@
     few = seq_count == 8
     layout = flat_expert
     if few:
-        layout = flat_expert ^ lax.axis_index("seq")
-        layout = (layout & 1) | ((layout & 2) << 1) | ((layout & 4) >> 1)
+        bits = flat_expert ^ lax.axis_index("seq")
+        order = PARTS[0] + PARTS[1]
+        layout = sum(jnp.where(bits == k, spot, 0) for spot, k in enumerate(order))
     placed = layout * slot_count + rank
     spots = placed[:, None] == jnp.arange(slots, dtype=jnp.int32)[None, :]
     spots = spots.reshape(top_count, tok_rows, slots)
@@ -395,10 +396,10 @@
     ).astype(BF)
     outgoing = outgoing.reshape(expert_count, slot_count, share)
 
-    cut = slots // 2
-    middle = expert_count // 2
+    middle = len(PARTS[0]) if few else expert_count // 2
+    cut = middle * slot_count
     if few:
-        own = exchange_halves((outgoing[:middle], outgoing[middle:]))
+        own = exchange_parts((outgoing[:middle], outgoing[middle:]))
     else:
         arrived = exchange(outgoing).reshape(slots, share)
         own = [arrived[:cut], arrived[cut:]]
@@ -429,8 +430,8 @@
         )
     ]
     if few:
-        results = [part.reshape(middle, slot_count, share) for part in results]
-        returned = jnp.concatenate(exchange_halves(results))
+        results = [part.reshape(-1, slot_count, share) for part in results]
+        returned = jnp.concatenate(exchange_parts(results))
     else:
         results = jnp.concatenate(results).reshape(expert_count, slot_count, share)
         returned = exchange(results).reshape(slots, share)

time: 102 us -> 121 us (1.19)
  waiting for transfers between devices: 40.7 us -> 53 us
  starting transfers between devices: 41.4 us -> 46.1 us
    ppermute x15, waiting for transfers between devices: 12.4 us -> 22.6 us  [swap(): return lax.ppermute(value, 'tp', [(i, i ^ bit) for i in range(count)])]
    ppermute x14, starting transfers between devices: 22.5 us -> 27.1 us  [exchange_parts(): piece = lax.ppermute(piece, 'seq', [(i, i ^ k) for i in range(8)])]
    ppermute x14, waiting for transfers between devices: 12.9 us -> 15 us  [exchange_parts(): piece = lax.ppermute(piece, 'seq', [(i, i ^ k) for i in range(8)])]
    pallas_call x2, Pallas kernels: 7.96 us -> 9.18 us  [run_expert(): pl.pallas_call(expert_kernel, in_specs=[pl.BlockSpec(memory_space=pltpu.S...]
  transfers between devices with their start and end apart: 31 -> 31, of which waited for: 15 -> 19; matrix products, arithmetic and copies ran while one was open for 1% -> 1% of each run, Pallas kernels for 9% -> 5%
where the time goes in v12:
time: 121 us; the launch traced here: 120 us
  waiting for transfers between devices  53 us (44%)
  starting transfers between devices  46.1 us (38%)
  Pallas kernels  17.7 us (15%)
  matrix products  1.58 us (1%)
    ppermute x14, starting transfers between devices, exchange_parts(): piece = lax.ppermute(piece, 'seq', [(i, i ^ k) for i in range(8)])  27.1 us
    ppermute x15, waiting for transfers between devices, swap(): return lax.ppermute(value, 'tp', [(i, i ^ bit) for i in range(count)])  22.6 us
    all_to_all x2, waiting for transfers between devices, exchange(): return lax.all_to_all(value, 'seq', split_axis=0, concat_axis=0, tiled=True)  15.4 us
    ppermute x14, waiting for transfers between devices, exchange_parts(): piece = lax.ppermute(piece, 'seq', [(i, i ^ k) for i in range(8)])  15 us
    all_to_all x2, starting transfers between devices, exchange(): return lax.all_to_all(value, 'seq', split_axis=0, concat_axis=0, tiled=True)  10.8 us
    pallas_call x2, Pallas kernels, run_expert(): pl.pallas_call(expert_kernel, in_specs=[pl.BlockSpec(memory_space=pltpu.S...  9.18 us
    ppermute x15, starting transfers between devices, swap(): return lax.ppermute(value, 'tp', [(i, i ^ bit) for i in range(count)])  8.2 us
    pallas_call x1, Pallas kernels, mixer_tail(): pl.pallas_call(tail_kernel, in_specs=[pl.BlockSpec(memory_space=pltpu.SME...  3.17 us
  transfers between devices with their start and end apart: 31, of which 19 were waited for; matrix products, arithmetic and copies ran while one was open for 1% of the time, Pallas kernels for 5%

profile of v12, /device:TPU:0, one launch (start us, length us, event | category | flops | bytes accessed | tf_op | source)
XLA Modules:
  0.0 120.1 jit_solution(17380519330288350612)
XLA Ops:
  0.0 2.8 %own_state.1 = (bf16[8,144,128]{2,1,0:T(8,128)(2,1)}, f32[16,128]{1,0:T(8,128)S(1)}) custom-call(bf16[128,1024]{1,0:T(8,128)(2,1)} %x.3, f32[16,128]{1,0:T(8,128)} %bitcast.32, f32[16,128]{1,0:T(8,128)} %bitcast.36, bf16[128,128]{1,0:T(8,128)(2,1)} %b.3), custom_call_target="tpu_custom_call" | custom-call | tf_op jit(solution)/shard_map/own_state/pallas_call | solution.py:78
  2.8 7.3 %all-to-all-start = ((bf16[8,144,128]{2,1,0:T(8,128)(2,1)}), bf16[8,144,128]{2,1,0:T(8,128)(2,1)S(1)}, u32[]{:S(2)}, u32[]{:S(2)}) async-start(bf16[8,144,128]{2,1,0:T(8,128)(2,1)} %get-tuple-element.25), calls=%async_computation | async-start | bytes 589824 | tf_op jit(solution)/shard_map/all_to_all | solution.py:20
  10.7 1.7 %within_block.1.direct_in = f32[128,1024]{1,0:T(8,128)S(1)} custom-call(f32[16]{0:T(128)S(1)} %copy-done.1, bf16[128,1024]{1,0:T(8,128)(2,1)} %x.3, f32[16,128]{1,0:T(8,128)} %bitcast.33, f32[16,128]{1,0:T(8,128)S(1)} %get-tuple-element.24.cum_t.cum_in, bf16[128,128]{1,0:T(8,128)(2,1)} %b.3, bf16[128,128]{1,0:T(8,128)(2,1)} %c_in.1), custom_call_target="tpu_custom_call" | custom-call | flops 134217728 | bytes 786432 | tf_op jit(solution)/shard_map/within_block/pallas_call | solution.py:164
  12.4 7.3 %all-to-all-done.got = bf16[8,144,128]{2,1,0:T(8,128)(2,1)S(1)} async-done(((bf16[8,144,128]{2,1,0:T(8,128)(2,1)}), bf16[8,144,128]{2,1,0:T(8,128)(2,1)S(1)}, u32[]{:S(2)}, u32[]{:S(2)}) %all-to-all-start) | async-done | bytes 294944 | tf_op jit(solution)/shard_map/all_to_all | solution.py:20
  20.6 3.6 %all-to-all-start.1 = ((bf16[8,128,128]{2,1,0:T(8,128)(2,1)}), bf16[8,128,128]{2,1,0:T(8,128)(2,1)S(1)}, u32[]{:S(2)}, u32[]{:S(2)}) async-start(bf16[8,128,128]{2,1,0:T(8,128)(2,1)} %prefix.1), calls=%async_computation.1 | async-start | bytes 524288 | tf_op jit(solution)/shard_map/all_to_all | solution.py:20
  24.5 8.1 %all-to-all-done.1 = bf16[8,128,128]{2,1,0:T(8,128)(2,1)S(1)} async-done(((bf16[8,128,128]{2,1,0:T(8,128)(2,1)}), bf16[8,128,128]{2,1,0:T(8,128)(2,1)S(1)}, u32[]{:S(2)}, u32[]{:S(2)}) %all-to-all-start.1) | async-done | bytes 262176 | tf_op jit(solution)/shard_map/all_to_all | solution.py:20
  32.7 3.2 %mixer_tail.1 = (bf16[128,512]{1,0:T(8,128)(2,1)S(1)}, bf16[128,512]{1,0:T(8,128)(2,1)S(1)}, f32[128,512]{1,0:T(8,128)S(1)}, f32[128,512]{1,0:T(8,128)S(1)}) custom-call(s32[1]{0:T(128)} %bitcast.place_ref, bf16[128,128]{1,0:T(8,128)(2,1)} %c_in.1, f32[16,128]{1,0:T(8,128)S(1)} %get-tuple-element.24.cum_t.cum_in, f32[1,1024]{1,0:T(1,128)} %bitcast.37, ...), custom_call_target="tpu_custom_call" | custom-call | flops 536870912 | bytes 6029312 | tf_op jit(solution)/shard_map/mixer_tail/pallas_call | solution.py:246
  37.3 1.6 %collective-permute-start.2 = (bf16[128,512]{1,0:T(8,128)(2,1)S(1)}, bf16[128,512]{1,0:T(8,128)(2,1)S(1)}, u32[]{:S(2)}, u32[]{:S(2)}) collective-permute-start(bf16[128,512]{1,0:T(8,128)(2,1)S(1)} %add_convert_fusion.6), channel_id=1, source_target_pairs={{0,2},{1,3},{2,0},{3,1},{4,6},{5,7},{6,4},{7,5},{8,10},{9,11},{10,... | collective-permute-start | bytes 393224 | tf_op jit(solution)/shard_map/ppermute | solution.py:16
  39.0 3.9 %collective-permute-done.2 = bf16[128,512]{1,0:T(8,128)(2,1)S(1)} collective-permute-done((bf16[128,512]{1,0:T(8,128)(2,1)S(1)}, bf16[128,512]{1,0:T(8,128)(2,1)S(1)}, u32[]{:S(2)}, u32[]{:S(2)}) %collective-permute-start.2) | collective-permute-done | bytes 131104 | tf_op jit(solution)/shard_map/ppermute | solution.py:16
  44.6 1.8 %collective-permute-start.4 = (bf16[64,512]{1,0:T(8,128)(2,1)S(1)}, bf16[64,512]{1,0:T(8,128)(2,1)S(1)}, u32[]{:S(2)}, u32[]{:S(2)}) collective-permute-start(bf16[64,512]{1,0:T(8,128)(2,1)S(1)} %get-tuple-element.49), channel_id=1, source_target_pairs={{0,12},{4,8},{8,4},{12,0},{16,28},{20,24},{24,20},{28,16},{1,13},{... | collective-permute-start | bytes 196616 | tf_op jit(solution)/shard_map/ppermute | solution.py:117
  47.4 2.4 %collective-permute-start.6 = (bf16[64,512]{1,0:T(8,128)(2,1)S(1)}, bf16[64,512]{1,0:T(8,128)(2,1)S(1)}, u32[]{:S(2)}, u32[]{:S(2)}) collective-permute-start(bf16[64,512]{1,0:T(8,128)(2,1)S(1)} %get-tuple-element.47), channel_id=1, source_target_pairs={{0,24},{4,28},{8,16},{12,20},{16,8},{20,12},{24,0},{28,4},{1,25},{... | collective-permute-start | bytes 196616 | tf_op jit(solution)/shard_map/ppermute | solution.py:117
  51.2 3.7 %collective-permute-done.5 = bf16[64,512]{1,0:T(8,128)(2,1)S(1)} collective-permute-done((bf16[64,512]{1,0:T(8,128)(2,1)S(1)}, bf16[64,512]{1,0:T(8,128)(2,1)S(1)}, u32[]{:S(2)}, u32[]{:S(2)}) %collective-permute-start.5) | collective-permute-done | bytes 65568 | tf_op jit(solution)/shard_map/ppermute | solution.py:117
  54.8 2.1 %collective-permute-done.7 = bf16[64,512]{1,0:T(8,128)(2,1)S(1)} collective-permute-done((bf16[64,512]{1,0:T(8,128)(2,1)S(1)}, bf16[64,512]{1,0:T(8,128)(2,1)S(1)}, u32[]{:S(2)}, u32[]{:S(2)}) %collective-permute-start.7) | collective-permute-done | bytes 65568 | tf_op jit(solution)/shard_map/ppermute | solution.py:117
  56.9 1.5 %collective-permute-start.9 = (bf16[320,512]{1,0:T(8,128)(2,1)S(1)}, bf16[320,512]{1,0:T(8,128)(2,1)S(1)}, u32[]{:S(2)}, u32[]{:S(2)}) collective-permute-start(bf16[320,512]{1,0:T(8,128)(2,1)S(1)} %constant_dynamic-update-slice_fusion.own_in), channel_id=1, source_target_pairs={{0,2},{1,3},{2,0},{3,1},{4,6},{5,7},{6,4},{7,5},{8,10},{9,11},{10,... | collective-permute-start | bytes 983048 | tf_op jit(solution)/shard_map/ppermute | solution.py:16
  58.4 5.5 %collective-permute-done.9.far_in = bf16[320,512]{1,0:T(8,128)(2,1)S(1)} collective-permute-done((bf16[320,512]{1,0:T(8,128)(2,1)S(1)}, bf16[320,512]{1,0:T(8,128)(2,1)S(1)}, u32[]{:S(2)}, u32[]{:S(2)}) %collective-permute-start.9) | collective-permute-done | bytes 327712 | tf_op jit(solution)/shard_map/ppermute | solution.py:16
  64.0 1.6 %collective-permute-done.10.last_in = bf16[320,512]{1,0:T(8,128)(2,1)S(1)} collective-permute-done((bf16[320,512]{1,0:T(8,128)(2,1)S(1)}, bf16[320,512]{1,0:T(8,128)(2,1)S(1)}, u32[]{:S(2)}, u32[]{:S(2)}) %collective-permute-start.10) | collective-permute-done | bytes 327712 | tf_op jit(solution)/shard_map/ppermute | solution.py:16
  65.6 4.7 %expert.2 = (bf16[320,512]{1,0:T(8,128)(2,1)S(1)}, bf16[320,512]{1,0:T(8,128)(2,1)S(1)}, bf16[320,512]{1,0:T(8,128)(2,1)S(1)}, bf16[320,512]{1,0:T(8,128)(2,1)S(1)}) custom-call(s32[1]{0:T(128)} %bitcast.place_ref, f32[1,2048]{1,0:T(1,128)} %bitcast.34, bf16[320,512]{1,0:T(8,128)(2,1)S(1)} %constant_dynamic-update-slice_fusion.own_in, ...), custom_call_target="tpu_custom_call" | custom-call | flops 1 | bytes 1 | tf_op jit(solution)/shard_map/expert/pallas_call | solution.py:315
  70.5 2.0 %collective-permute-start.20 = (bf16[64,512]{1,0:T(8,128)(2,1)S(1)}, bf16[64,512]{1,0:T(8,128)(2,1)S(1)}, u32[]{:S(2)}, u32[]{:S(2)}) collective-permute-start(bf16[64,512]{1,0:T(8,128)(2,1)S(1)} %get-tuple-element.44), channel_id=1, source_target_pairs={{0,16},{4,20},{8,24},{12,28},{16,0},{20,4},{24,8},{28,12},{1,17},{... | collective-permute-start | bytes 196616 | tf_op jit(solution)/shard_map/ppermute | solution.py:117
  72.6 2.1 %collective-permute-start.19 = (bf16[64,512]{1,0:T(8,128)(2,1)S(1)}, bf16[64,512]{1,0:T(8,128)(2,1)S(1)}, u32[]{:S(2)}, u32[]{:S(2)}) collective-permute-start(bf16[64,512]{1,0:T(8,128)(2,1)S(1)} %get-tuple-element.45), channel_id=1, source_target_pairs={{0,4},{4,0},{8,12},{12,8},{16,20},{20,16},{24,28},{28,24},{1,5},{5... | collective-permute-start | bytes 196616 | tf_op jit(solution)/shard_map/ppermute | solution.py:117
  77.0 1.6 %collective-permute-start.22 = (bf16[192,512]{1,0:T(8,128)(2,1)S(1)}, bf16[192,512]{1,0:T(8,128)(2,1)S(1)}, u32[]{:S(2)}, u32[]{:S(2)}) collective-permute-start(bf16[192,512]{1,0:T(8,128)(2,1)S(1)} %pad_maximum_fusion.own_in), channel_id=1, source_target_pairs={{0,2},{1,3},{2,0},{3,1},{4,6},{5,7},{6,4},{7,5},{8,10},{9,11},{10,... | collective-permute-start | bytes 589832 | tf_op jit(solution)/shard_map/ppermute | solution.py:16
  79.2 5.6 %collective-permute-done.22.far_in = bf16[192,512]{1,0:T(8,128)(2,1)S(1)} collective-permute-done((bf16[192,512]{1,0:T(8,128)(2,1)S(1)}, bf16[192,512]{1,0:T(8,128)(2,1)S(1)}, u32[]{:S(2)}, u32[]{:S(2)}) %collective-permute-start.22) | collective-permute-done | bytes 196640 | tf_op jit(solution)/shard_map/ppermute | solution.py:16
  84.9 1.4 %collective-permute-done.23.last_in = bf16[192,512]{1,0:T(8,128)(2,1)S(1)} collective-permute-done((bf16[192,512]{1,0:T(8,128)(2,1)S(1)}, bf16[192,512]{1,0:T(8,128)(2,1)S(1)}, u32[]{:S(2)}, u32[]{:S(2)}) %collective-permute-start.23) | collective-permute-done | bytes 196640 | tf_op jit(solution)/shard_map/ppermute | solution.py:16
  86.3 4.5 %expert.3 = (bf16[192,512]{1,0:T(8,128)(2,1)S(1)}, bf16[192,512]{1,0:T(8,128)(2,1)S(1)}, bf16[192,512]{1,0:T(8,128)(2,1)S(1)}, bf16[192,512]{1,0:T(8,128)(2,1)S(1)}) custom-call(s32[1]{0:T(128)} %bitcast.place_ref, f32[1,2048]{1,0:T(1,128)} %bitcast.35, bf16[192,512]{1,0:T(8,128)(2,1)S(1)} %pad_maximum_fusion.own_in, ...), custom_call_target="tpu_custom_call" | custom-call | flops 1 | bytes 1 | tf_op jit(solution)/shard_map/expert/pallas_call | solution.py:315
  92.4 1.6 %collective-permute-start.26 = (bf16[192,512]{1,0:T(8,128)(2,1)S(1)}, bf16[192,512]{1,0:T(8,128)(2,1)S(1)}, u32[]{:S(2)}, u32[]{:S(2)}) collective-permute-start(bf16[192,512]{1,0:T(8,128)(2,1)S(1)} %add_convert_fusion.3), channel_id=1, source_target_pairs={{0,2},{1,3},{2,0},{3,1},{4,6},{5,7},{6,4},{7,5},{8,10},{9,11},{10,... | collective-permute-start | bytes 589832 | tf_op jit(solution)/shard_map/ppermute | solution.py:16
  94.1 2.6 %collective-permute-start.14 = (bf16[64,512]{1,0:T(8,128)(2,1)S(1)}, bf16[64,512]{1,0:T(8,128)(2,1)S(1)}, u32[]{:S(2)}, u32[]{:S(2)}) collective-permute-start(bf16[64,512]{1,0:T(8,128)(2,1)S(1)} %get-tuple-element.55), channel_id=1, source_target_pairs={{0,8},{4,12},{8,0},{12,4},{16,24},{20,28},{24,16},{28,20},{1,9},{5... | collective-permute-start | bytes 196616 | tf_op jit(solution)/shard_map/ppermute | solution.py:117
  96.7 2.7 %collective-permute-done.26 = bf16[192,512]{1,0:T(8,128)(2,1)S(1)} collective-permute-done((bf16[192,512]{1,0:T(8,128)(2,1)S(1)}, bf16[192,512]{1,0:T(8,128)(2,1)S(1)}, u32[]{:S(2)}, u32[]{:S(2)}) %collective-permute-start.26) | collective-permute-done | bytes 196640 | tf_op jit(solution)/shard_map/ppermute | solution.py:16
  100.8 4.0 %collective-permute-start.16 = (bf16[64,512]{1,0:T(8,128)(2,1)S(1)}, bf16[64,512]{1,0:T(8,128)(2,1)S(1)}, u32[]{:S(2)}, u32[]{:S(2)}) collective-permute-start(bf16[64,512]{1,0:T(8,128)(2,1)S(1)} %get-tuple-element.53), channel_id=1, source_target_pairs={{0,20},{4,16},{8,28},{12,24},{16,4},{20,0},{24,12},{28,8},{1,21},{... | collective-permute-start | bytes 196616 | tf_op jit(solution)/shard_map/ppermute | solution.py:117
  104.9 3.3 %collective-permute-start.18 = (bf16[64,512]{1,0:T(8,128)(2,1)S(1)}, bf16[64,512]{1,0:T(8,128)(2,1)S(1)}, u32[]{:S(2)}, u32[]{:S(2)}) collective-permute-start(bf16[64,512]{1,0:T(8,128)(2,1)S(1)} %get-tuple-element.51), channel_id=1, source_target_pairs={{0,28},{4,24},{8,20},{12,16},{16,12},{20,8},{24,4},{28,0},{1,29},{... | collective-permute-start | bytes 196616 | tf_op jit(solution)/shard_map/ppermute | solution.py:117
  108.3 2.5 %collective-permute-done.16 = bf16[64,512]{1,0:T(8,128)(2,1)S(1)} collective-permute-done((bf16[64,512]{1,0:T(8,128)(2,1)S(1)}, bf16[64,512]{1,0:T(8,128)(2,1)S(1)}, u32[]{:S(2)}, u32[]{:S(2)}) %collective-permute-start.16) | collective-permute-done | bytes 65568 | tf_op jit(solution)/shard_map/ppermute | solution.py:117
  112.0 1.9 %collective-permute-start.27 = (bf16[64,512]{1,0:T(8,128)(2,1)S(1)}, bf16[64,512]{1,0:T(8,128)(2,1)S(1)}, u32[]{:S(2)}, u32[]{:S(2)}) collective-permute-start(bf16[64,512]{1,0:T(8,128)(2,1)S(1)} %get-tuple-element.57), channel_id=1, source_target_pairs={{0,4},{4,0},{8,12},{12,8},{16,20},{20,16},{24,28},{28,24},{1,5},{5... | collective-permute-start | bytes 196616 | tf_op jit(solution)/shard_map/ppermute | solution.py:117
  113.9 1.9 %collective-permute-start.28 = (bf16[64,512]{1,0:T(8,128)(2,1)S(1)}, bf16[64,512]{1,0:T(8,128)(2,1)S(1)}, u32[]{:S(2)}, u32[]{:S(2)}) collective-permute-start(bf16[64,512]{1,0:T(8,128)(2,1)S(1)} %get-tuple-element.56), channel_id=1, source_target_pairs={{0,16},{4,20},{8,24},{12,28},{16,0},{20,4},{24,8},{28,12},{1,17},{... | collective-permute-start | bytes 196616 | tf_op jit(solution)/shard_map/ppermute | solution.py:117
  116.3 2.8 %collective-permute-done.28 = bf16[64,512]{1,0:T(8,128)(2,1)S(1)} collective-permute-done((bf16[64,512]{1,0:T(8,128)(2,1)S(1)}, bf16[64,512]{1,0:T(8,128)(2,1)S(1)}, u32[]{:S(2)}, u32[]{:S(2)}) %collective-permute-start.28) | collective-permute-done | bytes 65568 | tf_op jit(solution)/shard_map/ppermute | solution.py:117
  (73 shorter events, 16.6 us)
Async XLA Ops:
  0.0 24.4 %copy-start.2 = (f32[128,2]{0,1:T(2,128)S(1)}, f32[128,2]{0,1:T(2,128)}, u32[]{:S(2)}) copy-start(f32[128,2]{0,1:T(2,128)} %param.30) | copy-start | bytes 3076
  2.8 16.9 %all-to-all-start = ((bf16[8,144,128]{2,1,0:T(8,128)(2,1)}), bf16[8,144,128]{2,1,0:T(8,128)(2,1)S(1)}, u32[]{:S(2)}, u32[]{:S(2)}) async-start(bf16[8,144,128]{2,1,0:T(8,128)(2,1)} %get-tuple-element.25), calls=%async_computation | async-start | bytes 589824 | tf_op jit(solution)/shard_map/all_to_all | solution.py:20
  20.6 12.1 %all-to-all-start.1 = ((bf16[8,128,128]{2,1,0:T(8,128)(2,1)}), bf16[8,128,128]{2,1,0:T(8,128)(2,1)S(1)}, u32[]{:S(2)}, u32[]{:S(2)}) async-start(bf16[8,128,128]{2,1,0:T(8,128)(2,1)} %prefix.1), calls=%async_computation.1 | async-start | bytes 524288 | tf_op jit(solution)/shard_map/all_to_all | solution.py:20
  35.9 1.4 %collective-permute-start.1 = (bf16[128,512]{1,0:T(8,128)(2,1)S(1)}, bf16[128,512]{1,0:T(8,128)(2,1)S(1)}, u32[]{:S(2)}, u32[]{:S(2)}) collective-permute-start(bf16[128,512]{1,0:T(8,128)(2,1)S(1)} %get-tuple-element.30), channel_id=1, source_target_pairs={{0,1},{1,0},{2,3},{3,2},{4,5},{5,4},{6,7},{7,6},{8,9},{9,8},{10,11... | collective-permute-start | bytes 393224 | tf_op jit(solution)/shard_map/ppermute | solution.py:16
  35.9 3.1 %collective-permute-start = (bf16[128,512]{1,0:T(8,128)(2,1)S(1)}, bf16[128,512]{1,0:T(8,128)(2,1)S(1)}, u32[]{:S(2)}, u32[]{:S(2)}) collective-permute-start(bf16[128,512]{1,0:T(8,128)(2,1)S(1)} %get-tuple-element.28), channel_id=1, source_target_pairs={{0,1},{1,0},{2,3},{3,2},{4,5},{5,4},{6,7},{7,6},{8,9},{9,8},{10,11... | collective-permute-start | bytes 393224 | tf_op jit(solution)/shard_map/ppermute | solution.py:16
  37.3 5.6 %collective-permute-start.2 = (bf16[128,512]{1,0:T(8,128)(2,1)S(1)}, bf16[128,512]{1,0:T(8,128)(2,1)S(1)}, u32[]{:S(2)}, u32[]{:S(2)}) collective-permute-start(bf16[128,512]{1,0:T(8,128)(2,1)S(1)} %add_convert_fusion.6), channel_id=1, source_target_pairs={{0,2},{1,3},{2,0},{3,1},{4,6},{5,7},{6,4},{7,5},{8,10},{9,11},{10,... | collective-permute-start | bytes 393224 | tf_op jit(solution)/shard_map/ppermute | solution.py:16
  43.4 7.7 %collective-permute-start.3 = (bf16[64,512]{1,0:T(8,128)(2,1)S(1)}, bf16[64,512]{1,0:T(8,128)(2,1)S(1)}, u32[]{:S(2)}, u32[]{:S(2)}) collective-permute-start(bf16[64,512]{1,0:T(8,128)(2,1)S(1)} %get-tuple-element.50), channel_id=1, source_target_pairs={{0,8},{4,12},{8,0},{12,4},{16,24},{20,28},{24,16},{28,20},{1,9},{5... | collective-permute-start | bytes 196616 | tf_op jit(solution)/shard_map/ppermute | solution.py:117
  44.6 6.6 %collective-permute-start.4 = (bf16[64,512]{1,0:T(8,128)(2,1)S(1)}, bf16[64,512]{1,0:T(8,128)(2,1)S(1)}, u32[]{:S(2)}, u32[]{:S(2)}) collective-permute-start(bf16[64,512]{1,0:T(8,128)(2,1)S(1)} %get-tuple-element.49), channel_id=1, source_target_pairs={{0,12},{4,8},{8,4},{12,0},{16,28},{20,24},{24,20},{28,16},{1,13},{... | collective-permute-start | bytes 196616 | tf_op jit(solution)/shard_map/ppermute | solution.py:117
  46.4 8.4 %collective-permute-start.5 = (bf16[64,512]{1,0:T(8,128)(2,1)S(1)}, bf16[64,512]{1,0:T(8,128)(2,1)S(1)}, u32[]{:S(2)}, u32[]{:S(2)}) collective-permute-start(bf16[64,512]{1,0:T(8,128)(2,1)S(1)} %get-tuple-element.48), channel_id=1, source_target_pairs={{0,20},{4,16},{8,28},{12,24},{16,4},{20,0},{24,12},{28,8},{1,21},{... | collective-permute-start | bytes 196616 | tf_op jit(solution)/shard_map/ppermute | solution.py:117
  47.4 7.4 %collective-permute-start.6 = (bf16[64,512]{1,0:T(8,128)(2,1)S(1)}, bf16[64,512]{1,0:T(8,128)(2,1)S(1)}, u32[]{:S(2)}, u32[]{:S(2)}) collective-permute-start(bf16[64,512]{1,0:T(8,128)(2,1)S(1)} %get-tuple-element.47), channel_id=1, source_target_pairs={{0,24},{4,28},{8,16},{12,20},{16,8},{20,12},{24,0},{28,4},{1,25},{... | collective-permute-start | bytes 196616 | tf_op jit(solution)/shard_map/ppermute | solution.py:117
  49.8 7.1 %collective-permute-start.7 = (bf16[64,512]{1,0:T(8,128)(2,1)S(1)}, bf16[64,512]{1,0:T(8,128)(2,1)S(1)}, u32[]{:S(2)}, u32[]{:S(2)}) collective-permute-start(bf16[64,512]{1,0:T(8,128)(2,1)S(1)} %get-tuple-element.46), channel_id=1, source_target_pairs={{0,28},{4,24},{8,20},{12,16},{16,12},{20,8},{24,4},{28,0},{1,29},{... | collective-permute-start | bytes 196616 | tf_op jit(solution)/shard_map/ppermute | solution.py:117
  56.9 7.1 %collective-permute-start.9 = (bf16[320,512]{1,0:T(8,128)(2,1)S(1)}, bf16[320,512]{1,0:T(8,128)(2,1)S(1)}, u32[]{:S(2)}, u32[]{:S(2)}) collective-permute-start(bf16[320,512]{1,0:T(8,128)(2,1)S(1)} %constant_dynamic-update-slice_fusion.own_in), channel_id=1, source_target_pairs={{0,2},{1,3},{2,0},{3,1},{4,6},{5,7},{6,4},{7,5},{8,10},{9,11},{10,... | collective-permute-start | bytes 983048 | tf_op jit(solution)/shard_map/ppermute | solution.py:16
  58.4 5.6 %collective-permute-start.8 = (bf16[320,512]{1,0:T(8,128)(2,1)S(1)}, bf16[320,512]{1,0:T(8,128)(2,1)S(1)}, u32[]{:S(2)}, u32[]{:S(2)}) collective-permute-start(bf16[320,512]{1,0:T(8,128)(2,1)S(1)} %constant_dynamic-update-slice_fusion.own_in), channel_id=1, source_target_pairs={{0,1},{1,0},{2,3},{3,2},{4,5},{5,4},{6,7},{7,6},{8,9},{9,8},{10,11... | collective-permute-start | bytes 983048 | tf_op jit(solution)/shard_map/ppermute | solution.py:16
  64.0 1.6 %collective-permute-start.10 = (bf16[320,512]{1,0:T(8,128)(2,1)S(1)}, bf16[320,512]{1,0:T(8,128)(2,1)S(1)}, u32[]{:S(2)}, u32[]{:S(2)}) collective-permute-start(bf16[320,512]{1,0:T(8,128)(2,1)S(1)} %collective-permute-done.9.far_in), channel_id=1, source_target_pairs={{0,1},{1,0},{2,3},{3,2},{4,5},{5,4},{6,7},{7,6},{8,9},{9,8},{10,11... | collective-permute-start | bytes 983048 | tf_op jit(solution)/shard_map/ppermute | solution.py:16
  70.3 8.2 %collective-permute-start.11 = (bf16[320,512]{1,0:T(8,128)(2,1)S(1)}, bf16[320,512]{1,0:T(8,128)(2,1)S(1)}, u32[]{:S(2)}, u32[]{:S(2)}) collective-permute-start(bf16[320,512]{1,0:T(8,128)(2,1)S(1)} %get-tuple-element.34), channel_id=1, source_target_pairs={{0,1},{1,0},{2,3},{3,2},{4,5},{5,4},{6,7},{7,6},{8,9},{9,8},{10,11... | collective-permute-start | bytes 983048 | tf_op jit(solution)/shard_map/ppermute | solution.py:16
  70.5 5.3 %collective-permute-start.20 = (bf16[64,512]{1,0:T(8,128)(2,1)S(1)}, bf16[64,512]{1,0:T(8,128)(2,1)S(1)}, u32[]{:S(2)}, u32[]{:S(2)}) collective-permute-start(bf16[64,512]{1,0:T(8,128)(2,1)S(1)} %get-tuple-element.44), channel_id=1, source_target_pairs={{0,16},{4,20},{8,24},{12,28},{16,0},{20,4},{24,8},{28,12},{1,17},{... | collective-permute-start | bytes 196616 | tf_op jit(solution)/shard_map/ppermute | solution.py:117
  72.6 4.4 %collective-permute-start.19 = (bf16[64,512]{1,0:T(8,128)(2,1)S(1)}, bf16[64,512]{1,0:T(8,128)(2,1)S(1)}, u32[]{:S(2)}, u32[]{:S(2)}) collective-permute-start(bf16[64,512]{1,0:T(8,128)(2,1)S(1)} %get-tuple-element.45), channel_id=1, source_target_pairs={{0,4},{4,0},{8,12},{12,8},{16,20},{20,16},{24,28},{28,24},{1,5},{5... | collective-permute-start | bytes 196616 | tf_op jit(solution)/shard_map/ppermute | solution.py:117
  77.0 7.9 %collective-permute-start.22 = (bf16[192,512]{1,0:T(8,128)(2,1)S(1)}, bf16[192,512]{1,0:T(8,128)(2,1)S(1)}, u32[]{:S(2)}, u32[]{:S(2)}) collective-permute-start(bf16[192,512]{1,0:T(8,128)(2,1)S(1)} %pad_maximum_fusion.own_in), channel_id=1, source_target_pairs={{0,2},{1,3},{2,0},{3,1},{4,6},{5,7},{6,4},{7,5},{8,10},{9,11},{10,... | collective-permute-start | bytes 589832 | tf_op jit(solution)/shard_map/ppermute | solution.py:16
  78.7 12.4 %collective-permute-start.12 = (bf16[320,512]{1,0:T(8,128)(2,1)S(1)}, bf16[320,512]{1,0:T(8,128)(2,1)S(1)}, u32[]{:S(2)}, u32[]{:S(2)}) collective-permute-start(bf16[320,512]{1,0:T(8,128)(2,1)S(1)} %add_convert_fusion.1), channel_id=1, source_target_pairs={{0,2},{1,3},{2,0},{3,1},{4,6},{5,7},{6,4},{7,5},{8,10},{9,11},{10,... | collective-permute-start | bytes 983048 | tf_op jit(solution)/shard_map/ppermute | solution.py:16
  79.2 5.6 %collective-permute-start.21 = (bf16[192,512]{1,0:T(8,128)(2,1)S(1)}, bf16[192,512]{1,0:T(8,128)(2,1)S(1)}, u32[]{:S(2)}, u32[]{:S(2)}) collective-permute-start(bf16[192,512]{1,0:T(8,128)(2,1)S(1)} %pad_maximum_fusion.own_in), channel_id=1, source_target_pairs={{0,1},{1,0},{2,3},{3,2},{4,5},{5,4},{6,7},{7,6},{8,9},{9,8},{10,11... | collective-permute-start | bytes 589832 | tf_op jit(solution)/shard_map/ppermute | solution.py:16
  84.9 1.4 %collective-permute-start.23 = (bf16[192,512]{1,0:T(8,128)(2,1)S(1)}, bf16[192,512]{1,0:T(8,128)(2,1)S(1)}, u32[]{:S(2)}, u32[]{:S(2)}) collective-permute-start(bf16[192,512]{1,0:T(8,128)(2,1)S(1)} %collective-permute-done.22.far_in), channel_id=1, source_target_pairs={{0,1},{1,0},{2,3},{3,2},{4,5},{5,4},{6,7},{7,6},{8,9},{9,8},{10,11... | collective-permute-start | bytes 589832 | tf_op jit(solution)/shard_map/ppermute | solution.py:16
  90.8 1.5 %collective-permute-start.24 = (bf16[192,512]{1,0:T(8,128)(2,1)S(1)}, bf16[192,512]{1,0:T(8,128)(2,1)S(1)}, u32[]{:S(2)}, u32[]{:S(2)}) collective-permute-start(bf16[192,512]{1,0:T(8,128)(2,1)S(1)} %get-tuple-element.41), channel_id=1, source_target_pairs={{0,1},{1,0},{2,3},{3,2},{4,5},{5,4},{6,7},{7,6},{8,9},{9,8},{10,11... | collective-permute-start | bytes 589832 | tf_op jit(solution)/shard_map/ppermute | solution.py:16
  91.0 2.9 %collective-permute-start.13 = (bf16[320,512]{1,0:T(8,128)(2,1)S(1)}, bf16[320,512]{1,0:T(8,128)(2,1)S(1)}, u32[]{:S(2)}, u32[]{:S(2)}) collective-permute-start(bf16[320,512]{1,0:T(8,128)(2,1)S(1)} %get-tuple-element.35), channel_id=1, source_target_pairs={{0,1},{1,0},{2,3},{3,2},{4,5},{5,4},{6,7},{7,6},{8,9},{9,8},{10,11... | collective-permute-start | bytes 983048 | tf_op jit(solution)/shard_map/ppermute | solution.py:16
  92.4 7.0 %collective-permute-start.26 = (bf16[192,512]{1,0:T(8,128)(2,1)S(1)}, bf16[192,512]{1,0:T(8,128)(2,1)S(1)}, u32[]{:S(2)}, u32[]{:S(2)}) collective-permute-start(bf16[192,512]{1,0:T(8,128)(2,1)S(1)} %add_convert_fusion.3), channel_id=1, source_target_pairs={{0,2},{1,3},{2,0},{3,1},{4,6},{5,7},{6,4},{7,5},{8,10},{9,11},{10,... | collective-permute-start | bytes 589832 | tf_op jit(solution)/shard_map/ppermute | solution.py:16
  94.0 5.4 %collective-permute-start.25 = (bf16[192,512]{1,0:T(8,128)(2,1)S(1)}, bf16[192,512]{1,0:T(8,128)(2,1)S(1)}, u32[]{:S(2)}, u32[]{:S(2)}) collective-permute-start(bf16[192,512]{1,0:T(8,128)(2,1)S(1)} %get-tuple-element.42), channel_id=1, source_target_pairs={{0,1},{1,0},{2,3},{3,2},{4,5},{5,4},{6,7},{7,6},{8,9},{9,8},{10,11... | collective-permute-start | bytes 589832 | tf_op jit(solution)/shard_map/ppermute | solution.py:16
  94.1 14.1 %collective-permute-start.14 = (bf16[64,512]{1,0:T(8,128)(2,1)S(1)}, bf16[64,512]{1,0:T(8,128)(2,1)S(1)}, u32[]{:S(2)}, u32[]{:S(2)}) collective-permute-start(bf16[64,512]{1,0:T(8,128)(2,1)S(1)} %get-tuple-element.55), channel_id=1, source_target_pairs={{0,8},{4,12},{8,0},{12,4},{16,24},{20,28},{24,16},{28,20},{1,9},{5... | collective-permute-start | bytes 196616 | tf_op jit(solution)/shard_map/ppermute | solution.py:117
  99.5 8.8 %collective-permute-start.15 = (bf16[64,512]{1,0:T(8,128)(2,1)S(1)}, bf16[64,512]{1,0:T(8,128)(2,1)S(1)}, u32[]{:S(2)}, u32[]{:S(2)}) collective-permute-start(bf16[64,512]{1,0:T(8,128)(2,1)S(1)} %get-tuple-element.54), channel_id=1, source_target_pairs={{0,12},{4,8},{8,4},{12,0},{16,28},{20,24},{24,20},{28,16},{1,13},{... | collective-permute-start | bytes 196616 | tf_op jit(solution)/shard_map/ppermute | solution.py:117
  100.8 9.9 %collective-permute-start.16 = (bf16[64,512]{1,0:T(8,128)(2,1)S(1)}, bf16[64,512]{1,0:T(8,128)(2,1)S(1)}, u32[]{:S(2)}, u32[]{:S(2)}) collective-permute-start(bf16[64,512]{1,0:T(8,128)(2,1)S(1)} %get-tuple-element.53), channel_id=1, source_target_pairs={{0,20},{4,16},{8,28},{12,24},{16,4},{20,0},{24,12},{28,8},{1,21},{... | collective-permute-start | bytes 196616 | tf_op jit(solution)/shard_map/ppermute | solution.py:117
  104.9 6.2 %collective-permute-start.17 = (bf16[64,512]{1,0:T(8,128)(2,1)S(1)}, bf16[64,512]{1,0:T(8,128)(2,1)S(1)}, u32[]{:S(2)}, u32[]{:S(2)}) collective-permute-start(bf16[64,512]{1,0:T(8,128)(2,1)S(1)} %get-tuple-element.52), channel_id=1, source_target_pairs={{0,24},{4,28},{8,16},{12,20},{16,8},{20,12},{24,0},{28,4},{1,25},{... | collective-permute-start | bytes 196616 | tf_op jit(solution)/shard_map/ppermute | solution.py:117
  104.9 7.1 %collective-permute-start.18 = (bf16[64,512]{1,0:T(8,128)(2,1)S(1)}, bf16[64,512]{1,0:T(8,128)(2,1)S(1)}, u32[]{:S(2)}, u32[]{:S(2)}) collective-permute-start(bf16[64,512]{1,0:T(8,128)(2,1)S(1)} %get-tuple-element.51), channel_id=1, source_target_pairs={{0,28},{4,24},{8,20},{12,16},{16,12},{20,8},{24,4},{28,0},{1,29},{... | collective-permute-start | bytes 196616 | tf_op jit(solution)/shard_map/ppermute | solution.py:117
  112.0 4.3 %collective-permute-start.27 = (bf16[64,512]{1,0:T(8,128)(2,1)S(1)}, bf16[64,512]{1,0:T(8,128)(2,1)S(1)}, u32[]{:S(2)}, u32[]{:S(2)}) collective-permute-start(bf16[64,512]{1,0:T(8,128)(2,1)S(1)} %get-tuple-element.57), channel_id=1, source_target_pairs={{0,4},{4,0},{8,12},{12,8},{16,20},{20,16},{24,28},{28,24},{1,5},{5... | collective-permute-start | bytes 196616 | tf_op jit(solution)/shard_map/ppermute | solution.py:117
  113.9 5.2 %collective-permute-start.28 = (bf16[64,512]{1,0:T(8,128)(2,1)S(1)}, bf16[64,512]{1,0:T(8,128)(2,1)S(1)}, u32[]{:S(2)}, u32[]{:S(2)}) collective-permute-start(bf16[64,512]{1,0:T(8,128)(2,1)S(1)} %get-tuple-element.56), channel_id=1, source_target_pairs={{0,16},{4,20},{8,24},{12,28},{16,0},{20,4},{24,8},{28,12},{1,17},{... | collective-permute-start | bytes 196616 | tf_op jit(solution)/shard_map/ppermute | solution.py:117
  (3 other events, 37.2 us)

commit v13 on v12

--- a/solution.py
+++ b/solution.py
@@ -104,10 +104,10 @@
             carries[h] = factor * carries[h] + got[turn, spot, :].astype(F32)
 
 
-PARTS = ((2, 3, 5, 6, 7), (0, 1, 4))
-
-
-def exchange_parts(pieces):
+PARTS = ((0, 1, 4, 5), (6, 7, 2, 3))
+
+
+def exchange_parts(pieces, early=False):
     parts = []
     for order, part in zip(PARTS, pieces):
         got = []
@@ -116,8 +116,10 @@
             if k > 0:
                 piece = lax.ppermute(piece, "seq", [(i, i ^ k) for i in range(8)])
             got.append(piece)
-        parts.append(jnp.concatenate(got))
-    return parts
+        parts.append(got)
+    if early:
+        parts[0][0] = after(parts[0][0], parts[1][0])
+    return [jnp.concatenate(got) for got in parts]
 
 
 def entering_state(got, init_rows):
@@ -399,7 +401,7 @@
     middle = len(PARTS[0]) if few else expert_count // 2
     cut = middle * slot_count
     if few:
-        own = exchange_parts((outgoing[:middle], outgoing[middle:]))
+        own = exchange_parts((outgoing[:middle], outgoing[middle:]), early=True)
     else:
         arrived = exchange(outgoing).reshape(slots, share)
         own = [arrived[:cut], arrived[cut:]]

time: 121 us -> 102 us (0.84)
  waiting for transfers between devices: 53 us -> 41 us
  starting transfers between devices: 46.1 us -> 40.9 us
    ppermute x15, waiting for transfers between devices: 22.6 us -> 12.5 us  [swap(): return lax.ppermute(value, 'tp', [(i, i ^ bit) for i in range(count)])]
    ppermute x14, starting transfers between devices: 27.1 us -> 21.7 us  [exchange_parts(): piece = lax.ppermute(piece, 'seq', [(i, i ^ k) for i in range(8)])]
    ppermute x14, waiting for transfers between devices: 15 us -> 13.1 us  [exchange_parts(): piece = lax.ppermute(piece, 'seq', [(i, i ^ k) for i in range(8)])]
    pallas_call x2, Pallas kernels: 9.18 us -> 7.96 us  [run_expert(): pl.pallas_call(expert_kernel, in_specs=[pl.BlockSpec(memory_space=pltpu.S...]
  transfers between devices with their start and end apart: 31 -> 31, of which waited for: 19 -> 16; matrix products, arithmetic and copies ran while one was open for 1% -> 1% of each run, Pallas kernels for 5% -> 9%
where the time goes in v13:
time: 102 us
  waiting for transfers between devices  41 us (40%)
  starting transfers between devices  40.9 us (40%)
  Pallas kernels  16.5 us (16%)
  matrix products  1.58 us (2%)
    ppermute x14, starting transfers between devices, exchange_parts(): piece = lax.ppermute(piece, 'seq', [(i, i ^ k) for i in range(8)])  21.7 us
    all_to_all x2, waiting for transfers between devices, exchange(): return lax.all_to_all(value, 'seq', split_axis=0, concat_axis=0, tiled=True)  15.4 us
    ppermute x14, waiting for transfers between devices, exchange_parts(): piece = lax.ppermute(piece, 'seq', [(i, i ^ k) for i in range(8)])  13.1 us
    ppermute x15, waiting for transfers between devices, swap(): return lax.ppermute(value, 'tp', [(i, i ^ bit) for i in range(count)])  12.5 us
    all_to_all x2, starting transfers between devices, exchange(): return lax.all_to_all(value, 'seq', split_axis=0, concat_axis=0, tiled=True)  10.8 us
    ppermute x15, starting transfers between devices, swap(): return lax.ppermute(value, 'tp', [(i, i ^ bit) for i in range(count)])  8.35 us
    pallas_call x2, Pallas kernels, run_expert(): pl.pallas_call(expert_kernel, in_specs=[pl.BlockSpec(memory_space=pltpu.S...  7.96 us
    pallas_call x1, Pallas kernels, mixer_tail(): pl.pallas_call(tail_kernel, in_specs=[pl.BlockSpec(memory_space=pltpu.SME...  3.17 us
  transfers between devices with their start and end apart: 31, of which 16 were waited for; matrix products, arithmetic and copies ran while one was open for 1% of the time, Pallas kernels for 9%

profile of v13, /device:TPU:0, one launch (start us, length us, event | category | flops | bytes accessed | tf_op | source)
XLA Modules:
  0.0 101.7 jit_solution(16517848820440207336)
XLA Ops:
  0.0 2.8 %own_state.1 = (bf16[8,144,128]{2,1,0:T(8,128)(2,1)}, f32[16,128]{1,0:T(8,128)S(1)}) custom-call(bf16[128,1024]{1,0:T(8,128)(2,1)} %x.3, f32[16,128]{1,0:T(8,128)} %bitcast.34, f32[16,128]{1,0:T(8,128)} %bitcast.36, bf16[128,128]{1,0:T(8,128)(2,1)} %b.3), custom_call_target="tpu_custom_call" | custom-call | tf_op jit(solution)/shard_map/own_state/pallas_call | solution.py:78
  2.8 7.3 %all-to-all-start = ((bf16[8,144,128]{2,1,0:T(8,128)(2,1)}), bf16[8,144,128]{2,1,0:T(8,128)(2,1)S(1)}, u32[]{:S(2)}, u32[]{:S(2)}) async-start(bf16[8,144,128]{2,1,0:T(8,128)(2,1)} %get-tuple-element.26), calls=%async_computation | async-start | bytes 589824 | tf_op jit(solution)/shard_map/all_to_all | solution.py:20
  10.7 1.7 %within_block.1.direct_in = f32[128,1024]{1,0:T(8,128)S(1)} custom-call(f32[16]{0:T(128)S(1)} %copy-done.1, bf16[128,1024]{1,0:T(8,128)(2,1)} %x.3, f32[16,128]{1,0:T(8,128)} %bitcast.35, f32[16,128]{1,0:T(8,128)S(1)} %get-tuple-element.25.cum_t.cum_in, bf16[128,128]{1,0:T(8,128)(2,1)} %b.3, bf16[128,128]{1,0:T(8,128)(2,1)} %c_in.1), custom_call_target="tpu_custom_call" | custom-call | flops 134217728 | bytes 786432 | tf_op jit(solution)/shard_map/within_block/pallas_call | solution.py:166
  12.4 7.3 %all-to-all-done.got = bf16[8,144,128]{2,1,0:T(8,128)(2,1)S(1)} async-done(((bf16[8,144,128]{2,1,0:T(8,128)(2,1)}), bf16[8,144,128]{2,1,0:T(8,128)(2,1)S(1)}, u32[]{:S(2)}, u32[]{:S(2)}) %all-to-all-start) | async-done | bytes 294944 | tf_op jit(solution)/shard_map/all_to_all | solution.py:20
  20.6 3.6 %all-to-all-start.1 = ((bf16[8,128,128]{2,1,0:T(8,128)(2,1)}), bf16[8,128,128]{2,1,0:T(8,128)(2,1)S(1)}, u32[]{:S(2)}, u32[]{:S(2)}) async-start(bf16[8,128,128]{2,1,0:T(8,128)(2,1)} %prefix.1), calls=%async_computation.1 | async-start | bytes 524288 | tf_op jit(solution)/shard_map/all_to_all | solution.py:20
  24.5 8.1 %all-to-all-done.1 = bf16[8,128,128]{2,1,0:T(8,128)(2,1)S(1)} async-done(((bf16[8,128,128]{2,1,0:T(8,128)(2,1)}), bf16[8,128,128]{2,1,0:T(8,128)(2,1)S(1)}, u32[]{:S(2)}, u32[]{:S(2)}) %all-to-all-start.1) | async-done | bytes 262176 | tf_op jit(solution)/shard_map/all_to_all | solution.py:20
  32.7 3.2 %mixer_tail.1 = (bf16[128,512]{1,0:T(8,128)(2,1)S(1)}, bf16[128,512]{1,0:T(8,128)(2,1)S(1)}, f32[128,512]{1,0:T(8,128)S(1)}, f32[128,512]{1,0:T(8,128)S(1)}) custom-call(s32[1]{0:T(128)} %bitcast.place_ref, bf16[128,128]{1,0:T(8,128)(2,1)} %c_in.1, f32[16,128]{1,0:T(8,128)S(1)} %get-tuple-element.25.cum_t.cum_in, f32[1,1024]{1,0:T(1,128)} %bitcast.37, ...), custom_call_target="tpu_custom_call" | custom-call | flops 536870912 | bytes 6029312 | tf_op jit(solution)/shard_map/mixer_tail/pallas_call | solution.py:248
  37.3 1.6 %collective-permute-start.2 = (bf16[128,512]{1,0:T(8,128)(2,1)S(1)}, bf16[128,512]{1,0:T(8,128)(2,1)S(1)}, u32[]{:S(2)}, u32[]{:S(2)}) collective-permute-start(bf16[128,512]{1,0:T(8,128)(2,1)S(1)} %add_convert_fusion.6), channel_id=1, source_target_pairs={{0,2},{1,3},{2,0},{3,1},{4,6},{5,7},{6,4},{7,5},{8,10},{9,11},{10,... | collective-permute-start | bytes 393224 | tf_op jit(solution)/shard_map/ppermute | solution.py:16
  39.0 3.9 %collective-permute-done.2 = bf16[128,512]{1,0:T(8,128)(2,1)S(1)} collective-permute-done((bf16[128,512]{1,0:T(8,128)(2,1)S(1)}, bf16[128,512]{1,0:T(8,128)(2,1)S(1)}, u32[]{:S(2)}, u32[]{:S(2)}) %collective-permute-start.2) | collective-permute-done | bytes 131104 | tf_op jit(solution)/shard_map/ppermute | solution.py:16
  43.4 1.2 %collective-permute-start.3 = (bf16[64,512]{1,0:T(8,128)(2,1)S(1)}, bf16[64,512]{1,0:T(8,128)(2,1)S(1)}, u32[]{:S(2)}, u32[]{:S(2)}) collective-permute-start(bf16[64,512]{1,0:T(8,128)(2,1)S(1)} %get-tuple-element.51), channel_id=1, source_target_pairs={{0,24},{4,28},{8,16},{12,20},{16,8},{20,12},{24,0},{28,4},{1,25},{... | collective-permute-start | bytes 196616 | tf_op jit(solution)/shard_map/ppermute | solution.py:117
  44.6 1.7 %collective-permute-start.4 = (bf16[64,512]{1,0:T(8,128)(2,1)S(1)}, bf16[64,512]{1,0:T(8,128)(2,1)S(1)}, u32[]{:S(2)}, u32[]{:S(2)}) collective-permute-start(bf16[64,512]{1,0:T(8,128)(2,1)S(1)} %get-tuple-element.50), channel_id=1, source_target_pairs={{0,4},{4,0},{8,12},{12,8},{16,20},{20,16},{24,28},{28,24},{1,5},{5... | collective-permute-start | bytes 196616 | tf_op jit(solution)/shard_map/ppermute | solution.py:117
  46.4 2.6 %collective-permute-start.6 = (bf16[64,512]{1,0:T(8,128)(2,1)S(1)}, bf16[64,512]{1,0:T(8,128)(2,1)S(1)}, u32[]{:S(2)}, u32[]{:S(2)}) collective-permute-start(bf16[64,512]{1,0:T(8,128)(2,1)S(1)} %get-tuple-element.48), channel_id=1, source_target_pairs={{0,20},{4,16},{8,28},{12,24},{16,4},{20,0},{24,12},{28,8},{1,21},{... | collective-permute-start | bytes 196616 | tf_op jit(solution)/shard_map/ppermute | solution.py:117
  49.8 3.5 %collective-permute-done.5 = bf16[64,512]{1,0:T(8,128)(2,1)S(1)} collective-permute-done((bf16[64,512]{1,0:T(8,128)(2,1)S(1)}, bf16[64,512]{1,0:T(8,128)(2,1)S(1)}, u32[]{:S(2)}, u32[]{:S(2)}) %collective-permute-start.5) | collective-permute-done | bytes 65568 | tf_op jit(solution)/shard_map/ppermute | solution.py:117
  53.3 1.8 %collective-permute-done.6 = bf16[64,512]{1,0:T(8,128)(2,1)S(1)} collective-permute-done((bf16[64,512]{1,0:T(8,128)(2,1)S(1)}, bf16[64,512]{1,0:T(8,128)(2,1)S(1)}, u32[]{:S(2)}, u32[]{:S(2)}) %collective-permute-start.6) | collective-permute-done | bytes 65568 | tf_op jit(solution)/shard_map/ppermute | solution.py:117
  55.1 1.5 %collective-permute-start.8 = (bf16[256,512]{1,0:T(8,128)(2,1)S(1)}, bf16[256,512]{1,0:T(8,128)(2,1)S(1)}, u32[]{:S(2)}, u32[]{:S(2)}) collective-permute-start(bf16[256,512]{1,0:T(8,128)(2,1)S(1)} %constant_dynamic-update-slice_fusion.own_in), channel_id=1, source_target_pairs={{0,2},{1,3},{2,0},{3,1},{4,6},{5,7},{6,4},{7,5},{8,10},{9,11},{10,... | collective-permute-start | bytes 786440 | tf_op jit(solution)/shard_map/ppermute | solution.py:16
  56.6 1.9 %collective-permute-start.16 = (bf16[64,512]{1,0:T(8,128)(2,1)S(1)}, bf16[64,512]{1,0:T(8,128)(2,1)S(1)}, u32[]{:S(2)}, u32[]{:S(2)}) collective-permute-start(bf16[64,512]{1,0:T(8,128)(2,1)S(1)} %get-tuple-element.47), channel_id=1, source_target_pairs={{0,28},{4,24},{8,20},{12,16},{16,12},{20,8},{24,4},{28,0},{1,29},{... | collective-permute-start | bytes 196616 | tf_op jit(solution)/shard_map/ppermute | solution.py:117
  58.5 2.9 %collective-permute-start.18 = (bf16[64,512]{1,0:T(8,128)(2,1)S(1)}, bf16[64,512]{1,0:T(8,128)(2,1)S(1)}, u32[]{:S(2)}, u32[]{:S(2)}) collective-permute-start(bf16[64,512]{1,0:T(8,128)(2,1)S(1)} %get-tuple-element.45), channel_id=1, source_target_pairs={{0,12},{4,8},{8,4},{12,0},{16,28},{20,24},{24,20},{28,16},{1,13},{... | collective-permute-start | bytes 196616 | tf_op jit(solution)/shard_map/ppermute | solution.py:117
  62.5 1.2 %collective-permute-done.16 = bf16[64,512]{1,0:T(8,128)(2,1)S(1)} collective-permute-done((bf16[64,512]{1,0:T(8,128)(2,1)S(1)}, bf16[64,512]{1,0:T(8,128)(2,1)S(1)}, u32[]{:S(2)}, u32[]{:S(2)}) %collective-permute-start.16) | collective-permute-done | bytes 65568 | tf_op jit(solution)/shard_map/ppermute | solution.py:117
  63.7 1.3 %collective-permute-done.18 = bf16[64,512]{1,0:T(8,128)(2,1)S(1)} collective-permute-done((bf16[64,512]{1,0:T(8,128)(2,1)S(1)}, bf16[64,512]{1,0:T(8,128)(2,1)S(1)}, u32[]{:S(2)}, u32[]{:S(2)}) %collective-permute-start.18) | collective-permute-done | bytes 65568 | tf_op jit(solution)/shard_map/ppermute | solution.py:117
  65.5 4.0 %expert.2 = (bf16[256,512]{1,0:T(8,128)(2,1)S(1)}, bf16[256,512]{1,0:T(8,128)(2,1)S(1)}, bf16[256,512]{1,0:T(8,128)(2,1)S(1)}, bf16[256,512]{1,0:T(8,128)(2,1)S(1)}) custom-call(s32[1]{0:T(128)} %bitcast.place_ref, f32[1,2048]{1,0:T(1,128)} %bitcast.32, bf16[256,512]{1,0:T(8,128)(2,1)S(1)} %constant_dynamic-update-slice_fusion.own_in, ...), custom_call_target="tpu_custom_call" | custom-call | flops 1 | bytes 1 | tf_op jit(solution)/shard_map/expert/pallas_call | solution.py:317
  70.1 1.3 %collective-permute-done.20.far_in = bf16[256,512]{1,0:T(8,128)(2,1)S(1)} collective-permute-done((bf16[256,512]{1,0:T(8,128)(2,1)S(1)}, bf16[256,512]{1,0:T(8,128)(2,1)S(1)}, u32[]{:S(2)}, u32[]{:S(2)}) %collective-permute-start.20) | collective-permute-done | bytes 262176 | tf_op jit(solution)/shard_map/ppermute | solution.py:16
  71.4 1.5 %collective-permute-start.11 = (bf16[256,512]{1,0:T(8,128)(2,1)S(1)}, bf16[256,512]{1,0:T(8,128)(2,1)S(1)}, u32[]{:S(2)}, u32[]{:S(2)}) collective-permute-start(bf16[256,512]{1,0:T(8,128)(2,1)S(1)} %add_convert_fusion.3), channel_id=1, source_target_pairs={{0,2},{1,3},{2,0},{3,1},{4,6},{5,7},{6,4},{7,5},{8,10},{9,11},{10,... | collective-permute-start | bytes 786440 | tf_op jit(solution)/shard_map/ppermute | solution.py:16
  73.0 4.0 %expert.3 = (bf16[256,512]{1,0:T(8,128)(2,1)S(1)}, bf16[256,512]{1,0:T(8,128)(2,1)S(1)}, bf16[256,512]{1,0:T(8,128)(2,1)S(1)}, bf16[256,512]{1,0:T(8,128)(2,1)S(1)}) custom-call(s32[1]{0:T(128)} %bitcast.place_ref, f32[1,2048]{1,0:T(1,128)} %bitcast.33, bf16[256,512]{1,0:T(8,128)(2,1)S(1)} %constant_dynamic-update-slice_fusion.4.own_in, ...), custom_call_target="tpu_custom_call" | custom-call | flops 1 | bytes 1 | tf_op jit(solution)/shard_map/expert/pallas_call | solution.py:317
  77.3 3.0 %collective-permute-done.11 = bf16[256,512]{1,0:T(8,128)(2,1)S(1)} collective-permute-done((bf16[256,512]{1,0:T(8,128)(2,1)S(1)}, bf16[256,512]{1,0:T(8,128)(2,1)S(1)}, u32[]{:S(2)}, u32[]{:S(2)}) %collective-permute-start.11) | collective-permute-done | bytes 262176 | tf_op jit(solution)/shard_map/ppermute | solution.py:16
  80.3 1.5 %collective-permute-start.24 = (bf16[256,512]{1,0:T(8,128)(2,1)S(1)}, bf16[256,512]{1,0:T(8,128)(2,1)S(1)}, u32[]{:S(2)}, u32[]{:S(2)}) collective-permute-start(bf16[256,512]{1,0:T(8,128)(2,1)S(1)} %add_convert_fusion.1), channel_id=1, source_target_pairs={{0,2},{1,3},{2,0},{3,1},{4,6},{5,7},{6,4},{7,5},{8,10},{9,11},{10,... | collective-permute-start | bytes 786440 | tf_op jit(solution)/shard_map/ppermute | solution.py:16
  82.2 2.0 %collective-permute-start.13 = (bf16[64,512]{1,0:T(8,128)(2,1)S(1)}, bf16[64,512]{1,0:T(8,128)(2,1)S(1)}, u32[]{:S(2)}, u32[]{:S(2)}) collective-permute-start(bf16[64,512]{1,0:T(8,128)(2,1)S(1)} %get-tuple-element.59), channel_id=1, source_target_pairs={{0,4},{4,0},{8,12},{12,8},{16,20},{20,16},{24,28},{28,24},{1,5},{5... | collective-permute-start | bytes 196616 | tf_op jit(solution)/shard_map/ppermute | solution.py:117
  84.6 2.0 %collective-permute-start.15 = (bf16[64,512]{1,0:T(8,128)(2,1)S(1)}, bf16[64,512]{1,0:T(8,128)(2,1)S(1)}, u32[]{:S(2)}, u32[]{:S(2)}) collective-permute-start(bf16[64,512]{1,0:T(8,128)(2,1)S(1)} %get-tuple-element.57), channel_id=1, source_target_pairs={{0,20},{4,16},{8,28},{12,24},{16,4},{20,0},{24,12},{28,8},{1,21},{... | collective-permute-start | bytes 196616 | tf_op jit(solution)/shard_map/ppermute | solution.py:117
  86.6 2.4 %collective-permute-done.24 = bf16[256,512]{1,0:T(8,128)(2,1)S(1)} collective-permute-done((bf16[256,512]{1,0:T(8,128)(2,1)S(1)}, bf16[256,512]{1,0:T(8,128)(2,1)S(1)}, u32[]{:S(2)}, u32[]{:S(2)}) %collective-permute-start.24) | collective-permute-done | bytes 262176 | tf_op jit(solution)/shard_map/ppermute | solution.py:16
  89.2 2.0 %collective-permute-start.25 = (bf16[64,512]{1,0:T(8,128)(2,1)S(1)}, bf16[64,512]{1,0:T(8,128)(2,1)S(1)}, u32[]{:S(2)}, u32[]{:S(2)}) collective-permute-start(bf16[64,512]{1,0:T(8,128)(2,1)S(1)} %get-tuple-element.56), channel_id=1, source_target_pairs={{0,24},{4,28},{8,16},{12,20},{16,8},{20,12},{24,0},{28,4},{1,25},{... | collective-permute-start | bytes 196616 | tf_op jit(solution)/shard_map/ppermute | solution.py:117
  91.2 3.1 %collective-permute-start.26 = (bf16[64,512]{1,0:T(8,128)(2,1)S(1)}, bf16[64,512]{1,0:T(8,128)(2,1)S(1)}, u32[]{:S(2)}, u32[]{:S(2)}) collective-permute-start(bf16[64,512]{1,0:T(8,128)(2,1)S(1)} %get-tuple-element.55), channel_id=1, source_target_pairs={{0,28},{4,24},{8,20},{12,16},{16,12},{20,8},{24,4},{28,0},{1,29},{... | collective-permute-start | bytes 196616 | tf_op jit(solution)/shard_map/ppermute | solution.py:117
  94.3 1.8 %collective-permute-start.28 = (bf16[64,512]{1,0:T(8,128)(2,1)S(1)}, bf16[64,512]{1,0:T(8,128)(2,1)S(1)}, u32[]{:S(2)}, u32[]{:S(2)}) collective-permute-start(bf16[64,512]{1,0:T(8,128)(2,1)S(1)} %get-tuple-element.53), channel_id=1, source_target_pairs={{0,12},{4,8},{8,4},{12,0},{16,28},{20,24},{24,20},{28,16},{1,13},{... | collective-permute-start | bytes 196616 | tf_op jit(solution)/shard_map/ppermute | solution.py:117
  96.2 2.5 %collective-permute-done.26 = bf16[64,512]{1,0:T(8,128)(2,1)S(1)} collective-permute-done((bf16[64,512]{1,0:T(8,128)(2,1)S(1)}, bf16[64,512]{1,0:T(8,128)(2,1)S(1)}, u32[]{:S(2)}, u32[]{:S(2)}) %collective-permute-start.26) | collective-permute-done | bytes 65568 | tf_op jit(solution)/shard_map/ppermute | solution.py:117
  (75 shorter events, 11.4 us)
Async XLA Ops:
  0.0 24.4 %copy-start.2 = (f32[128,2]{0,1:T(2,128)S(1)}, f32[128,2]{0,1:T(2,128)}, u32[]{:S(2)}) copy-start(f32[128,2]{0,1:T(2,128)} %param.30) | copy-start | bytes 3076
  2.8 16.9 %all-to-all-start = ((bf16[8,144,128]{2,1,0:T(8,128)(2,1)}), bf16[8,144,128]{2,1,0:T(8,128)(2,1)S(1)}, u32[]{:S(2)}, u32[]{:S(2)}) async-start(bf16[8,144,128]{2,1,0:T(8,128)(2,1)} %get-tuple-element.26), calls=%async_computation | async-start | bytes 589824 | tf_op jit(solution)/shard_map/all_to_all | solution.py:20
  20.6 12.1 %all-to-all-start.1 = ((bf16[8,128,128]{2,1,0:T(8,128)(2,1)}), bf16[8,128,128]{2,1,0:T(8,128)(2,1)S(1)}, u32[]{:S(2)}, u32[]{:S(2)}) async-start(bf16[8,128,128]{2,1,0:T(8,128)(2,1)} %prefix.1), calls=%async_computation.1 | async-start | bytes 524288 | tf_op jit(solution)/shard_map/all_to_all | solution.py:20
  35.9 1.4 %collective-permute-start.1 = (bf16[128,512]{1,0:T(8,128)(2,1)S(1)}, bf16[128,512]{1,0:T(8,128)(2,1)S(1)}, u32[]{:S(2)}, u32[]{:S(2)}) collective-permute-start(bf16[128,512]{1,0:T(8,128)(2,1)S(1)} %get-tuple-element.31), channel_id=1, source_target_pairs={{0,1},{1,0},{2,3},{3,2},{4,5},{5,4},{6,7},{7,6},{8,9},{9,8},{10,11... | collective-permute-start | bytes 393224 | tf_op jit(solution)/shard_map/ppermute | solution.py:16
  35.9 3.1 %collective-permute-start = (bf16[128,512]{1,0:T(8,128)(2,1)S(1)}, bf16[128,512]{1,0:T(8,128)(2,1)S(1)}, u32[]{:S(2)}, u32[]{:S(2)}) collective-permute-start(bf16[128,512]{1,0:T(8,128)(2,1)S(1)} %get-tuple-element.29), channel_id=1, source_target_pairs={{0,1},{1,0},{2,3},{3,2},{4,5},{5,4},{6,7},{7,6},{8,9},{9,8},{10,11... | collective-permute-start | bytes 393224 | tf_op jit(solution)/shard_map/ppermute | solution.py:16
  37.3 5.6 %collective-permute-start.2 = (bf16[128,512]{1,0:T(8,128)(2,1)S(1)}, bf16[128,512]{1,0:T(8,128)(2,1)S(1)}, u32[]{:S(2)}, u32[]{:S(2)}) collective-permute-start(bf16[128,512]{1,0:T(8,128)(2,1)S(1)} %add_convert_fusion.6), channel_id=1, source_target_pairs={{0,2},{1,3},{2,0},{3,1},{4,6},{5,7},{6,4},{7,5},{8,10},{9,11},{10,... | collective-permute-start | bytes 393224 | tf_op jit(solution)/shard_map/ppermute | solution.py:16
  43.4 6.4 %collective-permute-start.3 = (bf16[64,512]{1,0:T(8,128)(2,1)S(1)}, bf16[64,512]{1,0:T(8,128)(2,1)S(1)}, u32[]{:S(2)}, u32[]{:S(2)}) collective-permute-start(bf16[64,512]{1,0:T(8,128)(2,1)S(1)} %get-tuple-element.51), channel_id=1, source_target_pairs={{0,24},{4,28},{8,16},{12,20},{16,8},{20,12},{24,0},{28,4},{1,25},{... | collective-permute-start | bytes 196616 | tf_op jit(solution)/shard_map/ppermute | solution.py:117
  44.6 5.2 %collective-permute-start.4 = (bf16[64,512]{1,0:T(8,128)(2,1)S(1)}, bf16[64,512]{1,0:T(8,128)(2,1)S(1)}, u32[]{:S(2)}, u32[]{:S(2)}) collective-permute-start(bf16[64,512]{1,0:T(8,128)(2,1)S(1)} %get-tuple-element.50), channel_id=1, source_target_pairs={{0,4},{4,0},{8,12},{12,8},{16,20},{20,16},{24,28},{28,24},{1,5},{5... | collective-permute-start | bytes 196616 | tf_op jit(solution)/shard_map/ppermute | solution.py:117
  46.3 6.9 %collective-permute-start.5 = (bf16[64,512]{1,0:T(8,128)(2,1)S(1)}, bf16[64,512]{1,0:T(8,128)(2,1)S(1)}, u32[]{:S(2)}, u32[]{:S(2)}) collective-permute-start(bf16[64,512]{1,0:T(8,128)(2,1)S(1)} %get-tuple-element.49), channel_id=1, source_target_pairs={{0,16},{4,20},{8,24},{12,28},{16,0},{20,4},{24,8},{28,12},{1,17},{... | collective-permute-start | bytes 196616 | tf_op jit(solution)/shard_map/ppermute | solution.py:117
  46.4 8.7 %collective-permute-start.6 = (bf16[64,512]{1,0:T(8,128)(2,1)S(1)}, bf16[64,512]{1,0:T(8,128)(2,1)S(1)}, u32[]{:S(2)}, u32[]{:S(2)}) collective-permute-start(bf16[64,512]{1,0:T(8,128)(2,1)S(1)} %get-tuple-element.48), channel_id=1, source_target_pairs={{0,20},{4,16},{8,28},{12,24},{16,4},{20,0},{24,12},{28,8},{1,21},{... | collective-permute-start | bytes 196616 | tf_op jit(solution)/shard_map/ppermute | solution.py:117
  55.1 7.4 %collective-permute-start.8 = (bf16[256,512]{1,0:T(8,128)(2,1)S(1)}, bf16[256,512]{1,0:T(8,128)(2,1)S(1)}, u32[]{:S(2)}, u32[]{:S(2)}) collective-permute-start(bf16[256,512]{1,0:T(8,128)(2,1)S(1)} %constant_dynamic-update-slice_fusion.own_in), channel_id=1, source_target_pairs={{0,2},{1,3},{2,0},{3,1},{4,6},{5,7},{6,4},{7,5},{8,10},{9,11},{10,... | collective-permute-start | bytes 786440 | tf_op jit(solution)/shard_map/ppermute | solution.py:16
  56.6 7.0 %collective-permute-start.16 = (bf16[64,512]{1,0:T(8,128)(2,1)S(1)}, bf16[64,512]{1,0:T(8,128)(2,1)S(1)}, u32[]{:S(2)}, u32[]{:S(2)}) collective-permute-start(bf16[64,512]{1,0:T(8,128)(2,1)S(1)} %get-tuple-element.47), channel_id=1, source_target_pairs={{0,28},{4,24},{8,20},{12,16},{16,12},{20,8},{24,4},{28,0},{1,29},{... | collective-permute-start | bytes 196616 | tf_op jit(solution)/shard_map/ppermute | solution.py:117
  58.5 5.1 %collective-permute-start.17 = (bf16[64,512]{1,0:T(8,128)(2,1)S(1)}, bf16[64,512]{1,0:T(8,128)(2,1)S(1)}, u32[]{:S(2)}, u32[]{:S(2)}) collective-permute-start(bf16[64,512]{1,0:T(8,128)(2,1)S(1)} %get-tuple-element.46), channel_id=1, source_target_pairs={{0,8},{4,12},{8,0},{12,4},{16,24},{20,28},{24,16},{28,20},{1,9},{5... | collective-permute-start | bytes 196616 | tf_op jit(solution)/shard_map/ppermute | solution.py:117
  58.5 6.5 %collective-permute-start.18 = (bf16[64,512]{1,0:T(8,128)(2,1)S(1)}, bf16[64,512]{1,0:T(8,128)(2,1)S(1)}, u32[]{:S(2)}, u32[]{:S(2)}) collective-permute-start(bf16[64,512]{1,0:T(8,128)(2,1)S(1)} %get-tuple-element.45), channel_id=1, source_target_pairs={{0,12},{4,8},{8,4},{12,0},{16,28},{20,24},{24,20},{28,16},{1,13},{... | collective-permute-start | bytes 196616 | tf_op jit(solution)/shard_map/ppermute | solution.py:117
  61.4 4.1 %collective-permute-start.7 = (bf16[256,512]{1,0:T(8,128)(2,1)S(1)}, bf16[256,512]{1,0:T(8,128)(2,1)S(1)}, u32[]{:S(2)}, u32[]{:S(2)}) collective-permute-start(bf16[256,512]{1,0:T(8,128)(2,1)S(1)} %constant_dynamic-update-slice_fusion.own_in), channel_id=1, source_target_pairs={{0,1},{1,0},{2,3},{3,2},{4,5},{5,4},{6,7},{7,6},{8,9},{9,8},{10,11... | collective-permute-start | bytes 786440 | tf_op jit(solution)/shard_map/ppermute | solution.py:16
  62.5 3.0 %collective-permute-start.9 = (bf16[256,512]{1,0:T(8,128)(2,1)S(1)}, bf16[256,512]{1,0:T(8,128)(2,1)S(1)}, u32[]{:S(2)}, u32[]{:S(2)}) collective-permute-start(bf16[256,512]{1,0:T(8,128)(2,1)S(1)} %collective-permute-done.8.far_in), channel_id=1, source_target_pairs={{0,1},{1,0},{2,3},{3,2},{4,5},{5,4},{6,7},{7,6},{8,9},{9,8},{10,11... | collective-permute-start | bytes 786440 | tf_op jit(solution)/shard_map/ppermute | solution.py:16
  65.0 6.4 %collective-permute-start.20 = (bf16[256,512]{1,0:T(8,128)(2,1)S(1)}, bf16[256,512]{1,0:T(8,128)(2,1)S(1)}, u32[]{:S(2)}, u32[]{:S(2)}) collective-permute-start(bf16[256,512]{1,0:T(8,128)(2,1)S(1)} %constant_dynamic-update-slice_fusion.4.own_in), channel_id=1, source_target_pairs={{0,2},{1,3},{2,0},{3,1},{4,6},{5,7},{6,4},{7,5},{8,10},{9,11},{10,... | collective-permute-start | bytes 786440 | tf_op jit(solution)/shard_map/ppermute | solution.py:16
  69.5 1.9 %collective-permute-start.10 = (bf16[256,512]{1,0:T(8,128)(2,1)S(1)}, bf16[256,512]{1,0:T(8,128)(2,1)S(1)}, u32[]{:S(2)}, u32[]{:S(2)}) collective-permute-start(bf16[256,512]{1,0:T(8,128)(2,1)S(1)} %get-tuple-element.36), channel_id=1, source_target_pairs={{0,1},{1,0},{2,3},{3,2},{4,5},{5,4},{6,7},{7,6},{8,9},{9,8},{10,11... | collective-permute-start | bytes 786440 | tf_op jit(solution)/shard_map/ppermute | solution.py:16
  69.6 3.4 %collective-permute-start.19 = (bf16[256,512]{1,0:T(8,128)(2,1)S(1)}, bf16[256,512]{1,0:T(8,128)(2,1)S(1)}, u32[]{:S(2)}, u32[]{:S(2)}) collective-permute-start(bf16[256,512]{1,0:T(8,128)(2,1)S(1)} %constant_dynamic-update-slice_fusion.4.own_in), channel_id=1, source_target_pairs={{0,1},{1,0},{2,3},{3,2},{4,5},{5,4},{6,7},{7,6},{8,9},{9,8},{10,11... | collective-permute-start | bytes 786440 | tf_op jit(solution)/shard_map/ppermute | solution.py:16
  71.4 1.6 %collective-permute-start.21 = (bf16[256,512]{1,0:T(8,128)(2,1)S(1)}, bf16[256,512]{1,0:T(8,128)(2,1)S(1)}, u32[]{:S(2)}, u32[]{:S(2)}) collective-permute-start(bf16[256,512]{1,0:T(8,128)(2,1)S(1)} %collective-permute-done.20.far_in), channel_id=1, source_target_pairs={{0,1},{1,0},{2,3},{3,2},{4,5},{5,4},{6,7},{7,6},{8,9},{9,8},{10,11... | collective-permute-start | bytes 786440 | tf_op jit(solution)/shard_map/ppermute | solution.py:16
  71.4 8.8 %collective-permute-start.11 = (bf16[256,512]{1,0:T(8,128)(2,1)S(1)}, bf16[256,512]{1,0:T(8,128)(2,1)S(1)}, u32[]{:S(2)}, u32[]{:S(2)}) collective-permute-start(bf16[256,512]{1,0:T(8,128)(2,1)S(1)} %add_convert_fusion.3), channel_id=1, source_target_pairs={{0,2},{1,3},{2,0},{3,1},{4,6},{5,7},{6,4},{7,5},{8,10},{9,11},{10,... | collective-permute-start | bytes 786440 | tf_op jit(solution)/shard_map/ppermute | solution.py:16
  77.0 3.3 %collective-permute-start.22 = (bf16[256,512]{1,0:T(8,128)(2,1)S(1)}, bf16[256,512]{1,0:T(8,128)(2,1)S(1)}, u32[]{:S(2)}, u32[]{:S(2)}) collective-permute-start(bf16[256,512]{1,0:T(8,128)(2,1)S(1)} %get-tuple-element.43), channel_id=1, source_target_pairs={{0,1},{1,0},{2,3},{3,2},{4,5},{5,4},{6,7},{7,6},{8,9},{9,8},{10,11... | collective-permute-start | bytes 786440 | tf_op jit(solution)/shard_map/ppermute | solution.py:16
  80.2 1.8 %collective-permute-start.12 = (bf16[256,512]{1,0:T(8,128)(2,1)S(1)}, bf16[256,512]{1,0:T(8,128)(2,1)S(1)}, u32[]{:S(2)}, u32[]{:S(2)}) collective-permute-start(bf16[256,512]{1,0:T(8,128)(2,1)S(1)} %get-tuple-element.37), channel_id=1, source_target_pairs={{0,1},{1,0},{2,3},{3,2},{4,5},{5,4},{6,7},{7,6},{8,9},{9,8},{10,11... | collective-permute-start | bytes 786440 | tf_op jit(solution)/shard_map/ppermute | solution.py:16
  80.3 8.8 %collective-permute-start.24 = (bf16[256,512]{1,0:T(8,128)(2,1)S(1)}, bf16[256,512]{1,0:T(8,128)(2,1)S(1)}, u32[]{:S(2)}, u32[]{:S(2)}) collective-permute-start(bf16[256,512]{1,0:T(8,128)(2,1)S(1)} %add_convert_fusion.1), channel_id=1, source_target_pairs={{0,2},{1,3},{2,0},{3,1},{4,6},{5,7},{6,4},{7,5},{8,10},{9,11},{10,... | collective-permute-start | bytes 786440 | tf_op jit(solution)/shard_map/ppermute | solution.py:16
  81.8 7.3 %collective-permute-start.23 = (bf16[256,512]{1,0:T(8,128)(2,1)S(1)}, bf16[256,512]{1,0:T(8,128)(2,1)S(1)}, u32[]{:S(2)}, u32[]{:S(2)}) collective-permute-start(bf16[256,512]{1,0:T(8,128)(2,1)S(1)} %get-tuple-element.44), channel_id=1, source_target_pairs={{0,1},{1,0},{2,3},{3,2},{4,5},{5,4},{6,7},{7,6},{8,9},{9,8},{10,11... | collective-permute-start | bytes 786440 | tf_op jit(solution)/shard_map/ppermute | solution.py:16
  82.2 12.1 %collective-permute-start.13 = (bf16[64,512]{1,0:T(8,128)(2,1)S(1)}, bf16[64,512]{1,0:T(8,128)(2,1)S(1)}, u32[]{:S(2)}, u32[]{:S(2)}) collective-permute-start(bf16[64,512]{1,0:T(8,128)(2,1)S(1)} %get-tuple-element.59), channel_id=1, source_target_pairs={{0,4},{4,0},{8,12},{12,8},{16,20},{20,16},{24,28},{28,24},{1,5},{5... | collective-permute-start | bytes 196616 | tf_op jit(solution)/shard_map/ppermute | solution.py:117
  84.2 10.1 %collective-permute-start.14 = (bf16[64,512]{1,0:T(8,128)(2,1)S(1)}, bf16[64,512]{1,0:T(8,128)(2,1)S(1)}, u32[]{:S(2)}, u32[]{:S(2)}) collective-permute-start(bf16[64,512]{1,0:T(8,128)(2,1)S(1)} %get-tuple-element.58), channel_id=1, source_target_pairs={{0,16},{4,20},{8,24},{12,28},{16,0},{20,4},{24,8},{28,12},{1,17},{... | collective-permute-start | bytes 196616 | tf_op jit(solution)/shard_map/ppermute | solution.py:117
  84.6 11.5 %collective-permute-start.15 = (bf16[64,512]{1,0:T(8,128)(2,1)S(1)}, bf16[64,512]{1,0:T(8,128)(2,1)S(1)}, u32[]{:S(2)}, u32[]{:S(2)}) collective-permute-start(bf16[64,512]{1,0:T(8,128)(2,1)S(1)} %get-tuple-element.57), channel_id=1, source_target_pairs={{0,20},{4,16},{8,28},{12,24},{16,4},{20,0},{24,12},{28,8},{1,21},{... | collective-permute-start | bytes 196616 | tf_op jit(solution)/shard_map/ppermute | solution.py:117
  89.2 6.9 %collective-permute-start.25 = (bf16[64,512]{1,0:T(8,128)(2,1)S(1)}, bf16[64,512]{1,0:T(8,128)(2,1)S(1)}, u32[]{:S(2)}, u32[]{:S(2)}) collective-permute-start(bf16[64,512]{1,0:T(8,128)(2,1)S(1)} %get-tuple-element.56), channel_id=1, source_target_pairs={{0,24},{4,28},{8,16},{12,20},{16,8},{20,12},{24,0},{28,4},{1,25},{... | collective-permute-start | bytes 196616 | tf_op jit(solution)/shard_map/ppermute | solution.py:117
  91.2 7.5 %collective-permute-start.26 = (bf16[64,512]{1,0:T(8,128)(2,1)S(1)}, bf16[64,512]{1,0:T(8,128)(2,1)S(1)}, u32[]{:S(2)}, u32[]{:S(2)}) collective-permute-start(bf16[64,512]{1,0:T(8,128)(2,1)S(1)} %get-tuple-element.55), channel_id=1, source_target_pairs={{0,28},{4,24},{8,20},{12,16},{16,12},{20,8},{24,4},{28,0},{1,29},{... | collective-permute-start | bytes 196616 | tf_op jit(solution)/shard_map/ppermute | solution.py:117
  94.3 5.3 %collective-permute-start.27 = (bf16[64,512]{1,0:T(8,128)(2,1)S(1)}, bf16[64,512]{1,0:T(8,128)(2,1)S(1)}, u32[]{:S(2)}, u32[]{:S(2)}) collective-permute-start(bf16[64,512]{1,0:T(8,128)(2,1)S(1)} %get-tuple-element.54), channel_id=1, source_target_pairs={{0,8},{4,12},{8,0},{12,4},{16,24},{20,28},{24,16},{28,20},{1,9},{5... | collective-permute-start | bytes 196616 | tf_op jit(solution)/shard_map/ppermute | solution.py:117
  94.3 6.4 %collective-permute-start.28 = (bf16[64,512]{1,0:T(8,128)(2,1)S(1)}, bf16[64,512]{1,0:T(8,128)(2,1)S(1)}, u32[]{:S(2)}, u32[]{:S(2)}) collective-permute-start(bf16[64,512]{1,0:T(8,128)(2,1)S(1)} %get-tuple-element.53), channel_id=1, source_target_pairs={{0,12},{4,8},{8,4},{12,0},{16,28},{20,24},{24,20},{28,16},{1,13},{... | collective-permute-start | bytes 196616 | tf_op jit(solution)/shard_map/ppermute | solution.py:117
  (3 other events, 37.2 us)

commit v14 on v13

--- a/solution.py
+++ b/solution.py
@@ -312,7 +312,7 @@
 def run_expert(place, gain, own, near, far, last, wg, wu, wd):
     rows, share = own.shape
     width, inner = wg.shape
-    weights = (in_hbm(wg), in_hbm(wu), in_hbm(wd))
+    weights = (wg, wu, wd)
     operands = (in_hbm(gain.reshape(1, width)), own, near, far, last, *weights)
     return pl.pallas_call(
         expert_kernel,

time: 102 us -> 102 us (level)
  no operation moved by 1% of the time
where the time goes in v14:
time: 102 us
  waiting for transfers between devices  41 us (40%)
  starting transfers between devices  40.9 us (40%)
  Pallas kernels  16.6 us (16%)
  matrix products  1.58 us (2%)
    ppermute x14, starting transfers between devices, exchange_parts(): piece = lax.ppermute(piece, 'seq', [(i, i ^ k) for i in range(8)])  21.7 us
    all_to_all x2, waiting for transfers between devices, exchange(): return lax.all_to_all(value, 'seq', split_axis=0, concat_axis=0, tiled=True)  15.4 us
    ppermute x14, waiting for transfers between devices, exchange_parts(): piece = lax.ppermute(piece, 'seq', [(i, i ^ k) for i in range(8)])  13.1 us
    ppermute x15, waiting for transfers between devices, swap(): return lax.ppermute(value, 'tp', [(i, i ^ bit) for i in range(count)])  12.4 us
    all_to_all x2, starting transfers between devices, exchange(): return lax.all_to_all(value, 'seq', split_axis=0, concat_axis=0, tiled=True)  10.8 us
    ppermute x15, starting transfers between devices, swap(): return lax.ppermute(value, 'tp', [(i, i ^ bit) for i in range(count)])  8.35 us
    pallas_call x2, Pallas kernels, run_expert(): pl.pallas_call(expert_kernel, in_specs=[pl.BlockSpec(memory_space=pltpu.S...  7.97 us
    pallas_call x1, Pallas kernels, mixer_tail(): pl.pallas_call(tail_kernel, in_specs=[pl.BlockSpec(memory_space=pltpu.SME...  3.31 us
  transfers between devices with their start and end apart: 31, of which 16 were waited for; matrix products, arithmetic and copies ran while one was open for 1% of the time, Pallas kernels for 9%

profile of v14, /device:TPU:0, one launch (start us, length us, event | category | flops | bytes accessed | tf_op | source)
XLA Modules:
  0.0 101.9 jit_solution(7783815497564186492)
XLA Ops:
  0.0 2.8 %own_state.1 = (bf16[8,144,128]{2,1,0:T(8,128)(2,1)}, f32[16,128]{1,0:T(8,128)S(1)}) custom-call(bf16[128,1024]{1,0:T(8,128)(2,1)} %x.3, f32[16,128]{1,0:T(8,128)} %bitcast.34, f32[16,128]{1,0:T(8,128)} %bitcast.36, bf16[128,128]{1,0:T(8,128)(2,1)} %b.3), custom_call_target="tpu_custom_call" | custom-call | tf_op jit(solution)/shard_map/own_state/pallas_call | solution.py:78
  2.8 7.3 %all-to-all-start = ((bf16[8,144,128]{2,1,0:T(8,128)(2,1)}), bf16[8,144,128]{2,1,0:T(8,128)(2,1)S(1)}, u32[]{:S(2)}, u32[]{:S(2)}) async-start(bf16[8,144,128]{2,1,0:T(8,128)(2,1)} %get-tuple-element.26), calls=%async_computation | async-start | bytes 589824 | tf_op jit(solution)/shard_map/all_to_all | solution.py:20
  10.7 1.7 %within_block.1.direct_in = f32[128,1024]{1,0:T(8,128)S(1)} custom-call(f32[16]{0:T(128)S(1)} %copy-done.4, bf16[128,1024]{1,0:T(8,128)(2,1)} %x.3, f32[16,128]{1,0:T(8,128)} %bitcast.35, f32[16,128]{1,0:T(8,128)S(1)} %get-tuple-element.25.cum_t.cum_in, bf16[128,128]{1,0:T(8,128)(2,1)} %b.3, bf16[128,128]{1,0:T(8,128)(2,1)} %c_in.1), custom_call_target="tpu_custom_call" | custom-call | flops 134217728 | bytes 786432 | tf_op jit(solution)/shard_map/within_block/pallas_call | solution.py:166
  12.4 7.3 %all-to-all-done.got = bf16[8,144,128]{2,1,0:T(8,128)(2,1)S(1)} async-done(((bf16[8,144,128]{2,1,0:T(8,128)(2,1)}), bf16[8,144,128]{2,1,0:T(8,128)(2,1)S(1)}, u32[]{:S(2)}, u32[]{:S(2)}) %all-to-all-start) | async-done | bytes 294944 | tf_op jit(solution)/shard_map/all_to_all | solution.py:20
  20.6 3.6 %all-to-all-start.1 = ((bf16[8,128,128]{2,1,0:T(8,128)(2,1)}), bf16[8,128,128]{2,1,0:T(8,128)(2,1)S(1)}, u32[]{:S(2)}, u32[]{:S(2)}) async-start(bf16[8,128,128]{2,1,0:T(8,128)(2,1)} %prefix.1), calls=%async_computation.1 | async-start | bytes 524288 | tf_op jit(solution)/shard_map/all_to_all | solution.py:20
  24.6 8.1 %all-to-all-done.1 = bf16[8,128,128]{2,1,0:T(8,128)(2,1)S(1)} async-done(((bf16[8,128,128]{2,1,0:T(8,128)(2,1)}), bf16[8,128,128]{2,1,0:T(8,128)(2,1)S(1)}, u32[]{:S(2)}, u32[]{:S(2)}) %all-to-all-start.1) | async-done | bytes 262176 | tf_op jit(solution)/shard_map/all_to_all | solution.py:20
  32.7 3.3 %mixer_tail.1 = (bf16[128,512]{1,0:T(8,128)(2,1)S(1)}, bf16[128,512]{1,0:T(8,128)(2,1)S(1)}, f32[128,512]{1,0:T(8,128)S(1)}, f32[128,512]{1,0:T(8,128)S(1)}) custom-call(s32[1]{0:T(128)} %bitcast.place_ref, bf16[128,128]{1,0:T(8,128)(2,1)} %c_in.1, f32[16,128]{1,0:T(8,128)S(1)} %get-tuple-element.25.cum_t.cum_in, f32[1,1024]{1,0:T(1,128)} %bitcast.37, ...), custom_call_target="tpu_custom_call" | custom-call | flops 536870912 | bytes 6029312 | tf_op jit(solution)/shard_map/mixer_tail/pallas_call | solution.py:248
  37.5 1.6 %collective-permute-start.2 = (bf16[128,512]{1,0:T(8,128)(2,1)S(1)}, bf16[128,512]{1,0:T(8,128)(2,1)S(1)}, u32[]{:S(2)}, u32[]{:S(2)}) collective-permute-start(bf16[128,512]{1,0:T(8,128)(2,1)S(1)} %add_convert_fusion.6), channel_id=1, source_target_pairs={{0,2},{1,3},{2,0},{3,1},{4,6},{5,7},{6,4},{7,5},{8,10},{9,11},{10,... | collective-permute-start | bytes 393224 | tf_op jit(solution)/shard_map/ppermute | solution.py:16
  39.2 3.9 %collective-permute-done.2 = bf16[128,512]{1,0:T(8,128)(2,1)S(1)} collective-permute-done((bf16[128,512]{1,0:T(8,128)(2,1)S(1)}, bf16[128,512]{1,0:T(8,128)(2,1)S(1)}, u32[]{:S(2)}, u32[]{:S(2)}) %collective-permute-start.2) | collective-permute-done | bytes 131104 | tf_op jit(solution)/shard_map/ppermute | solution.py:16
  43.6 1.2 %collective-permute-start.3 = (bf16[64,512]{1,0:T(8,128)(2,1)S(1)}, bf16[64,512]{1,0:T(8,128)(2,1)S(1)}, u32[]{:S(2)}, u32[]{:S(2)}) collective-permute-start(bf16[64,512]{1,0:T(8,128)(2,1)S(1)} %get-tuple-element.51), channel_id=1, source_target_pairs={{0,24},{4,28},{8,16},{12,20},{16,8},{20,12},{24,0},{28,4},{1,25},{... | collective-permute-start | bytes 196616 | tf_op jit(solution)/shard_map/ppermute | solution.py:117
  44.8 1.7 %collective-permute-start.4 = (bf16[64,512]{1,0:T(8,128)(2,1)S(1)}, bf16[64,512]{1,0:T(8,128)(2,1)S(1)}, u32[]{:S(2)}, u32[]{:S(2)}) collective-permute-start(bf16[64,512]{1,0:T(8,128)(2,1)S(1)} %get-tuple-element.50), channel_id=1, source_target_pairs={{0,4},{4,0},{8,12},{12,8},{16,20},{20,16},{24,28},{28,24},{1,5},{5... | collective-permute-start | bytes 196616 | tf_op jit(solution)/shard_map/ppermute | solution.py:117
  46.6 2.6 %collective-permute-start.6 = (bf16[64,512]{1,0:T(8,128)(2,1)S(1)}, bf16[64,512]{1,0:T(8,128)(2,1)S(1)}, u32[]{:S(2)}, u32[]{:S(2)}) collective-permute-start(bf16[64,512]{1,0:T(8,128)(2,1)S(1)} %get-tuple-element.48), channel_id=1, source_target_pairs={{0,20},{4,16},{8,28},{12,24},{16,4},{20,0},{24,12},{28,8},{1,21},{... | collective-permute-start | bytes 196616 | tf_op jit(solution)/shard_map/ppermute | solution.py:117
  50.1 3.2 %collective-permute-done.5 = bf16[64,512]{1,0:T(8,128)(2,1)S(1)} collective-permute-done((bf16[64,512]{1,0:T(8,128)(2,1)S(1)}, bf16[64,512]{1,0:T(8,128)(2,1)S(1)}, u32[]{:S(2)}, u32[]{:S(2)}) %collective-permute-start.5) | collective-permute-done | bytes 65568 | tf_op jit(solution)/shard_map/ppermute | solution.py:117
  53.3 2.0 %collective-permute-done.6 = bf16[64,512]{1,0:T(8,128)(2,1)S(1)} collective-permute-done((bf16[64,512]{1,0:T(8,128)(2,1)S(1)}, bf16[64,512]{1,0:T(8,128)(2,1)S(1)}, u32[]{:S(2)}, u32[]{:S(2)}) %collective-permute-start.6) | collective-permute-done | bytes 65568 | tf_op jit(solution)/shard_map/ppermute | solution.py:117
  55.3 1.5 %collective-permute-start.8 = (bf16[256,512]{1,0:T(8,128)(2,1)S(1)}, bf16[256,512]{1,0:T(8,128)(2,1)S(1)}, u32[]{:S(2)}, u32[]{:S(2)}) collective-permute-start(bf16[256,512]{1,0:T(8,128)(2,1)S(1)} %constant_dynamic-update-slice_fusion.own_in), channel_id=1, source_target_pairs={{0,2},{1,3},{2,0},{3,1},{4,6},{5,7},{6,4},{7,5},{8,10},{9,11},{10,... | collective-permute-start | bytes 786440 | tf_op jit(solution)/shard_map/ppermute | solution.py:16
  56.8 1.9 %collective-permute-start.16 = (bf16[64,512]{1,0:T(8,128)(2,1)S(1)}, bf16[64,512]{1,0:T(8,128)(2,1)S(1)}, u32[]{:S(2)}, u32[]{:S(2)}) collective-permute-start(bf16[64,512]{1,0:T(8,128)(2,1)S(1)} %get-tuple-element.47), channel_id=1, source_target_pairs={{0,28},{4,24},{8,20},{12,16},{16,12},{20,8},{24,4},{28,0},{1,29},{... | collective-permute-start | bytes 196616 | tf_op jit(solution)/shard_map/ppermute | solution.py:117
  58.7 2.9 %collective-permute-start.18 = (bf16[64,512]{1,0:T(8,128)(2,1)S(1)}, bf16[64,512]{1,0:T(8,128)(2,1)S(1)}, u32[]{:S(2)}, u32[]{:S(2)}) collective-permute-start(bf16[64,512]{1,0:T(8,128)(2,1)S(1)} %get-tuple-element.45), channel_id=1, source_target_pairs={{0,12},{4,8},{8,4},{12,0},{16,28},{20,24},{24,20},{28,16},{1,13},{... | collective-permute-start | bytes 196616 | tf_op jit(solution)/shard_map/ppermute | solution.py:117
  62.6 1.2 %collective-permute-done.16 = bf16[64,512]{1,0:T(8,128)(2,1)S(1)} collective-permute-done((bf16[64,512]{1,0:T(8,128)(2,1)S(1)}, bf16[64,512]{1,0:T(8,128)(2,1)S(1)}, u32[]{:S(2)}, u32[]{:S(2)}) %collective-permute-start.16) | collective-permute-done | bytes 65568 | tf_op jit(solution)/shard_map/ppermute | solution.py:117
  63.9 1.3 %collective-permute-done.18 = bf16[64,512]{1,0:T(8,128)(2,1)S(1)} collective-permute-done((bf16[64,512]{1,0:T(8,128)(2,1)S(1)}, bf16[64,512]{1,0:T(8,128)(2,1)S(1)}, u32[]{:S(2)}, u32[]{:S(2)}) %collective-permute-start.18) | collective-permute-done | bytes 65568 | tf_op jit(solution)/shard_map/ppermute | solution.py:117
  65.7 4.0 %expert.2 = (bf16[256,512]{1,0:T(8,128)(2,1)S(1)}, bf16[256,512]{1,0:T(8,128)(2,1)S(1)}, bf16[256,512]{1,0:T(8,128)(2,1)S(1)}, bf16[256,512]{1,0:T(8,128)(2,1)S(1)}) custom-call(s32[1]{0:T(128)} %bitcast.place_ref, f32[1,2048]{1,0:T(1,128)} %bitcast.32, bf16[256,512]{1,0:T(8,128)(2,1)S(1)} %constant_dynamic-update-slice_fusion.own_in, ...), custom_call_target="tpu_custom_call" | custom-call | flops 1 | bytes 1 | tf_op jit(solution)/shard_map/expert/pallas_call | solution.py:317
  70.3 1.3 %collective-permute-done.20.far_in = bf16[256,512]{1,0:T(8,128)(2,1)S(1)} collective-permute-done((bf16[256,512]{1,0:T(8,128)(2,1)S(1)}, bf16[256,512]{1,0:T(8,128)(2,1)S(1)}, u32[]{:S(2)}, u32[]{:S(2)}) %collective-permute-start.20) | collective-permute-done | bytes 262176 | tf_op jit(solution)/shard_map/ppermute | solution.py:16
  71.6 1.5 %collective-permute-start.11 = (bf16[256,512]{1,0:T(8,128)(2,1)S(1)}, bf16[256,512]{1,0:T(8,128)(2,1)S(1)}, u32[]{:S(2)}, u32[]{:S(2)}) collective-permute-start(bf16[256,512]{1,0:T(8,128)(2,1)S(1)} %add_convert_fusion.3), channel_id=1, source_target_pairs={{0,2},{1,3},{2,0},{3,1},{4,6},{5,7},{6,4},{7,5},{8,10},{9,11},{10,... | collective-permute-start | bytes 786440 | tf_op jit(solution)/shard_map/ppermute | solution.py:16
  73.2 4.0 %expert.3 = (bf16[256,512]{1,0:T(8,128)(2,1)S(1)}, bf16[256,512]{1,0:T(8,128)(2,1)S(1)}, bf16[256,512]{1,0:T(8,128)(2,1)S(1)}, bf16[256,512]{1,0:T(8,128)(2,1)S(1)}) custom-call(s32[1]{0:T(128)} %bitcast.place_ref, f32[1,2048]{1,0:T(1,128)} %bitcast.33, bf16[256,512]{1,0:T(8,128)(2,1)S(1)} %constant_dynamic-update-slice_fusion.4.own_in, ...), custom_call_target="tpu_custom_call" | custom-call | flops 1 | bytes 1 | tf_op jit(solution)/shard_map/expert/pallas_call | solution.py:317
  77.4 3.0 %collective-permute-done.11 = bf16[256,512]{1,0:T(8,128)(2,1)S(1)} collective-permute-done((bf16[256,512]{1,0:T(8,128)(2,1)S(1)}, bf16[256,512]{1,0:T(8,128)(2,1)S(1)}, u32[]{:S(2)}, u32[]{:S(2)}) %collective-permute-start.11) | collective-permute-done | bytes 262176 | tf_op jit(solution)/shard_map/ppermute | solution.py:16
  80.5 1.5 %collective-permute-start.24 = (bf16[256,512]{1,0:T(8,128)(2,1)S(1)}, bf16[256,512]{1,0:T(8,128)(2,1)S(1)}, u32[]{:S(2)}, u32[]{:S(2)}) collective-permute-start(bf16[256,512]{1,0:T(8,128)(2,1)S(1)} %add_convert_fusion.1), channel_id=1, source_target_pairs={{0,2},{1,3},{2,0},{3,1},{4,6},{5,7},{6,4},{7,5},{8,10},{9,11},{10,... | collective-permute-start | bytes 786440 | tf_op jit(solution)/shard_map/ppermute | solution.py:16
  82.4 2.0 %collective-permute-start.13 = (bf16[64,512]{1,0:T(8,128)(2,1)S(1)}, bf16[64,512]{1,0:T(8,128)(2,1)S(1)}, u32[]{:S(2)}, u32[]{:S(2)}) collective-permute-start(bf16[64,512]{1,0:T(8,128)(2,1)S(1)} %get-tuple-element.59), channel_id=1, source_target_pairs={{0,4},{4,0},{8,12},{12,8},{16,20},{20,16},{24,28},{28,24},{1,5},{5... | collective-permute-start | bytes 196616 | tf_op jit(solution)/shard_map/ppermute | solution.py:117
  84.8 2.0 %collective-permute-start.15 = (bf16[64,512]{1,0:T(8,128)(2,1)S(1)}, bf16[64,512]{1,0:T(8,128)(2,1)S(1)}, u32[]{:S(2)}, u32[]{:S(2)}) collective-permute-start(bf16[64,512]{1,0:T(8,128)(2,1)S(1)} %get-tuple-element.57), channel_id=1, source_target_pairs={{0,20},{4,16},{8,28},{12,24},{16,4},{20,0},{24,12},{28,8},{1,21},{... | collective-permute-start | bytes 196616 | tf_op jit(solution)/shard_map/ppermute | solution.py:117
  86.8 2.4 %collective-permute-done.24 = bf16[256,512]{1,0:T(8,128)(2,1)S(1)} collective-permute-done((bf16[256,512]{1,0:T(8,128)(2,1)S(1)}, bf16[256,512]{1,0:T(8,128)(2,1)S(1)}, u32[]{:S(2)}, u32[]{:S(2)}) %collective-permute-start.24) | collective-permute-done | bytes 262176 | tf_op jit(solution)/shard_map/ppermute | solution.py:16
  89.4 1.9 %collective-permute-start.25 = (bf16[64,512]{1,0:T(8,128)(2,1)S(1)}, bf16[64,512]{1,0:T(8,128)(2,1)S(1)}, u32[]{:S(2)}, u32[]{:S(2)}) collective-permute-start(bf16[64,512]{1,0:T(8,128)(2,1)S(1)} %get-tuple-element.56), channel_id=1, source_target_pairs={{0,24},{4,28},{8,16},{12,20},{16,8},{20,12},{24,0},{28,4},{1,25},{... | collective-permute-start | bytes 196616 | tf_op jit(solution)/shard_map/ppermute | solution.py:117
  91.3 3.3 %collective-permute-start.26 = (bf16[64,512]{1,0:T(8,128)(2,1)S(1)}, bf16[64,512]{1,0:T(8,128)(2,1)S(1)}, u32[]{:S(2)}, u32[]{:S(2)}) collective-permute-start(bf16[64,512]{1,0:T(8,128)(2,1)S(1)} %get-tuple-element.55), channel_id=1, source_target_pairs={{0,28},{4,24},{8,20},{12,16},{16,12},{20,8},{24,4},{28,0},{1,29},{... | collective-permute-start | bytes 196616 | tf_op jit(solution)/shard_map/ppermute | solution.py:117
  94.6 1.7 %collective-permute-start.28 = (bf16[64,512]{1,0:T(8,128)(2,1)S(1)}, bf16[64,512]{1,0:T(8,128)(2,1)S(1)}, u32[]{:S(2)}, u32[]{:S(2)}) collective-permute-start(bf16[64,512]{1,0:T(8,128)(2,1)S(1)} %get-tuple-element.53), channel_id=1, source_target_pairs={{0,12},{4,8},{8,4},{12,0},{16,28},{20,24},{24,20},{28,16},{1,13},{... | collective-permute-start | bytes 196616 | tf_op jit(solution)/shard_map/ppermute | solution.py:117
  96.4 2.7 %collective-permute-done.26 = bf16[64,512]{1,0:T(8,128)(2,1)S(1)} collective-permute-done((bf16[64,512]{1,0:T(8,128)(2,1)S(1)}, bf16[64,512]{1,0:T(8,128)(2,1)S(1)}, u32[]{:S(2)}, u32[]{:S(2)}) %collective-permute-start.26) | collective-permute-done | bytes 65568 | tf_op jit(solution)/shard_map/ppermute | solution.py:117
  (81 shorter events, 11.3 us)
Async XLA Ops:
  2.8 16.9 %all-to-all-start = ((bf16[8,144,128]{2,1,0:T(8,128)(2,1)}), bf16[8,144,128]{2,1,0:T(8,128)(2,1)S(1)}, u32[]{:S(2)}, u32[]{:S(2)}) async-start(bf16[8,144,128]{2,1,0:T(8,128)(2,1)} %get-tuple-element.26), calls=%async_computation | async-start | bytes 589824 | tf_op jit(solution)/shard_map/all_to_all | solution.py:20
  20.6 12.1 %all-to-all-start.1 = ((bf16[8,128,128]{2,1,0:T(8,128)(2,1)}), bf16[8,128,128]{2,1,0:T(8,128)(2,1)S(1)}, u32[]{:S(2)}, u32[]{:S(2)}) async-start(bf16[8,128,128]{2,1,0:T(8,128)(2,1)} %prefix.1), calls=%async_computation.1 | async-start | bytes 524288 | tf_op jit(solution)/shard_map/all_to_all | solution.py:20
  32.7 33.0 %copy-start.3 = (bf16[1,512,2048]{2,1,0:T(8,128)(2,1)S(1)}, bf16[1,512,2048]{2,1,0:T(8,128)(2,1)}, u32[]{:S(2)}) copy-start(bf16[1,512,2048]{2,1,0:T(8,128)(2,1)} %param.33) | copy-start | bytes 6291460
  36.0 1.4 %collective-permute-start.1 = (bf16[128,512]{1,0:T(8,128)(2,1)S(1)}, bf16[128,512]{1,0:T(8,128)(2,1)S(1)}, u32[]{:S(2)}, u32[]{:S(2)}) collective-permute-start(bf16[128,512]{1,0:T(8,128)(2,1)S(1)} %get-tuple-element.31), channel_id=1, source_target_pairs={{0,1},{1,0},{2,3},{3,2},{4,5},{5,4},{6,7},{7,6},{8,9},{9,8},{10,11... | collective-permute-start | bytes 393224 | tf_op jit(solution)/shard_map/ppermute | solution.py:16
  36.1 3.1 %collective-permute-start = (bf16[128,512]{1,0:T(8,128)(2,1)S(1)}, bf16[128,512]{1,0:T(8,128)(2,1)S(1)}, u32[]{:S(2)}, u32[]{:S(2)}) collective-permute-start(bf16[128,512]{1,0:T(8,128)(2,1)S(1)} %get-tuple-element.29), channel_id=1, source_target_pairs={{0,1},{1,0},{2,3},{3,2},{4,5},{5,4},{6,7},{7,6},{8,9},{9,8},{10,11... | collective-permute-start | bytes 393224 | tf_op jit(solution)/shard_map/ppermute | solution.py:16
  37.5 5.6 %collective-permute-start.2 = (bf16[128,512]{1,0:T(8,128)(2,1)S(1)}, bf16[128,512]{1,0:T(8,128)(2,1)S(1)}, u32[]{:S(2)}, u32[]{:S(2)}) collective-permute-start(bf16[128,512]{1,0:T(8,128)(2,1)S(1)} %add_convert_fusion.6), channel_id=1, source_target_pairs={{0,2},{1,3},{2,0},{3,1},{4,6},{5,7},{6,4},{7,5},{8,10},{9,11},{10,... | collective-permute-start | bytes 393224 | tf_op jit(solution)/shard_map/ppermute | solution.py:16
  43.6 6.5 %collective-permute-start.3 = (bf16[64,512]{1,0:T(8,128)(2,1)S(1)}, bf16[64,512]{1,0:T(8,128)(2,1)S(1)}, u32[]{:S(2)}, u32[]{:S(2)}) collective-permute-start(bf16[64,512]{1,0:T(8,128)(2,1)S(1)} %get-tuple-element.51), channel_id=1, source_target_pairs={{0,24},{4,28},{8,16},{12,20},{16,8},{20,12},{24,0},{28,4},{1,25},{... | collective-permute-start | bytes 196616 | tf_op jit(solution)/shard_map/ppermute | solution.py:117
  44.8 5.3 %collective-permute-start.4 = (bf16[64,512]{1,0:T(8,128)(2,1)S(1)}, bf16[64,512]{1,0:T(8,128)(2,1)S(1)}, u32[]{:S(2)}, u32[]{:S(2)}) collective-permute-start(bf16[64,512]{1,0:T(8,128)(2,1)S(1)} %get-tuple-element.50), channel_id=1, source_target_pairs={{0,4},{4,0},{8,12},{12,8},{16,20},{20,16},{24,28},{28,24},{1,5},{5... | collective-permute-start | bytes 196616 | tf_op jit(solution)/shard_map/ppermute | solution.py:117
  46.5 6.8 %collective-permute-start.5 = (bf16[64,512]{1,0:T(8,128)(2,1)S(1)}, bf16[64,512]{1,0:T(8,128)(2,1)S(1)}, u32[]{:S(2)}, u32[]{:S(2)}) collective-permute-start(bf16[64,512]{1,0:T(8,128)(2,1)S(1)} %get-tuple-element.49), channel_id=1, source_target_pairs={{0,16},{4,20},{8,24},{12,28},{16,0},{20,4},{24,8},{28,12},{1,17},{... | collective-permute-start | bytes 196616 | tf_op jit(solution)/shard_map/ppermute | solution.py:117
  46.6 8.7 %collective-permute-start.6 = (bf16[64,512]{1,0:T(8,128)(2,1)S(1)}, bf16[64,512]{1,0:T(8,128)(2,1)S(1)}, u32[]{:S(2)}, u32[]{:S(2)}) collective-permute-start(bf16[64,512]{1,0:T(8,128)(2,1)S(1)} %get-tuple-element.48), channel_id=1, source_target_pairs={{0,20},{4,16},{8,28},{12,24},{16,4},{20,0},{24,12},{28,8},{1,21},{... | collective-permute-start | bytes 196616 | tf_op jit(solution)/shard_map/ppermute | solution.py:117
  55.3 7.3 %collective-permute-start.8 = (bf16[256,512]{1,0:T(8,128)(2,1)S(1)}, bf16[256,512]{1,0:T(8,128)(2,1)S(1)}, u32[]{:S(2)}, u32[]{:S(2)}) collective-permute-start(bf16[256,512]{1,0:T(8,128)(2,1)S(1)} %constant_dynamic-update-slice_fusion.own_in), channel_id=1, source_target_pairs={{0,2},{1,3},{2,0},{3,1},{4,6},{5,7},{6,4},{7,5},{8,10},{9,11},{10,... | collective-permute-start | bytes 786440 | tf_op jit(solution)/shard_map/ppermute | solution.py:16
  56.8 7.0 %collective-permute-start.16 = (bf16[64,512]{1,0:T(8,128)(2,1)S(1)}, bf16[64,512]{1,0:T(8,128)(2,1)S(1)}, u32[]{:S(2)}, u32[]{:S(2)}) collective-permute-start(bf16[64,512]{1,0:T(8,128)(2,1)S(1)} %get-tuple-element.47), channel_id=1, source_target_pairs={{0,28},{4,24},{8,20},{12,16},{16,12},{20,8},{24,4},{28,0},{1,29},{... | collective-permute-start | bytes 196616 | tf_op jit(solution)/shard_map/ppermute | solution.py:117
  58.7 5.2 %collective-permute-start.17 = (bf16[64,512]{1,0:T(8,128)(2,1)S(1)}, bf16[64,512]{1,0:T(8,128)(2,1)S(1)}, u32[]{:S(2)}, u32[]{:S(2)}) collective-permute-start(bf16[64,512]{1,0:T(8,128)(2,1)S(1)} %get-tuple-element.46), channel_id=1, source_target_pairs={{0,8},{4,12},{8,0},{12,4},{16,24},{20,28},{24,16},{28,20},{1,9},{5... | collective-permute-start | bytes 196616 | tf_op jit(solution)/shard_map/ppermute | solution.py:117
  58.7 6.5 %collective-permute-start.18 = (bf16[64,512]{1,0:T(8,128)(2,1)S(1)}, bf16[64,512]{1,0:T(8,128)(2,1)S(1)}, u32[]{:S(2)}, u32[]{:S(2)}) collective-permute-start(bf16[64,512]{1,0:T(8,128)(2,1)S(1)} %get-tuple-element.45), channel_id=1, source_target_pairs={{0,12},{4,8},{8,4},{12,0},{16,28},{20,24},{24,20},{28,16},{1,13},{... | collective-permute-start | bytes 196616 | tf_op jit(solution)/shard_map/ppermute | solution.py:117
  61.6 4.1 %collective-permute-start.7 = (bf16[256,512]{1,0:T(8,128)(2,1)S(1)}, bf16[256,512]{1,0:T(8,128)(2,1)S(1)}, u32[]{:S(2)}, u32[]{:S(2)}) collective-permute-start(bf16[256,512]{1,0:T(8,128)(2,1)S(1)} %constant_dynamic-update-slice_fusion.own_in), channel_id=1, source_target_pairs={{0,1},{1,0},{2,3},{3,2},{4,5},{5,4},{6,7},{7,6},{8,9},{9,8},{10,11... | collective-permute-start | bytes 786440 | tf_op jit(solution)/shard_map/ppermute | solution.py:16
  62.6 3.1 %collective-permute-start.9 = (bf16[256,512]{1,0:T(8,128)(2,1)S(1)}, bf16[256,512]{1,0:T(8,128)(2,1)S(1)}, u32[]{:S(2)}, u32[]{:S(2)}) collective-permute-start(bf16[256,512]{1,0:T(8,128)(2,1)S(1)} %collective-permute-done.8.far_in), channel_id=1, source_target_pairs={{0,1},{1,0},{2,3},{3,2},{4,5},{5,4},{6,7},{7,6},{8,9},{9,8},{10,11... | collective-permute-start | bytes 786440 | tf_op jit(solution)/shard_map/ppermute | solution.py:16
  65.2 6.4 %collective-permute-start.20 = (bf16[256,512]{1,0:T(8,128)(2,1)S(1)}, bf16[256,512]{1,0:T(8,128)(2,1)S(1)}, u32[]{:S(2)}, u32[]{:S(2)}) collective-permute-start(bf16[256,512]{1,0:T(8,128)(2,1)S(1)} %constant_dynamic-update-slice_fusion.4.own_in), channel_id=1, source_target_pairs={{0,2},{1,3},{2,0},{3,1},{4,6},{5,7},{6,4},{7,5},{8,10},{9,11},{10,... | collective-permute-start | bytes 786440 | tf_op jit(solution)/shard_map/ppermute | solution.py:16
  69.7 1.8 %collective-permute-start.10 = (bf16[256,512]{1,0:T(8,128)(2,1)S(1)}, bf16[256,512]{1,0:T(8,128)(2,1)S(1)}, u32[]{:S(2)}, u32[]{:S(2)}) collective-permute-start(bf16[256,512]{1,0:T(8,128)(2,1)S(1)} %get-tuple-element.36), channel_id=1, source_target_pairs={{0,1},{1,0},{2,3},{3,2},{4,5},{5,4},{6,7},{7,6},{8,9},{9,8},{10,11... | collective-permute-start | bytes 786440 | tf_op jit(solution)/shard_map/ppermute | solution.py:16
  69.8 3.4 %collective-permute-start.19 = (bf16[256,512]{1,0:T(8,128)(2,1)S(1)}, bf16[256,512]{1,0:T(8,128)(2,1)S(1)}, u32[]{:S(2)}, u32[]{:S(2)}) collective-permute-start(bf16[256,512]{1,0:T(8,128)(2,1)S(1)} %constant_dynamic-update-slice_fusion.4.own_in), channel_id=1, source_target_pairs={{0,1},{1,0},{2,3},{3,2},{4,5},{5,4},{6,7},{7,6},{8,9},{9,8},{10,11... | collective-permute-start | bytes 786440 | tf_op jit(solution)/shard_map/ppermute | solution.py:16
  71.5 1.6 %collective-permute-start.21 = (bf16[256,512]{1,0:T(8,128)(2,1)S(1)}, bf16[256,512]{1,0:T(8,128)(2,1)S(1)}, u32[]{:S(2)}, u32[]{:S(2)}) collective-permute-start(bf16[256,512]{1,0:T(8,128)(2,1)S(1)} %collective-permute-done.20.far_in), channel_id=1, source_target_pairs={{0,1},{1,0},{2,3},{3,2},{4,5},{5,4},{6,7},{7,6},{8,9},{9,8},{10,11... | collective-permute-start | bytes 786440 | tf_op jit(solution)/shard_map/ppermute | solution.py:16
  71.6 8.8 %collective-permute-start.11 = (bf16[256,512]{1,0:T(8,128)(2,1)S(1)}, bf16[256,512]{1,0:T(8,128)(2,1)S(1)}, u32[]{:S(2)}, u32[]{:S(2)}) collective-permute-start(bf16[256,512]{1,0:T(8,128)(2,1)S(1)} %add_convert_fusion.3), channel_id=1, source_target_pairs={{0,2},{1,3},{2,0},{3,1},{4,6},{5,7},{6,4},{7,5},{8,10},{9,11},{10,... | collective-permute-start | bytes 786440 | tf_op jit(solution)/shard_map/ppermute | solution.py:16
  77.2 3.3 %collective-permute-start.22 = (bf16[256,512]{1,0:T(8,128)(2,1)S(1)}, bf16[256,512]{1,0:T(8,128)(2,1)S(1)}, u32[]{:S(2)}, u32[]{:S(2)}) collective-permute-start(bf16[256,512]{1,0:T(8,128)(2,1)S(1)} %get-tuple-element.43), channel_id=1, source_target_pairs={{0,1},{1,0},{2,3},{3,2},{4,5},{5,4},{6,7},{7,6},{8,9},{9,8},{10,11... | collective-permute-start | bytes 786440 | tf_op jit(solution)/shard_map/ppermute | solution.py:16
  80.4 1.8 %collective-permute-start.12 = (bf16[256,512]{1,0:T(8,128)(2,1)S(1)}, bf16[256,512]{1,0:T(8,128)(2,1)S(1)}, u32[]{:S(2)}, u32[]{:S(2)}) collective-permute-start(bf16[256,512]{1,0:T(8,128)(2,1)S(1)} %get-tuple-element.37), channel_id=1, source_target_pairs={{0,1},{1,0},{2,3},{3,2},{4,5},{5,4},{6,7},{7,6},{8,9},{9,8},{10,11... | collective-permute-start | bytes 786440 | tf_op jit(solution)/shard_map/ppermute | solution.py:16
  80.5 8.8 %collective-permute-start.24 = (bf16[256,512]{1,0:T(8,128)(2,1)S(1)}, bf16[256,512]{1,0:T(8,128)(2,1)S(1)}, u32[]{:S(2)}, u32[]{:S(2)}) collective-permute-start(bf16[256,512]{1,0:T(8,128)(2,1)S(1)} %add_convert_fusion.1), channel_id=1, source_target_pairs={{0,2},{1,3},{2,0},{3,1},{4,6},{5,7},{6,4},{7,5},{8,10},{9,11},{10,... | collective-permute-start | bytes 786440 | tf_op jit(solution)/shard_map/ppermute | solution.py:16
  82.0 7.2 %collective-permute-start.23 = (bf16[256,512]{1,0:T(8,128)(2,1)S(1)}, bf16[256,512]{1,0:T(8,128)(2,1)S(1)}, u32[]{:S(2)}, u32[]{:S(2)}) collective-permute-start(bf16[256,512]{1,0:T(8,128)(2,1)S(1)} %get-tuple-element.44), channel_id=1, source_target_pairs={{0,1},{1,0},{2,3},{3,2},{4,5},{5,4},{6,7},{7,6},{8,9},{9,8},{10,11... | collective-permute-start | bytes 786440 | tf_op jit(solution)/shard_map/ppermute | solution.py:16
  82.4 12.2 %collective-permute-start.13 = (bf16[64,512]{1,0:T(8,128)(2,1)S(1)}, bf16[64,512]{1,0:T(8,128)(2,1)S(1)}, u32[]{:S(2)}, u32[]{:S(2)}) collective-permute-start(bf16[64,512]{1,0:T(8,128)(2,1)S(1)} %get-tuple-element.59), channel_id=1, source_target_pairs={{0,4},{4,0},{8,12},{12,8},{16,20},{20,16},{24,28},{28,24},{1,5},{5... | collective-permute-start | bytes 196616 | tf_op jit(solution)/shard_map/ppermute | solution.py:117
  84.4 10.3 %collective-permute-start.14 = (bf16[64,512]{1,0:T(8,128)(2,1)S(1)}, bf16[64,512]{1,0:T(8,128)(2,1)S(1)}, u32[]{:S(2)}, u32[]{:S(2)}) collective-permute-start(bf16[64,512]{1,0:T(8,128)(2,1)S(1)} %get-tuple-element.58), channel_id=1, source_target_pairs={{0,16},{4,20},{8,24},{12,28},{16,0},{20,4},{24,8},{28,12},{1,17},{... | collective-permute-start | bytes 196616 | tf_op jit(solution)/shard_map/ppermute | solution.py:117
  84.8 11.5 %collective-permute-start.15 = (bf16[64,512]{1,0:T(8,128)(2,1)S(1)}, bf16[64,512]{1,0:T(8,128)(2,1)S(1)}, u32[]{:S(2)}, u32[]{:S(2)}) collective-permute-start(bf16[64,512]{1,0:T(8,128)(2,1)S(1)} %get-tuple-element.57), channel_id=1, source_target_pairs={{0,20},{4,16},{8,28},{12,24},{16,4},{20,0},{24,12},{28,8},{1,21},{... | collective-permute-start | bytes 196616 | tf_op jit(solution)/shard_map/ppermute | solution.py:117
  89.4 6.9 %collective-permute-start.25 = (bf16[64,512]{1,0:T(8,128)(2,1)S(1)}, bf16[64,512]{1,0:T(8,128)(2,1)S(1)}, u32[]{:S(2)}, u32[]{:S(2)}) collective-permute-start(bf16[64,512]{1,0:T(8,128)(2,1)S(1)} %get-tuple-element.56), channel_id=1, source_target_pairs={{0,24},{4,28},{8,16},{12,20},{16,8},{20,12},{24,0},{28,4},{1,25},{... | collective-permute-start | bytes 196616 | tf_op jit(solution)/shard_map/ppermute | solution.py:117
  91.3 7.7 %collective-permute-start.26 = (bf16[64,512]{1,0:T(8,128)(2,1)S(1)}, bf16[64,512]{1,0:T(8,128)(2,1)S(1)}, u32[]{:S(2)}, u32[]{:S(2)}) collective-permute-start(bf16[64,512]{1,0:T(8,128)(2,1)S(1)} %get-tuple-element.55), channel_id=1, source_target_pairs={{0,28},{4,24},{8,20},{12,16},{16,12},{20,8},{24,4},{28,0},{1,29},{... | collective-permute-start | bytes 196616 | tf_op jit(solution)/shard_map/ppermute | solution.py:117
  94.6 5.3 %collective-permute-start.27 = (bf16[64,512]{1,0:T(8,128)(2,1)S(1)}, bf16[64,512]{1,0:T(8,128)(2,1)S(1)}, u32[]{:S(2)}, u32[]{:S(2)}) collective-permute-start(bf16[64,512]{1,0:T(8,128)(2,1)S(1)} %get-tuple-element.54), channel_id=1, source_target_pairs={{0,8},{4,12},{8,0},{12,4},{16,24},{20,28},{24,16},{28,20},{1,9},{5... | collective-permute-start | bytes 196616 | tf_op jit(solution)/shard_map/ppermute | solution.py:117
  94.6 6.2 %collective-permute-start.28 = (bf16[64,512]{1,0:T(8,128)(2,1)S(1)}, bf16[64,512]{1,0:T(8,128)(2,1)S(1)}, u32[]{:S(2)}, u32[]{:S(2)}) collective-permute-start(bf16[64,512]{1,0:T(8,128)(2,1)S(1)} %get-tuple-element.53), channel_id=1, source_target_pairs={{0,12},{4,8},{8,4},{12,0},{16,28},{20,24},{24,20},{28,16},{1,13},{... | collective-permute-start | bytes 196616 | tf_op jit(solution)/shard_map/ppermute | solution.py:117
  (6 other events, 124.3 us)

commit v15 on v13

--- a/solution.py
+++ b/solution.py
@@ -420,7 +420,7 @@
         place, moe_gain, after(own[1], pass0), near[1], far[1], last, *weights
     )
     from_last1 = swap(to_last1, 1)
-    from_near0 = swap(after(to_near0, from_far0), 1)
+    from_near0 = swap(after(to_near0, pass0), 1)
     pass1 = (pass1.astype(F32) + from_last1.astype(F32)).astype(BF)
     from_far1 = swap(pass1, 2)
     from_near1 = swap(after(to_near1, pass1), 1)

time: 102 us -> 104 us (1.020)
  waiting for transfers between devices: 41 us -> 42.5 us
    ppermute x14, waiting for transfers between devices: 13.1 us -> 17.3 us  [exchange_parts(): piece = lax.ppermute(piece, 'seq', [(i, i ^ k) for i in range(8)])]
    ppermute x15, waiting for transfers between devices: 12.5 us -> 9.77 us  [swap(): return lax.ppermute(value, 'tp', [(i, i ^ bit) for i in range(count)])]
where the time goes in v15:
time: 104 us; the launch traced here: 103 us
  waiting for transfers between devices  42.5 us (41%)
  starting transfers between devices  41 us (39%)
  Pallas kernels  16.5 us (16%)
  matrix products  1.58 us (2%)
    ppermute x14, starting transfers between devices, exchange_parts(): piece = lax.ppermute(piece, 'seq', [(i, i ^ k) for i in range(8)])  21.5 us
    ppermute x14, waiting for transfers between devices, exchange_parts(): piece = lax.ppermute(piece, 'seq', [(i, i ^ k) for i in range(8)])  17.3 us
    all_to_all x2, waiting for transfers between devices, exchange(): return lax.all_to_all(value, 'seq', split_axis=0, concat_axis=0, tiled=True)  15.4 us
    all_to_all x2, starting transfers between devices, exchange(): return lax.all_to_all(value, 'seq', split_axis=0, concat_axis=0, tiled=True)  10.8 us
    ppermute x15, waiting for transfers between devices, swap(): return lax.ppermute(value, 'tp', [(i, i ^ bit) for i in range(count)])  9.77 us
    ppermute x15, starting transfers between devices, swap(): return lax.ppermute(value, 'tp', [(i, i ^ bit) for i in range(count)])  8.61 us
    pallas_call x2, Pallas kernels, run_expert(): pl.pallas_call(expert_kernel, in_specs=[pl.BlockSpec(memory_space=pltpu.S...  7.97 us
    pallas_call x1, Pallas kernels, mixer_tail(): pl.pallas_call(tail_kernel, in_specs=[pl.BlockSpec(memory_space=pltpu.SME...  3.17 us
  transfers between devices with their start and end apart: 31, of which 16 were waited for; matrix products, arithmetic and copies ran while one was open for 1% of the time, Pallas kernels for 9%

profile of v15, /device:TPU:0, one launch (start us, length us, event | category | flops | bytes accessed | tf_op | source)
XLA Modules:
  0.0 103.3 jit_solution(8445787903735841074)
XLA Ops:
  0.0 2.8 %own_state.1 = (bf16[8,144,128]{2,1,0:T(8,128)(2,1)}, f32[16,128]{1,0:T(8,128)S(1)}) custom-call(bf16[128,1024]{1,0:T(8,128)(2,1)} %x.3, f32[16,128]{1,0:T(8,128)} %bitcast.34, f32[16,128]{1,0:T(8,128)} %bitcast.36, bf16[128,128]{1,0:T(8,128)(2,1)} %b.3), custom_call_target="tpu_custom_call" | custom-call | tf_op jit(solution)/shard_map/own_state/pallas_call | solution.py:78
  2.8 7.3 %all-to-all-start = ((bf16[8,144,128]{2,1,0:T(8,128)(2,1)}), bf16[8,144,128]{2,1,0:T(8,128)(2,1)S(1)}, u32[]{:S(2)}, u32[]{:S(2)}) async-start(bf16[8,144,128]{2,1,0:T(8,128)(2,1)} %get-tuple-element.26), calls=%async_computation | async-start | bytes 589824 | tf_op jit(solution)/shard_map/all_to_all | solution.py:20
  10.7 1.7 %within_block.1.direct_in = f32[128,1024]{1,0:T(8,128)S(1)} custom-call(f32[16]{0:T(128)S(1)} %copy-done.1, bf16[128,1024]{1,0:T(8,128)(2,1)} %x.3, f32[16,128]{1,0:T(8,128)} %bitcast.35, f32[16,128]{1,0:T(8,128)S(1)} %get-tuple-element.25.cum_t.cum_in, bf16[128,128]{1,0:T(8,128)(2,1)} %b.3, bf16[128,128]{1,0:T(8,128)(2,1)} %c_in.1), custom_call_target="tpu_custom_call" | custom-call | flops 134217728 | bytes 786432 | tf_op jit(solution)/shard_map/within_block/pallas_call | solution.py:166
  12.4 7.3 %all-to-all-done.got = bf16[8,144,128]{2,1,0:T(8,128)(2,1)S(1)} async-done(((bf16[8,144,128]{2,1,0:T(8,128)(2,1)}), bf16[8,144,128]{2,1,0:T(8,128)(2,1)S(1)}, u32[]{:S(2)}, u32[]{:S(2)}) %all-to-all-start) | async-done | bytes 294944 | tf_op jit(solution)/shard_map/all_to_all | solution.py:20
  20.6 3.6 %all-to-all-start.1 = ((bf16[8,128,128]{2,1,0:T(8,128)(2,1)}), bf16[8,128,128]{2,1,0:T(8,128)(2,1)S(1)}, u32[]{:S(2)}, u32[]{:S(2)}) async-start(bf16[8,128,128]{2,1,0:T(8,128)(2,1)} %prefix.1), calls=%async_computation.1 | async-start | bytes 524288 | tf_op jit(solution)/shard_map/all_to_all | solution.py:20
  24.5 8.1 %all-to-all-done.1 = bf16[8,128,128]{2,1,0:T(8,128)(2,1)S(1)} async-done(((bf16[8,128,128]{2,1,0:T(8,128)(2,1)}), bf16[8,128,128]{2,1,0:T(8,128)(2,1)S(1)}, u32[]{:S(2)}, u32[]{:S(2)}) %all-to-all-start.1) | async-done | bytes 262176 | tf_op jit(solution)/shard_map/all_to_all | solution.py:20
  32.7 3.2 %mixer_tail.1 = (bf16[128,512]{1,0:T(8,128)(2,1)S(1)}, bf16[128,512]{1,0:T(8,128)(2,1)S(1)}, f32[128,512]{1,0:T(8,128)S(1)}, f32[128,512]{1,0:T(8,128)S(1)}) custom-call(s32[1]{0:T(128)} %bitcast.place_ref, bf16[128,128]{1,0:T(8,128)(2,1)} %c_in.1, f32[16,128]{1,0:T(8,128)S(1)} %get-tuple-element.25.cum_t.cum_in, f32[1,1024]{1,0:T(1,128)} %bitcast.37, ...), custom_call_target="tpu_custom_call" | custom-call | flops 536870912 | bytes 6029312 | tf_op jit(solution)/shard_map/mixer_tail/pallas_call | solution.py:248
  37.3 1.6 %collective-permute-start.2 = (bf16[128,512]{1,0:T(8,128)(2,1)S(1)}, bf16[128,512]{1,0:T(8,128)(2,1)S(1)}, u32[]{:S(2)}, u32[]{:S(2)}) collective-permute-start(bf16[128,512]{1,0:T(8,128)(2,1)S(1)} %add_convert_fusion.6), channel_id=1, source_target_pairs={{0,2},{1,3},{2,0},{3,1},{4,6},{5,7},{6,4},{7,5},{8,10},{9,11},{10,... | collective-permute-start | bytes 393224 | tf_op jit(solution)/shard_map/ppermute | solution.py:16
  39.0 3.9 %collective-permute-done.2 = bf16[128,512]{1,0:T(8,128)(2,1)S(1)} collective-permute-done((bf16[128,512]{1,0:T(8,128)(2,1)S(1)}, bf16[128,512]{1,0:T(8,128)(2,1)S(1)}, u32[]{:S(2)}, u32[]{:S(2)}) %collective-permute-start.2) | collective-permute-done | bytes 131104 | tf_op jit(solution)/shard_map/ppermute | solution.py:16
  43.4 1.2 %collective-permute-start.3 = (bf16[64,512]{1,0:T(8,128)(2,1)S(1)}, bf16[64,512]{1,0:T(8,128)(2,1)S(1)}, u32[]{:S(2)}, u32[]{:S(2)}) collective-permute-start(bf16[64,512]{1,0:T(8,128)(2,1)S(1)} %get-tuple-element.51), channel_id=1, source_target_pairs={{0,24},{4,28},{8,16},{12,20},{16,8},{20,12},{24,0},{28,4},{1,25},{... | collective-permute-start | bytes 196616 | tf_op jit(solution)/shard_map/ppermute | solution.py:117
  44.6 1.7 %collective-permute-start.4 = (bf16[64,512]{1,0:T(8,128)(2,1)S(1)}, bf16[64,512]{1,0:T(8,128)(2,1)S(1)}, u32[]{:S(2)}, u32[]{:S(2)}) collective-permute-start(bf16[64,512]{1,0:T(8,128)(2,1)S(1)} %get-tuple-element.50), channel_id=1, source_target_pairs={{0,4},{4,0},{8,12},{12,8},{16,20},{20,16},{24,28},{28,24},{1,5},{5... | collective-permute-start | bytes 196616 | tf_op jit(solution)/shard_map/ppermute | solution.py:117
  46.4 2.6 %collective-permute-start.6 = (bf16[64,512]{1,0:T(8,128)(2,1)S(1)}, bf16[64,512]{1,0:T(8,128)(2,1)S(1)}, u32[]{:S(2)}, u32[]{:S(2)}) collective-permute-start(bf16[64,512]{1,0:T(8,128)(2,1)S(1)} %get-tuple-element.48), channel_id=1, source_target_pairs={{0,20},{4,16},{8,28},{12,24},{16,4},{20,0},{24,12},{28,8},{1,21},{... | collective-permute-start | bytes 196616 | tf_op jit(solution)/shard_map/ppermute | solution.py:117
  49.8 3.5 %collective-permute-done.5 = bf16[64,512]{1,0:T(8,128)(2,1)S(1)} collective-permute-done((bf16[64,512]{1,0:T(8,128)(2,1)S(1)}, bf16[64,512]{1,0:T(8,128)(2,1)S(1)}, u32[]{:S(2)}, u32[]{:S(2)}) %collective-permute-start.5) | collective-permute-done | bytes 65568 | tf_op jit(solution)/shard_map/ppermute | solution.py:117
  53.3 1.8 %collective-permute-done.6 = bf16[64,512]{1,0:T(8,128)(2,1)S(1)} collective-permute-done((bf16[64,512]{1,0:T(8,128)(2,1)S(1)}, bf16[64,512]{1,0:T(8,128)(2,1)S(1)}, u32[]{:S(2)}, u32[]{:S(2)}) %collective-permute-start.6) | collective-permute-done | bytes 65568 | tf_op jit(solution)/shard_map/ppermute | solution.py:117
  55.1 1.5 %collective-permute-start.8 = (bf16[256,512]{1,0:T(8,128)(2,1)S(1)}, bf16[256,512]{1,0:T(8,128)(2,1)S(1)}, u32[]{:S(2)}, u32[]{:S(2)}) collective-permute-start(bf16[256,512]{1,0:T(8,128)(2,1)S(1)} %constant_dynamic-update-slice_fusion.own_in), channel_id=1, source_target_pairs={{0,2},{1,3},{2,0},{3,1},{4,6},{5,7},{6,4},{7,5},{8,10},{9,11},{10,... | collective-permute-start | bytes 786440 | tf_op jit(solution)/shard_map/ppermute | solution.py:16
  56.6 1.9 %collective-permute-start.16 = (bf16[64,512]{1,0:T(8,128)(2,1)S(1)}, bf16[64,512]{1,0:T(8,128)(2,1)S(1)}, u32[]{:S(2)}, u32[]{:S(2)}) collective-permute-start(bf16[64,512]{1,0:T(8,128)(2,1)S(1)} %get-tuple-element.47), channel_id=1, source_target_pairs={{0,28},{4,24},{8,20},{12,16},{16,12},{20,8},{24,4},{28,0},{1,29},{... | collective-permute-start | bytes 196616 | tf_op jit(solution)/shard_map/ppermute | solution.py:117
  58.5 2.9 %collective-permute-start.18 = (bf16[64,512]{1,0:T(8,128)(2,1)S(1)}, bf16[64,512]{1,0:T(8,128)(2,1)S(1)}, u32[]{:S(2)}, u32[]{:S(2)}) collective-permute-start(bf16[64,512]{1,0:T(8,128)(2,1)S(1)} %get-tuple-element.45), channel_id=1, source_target_pairs={{0,12},{4,8},{8,4},{12,0},{16,28},{20,24},{24,20},{28,16},{1,13},{... | collective-permute-start | bytes 196616 | tf_op jit(solution)/shard_map/ppermute | solution.py:117
  62.5 1.2 %collective-permute-done.16 = bf16[64,512]{1,0:T(8,128)(2,1)S(1)} collective-permute-done((bf16[64,512]{1,0:T(8,128)(2,1)S(1)}, bf16[64,512]{1,0:T(8,128)(2,1)S(1)}, u32[]{:S(2)}, u32[]{:S(2)}) %collective-permute-start.16) | collective-permute-done | bytes 65568 | tf_op jit(solution)/shard_map/ppermute | solution.py:117
  63.7 1.3 %collective-permute-done.18 = bf16[64,512]{1,0:T(8,128)(2,1)S(1)} collective-permute-done((bf16[64,512]{1,0:T(8,128)(2,1)S(1)}, bf16[64,512]{1,0:T(8,128)(2,1)S(1)}, u32[]{:S(2)}, u32[]{:S(2)}) %collective-permute-start.18) | collective-permute-done | bytes 65568 | tf_op jit(solution)/shard_map/ppermute | solution.py:117
  65.5 4.0 %expert.2 = (bf16[256,512]{1,0:T(8,128)(2,1)S(1)}, bf16[256,512]{1,0:T(8,128)(2,1)S(1)}, bf16[256,512]{1,0:T(8,128)(2,1)S(1)}, bf16[256,512]{1,0:T(8,128)(2,1)S(1)}) custom-call(s32[1]{0:T(128)} %bitcast.place_ref, f32[1,2048]{1,0:T(1,128)} %bitcast.32, bf16[256,512]{1,0:T(8,128)(2,1)S(1)} %constant_dynamic-update-slice_fusion.own_in, ...), custom_call_target="tpu_custom_call" | custom-call | flops 1 | bytes 1 | tf_op jit(solution)/shard_map/expert/pallas_call | solution.py:317
  70.1 1.3 %collective-permute-done.20.far_in = bf16[256,512]{1,0:T(8,128)(2,1)S(1)} collective-permute-done((bf16[256,512]{1,0:T(8,128)(2,1)S(1)}, bf16[256,512]{1,0:T(8,128)(2,1)S(1)}, u32[]{:S(2)}, u32[]{:S(2)}) %collective-permute-start.20) | collective-permute-done | bytes 262176 | tf_op jit(solution)/shard_map/ppermute | solution.py:16
  71.4 1.5 %collective-permute-start.12 = (bf16[256,512]{1,0:T(8,128)(2,1)S(1)}, bf16[256,512]{1,0:T(8,128)(2,1)S(1)}, u32[]{:S(2)}, u32[]{:S(2)}) collective-permute-start(bf16[256,512]{1,0:T(8,128)(2,1)S(1)} %add_convert_fusion.3), channel_id=1, source_target_pairs={{0,2},{1,3},{2,0},{3,1},{4,6},{5,7},{6,4},{7,5},{8,10},{9,11},{10,... | collective-permute-start | bytes 786440 | tf_op jit(solution)/shard_map/ppermute | solution.py:16
  73.2 4.0 %expert.3 = (bf16[256,512]{1,0:T(8,128)(2,1)S(1)}, bf16[256,512]{1,0:T(8,128)(2,1)S(1)}, bf16[256,512]{1,0:T(8,128)(2,1)S(1)}, bf16[256,512]{1,0:T(8,128)(2,1)S(1)}) custom-call(s32[1]{0:T(128)} %bitcast.place_ref, f32[1,2048]{1,0:T(1,128)} %bitcast.33, bf16[256,512]{1,0:T(8,128)(2,1)S(1)} %constant_dynamic-update-slice_fusion.4.own_in, ...), custom_call_target="tpu_custom_call" | custom-call | flops 1 | bytes 1 | tf_op jit(solution)/shard_map/expert/pallas_call | solution.py:317
  77.5 2.7 %collective-permute-done.12 = bf16[256,512]{1,0:T(8,128)(2,1)S(1)} collective-permute-done((bf16[256,512]{1,0:T(8,128)(2,1)S(1)}, bf16[256,512]{1,0:T(8,128)(2,1)S(1)}, u32[]{:S(2)}, u32[]{:S(2)}) %collective-permute-start.12) | collective-permute-done | bytes 262176 | tf_op jit(solution)/shard_map/ppermute | solution.py:16
  80.3 1.8 %collective-permute-start.13 = (bf16[64,512]{1,0:T(8,128)(2,1)S(1)}, bf16[64,512]{1,0:T(8,128)(2,1)S(1)}, u32[]{:S(2)}, u32[]{:S(2)}) collective-permute-start(bf16[64,512]{1,0:T(8,128)(2,1)S(1)} %get-tuple-element.59), channel_id=1, source_target_pairs={{0,4},{4,0},{8,12},{12,8},{16,20},{20,16},{24,28},{28,24},{1,5},{5... | collective-permute-start | bytes 196616 | tf_op jit(solution)/shard_map/ppermute | solution.py:117
  82.2 1.7 %collective-permute-start.24 = (bf16[256,512]{1,0:T(8,128)(2,1)S(1)}, bf16[256,512]{1,0:T(8,128)(2,1)S(1)}, u32[]{:S(2)}, u32[]{:S(2)}) collective-permute-start(bf16[256,512]{1,0:T(8,128)(2,1)S(1)} %add_convert_fusion.1), channel_id=1, source_target_pairs={{0,2},{1,3},{2,0},{3,1},{4,6},{5,7},{6,4},{7,5},{8,10},{9,11},{10,... | collective-permute-start | bytes 786440 | tf_op jit(solution)/shard_map/ppermute | solution.py:16
  84.1 2.3 %collective-permute-start.15 = (bf16[64,512]{1,0:T(8,128)(2,1)S(1)}, bf16[64,512]{1,0:T(8,128)(2,1)S(1)}, u32[]{:S(2)}, u32[]{:S(2)}) collective-permute-start(bf16[64,512]{1,0:T(8,128)(2,1)S(1)} %get-tuple-element.57), channel_id=1, source_target_pairs={{0,20},{4,16},{8,28},{12,24},{16,4},{20,0},{24,12},{28,8},{1,21},{... | collective-permute-start | bytes 196616 | tf_op jit(solution)/shard_map/ppermute | solution.py:117
  86.4 4.9 %collective-permute-done.14 = bf16[64,512]{1,0:T(8,128)(2,1)S(1)} collective-permute-done((bf16[64,512]{1,0:T(8,128)(2,1)S(1)}, bf16[64,512]{1,0:T(8,128)(2,1)S(1)}, u32[]{:S(2)}, u32[]{:S(2)}) %collective-permute-start.14) | collective-permute-done | bytes 65568 | tf_op jit(solution)/shard_map/ppermute | solution.py:117
  91.4 1.8 %collective-permute-start.25 = (bf16[64,512]{1,0:T(8,128)(2,1)S(1)}, bf16[64,512]{1,0:T(8,128)(2,1)S(1)}, u32[]{:S(2)}, u32[]{:S(2)}) collective-permute-start(bf16[64,512]{1,0:T(8,128)(2,1)S(1)} %get-tuple-element.56), channel_id=1, source_target_pairs={{0,24},{4,28},{8,16},{12,20},{16,8},{20,12},{24,0},{28,4},{1,25},{... | collective-permute-start | bytes 196616 | tf_op jit(solution)/shard_map/ppermute | solution.py:117
  93.3 2.2 %collective-permute-start.26 = (bf16[64,512]{1,0:T(8,128)(2,1)S(1)}, bf16[64,512]{1,0:T(8,128)(2,1)S(1)}, u32[]{:S(2)}, u32[]{:S(2)}) collective-permute-start(bf16[64,512]{1,0:T(8,128)(2,1)S(1)} %get-tuple-element.55), channel_id=1, source_target_pairs={{0,28},{4,24},{8,20},{12,16},{16,12},{20,8},{24,4},{28,0},{1,29},{... | collective-permute-start | bytes 196616 | tf_op jit(solution)/shard_map/ppermute | solution.py:117
  95.4 2.9 %collective-permute-start.28 = (bf16[64,512]{1,0:T(8,128)(2,1)S(1)}, bf16[64,512]{1,0:T(8,128)(2,1)S(1)}, u32[]{:S(2)}, u32[]{:S(2)}) collective-permute-start(bf16[64,512]{1,0:T(8,128)(2,1)S(1)} %get-tuple-element.53), channel_id=1, source_target_pairs={{0,12},{4,8},{8,4},{12,0},{16,28},{20,24},{24,20},{28,16},{1,13},{... | collective-permute-start | bytes 196616 | tf_op jit(solution)/shard_map/ppermute | solution.py:117
  98.4 2.0 %collective-permute-done.26 = bf16[64,512]{1,0:T(8,128)(2,1)S(1)} collective-permute-done((bf16[64,512]{1,0:T(8,128)(2,1)S(1)}, bf16[64,512]{1,0:T(8,128)(2,1)S(1)}, u32[]{:S(2)}, u32[]{:S(2)}) %collective-permute-start.26) | collective-permute-done | bytes 65568 | tf_op jit(solution)/shard_map/ppermute | solution.py:117
  (75 shorter events, 11.0 us)
Async XLA Ops:
  0.0 24.4 %copy-start.2 = (f32[128,2]{0,1:T(2,128)S(1)}, f32[128,2]{0,1:T(2,128)}, u32[]{:S(2)}) copy-start(f32[128,2]{0,1:T(2,128)} %param.30) | copy-start | bytes 3076
  2.8 16.9 %all-to-all-start = ((bf16[8,144,128]{2,1,0:T(8,128)(2,1)}), bf16[8,144,128]{2,1,0:T(8,128)(2,1)S(1)}, u32[]{:S(2)}, u32[]{:S(2)}) async-start(bf16[8,144,128]{2,1,0:T(8,128)(2,1)} %get-tuple-element.26), calls=%async_computation | async-start | bytes 589824 | tf_op jit(solution)/shard_map/all_to_all | solution.py:20
  20.6 12.1 %all-to-all-start.1 = ((bf16[8,128,128]{2,1,0:T(8,128)(2,1)}), bf16[8,128,128]{2,1,0:T(8,128)(2,1)S(1)}, u32[]{:S(2)}, u32[]{:S(2)}) async-start(bf16[8,128,128]{2,1,0:T(8,128)(2,1)} %prefix.1), calls=%async_computation.1 | async-start | bytes 524288 | tf_op jit(solution)/shard_map/all_to_all | solution.py:20
  35.9 1.4 %collective-permute-start.1 = (bf16[128,512]{1,0:T(8,128)(2,1)S(1)}, bf16[128,512]{1,0:T(8,128)(2,1)S(1)}, u32[]{:S(2)}, u32[]{:S(2)}) collective-permute-start(bf16[128,512]{1,0:T(8,128)(2,1)S(1)} %get-tuple-element.31), channel_id=1, source_target_pairs={{0,1},{1,0},{2,3},{3,2},{4,5},{5,4},{6,7},{7,6},{8,9},{9,8},{10,11... | collective-permute-start | bytes 393224 | tf_op jit(solution)/shard_map/ppermute | solution.py:16
  35.9 3.1 %collective-permute-start = (bf16[128,512]{1,0:T(8,128)(2,1)S(1)}, bf16[128,512]{1,0:T(8,128)(2,1)S(1)}, u32[]{:S(2)}, u32[]{:S(2)}) collective-permute-start(bf16[128,512]{1,0:T(8,128)(2,1)S(1)} %get-tuple-element.29), channel_id=1, source_target_pairs={{0,1},{1,0},{2,3},{3,2},{4,5},{5,4},{6,7},{7,6},{8,9},{9,8},{10,11... | collective-permute-start | bytes 393224 | tf_op jit(solution)/shard_map/ppermute | solution.py:16
  37.3 5.6 %collective-permute-start.2 = (bf16[128,512]{1,0:T(8,128)(2,1)S(1)}, bf16[128,512]{1,0:T(8,128)(2,1)S(1)}, u32[]{:S(2)}, u32[]{:S(2)}) collective-permute-start(bf16[128,512]{1,0:T(8,128)(2,1)S(1)} %add_convert_fusion.6), channel_id=1, source_target_pairs={{0,2},{1,3},{2,0},{3,1},{4,6},{5,7},{6,4},{7,5},{8,10},{9,11},{10,... | collective-permute-start | bytes 393224 | tf_op jit(solution)/shard_map/ppermute | solution.py:16
  43.4 6.4 %collective-permute-start.3 = (bf16[64,512]{1,0:T(8,128)(2,1)S(1)}, bf16[64,512]{1,0:T(8,128)(2,1)S(1)}, u32[]{:S(2)}, u32[]{:S(2)}) collective-permute-start(bf16[64,512]{1,0:T(8,128)(2,1)S(1)} %get-tuple-element.51), channel_id=1, source_target_pairs={{0,24},{4,28},{8,16},{12,20},{16,8},{20,12},{24,0},{28,4},{1,25},{... | collective-permute-start | bytes 196616 | tf_op jit(solution)/shard_map/ppermute | solution.py:117
  44.6 5.2 %collective-permute-start.4 = (bf16[64,512]{1,0:T(8,128)(2,1)S(1)}, bf16[64,512]{1,0:T(8,128)(2,1)S(1)}, u32[]{:S(2)}, u32[]{:S(2)}) collective-permute-start(bf16[64,512]{1,0:T(8,128)(2,1)S(1)} %get-tuple-element.50), channel_id=1, source_target_pairs={{0,4},{4,0},{8,12},{12,8},{16,20},{20,16},{24,28},{28,24},{1,5},{5... | collective-permute-start | bytes 196616 | tf_op jit(solution)/shard_map/ppermute | solution.py:117
  46.3 6.9 %collective-permute-start.5 = (bf16[64,512]{1,0:T(8,128)(2,1)S(1)}, bf16[64,512]{1,0:T(8,128)(2,1)S(1)}, u32[]{:S(2)}, u32[]{:S(2)}) collective-permute-start(bf16[64,512]{1,0:T(8,128)(2,1)S(1)} %get-tuple-element.49), channel_id=1, source_target_pairs={{0,16},{4,20},{8,24},{12,28},{16,0},{20,4},{24,8},{28,12},{1,17},{... | collective-permute-start | bytes 196616 | tf_op jit(solution)/shard_map/ppermute | solution.py:117
  46.4 8.7 %collective-permute-start.6 = (bf16[64,512]{1,0:T(8,128)(2,1)S(1)}, bf16[64,512]{1,0:T(8,128)(2,1)S(1)}, u32[]{:S(2)}, u32[]{:S(2)}) collective-permute-start(bf16[64,512]{1,0:T(8,128)(2,1)S(1)} %get-tuple-element.48), channel_id=1, source_target_pairs={{0,20},{4,16},{8,28},{12,24},{16,4},{20,0},{24,12},{28,8},{1,21},{... | collective-permute-start | bytes 196616 | tf_op jit(solution)/shard_map/ppermute | solution.py:117
  55.1 7.4 %collective-permute-start.8 = (bf16[256,512]{1,0:T(8,128)(2,1)S(1)}, bf16[256,512]{1,0:T(8,128)(2,1)S(1)}, u32[]{:S(2)}, u32[]{:S(2)}) collective-permute-start(bf16[256,512]{1,0:T(8,128)(2,1)S(1)} %constant_dynamic-update-slice_fusion.own_in), channel_id=1, source_target_pairs={{0,2},{1,3},{2,0},{3,1},{4,6},{5,7},{6,4},{7,5},{8,10},{9,11},{10,... | collective-permute-start | bytes 786440 | tf_op jit(solution)/shard_map/ppermute | solution.py:16
  56.6 7.0 %collective-permute-start.16 = (bf16[64,512]{1,0:T(8,128)(2,1)S(1)}, bf16[64,512]{1,0:T(8,128)(2,1)S(1)}, u32[]{:S(2)}, u32[]{:S(2)}) collective-permute-start(bf16[64,512]{1,0:T(8,128)(2,1)S(1)} %get-tuple-element.47), channel_id=1, source_target_pairs={{0,28},{4,24},{8,20},{12,16},{16,12},{20,8},{24,4},{28,0},{1,29},{... | collective-permute-start | bytes 196616 | tf_op jit(solution)/shard_map/ppermute | solution.py:117
  58.5 5.1 %collective-permute-start.17 = (bf16[64,512]{1,0:T(8,128)(2,1)S(1)}, bf16[64,512]{1,0:T(8,128)(2,1)S(1)}, u32[]{:S(2)}, u32[]{:S(2)}) collective-permute-start(bf16[64,512]{1,0:T(8,128)(2,1)S(1)} %get-tuple-element.46), channel_id=1, source_target_pairs={{0,8},{4,12},{8,0},{12,4},{16,24},{20,28},{24,16},{28,20},{1,9},{5... | collective-permute-start | bytes 196616 | tf_op jit(solution)/shard_map/ppermute | solution.py:117
  58.5 6.5 %collective-permute-start.18 = (bf16[64,512]{1,0:T(8,128)(2,1)S(1)}, bf16[64,512]{1,0:T(8,128)(2,1)S(1)}, u32[]{:S(2)}, u32[]{:S(2)}) collective-permute-start(bf16[64,512]{1,0:T(8,128)(2,1)S(1)} %get-tuple-element.45), channel_id=1, source_target_pairs={{0,12},{4,8},{8,4},{12,0},{16,28},{20,24},{24,20},{28,16},{1,13},{... | collective-permute-start | bytes 196616 | tf_op jit(solution)/shard_map/ppermute | solution.py:117
  61.4 4.1 %collective-permute-start.7 = (bf16[256,512]{1,0:T(8,128)(2,1)S(1)}, bf16[256,512]{1,0:T(8,128)(2,1)S(1)}, u32[]{:S(2)}, u32[]{:S(2)}) collective-permute-start(bf16[256,512]{1,0:T(8,128)(2,1)S(1)} %constant_dynamic-update-slice_fusion.own_in), channel_id=1, source_target_pairs={{0,1},{1,0},{2,3},{3,2},{4,5},{5,4},{6,7},{7,6},{8,9},{9,8},{10,11... | collective-permute-start | bytes 786440 | tf_op jit(solution)/shard_map/ppermute | solution.py:16
  62.5 3.0 %collective-permute-start.9 = (bf16[256,512]{1,0:T(8,128)(2,1)S(1)}, bf16[256,512]{1,0:T(8,128)(2,1)S(1)}, u32[]{:S(2)}, u32[]{:S(2)}) collective-permute-start(bf16[256,512]{1,0:T(8,128)(2,1)S(1)} %collective-permute-done.8.far_in), channel_id=1, source_target_pairs={{0,1},{1,0},{2,3},{3,2},{4,5},{5,4},{6,7},{7,6},{8,9},{9,8},{10,11... | collective-permute-start | bytes 786440 | tf_op jit(solution)/shard_map/ppermute | solution.py:16
  65.0 6.4 %collective-permute-start.20 = (bf16[256,512]{1,0:T(8,128)(2,1)S(1)}, bf16[256,512]{1,0:T(8,128)(2,1)S(1)}, u32[]{:S(2)}, u32[]{:S(2)}) collective-permute-start(bf16[256,512]{1,0:T(8,128)(2,1)S(1)} %constant_dynamic-update-slice_fusion.4.own_in), channel_id=1, source_target_pairs={{0,2},{1,3},{2,0},{3,1},{4,6},{5,7},{6,4},{7,5},{8,10},{9,11},{10,... | collective-permute-start | bytes 786440 | tf_op jit(solution)/shard_map/ppermute | solution.py:16
  69.5 1.9 %collective-permute-start.10 = (bf16[256,512]{1,0:T(8,128)(2,1)S(1)}, bf16[256,512]{1,0:T(8,128)(2,1)S(1)}, u32[]{:S(2)}, u32[]{:S(2)}) collective-permute-start(bf16[256,512]{1,0:T(8,128)(2,1)S(1)} %get-tuple-element.36), channel_id=1, source_target_pairs={{0,1},{1,0},{2,3},{3,2},{4,5},{5,4},{6,7},{7,6},{8,9},{9,8},{10,11... | collective-permute-start | bytes 786440 | tf_op jit(solution)/shard_map/ppermute | solution.py:16
  69.6 3.6 %collective-permute-start.19 = (bf16[256,512]{1,0:T(8,128)(2,1)S(1)}, bf16[256,512]{1,0:T(8,128)(2,1)S(1)}, u32[]{:S(2)}, u32[]{:S(2)}) collective-permute-start(bf16[256,512]{1,0:T(8,128)(2,1)S(1)} %constant_dynamic-update-slice_fusion.4.own_in), channel_id=1, source_target_pairs={{0,1},{1,0},{2,3},{3,2},{4,5},{5,4},{6,7},{7,6},{8,9},{9,8},{10,11... | collective-permute-start | bytes 786440 | tf_op jit(solution)/shard_map/ppermute | solution.py:16
  71.3 1.8 %collective-permute-start.21 = (bf16[256,512]{1,0:T(8,128)(2,1)S(1)}, bf16[256,512]{1,0:T(8,128)(2,1)S(1)}, u32[]{:S(2)}, u32[]{:S(2)}) collective-permute-start(bf16[256,512]{1,0:T(8,128)(2,1)S(1)} %collective-permute-done.20.far_in), channel_id=1, source_target_pairs={{0,1},{1,0},{2,3},{3,2},{4,5},{5,4},{6,7},{7,6},{8,9},{9,8},{10,11... | collective-permute-start | bytes 786440 | tf_op jit(solution)/shard_map/ppermute | solution.py:16
  71.4 8.8 %collective-permute-start.12 = (bf16[256,512]{1,0:T(8,128)(2,1)S(1)}, bf16[256,512]{1,0:T(8,128)(2,1)S(1)}, u32[]{:S(2)}, u32[]{:S(2)}) collective-permute-start(bf16[256,512]{1,0:T(8,128)(2,1)S(1)} %add_convert_fusion.3), channel_id=1, source_target_pairs={{0,2},{1,3},{2,0},{3,1},{4,6},{5,7},{6,4},{7,5},{8,10},{9,11},{10,... | collective-permute-start | bytes 786440 | tf_op jit(solution)/shard_map/ppermute | solution.py:16
  73.0 7.3 %collective-permute-start.11 = (bf16[256,512]{1,0:T(8,128)(2,1)S(1)}, bf16[256,512]{1,0:T(8,128)(2,1)S(1)}, u32[]{:S(2)}, u32[]{:S(2)}) collective-permute-start(bf16[256,512]{1,0:T(8,128)(2,1)S(1)} %get-tuple-element.37), channel_id=1, source_target_pairs={{0,1},{1,0},{2,3},{3,2},{4,5},{5,4},{6,7},{7,6},{8,9},{9,8},{10,11... | collective-permute-start | bytes 786440 | tf_op jit(solution)/shard_map/ppermute | solution.py:16
  77.2 4.9 %collective-permute-start.22 = (bf16[256,512]{1,0:T(8,128)(2,1)S(1)}, bf16[256,512]{1,0:T(8,128)(2,1)S(1)}, u32[]{:S(2)}, u32[]{:S(2)}) collective-permute-start(bf16[256,512]{1,0:T(8,128)(2,1)S(1)} %get-tuple-element.43), channel_id=1, source_target_pairs={{0,1},{1,0},{2,3},{3,2},{4,5},{5,4},{6,7},{7,6},{8,9},{9,8},{10,11... | collective-permute-start | bytes 786440 | tf_op jit(solution)/shard_map/ppermute | solution.py:16
  80.3 6.1 %collective-permute-start.13 = (bf16[64,512]{1,0:T(8,128)(2,1)S(1)}, bf16[64,512]{1,0:T(8,128)(2,1)S(1)}, u32[]{:S(2)}, u32[]{:S(2)}) collective-permute-start(bf16[64,512]{1,0:T(8,128)(2,1)S(1)} %get-tuple-element.59), channel_id=1, source_target_pairs={{0,4},{4,0},{8,12},{12,8},{16,20},{20,16},{24,28},{28,24},{1,5},{5... | collective-permute-start | bytes 196616 | tf_op jit(solution)/shard_map/ppermute | solution.py:117
  82.2 9.1 %collective-permute-start.24 = (bf16[256,512]{1,0:T(8,128)(2,1)S(1)}, bf16[256,512]{1,0:T(8,128)(2,1)S(1)}, u32[]{:S(2)}, u32[]{:S(2)}) collective-permute-start(bf16[256,512]{1,0:T(8,128)(2,1)S(1)} %add_convert_fusion.1), channel_id=1, source_target_pairs={{0,2},{1,3},{2,0},{3,1},{4,6},{5,7},{6,4},{7,5},{8,10},{9,11},{10,... | collective-permute-start | bytes 786440 | tf_op jit(solution)/shard_map/ppermute | solution.py:16
  84.0 7.3 %collective-permute-start.23 = (bf16[256,512]{1,0:T(8,128)(2,1)S(1)}, bf16[256,512]{1,0:T(8,128)(2,1)S(1)}, u32[]{:S(2)}, u32[]{:S(2)}) collective-permute-start(bf16[256,512]{1,0:T(8,128)(2,1)S(1)} %get-tuple-element.44), channel_id=1, source_target_pairs={{0,1},{1,0},{2,3},{3,2},{4,5},{5,4},{6,7},{7,6},{8,9},{9,8},{10,11... | collective-permute-start | bytes 786440 | tf_op jit(solution)/shard_map/ppermute | solution.py:16
  84.0 7.3 %collective-permute-start.14 = (bf16[64,512]{1,0:T(8,128)(2,1)S(1)}, bf16[64,512]{1,0:T(8,128)(2,1)S(1)}, u32[]{:S(2)}, u32[]{:S(2)}) collective-permute-start(bf16[64,512]{1,0:T(8,128)(2,1)S(1)} %get-tuple-element.58), channel_id=1, source_target_pairs={{0,16},{4,20},{8,24},{12,28},{16,0},{20,4},{24,8},{28,12},{1,17},{... | collective-permute-start | bytes 196616 | tf_op jit(solution)/shard_map/ppermute | solution.py:117
  84.1 9.2 %collective-permute-start.15 = (bf16[64,512]{1,0:T(8,128)(2,1)S(1)}, bf16[64,512]{1,0:T(8,128)(2,1)S(1)}, u32[]{:S(2)}, u32[]{:S(2)}) collective-permute-start(bf16[64,512]{1,0:T(8,128)(2,1)S(1)} %get-tuple-element.57), channel_id=1, source_target_pairs={{0,20},{4,16},{8,28},{12,24},{16,4},{20,0},{24,12},{28,8},{1,21},{... | collective-permute-start | bytes 196616 | tf_op jit(solution)/shard_map/ppermute | solution.py:117
  91.4 6.9 %collective-permute-start.25 = (bf16[64,512]{1,0:T(8,128)(2,1)S(1)}, bf16[64,512]{1,0:T(8,128)(2,1)S(1)}, u32[]{:S(2)}, u32[]{:S(2)}) collective-permute-start(bf16[64,512]{1,0:T(8,128)(2,1)S(1)} %get-tuple-element.56), channel_id=1, source_target_pairs={{0,24},{4,28},{8,16},{12,20},{16,8},{20,12},{24,0},{28,4},{1,25},{... | collective-permute-start | bytes 196616 | tf_op jit(solution)/shard_map/ppermute | solution.py:117
  93.3 7.1 %collective-permute-start.26 = (bf16[64,512]{1,0:T(8,128)(2,1)S(1)}, bf16[64,512]{1,0:T(8,128)(2,1)S(1)}, u32[]{:S(2)}, u32[]{:S(2)}) collective-permute-start(bf16[64,512]{1,0:T(8,128)(2,1)S(1)} %get-tuple-element.55), channel_id=1, source_target_pairs={{0,28},{4,24},{8,20},{12,16},{16,12},{20,8},{24,4},{28,0},{1,29},{... | collective-permute-start | bytes 196616 | tf_op jit(solution)/shard_map/ppermute | solution.py:117
  95.4 5.7 %collective-permute-start.27 = (bf16[64,512]{1,0:T(8,128)(2,1)S(1)}, bf16[64,512]{1,0:T(8,128)(2,1)S(1)}, u32[]{:S(2)}, u32[]{:S(2)}) collective-permute-start(bf16[64,512]{1,0:T(8,128)(2,1)S(1)} %get-tuple-element.54), channel_id=1, source_target_pairs={{0,8},{4,12},{8,0},{12,4},{16,24},{20,28},{24,16},{28,20},{1,9},{5... | collective-permute-start | bytes 196616 | tf_op jit(solution)/shard_map/ppermute | solution.py:117
  95.4 6.8 %collective-permute-start.28 = (bf16[64,512]{1,0:T(8,128)(2,1)S(1)}, bf16[64,512]{1,0:T(8,128)(2,1)S(1)}, u32[]{:S(2)}, u32[]{:S(2)}) collective-permute-start(bf16[64,512]{1,0:T(8,128)(2,1)S(1)} %get-tuple-element.53), channel_id=1, source_target_pairs={{0,12},{4,8},{8,4},{12,0},{16,28},{20,24},{24,20},{28,16},{1,13},{... | collective-permute-start | bytes 196616 | tf_op jit(solution)/shard_map/ppermute | solution.py:117
  (3 other events, 37.2 us)
